TPU v7x, 32 devices: a whole 2x2x4 slice. The times are simulated.
32 devices in a mesh: wide: 16 (over z, x, core), dp: 2 (over y).
Axes of the slice: x: 2, y: 2, z: 4, core: 2. Of those that a mesh axis runs over, the one named last changes fastest.
Arguments:
- queries: bfloat16 [16384, 4096], P(('wide', 'dp')), may hold values from -20 to 20
- teacher_queries: bfloat16 [16384, 4096], P(('wide', 'dp')), may hold values from -6 to 6
- passages: bfloat16 [256, 4096], P('wide'), may hold values from -6 to 6
- bank_student: bfloat16 [4096, 4096], P('wide'), may hold values from -6 to 6
- bank_teacher: bfloat16 [4096, 4096], P('wide'), may hold values from -6 to 6
- owner: int32 [2], P('dp'), may hold values from 0 to 15
- positives: int32 [16384], P(('wide', 'dp')), may hold values from 0 to 255
- keep_mask: int32 [16384, 256], P(('wide', 'dp')), may hold values 0 or 1
Outputs:
- row_loss: float32 [16384], P(('wide', 'dp'))
- query_grad: bfloat16 [16384, 4096], P(('wide', 'dp'))
- passage_grad: float32 [256, 4096], P('wide')
All inputs are finite; a program needn't handle non-finite values. No bound on the sum of `keep_mask` on one device may be relied on, other than what follows from the above.
Results may differ from a plain program's by a relative error of at most 0.0033.
Values may be sent and summed in bfloat16 or wider, within the bound.
No kernel may reach another device: no remote copies, remote signals or barrier semaphores. Data moves between devices by JAX's collectives and lax.ppermute only.
A program may use at most 128 MiB of HBM per device.

v0:
```python
import math

import jax
import jax.numpy as jnp
from jax import lax
from jax.sharding import PartitionSpec as P

E = 4096


def broadcast(block, axis, holder):
    block = jnp.where(lax.axis_index(axis) == holder, block, jnp.zeros_like(block))
    return lax.psum(block, axis)


def body(
    queries, teacher_queries, passages, bank_student, bank_teacher, owner, positives, keep_mask
):
    scale = 2.0 / math.sqrt(E)
    block = passages.shape[0]
    cycle_size = lax.axis_size("wide")
    total_rows = block * cycle_size
    pool_s, pool_t = (
        broadcast(bank_student, "wide", owner[0]),
        broadcast(bank_teacher, "wide", owner[0]),
    )
    zq = jnp.dot(queries, pool_s.T, preferred_element_type=jnp.float32) * scale
    tt = jnp.dot(teacher_queries, pool_t.T, preferred_element_type=jnp.float32) * scale
    weight = keep_mask.astype(jnp.float32) * jax.nn.sigmoid(-tt)
    pool_top = jnp.max(zq, axis=1)
    pool_total = jnp.sum(weight * jnp.exp(zq - pool_top[:, None]), axis=1)
    piece = lax.all_gather(passages, "wide", axis=0, tiled=True)
    run_top = pool_top
    run_total = pool_total
    scores = jnp.dot(queries, piece.T, preferred_element_type=jnp.float32) * scale
    new_top = jnp.maximum(run_top, jnp.max(scores, axis=1))
    run_total = run_total * jnp.exp(run_top - new_top) + jnp.sum(
        jnp.exp(scores - new_top[:, None]), axis=1
    )
    score_store = scores
    passage_store = piece
    run_top, run_total, score_store, passage_store = (
        new_top,
        run_total,
        score_store,
        passage_store,
    )
    lse = run_top + jnp.log(run_total)
    columns = jnp.arange(total_rows, dtype=jnp.int32)
    hit = (columns[None, :] == positives[:, None]).astype(jnp.float32)
    row_loss = lse - jnp.sum(score_store * hit, axis=1)
    grad_p = (jnp.exp(score_store - lse[:, None]) - hit).astype(jnp.bfloat16)
    grad_q = (weight * jnp.exp(zq - lse[:, None])).astype(jnp.bfloat16)
    qgrad = jnp.dot(grad_p, passage_store, preferred_element_type=jnp.float32) + jnp.dot(
        grad_q, pool_s, preferred_element_type=jnp.float32
    )
    local_sums = lax.psum_scatter(
        lax.dot_general(
            grad_p, queries, (((0,), (0,)), ((), ())), preferred_element_type=jnp.float32
        ),
        "wide",
        scatter_dimension=0,
        tiled=True,
    )
    passage_grad = lax.psum(local_sums, "dp") * scale
    query_grad = (qgrad * scale).astype(jnp.bfloat16)
    return (row_loss, query_grad, passage_grad)


def solution(mesh):
    placed = (
        P(("wide", "dp"), None),
        P(("wide", "dp"), None),
        P("wide", None),
        P("wide", None),
        P("wide", None),
        P("dp"),
        P(("wide", "dp")),
        P(("wide", "dp"), None),
    )
    return jax.shard_map(
        body,
        mesh=mesh,
        in_specs=placed,
        out_specs=(P(("wide", "dp")), P(("wide", "dp"), None), P("wide", None)),
        check_vma=False,
    )
```

profile of v0, /device:TPU:0, one launch (start us, length us, event | category | flops | bytes accessed | tf_op | source)
XLA Modules:
  0.0 281.9 jit_solution(17718159648737804213)
XLA Ops:
  7.2 0.0 all-reduce.6.cloned.1.call-start
  7.9 2.3 broadcast_select_fusion
  10.1 0.0 copy-start.2
  10.1 0.0 all-reduce.6.cloned.1.call-update
  10.2 0.0 all-gather.2.cloned.1.call-start
  10.2 0.7 all-gather.2.cloned.1.call-update
  10.9 0.0 reduce-scatter.2.cloned.1.call-start
  11.0 0.2 copy-done.2
  11.2 0.2 copy.11
  11.4 115.2 %all-reduce.6.cloned.1.call-done = (bf16[256,4096]{1,0:T(8,128)(2,1)}, bf16[256,4096]{1,0:T(8,128)(2,1)}) async-done(((bf16[256,4096]{1,0:T(8,128)(2,1)}, bf16[256,4096]{1,0:T(8,128)(2,1)}), (bf16[256,4096]{1,0:T(8,128)(2,1)}, bf16[256,4096]{1,0:T(8,128)(2,1)})) %all-reduce.6.cloned.1.call-update) | async-done | bytes 4194320 | tf_op jit(solution)/shard_map/psum | solution.py:13
  126.6 0.0 copy-start.4
  126.6 4.3 %fusion.12 = (f32[512]{0:T(512)S(1)}, f32[256,512]{1,0:T(8,128)S(1)}) fusion(bf16[256,4096]{1,0:T(8,128)(2,1)} %get-tuple-element.5, bf16[512,4096]{1,0:T(8,128)(2,1)} %param.8), kind=kOutput, calls=%fused_computation.25 | convolution fusion | flops 1074003456 | bytes 6817792 | tf_op jit(solution)/shard_map/dot_general | solution.py:27
  130.9 0.0 copy-done.4
  130.9 0.4 copy-done.5
  131.3 2.2 fusion.6
  133.5 36.0 %all-gather.2.cloned.1.call-done = bf16[256,4096]{1,0:T(8,128)(2,1)} async-done(((bf16[16,4096]{1,0:T(8,128)(2,1)}), bf16[256,4096]{1,0:T(8,128)(2,1)}) %all-gather.2.cloned.1.call-update) | async-done | bytes 2097168 | tf_op jit(solution)/shard_map/all_gather | solution.py:32
  169.6 4.3 %fusion.13 = (f32[512]{0:T(512)S(1)}, f32[512,256]{0,1:T(8,128)S(1)}) fusion(bf16[512,4096]{1,0:T(8,128)(2,1)} %param.8, bf16[256,4096]{1,0:T(8,128)(2,1)} %all-gather.2.cloned.1.call-done), kind=kOutput, calls=%fused_computation.26 | convolution fusion | flops 1074003456 | bytes 6817792 | tf_op jit(solution)/shard_map/dot_general | solution.py:35
  173.9 0.0 copy-done.3
  173.9 0.2 select_reduce_fusion
  174.1 0.6 fusion.11
  174.7 0.0 copy-done
  174.7 3.3 %fusion.9 = f32[256,4096]{1,0:T(8,128)} fusion(bf16[512,4096]{1,0:T(8,128)(2,1)S(1)} %copy-done, f32[512,256]{0,1:T(8,128)S(1)} %get-tuple-element.12, f32[512]{0:T(512)S(1)} %get-tuple-element.8, s32[512]{0:T(512)S(1)} %copy-done.3), kind=kOutput, calls=%fused_computation.21 | convolution fusion | flops 1074397184 | bytes 8916992 | tf_op jit(solution)/shard_map/dot_general | solution.py:58
  177.9 0.0 reduce-scatter.2.cloned.1.call-update
  178.0 0.0 copy-start.1
  178.0 0.0 all-reduce.4.cloned.1.call-start
  178.0 6.3 %fusion.10 = f32[512,4096]{1,0:T(8,128)} fusion(bf16[256,4096]{1,0:T(8,128)(2,1)} %all-gather.2.cloned.1.call-done, f32[512,256]{0,1:T(8,128)S(1)} %get-tuple-element.12, f32[512]{0:T(512)S(1)} %get-tuple-element.8, s32[512]{0:T(512)S(1)} %copy-done.3), kind=kOutput, calls=%fused_computation.22 | convolution fusion | flops 1074397184 | bytes 11014144 | tf_op jit(solution)/shard_map/dot_general | solution.py:54
  184.3 64.9 %reduce-scatter.2.cloned.1.call-done = f32[16,4096]{1,0:T(8,128)} async-done(((f32[256,4096]{1,0:T(8,128)}), f32[16,4096]{1,0:T(8,128)}) %reduce-scatter.2.cloned.1.call-update) | async-done | bytes 262160 | tf_op jit(solution)/shard_map/reduce_scatter | solution.py:57
  249.2 0.0 all-reduce.4.cloned.1.call-update
  249.3 0.0 copy-done.1
  249.3 6.9 %multiply_convert_fusion = bf16[512,4096]{1,0:T(8,128)(2,1)} fusion(f32[512,4096]{1,0:T(8,128)} %fusion.10, bf16[256,4096]{1,0:T(8,128)(2,1)S(1)} %copy-done.1, f32[512,256]{0,1:T(8,128)} %get-tuple-element.14, f32[256,512]{1,0:T(8,128)S(1)} %get-tuple-element.10, f32[512]{0:T(512)S(1)} %get-tuple-element.8), kind=kOutput, calls=%fused_computation | convolution fusion | flops 1080426496 | bytes 15730688 | tf_op jit(solution)/shard_map/dot_general | solution.py:54
  256.2 17.5 %all-reduce.4.cloned.1.call-done = f32[16,4096]{1,0:T(8,128)} async-done(((f32[16,4096]{1,0:T(8,128)}), f32[16,4096]{1,0:T(8,128)}) %all-reduce.4.cloned.1.call-update) | async-done | bytes 262160 | tf_op jit(solution)/shard_map/psum | solution.py:65
  273.7 1.7 broadcast_multiply_fusion
  (4 shorter events, 0.0 us)
Async XLA Ops:
  7.2 119.4 %all-reduce.6.cloned.1.call-start = ((), (), s32[]{:S(2)}) async-start(), calls=%async_computation.4 | async-start | bytes 8388608 | tf_op jit(solution)/shard_map/psum | solution.py:13
  10.1 1.0 copy-start.2
  10.2 159.4 %all-gather.2.cloned.1.call-start = ((), (), s32[]{:S(2)}) async-start(), calls=%async_computation.1 | async-start | bytes 2228224 | tf_op jit(solution)/shard_map/all_gather | solution.py:32
  10.9 238.3 %reduce-scatter.2.cloned.1.call-start = ((), (), s32[]{:S(2)}) async-start(), calls=%async_computation.2 | async-start | bytes 4456448 | tf_op jit(solution)/shard_map/reduce_scatter | solution.py:57
  126.6 4.3 %copy-start.4 = (bf16[512,4096]{1,0:T(8,128)(2,1)S(1)}, bf16[512,4096]{1,0:T(8,128)(2,1)}, u32[]{:S(2)}) copy-start(bf16[512,4096]{1,0:T(8,128)(2,1)} %param.9) | copy-start | bytes 12582916
  126.6 4.7 %copy-start.5 = (bf16[256,4096]{1,0:T(8,128)(2,1)S(1)}, bf16[256,4096]{1,0:T(8,128)(2,1)}, u32[]{:S(2)}) copy-start(bf16[256,4096]{1,0:T(8,128)(2,1)} %get-tuple-element.6) | copy-start | bytes 6291460
  133.5 40.4 %copy-start.3 = (s32[512]{0:T(512)S(1)}, s32[512]{0:T(512)}, u32[]{:S(2)}) copy-start(s32[512]{0:T(512)} %param.14) | copy-start | bytes 6148
  169.6 5.1 %copy-start = (bf16[512,4096]{1,0:T(8,128)(2,1)S(1)}, bf16[512,4096]{1,0:T(8,128)(2,1)}, u32[]{:S(2)}) copy-start(bf16[512,4096]{1,0:T(8,128)(2,1)} %param.8) | copy-start | bytes 12582916
  178.0 71.3 %copy-start.1 = (bf16[256,4096]{1,0:T(8,128)(2,1)S(1)}, bf16[256,4096]{1,0:T(8,128)(2,1)}, u32[]{:S(2)}) copy-start(bf16[256,4096]{1,0:T(8,128)(2,1)} %get-tuple-element.5) | copy-start | bytes 6291460
  178.0 95.7 %all-reduce.4.cloned.1.call-start = ((), (), s32[]{:S(2)}) async-start(), calls=%async_computation.3 | async-start | bytes 524288 | tf_op jit(solution)/shard_map/psum | solution.py:65
Sparse Core Ops, SparseCore 0:
  12.3 114.2 all-reduce.5
  129.0 40.5 all-gather.1
  178.1 71.0 reduce-scatter.1
  251.4 22.2 all-reduce.3
where the time goes:
time: 282 us
  waiting for transfers between devices  234 us (83%)
  matrix products  27.3 us (10%)
  between operations  14.5 us (5%)
  other arithmetic  4.71 us (2%)
    psum x1, waiting for transfers between devices, broadcast(): return lax.psum(block, axis)  115 us
    reduce_scatter x1, waiting for transfers between devices, body(): lax.psum_scatter(lax.dot_general(grad_p, queries, (((0,), (0,)), ((), ())...  64.9 us
    all_gather x1, waiting for transfers between devices, body(): piece = lax.all_gather(passages, 'wide', axis=0, tiled=True)  36 us
    psum x1, waiting for transfers between devices, body(): passage_grad = lax.psum(local_sums, 'dp') * scale  17.5 us
    dot_general x1, matrix products, body(): jnp.dot(grad_q, pool_s, preferred_element_type=jnp.float32)  6.93 us
    dot_general x1, matrix products, body(): jnp.dot(grad_p, passage_store, preferred_element_type=jnp.float32)  6.27 us
  transfers between devices with their start and end apart: 4, of which 4 were waited for; matrix products, arithmetic and copies ran while one was open for 7% of the time, Pallas kernels for 0%

commit v1 on v0

v1 whole, which is shorter than its diff:
```python
import math

import jax
import jax.numpy as jnp
from jax import lax
from jax.sharding import PartitionSpec as P

E = 4096
CHUNKS = 4


def ring_order(n_chip):
    nz = n_chip // 2
    return [2 * z for z in range(nz)] + [2 * z + 1 for z in reversed(range(nz))]


def ring_pairs(n_chip):
    order = ring_order(n_chip)
    pairs = []
    for i, chip in enumerate(order):
        pairs.append((2 * chip, 2 * order[(i + 1) % n_chip]))
        pairs.append((2 * chip + 1, 2 * order[(i - 1) % n_chip] + 1))
    return pairs


def pool_halves(bank_s, bank_t, owner, index, core):
    n_dev = lax.axis_size("wide")
    n_chip = n_dev // 2
    half = bank_s.shape[0] // 2
    step_rows = half // CHUNKS
    order = ring_order(n_chip)
    place = jnp.array([order.index(c) for c in range(n_chip)], jnp.int32)
    away = place[index // 2] - place[owner // 2]
    distance = jnp.where(core == 0, away, -away) % n_chip
    own_chip = owner // 2 == index // 2
    own_core = owner == index
    swap = [(i, i ^ 1) for i in range(n_dev)]
    pairs = ring_pairs(n_chip)
    mine = []
    for bank in (bank_s, bank_t):
        got = lax.ppermute(
            lax.dynamic_slice_in_dim(bank, (1 - core) * half, half, 0), "wide", swap
        )
        mine.append(
            jnp.where(own_core, lax.dynamic_slice_in_dim(bank, core * half, half, 0), got)
        )
    spare = jnp.zeros((step_rows, bank_s.shape[1]), bank_s.dtype)
    pools = [jnp.concatenate([m, spare], 0) for m in mine]
    moving = [m[:step_rows] for m in mine]
    for t in range(CHUNKS + n_chip - 2):
        slot = t - (distance - 1)
        slot = jnp.where(own_chip | (slot > CHUNKS), CHUNKS, jnp.maximum(slot, 0))
        for i in range(2):
            got = lax.ppermute(moving[i], "wide", pairs)
            pools[i] = lax.dynamic_update_slice_in_dim(pools[i], got, slot * step_rows, 0)
            if t + 1 < CHUNKS:
                got = jnp.where(own_chip, mine[i][(t + 1) * step_rows : (t + 2) * step_rows], got)
            moving[i] = got
    return [p[:half] for p in pools]


def dot_t(a, b):
    return lax.dot_general(a, b, (((1,), (1,)), ((), ())), preferred_element_type=jnp.float32)


def body(
    queries, teacher_queries, passages, bank_student, bank_teacher, owner, positives, keep_mask
):
    scale = 2.0 / math.sqrt(E)
    n_dev = lax.axis_size("wide")
    n_chip = n_dev // 2
    n_dp = lax.axis_size("dp")
    index = lax.axis_index("wide")
    replica = lax.axis_index("dp")
    core = index % 2
    block = passages.shape[0]
    n_pass = block * n_dev
    parts = 2 if n_dp == 2 else 1
    sub = block // parts
    swap = [(i, i ^ 1) for i in range(n_dev)]
    across = [(0, 1), (1, 0)]

    gathered = lax.all_gather(passages, "wide", axis=0, tiled=True)
    split = gathered.reshape(n_chip, 2, parts, sub, E)
    split = jnp.where(core == 0, split[:, ::-1], split)
    if parts == 2:
        split = jnp.where(replica == 0, split[:, :, ::-1], split)
    pieces = split.transpose(1, 2, 0, 3, 4).reshape(n_pass, E)
    chip_of = positives // (2 * block)
    core_of = (positives // block) % 2
    half_of = (positives // sub) % parts
    core_of = jnp.where(core == 0, 1 - core_of, core_of)
    if parts == 2:
        half_of = jnp.where(replica == 0, 1 - half_of, half_of)
    column = ((core_of * parts + half_of) * n_chip + chip_of) * sub + positives % sub

    zp = dot_t(queries, pieces) * scale
    top_p = jnp.max(zp, axis=1)

    pool_s, pool_t = pool_halves(bank_student, bank_teacher, owner[0], index, core)
    other_s = lax.ppermute(pool_s, "wide", swap)
    other_t = lax.ppermute(pool_t, "wide", swap)
    half = pool_s.shape[0]
    keep = jnp.where(core == 0, keep_mask, jnp.roll(keep_mask, half, 1)).astype(jnp.float32)
    zq = jnp.concatenate([dot_t(queries, pool_s), dot_t(queries, other_s)], 1) * scale
    tt = jnp.concatenate([dot_t(teacher_queries, pool_t), dot_t(teacher_queries, other_t)], 1) * scale
    weight = keep * jax.nn.sigmoid(-tt)
    top = jnp.maximum(top_p, jnp.max(zq, axis=1))
    total = jnp.sum(jnp.exp(zp - top[:, None]), axis=1) + jnp.sum(
        weight * jnp.exp(zq - top[:, None]), axis=1
    )
    lse = top + jnp.log(total)
    hit = (jnp.arange(n_pass, dtype=jnp.int32)[None, :] == column[:, None]).astype(jnp.float32)
    row_loss = lse - jnp.sum(zp * hit, axis=1)
    grad_p = (jnp.exp(zp - lse[:, None]) - hit).astype(jnp.bfloat16)
    grad_q = (weight * jnp.exp(zq - lse[:, None])).astype(jnp.bfloat16)

    def terms(columns):
        return lax.dot_general(
            columns, queries, (((0,), (0,)), ((), ())), preferred_element_type=jnp.float32
        )

    mid = n_pass // 2
    sent = lax.ppermute(terms(grad_p[:, :mid]).astype(jnp.bfloat16), "wide", swap)
    sums = terms(grad_p[:, mid:]) + sent.astype(jnp.float32)
    if parts == 2:
        sent = lax.ppermute(sums[: mid // 2].astype(jnp.bfloat16), "dp", across)
        sums = sums[mid // 2 :] + sent.astype(jnp.float32)
    sums = sums.reshape(n_chip, sub, E)
    chip = index // 2
    own = lax.dynamic_slice_in_dim(sums, chip, 1, 0)[0]
    packed = sums.astype(jnp.bfloat16)
    for j in range(1, n_chip):
        part = lax.dynamic_slice_in_dim(packed, chip ^ j, 1, 0)[0]
        got = lax.ppermute(part, "wide", [(i, i ^ (2 * j)) for i in range(n_dev)])
        own = own + got.astype(jnp.float32)
    if parts == 2:
        own = own * scale
        got = lax.ppermute(own, "dp", across)
        passage_grad = jnp.where(
            replica == 0, jnp.concatenate([own, got], 0), jnp.concatenate([got, own], 0)
        )
    else:
        passage_grad = lax.psum(own, "dp") * scale

    qgrad = (
        jnp.dot(grad_p, pieces, preferred_element_type=jnp.float32)
        + jnp.dot(grad_q[:, :half], pool_s, preferred_element_type=jnp.float32)
        + jnp.dot(grad_q[:, half:], other_s, preferred_element_type=jnp.float32)
    )
    query_grad = (qgrad * scale).astype(jnp.bfloat16)
    return (row_loss, query_grad, passage_grad)


def solution(mesh):
    placed = (
        P(("wide", "dp"), None),
        P(("wide", "dp"), None),
        P("wide", None),
        P("wide", None),
        P("wide", None),
        P("dp"),
        P(("wide", "dp")),
        P(("wide", "dp"), None),
    )
    return jax.shard_map(
        body,
        mesh=mesh,
        in_specs=placed,
        out_specs=(P(("wide", "dp")), P(("wide", "dp"), None), P("wide", None)),
        check_vma=False,
    )
```

time: 282 us -> 168 us (0.60)
  waiting for transfers between devices: 234 us -> 49.2 us
  starting transfers between devices: 0.16 us -> 55.5 us
  local copies, waits for them, and re-layouts: 0.85 us -> 14.3 us
  other arithmetic: 4.71 us -> 12.1 us
  matrix products: 27.3 us -> 20.1 us
    psum x2 -> x0, waiting for transfers between devices: 133 us -> none  [the longest x1 115 us: broadcast(): return lax.psum(block, axis)]
    reduce_scatter x1 -> x0, waiting for transfers between devices: 64.9 us -> none  [body(): lax.psum_scatter(lax.dot_general(grad_p, queries, (((0,), (0,)), ((), ())...]
    ppermute x0 -> x34, starting transfers between devices: none -> 55.4 us  [the longest x20 39.6 us: pool_halves(): got = lax.ppermute(moving[i], 'wide', pairs)]
    ppermute x0 -> x34, waiting for transfers between devices: none -> 49.1 us  [the longest x20 31.3 us: pool_halves(): got = lax.ppermute(moving[i], 'wide', pairs)]
    all_gather x1, waiting for transfers between devices: 36 us -> 0.01 us  [body(): gathered = lax.all_gather(passages, 'wide', axis=0, tiled=True)]
    dot_general x6 -> x10, matrix products: 27.3 us -> 20.1 us  [the longest x5 11.5 us: dot_t(): lax.dot_general(a, b, (((1,), (1,)), ((), ())), preferred_element_type=jn...]
    select_n x1 -> x10, other arithmetic: 2.28 us -> 7.94 us  [the longest x2 3.11 us: pool_halves(): jnp.where(own_core, lax.dynamic_slice_in_dim(bank, core * half, half, 0),...]
    slice x0 -> x6, local copies, waits for them, and re-layouts: none -> 3.89 us  [the longest x2 2.12 us: pool_halves(): return [p[:half] for p in pools]]
  transfers between devices with their start and end apart: 4 -> 35, of which waited for: 4 -> 25; matrix products, arithmetic and copies ran while one was open for 7% -> 19% of each run, Pallas kernels for 0% -> 0%
where the time goes in v1:
time: 168 us
  starting transfers between devices  55.5 us (33%)
  waiting for transfers between devices  49.2 us (29%)
  matrix products  20.1 us (12%)
  between operations  16.7 us (10%)
  local copies, waits for them, and re-layouts  14.3 us (9%)
  other arithmetic  12.1 us (7%)
    ppermute x20, starting transfers between devices, pool_halves(): got = lax.ppermute(moving[i], 'wide', pairs)  39.6 us
    ppermute x20, waiting for transfers between devices, pool_halves(): got = lax.ppermute(moving[i], 'wide', pairs)  31.3 us
    ppermute x1, waiting for transfers between devices, body(): sent = lax.ppermute(sums[:mid // 2].astype(jnp.bfloat16), 'dp', across)  12.8 us
    dot_general x5, matrix products, dot_t(): lax.dot_general(a, b, (((1,), (1,)), ((), ())), preferred_element_type=jn...  11.5 us
    ppermute x7, starting transfers between devices, body(): got = lax.ppermute(part, 'wide', [(i, i ^ 2 * j) for i in range(n_dev)])  11.4 us
    unnamed x39, local copies, waits for them, and re-layouts  4.67 us
  transfers between devices with their start and end apart: 35, of which 25 were waited for; matrix products, arithmetic and copies ran while one was open for 19% of the time, Pallas kernels for 0%

profile of v1, /device:TPU:0, one launch (start us, length us, event | category | flops | bytes accessed | tf_op | source)
XLA Modules:
  0.0 167.7 jit_solution(6710953569554663790)
XLA Ops:
  7.2 2.4 %constant_dynamic-slice_fusion.1 = bf16[128,4096]{1,0:T(8,128)(2,1)} fusion(bf16[256,4096]{1,0:T(8,128)(2,1)} %param.12, s32[]{:T(128)S(6)} %select_n.247), kind=kLoop, calls=%fused_computation.86 | loop fusion | bytes 2097156 | tf_op jit(solution)/shard_map/dynamic_slice | solution.py:42
  14.7 3.1 %collective-permute-start.1 = (bf16[32,4096]{1,0:T(8,128)(2,1)S(1)}, bf16[32,4096]{1,0:T(8,128)(2,1)S(1)}, u32[]{:S(2)}, u32[]{:S(2)}) collective-permute-start(bf16[32,4096]{1,0:T(8,128)(2,1)S(1)} %slice.75), channel_id=1, source_target_pairs={{0,8},{2,6},{8,16},{10,2},{16,24},{18,10},{24,28},{26,18},{28,20},... | collective-permute-start | bytes 786440 | tf_op jit(solution)/shard_map/ppermute | solution.py:54
  22.1 2.2 %collective-permute-start.2 = (bf16[32,4096]{1,0:T(8,128)(2,1)S(1)}, bf16[32,4096]{1,0:T(8,128)(2,1)S(1)}, u32[]{:S(2)}, u32[]{:S(2)}) collective-permute-start(bf16[32,4096]{1,0:T(8,128)(2,1)S(1)} %get-tuple-element.30), channel_id=1, source_target_pairs={{0,8},{2,6},{8,16},{10,2},{16,24},{18,10},{24,28},{26,18},{28,20},... | collective-permute-start | bytes 786440 | tf_op jit(solution)/shard_map/ppermute | solution.py:54
  24.3 3.1 %collective-permute-done.13 = bf16[32,4096]{1,0:T(8,128)(2,1)S(1)} collective-permute-done((bf16[32,4096]{1,0:T(8,128)(2,1)S(1)}, bf16[32,4096]{1,0:T(8,128)(2,1)S(1)}, u32[]{:S(2)}, u32[]{:S(2)}) %collective-permute-start.13) | collective-permute-done | bytes 262176 | tf_op jit(solution)/shard_map/ppermute | solution.py:54
  28.9 1.9 %collective-permute-done.2 = bf16[32,4096]{1,0:T(8,128)(2,1)S(1)} collective-permute-done((bf16[32,4096]{1,0:T(8,128)(2,1)S(1)}, bf16[32,4096]{1,0:T(8,128)(2,1)S(1)}, u32[]{:S(2)}, u32[]{:S(2)}) %collective-permute-start.2) | collective-permute-done | bytes 262176 | tf_op jit(solution)/shard_map/ppermute | solution.py:54
  30.8 2.5 %collective-permute-start.3 = (bf16[32,4096]{1,0:T(8,128)(2,1)S(1)}, bf16[32,4096]{1,0:T(8,128)(2,1)S(1)}, u32[]{:S(2)}, u32[]{:S(2)}) collective-permute-start(bf16[32,4096]{1,0:T(8,128)(2,1)S(1)} %get-tuple-element.28), channel_id=1, source_target_pairs={{0,8},{2,6},{8,16},{10,2},{16,24},{18,10},{24,28},{26,18},{28,20},... | collective-permute-start | bytes 786440 | tf_op jit(solution)/shard_map/ppermute | solution.py:54
  34.4 2.5 %collective-permute-start.15 = (bf16[32,4096]{1,0:T(8,128)(2,1)S(1)}, bf16[32,4096]{1,0:T(8,128)(2,1)S(1)}, u32[]{:S(2)}, u32[]{:S(2)}) collective-permute-start(bf16[32,4096]{1,0:T(8,128)(2,1)S(1)} %get-tuple-element.22), channel_id=1, source_target_pairs={{0,8},{2,6},{8,16},{10,2},{16,24},{18,10},{24,28},{26,18},{28,20},... | collective-permute-start | bytes 786440 | tf_op jit(solution)/shard_map/ppermute | solution.py:54
  37.4 2.4 %collective-permute-start.4 = (bf16[32,4096]{1,0:T(8,128)(2,1)S(1)}, bf16[32,4096]{1,0:T(8,128)(2,1)}, u32[]{:S(2)}, u32[]{:S(2)}) collective-permute-start(bf16[32,4096]{1,0:T(8,128)(2,1)S(1)} %get-tuple-element.26), channel_id=1, source_target_pairs={{0,8},{2,6},{8,16},{10,2},{16,24},{18,10},{24,28},{26,18},{28,20},... | collective-permute-start | bytes 786440 | tf_op jit(solution)/shard_map/ppermute | solution.py:54
  39.8 4.3 %collective-permute-done.15 = bf16[32,4096]{1,0:T(8,128)(2,1)S(1)} collective-permute-done((bf16[32,4096]{1,0:T(8,128)(2,1)S(1)}, bf16[32,4096]{1,0:T(8,128)(2,1)S(1)}, u32[]{:S(2)}, u32[]{:S(2)}) %collective-permute-start.15) | collective-permute-done | bytes 262176 | tf_op jit(solution)/shard_map/ppermute | solution.py:54
  45.0 2.5 %collective-permute-start.16 = (bf16[32,4096]{1,0:T(8,128)(2,1)}, bf16[32,4096]{1,0:T(8,128)(2,1)}, u32[]{:S(2)}, u32[]{:S(2)}) collective-permute-start(bf16[32,4096]{1,0:T(8,128)(2,1)} %get-tuple-element.20), channel_id=1, source_target_pairs={{0,8},{2,6},{8,16},{10,2},{16,24},{18,10},{24,28},{26,18},{28,20},... | collective-permute-start | bytes 786440 | tf_op jit(solution)/shard_map/ppermute | solution.py:54
  49.8 1.8 %collective-permute-start.5 = (bf16[32,4096]{1,0:T(8,128)(2,1)}, bf16[32,4096]{1,0:T(8,128)(2,1)S(1)}, u32[]{:S(2)}, u32[]{:S(2)}) collective-permute-start(bf16[32,4096]{1,0:T(8,128)(2,1)} %collective-permute-done.4), channel_id=1, source_target_pairs={{0,8},{2,6},{8,16},{10,2},{16,24},{18,10},{24,28},{26,18},{28,20},... | collective-permute-start | bytes 786440 | tf_op jit(solution)/shard_map/ppermute | solution.py:54
  51.6 3.4 %collective-permute-done.16 = bf16[32,4096]{1,0:T(8,128)(2,1)} collective-permute-done((bf16[32,4096]{1,0:T(8,128)(2,1)}, bf16[32,4096]{1,0:T(8,128)(2,1)}, u32[]{:S(2)}, u32[]{:S(2)}) %collective-permute-start.16) | collective-permute-done | bytes 262176 | tf_op jit(solution)/shard_map/ppermute | solution.py:54
  55.0 2.5 %collective-permute-start.17 = (bf16[32,4096]{1,0:T(8,128)(2,1)}, bf16[32,4096]{1,0:T(8,128)(2,1)S(1)}, u32[]{:S(2)}, u32[]{:S(2)}) collective-permute-start(bf16[32,4096]{1,0:T(8,128)(2,1)} %collective-permute-done.16), channel_id=1, source_target_pairs={{0,8},{2,6},{8,16},{10,2},{16,24},{18,10},{24,28},{26,18},{28,20},... | collective-permute-start | bytes 786440 | tf_op jit(solution)/shard_map/ppermute | solution.py:54
  62.0 2.1 %collective-permute-start.18 = (bf16[32,4096]{1,0:T(8,128)(2,1)S(1)}, bf16[32,4096]{1,0:T(8,128)(2,1)S(1)}, u32[]{:S(2)}, u32[]{:S(2)}) collective-permute-start(bf16[32,4096]{1,0:T(8,128)(2,1)S(1)} %collective-permute-done.17), channel_id=1, source_target_pairs={{0,8},{2,6},{8,16},{10,2},{16,24},{18,10},{24,28},{26,18},{28,20},... | collective-permute-start | bytes 786440 | tf_op jit(solution)/shard_map/ppermute | solution.py:54
  68.7 1.8 %collective-permute-start.19 = (bf16[32,4096]{1,0:T(8,128)(2,1)S(1)}, bf16[32,4096]{1,0:T(8,128)(2,1)S(1)}, u32[]{:S(2)}, u32[]{:S(2)}) collective-permute-start(bf16[32,4096]{1,0:T(8,128)(2,1)S(1)} %collective-permute-done.18), channel_id=1, source_target_pairs={{0,8},{2,6},{8,16},{10,2},{16,24},{18,10},{24,28},{26,18},{28,20},... | collective-permute-start | bytes 786440 | tf_op jit(solution)/shard_map/ppermute | solution.py:54
  75.0 1.8 %collective-permute-start.20 = (bf16[32,4096]{1,0:T(8,128)(2,1)S(1)}, bf16[32,4096]{1,0:T(8,128)(2,1)S(1)}, u32[]{:S(2)}, u32[]{:S(2)}) collective-permute-start(bf16[32,4096]{1,0:T(8,128)(2,1)S(1)} %collective-permute-done.19), channel_id=1, source_target_pairs={{0,8},{2,6},{8,16},{10,2},{16,24},{18,10},{24,28},{26,18},{28,20},... | collective-permute-start | bytes 786440 | tf_op jit(solution)/shard_map/ppermute | solution.py:54
  81.4 1.8 %collective-permute-start.21 = (bf16[32,4096]{1,0:T(8,128)(2,1)S(1)}, bf16[32,4096]{1,0:T(8,128)(2,1)S(1)}, u32[]{:S(2)}, u32[]{:S(2)}) collective-permute-start(bf16[32,4096]{1,0:T(8,128)(2,1)S(1)} %collective-permute-done.20), channel_id=1, source_target_pairs={{0,8},{2,6},{8,16},{10,2},{16,24},{18,10},{24,28},{26,18},{28,20},... | collective-permute-start | bytes 786440 | tf_op jit(solution)/shard_map/ppermute | solution.py:54
  87.8 1.8 %collective-permute-start.22 = (bf16[32,4096]{1,0:T(8,128)(2,1)S(1)}, bf16[32,4096]{1,0:T(8,128)(2,1)S(1)}, u32[]{:S(2)}, u32[]{:S(2)}) collective-permute-start(bf16[32,4096]{1,0:T(8,128)(2,1)S(1)} %collective-permute-done.21), channel_id=1, source_target_pairs={{0,8},{2,6},{8,16},{10,2},{16,24},{18,10},{24,28},{26,18},{28,20},... | collective-permute-start | bytes 786440 | tf_op jit(solution)/shard_map/ppermute | solution.py:54
  95.3 2.2 %convolution_bitcast_fusion.3 = f32[512,128]{0,1:T(8,128)} fusion(bf16[512,4096]{1,0:T(8,128)(2,1)S(1)} %copy-done, bf16[160,4096]{1,0:T(8,128)(2,1)S(1)} %constant_dynamic-update-slice_fusion.10), kind=kOutput, calls=%fused_computation.10 | convolution fusion | flops 536870912 | bytes 5505024 | tf_op jit(solution)/shard_map/dot_general | solution.py:63
  97.5 2.2 %convolution_bitcast_fusion.1 = f32[512,128]{0,1:T(8,128)} fusion(bf16[512,4096]{1,0:T(8,128)(2,1)S(1)} %copy-done.2, bf16[160,4096]{1,0:T(8,128)(2,1)S(1)} %constant_dynamic-update-slice_fusion), kind=kOutput, calls=%fused_computation.8 | convolution fusion | flops 536870912 | bytes 5505024 | tf_op jit(solution)/shard_map/dot_general | solution.py:63
  99.7 3.0 %reverse_select_fusion.1 = bf16[8,2,2,8,4096]{4,3,2,1,0:T(8,128)(2,1)S(1)} fusion(bf16[8,2,2,8,4096]{4,3,2,1,0:T(8,128)(2,1)} %bitcast.83, pred[]{:T(512)S(6)} %eq.38), kind=kLoop, calls=%fused_computation.3 | loop fusion | flops 1048576 | bytes 4194305 | tf_op jit(solution)/shard_map/jit(_where)/select_n | solution.py:85
  103.4 2.0 %copy-done.1 = bf16[512,4096]{1,0:T(8,128)(2,1)S(1)} copy-done((bf16[512,4096]{1,0:T(8,128)(2,1)S(1)}, bf16[512,4096]{1,0:T(8,128)(2,1)}, u32[]{:S(2)}) %copy-start.1) | copy-done | bytes 4194328
  106.8 2.9 %convolution_bitcast_fusion.2 = f32[512,128]{0,1:T(8,128)S(1)} fusion(bf16[128,4096]{1,0:T(8,128)(2,1)} %collective-permute-done.11, bf16[512,4096]{1,0:T(8,128)(2,1)S(1)} %copy-done.1), kind=kOutput, calls=%fused_computation.9 | convolution fusion | flops 536870912 | bytes 5505024 | tf_op jit(solution)/shard_map/dot_general | solution.py:63
  109.8 2.8 %convolution_bitcast_fusion = f32[512,128]{0,1:T(8,128)S(1)} fusion(bf16[128,4096]{1,0:T(8,128)(2,1)} %collective-permute-done.23, bf16[512,4096]{1,0:T(8,128)(2,1)S(1)} %copy-done.3), kind=kOutput, calls=%fused_computation.7 | convolution fusion | flops 536870912 | bytes 5505024 | tf_op jit(solution)/shard_map/dot_general | solution.py:63
  116.0 2.3 %collective-permute-done.24 = bf16[128,4096]{1,0:T(8,128)(2,1)S(1)} collective-permute-done((bf16[128,4096]{1,0:T(8,128)(2,1)S(1)}, bf16[128,4096]{1,0:T(8,128)(2,1)S(1)}, u32[]{:S(2)}, u32[]{:S(2)}) %collective-permute-start.24) | collective-permute-done | bytes 1048608 | tf_op jit(solution)/shard_map/ppermute | solution.py:124
  122.9 12.8 %collective-permute-done.25 = bf16[64,4096]{1,0:T(8,128)(2,1)} collective-permute-done((bf16[64,4096]{1,0:T(8,128)(2,1)}, bf16[64,4096]{1,0:T(8,128)(2,1)}, u32[]{:S(2)}, u32[]{:S(2)}) %collective-permute-start.25) | collective-permute-done | bytes 524320 | tf_op jit(solution)/shard_map/ppermute | solution.py:127
  139.0 3.6 %collective-permute-start.32 = (bf16[8,4096]{1,0:T(8,128)(2,1)S(1)}, bf16[8,4096]{1,0:T(8,128)(2,1)S(1)}, u32[]{:S(2)}, u32[]{:S(2)}) collective-permute-start(bf16[8,4096]{1,0:T(8,128)(2,1)S(1)} %get-tuple-element.12), channel_id=1, source_target_pairs={{0,28},{2,30},{4,24},{6,26},{8,20},{10,22},{12,16},{14,18},{16,12}... | collective-permute-start | bytes 196616 | tf_op jit(solution)/shard_map/ppermute | solution.py:135
  144.0 1.9 %collective-permute-start.30 = (bf16[8,4096]{1,0:T(8,128)(2,1)S(1)}, bf16[8,4096]{1,0:T(8,128)(2,1)S(1)}, u32[]{:S(2)}, u32[]{:S(2)}) collective-permute-start(bf16[8,4096]{1,0:T(8,128)(2,1)S(1)} %get-tuple-element.14), channel_id=1, source_target_pairs={{0,20},{2,22},{4,16},{6,18},{8,28},{10,30},{12,24},{14,26},{16,4},... | collective-permute-start | bytes 196616 | tf_op jit(solution)/shard_map/ppermute | solution.py:135
  145.9 2.1 %collective-permute-start.29 = (bf16[8,4096]{1,0:T(8,128)(2,1)S(1)}, bf16[8,4096]{1,0:T(8,128)(2,1)S(1)}, u32[]{:S(2)}, u32[]{:S(2)}) collective-permute-start(bf16[8,4096]{1,0:T(8,128)(2,1)S(1)} %get-tuple-element.15), channel_id=1, source_target_pairs={{0,16},{2,18},{4,20},{6,22},{8,24},{10,26},{12,28},{14,30},{16,0},... | collective-permute-start | bytes 196616 | tf_op jit(solution)/shard_map/ppermute | solution.py:135
  150.0 2.5 %fusion.19 = f32[512,4096]{1,0:T(8,128)S(1)} fusion(bf16[128,4096]{1,0:T(8,128)(2,1)} %collective-permute-done.11, bf16[512,256]{0,1:T(8,128)(2,1)S(1)} %copy-done.13), kind=kOutput, calls=%fused_computation.47 | convolution fusion | flops 536870912 | bytes 9568256 | tf_op jit(solution)/shard_map/dot_general | solution.py:149
  152.5 1.9 %collective-permute-done.30 = bf16[8,4096]{1,0:T(8,128)(2,1)S(1)} collective-permute-done((bf16[8,4096]{1,0:T(8,128)(2,1)S(1)}, bf16[8,4096]{1,0:T(8,128)(2,1)S(1)}, u32[]{:S(2)}, u32[]{:S(2)}) %collective-permute-start.30) | collective-permute-done | bytes 65568 | tf_op jit(solution)/shard_map/ppermute | solution.py:135
  156.7 3.3 %multiply_convert_fusion = bf16[512,4096]{1,0:T(8,128)(2,1)} fusion(f32[512,4096]{1,0:T(8,128)S(1)} %fusion.19, f32[512,4096]{1,0:T(8,128)S(1)} %fusion.50, bf16[512,256]{0,1:T(8,128)(2,1)S(1)} %copy-done.13, bf16[160,4096]{1,0:T(8,128)(2,1)S(1)} %constant_dynamic-update-slice_fusion.10), kind=kOutput, calls=%fused_computation | convolution fusion | flops 545259520 | bytes 22151168 | tf_op jit(solution)/shard_map/dot_general | solution.py:148
  (134 shorter events, 61.6 us)
Async XLA Ops:
  7.2 92.6 %all-gather.2.cloned.1.call-start = ((), (), s32[]{:S(2)}) async-start(), calls=%async_computation | async-start | bytes 2228224 | tf_op jit(solution)/shard_map/all_gather | solution.py:83
  10.2 7.6 %collective-permute-start.12 = (bf16[128,4096]{1,0:T(8,128)(2,1)S(1)}, bf16[128,4096]{1,0:T(8,128)(2,1)}, u32[]{:S(2)}, u32[]{:S(2)}) collective-permute-start(bf16[128,4096]{1,0:T(8,128)(2,1)S(1)} %constant_dynamic-slice_fusion), channel_id=1, source_target_pairs={{0,2},{2,0},{4,6},{6,4},{8,10},{10,8},{12,14},{14,12},{16,18},{18,... | collective-permute-start | bytes 3145736 | tf_op jit(solution)/shard_map/ppermute | solution.py:41
  14.7 7.3 %collective-permute-start.1 = (bf16[32,4096]{1,0:T(8,128)(2,1)S(1)}, bf16[32,4096]{1,0:T(8,128)(2,1)S(1)}, u32[]{:S(2)}, u32[]{:S(2)}) collective-permute-start(bf16[32,4096]{1,0:T(8,128)(2,1)S(1)} %slice.75), channel_id=1, source_target_pairs={{0,8},{2,6},{8,16},{10,2},{16,24},{18,10},{24,28},{26,18},{28,20},... | collective-permute-start | bytes 786440 | tf_op jit(solution)/shard_map/ppermute | solution.py:54
  19.6 7.8 %collective-permute-start.13 = (bf16[32,4096]{1,0:T(8,128)(2,1)S(1)}, bf16[32,4096]{1,0:T(8,128)(2,1)S(1)}, u32[]{:S(2)}, u32[]{:S(2)}) collective-permute-start(bf16[32,4096]{1,0:T(8,128)(2,1)S(1)} %slice.82), channel_id=1, source_target_pairs={{0,8},{2,6},{8,16},{10,2},{16,24},{18,10},{24,28},{26,18},{28,20},... | collective-permute-start | bytes 786440 | tf_op jit(solution)/shard_map/ppermute | solution.py:54
  22.1 8.6 %collective-permute-start.2 = (bf16[32,4096]{1,0:T(8,128)(2,1)S(1)}, bf16[32,4096]{1,0:T(8,128)(2,1)S(1)}, u32[]{:S(2)}, u32[]{:S(2)}) collective-permute-start(bf16[32,4096]{1,0:T(8,128)(2,1)S(1)} %get-tuple-element.30), channel_id=1, source_target_pairs={{0,8},{2,6},{8,16},{10,2},{16,24},{18,10},{24,28},{26,18},{28,20},... | collective-permute-start | bytes 786440 | tf_op jit(solution)/shard_map/ppermute | solution.py:54
  27.5 6.9 %collective-permute-start.14 = (bf16[32,4096]{1,0:T(8,128)(2,1)S(1)}, bf16[32,4096]{1,0:T(8,128)(2,1)S(1)}, u32[]{:S(2)}, u32[]{:S(2)}) collective-permute-start(bf16[32,4096]{1,0:T(8,128)(2,1)S(1)} %get-tuple-element.24), channel_id=1, source_target_pairs={{0,8},{2,6},{8,16},{10,2},{16,24},{18,10},{24,28},{26,18},{28,20},... | collective-permute-start | bytes 786440 | tf_op jit(solution)/shard_map/ppermute | solution.py:54
  30.8 6.5 %collective-permute-start.3 = (bf16[32,4096]{1,0:T(8,128)(2,1)S(1)}, bf16[32,4096]{1,0:T(8,128)(2,1)S(1)}, u32[]{:S(2)}, u32[]{:S(2)}) collective-permute-start(bf16[32,4096]{1,0:T(8,128)(2,1)S(1)} %get-tuple-element.28), channel_id=1, source_target_pairs={{0,8},{2,6},{8,16},{10,2},{16,24},{18,10},{24,28},{26,18},{28,20},... | collective-permute-start | bytes 786440 | tf_op jit(solution)/shard_map/ppermute | solution.py:54
  34.4 9.8 %collective-permute-start.15 = (bf16[32,4096]{1,0:T(8,128)(2,1)S(1)}, bf16[32,4096]{1,0:T(8,128)(2,1)S(1)}, u32[]{:S(2)}, u32[]{:S(2)}) collective-permute-start(bf16[32,4096]{1,0:T(8,128)(2,1)S(1)} %get-tuple-element.22), channel_id=1, source_target_pairs={{0,8},{2,6},{8,16},{10,2},{16,24},{18,10},{24,28},{26,18},{28,20},... | collective-permute-start | bytes 786440 | tf_op jit(solution)/shard_map/ppermute | solution.py:54
  37.4 12.3 %collective-permute-start.4 = (bf16[32,4096]{1,0:T(8,128)(2,1)S(1)}, bf16[32,4096]{1,0:T(8,128)(2,1)}, u32[]{:S(2)}, u32[]{:S(2)}) collective-permute-start(bf16[32,4096]{1,0:T(8,128)(2,1)S(1)} %get-tuple-element.26), channel_id=1, source_target_pairs={{0,8},{2,6},{8,16},{10,2},{16,24},{18,10},{24,28},{26,18},{28,20},... | collective-permute-start | bytes 786440 | tf_op jit(solution)/shard_map/ppermute | solution.py:54
  45.0 10.0 %collective-permute-start.16 = (bf16[32,4096]{1,0:T(8,128)(2,1)}, bf16[32,4096]{1,0:T(8,128)(2,1)}, u32[]{:S(2)}, u32[]{:S(2)}) collective-permute-start(bf16[32,4096]{1,0:T(8,128)(2,1)} %get-tuple-element.20), channel_id=1, source_target_pairs={{0,8},{2,6},{8,16},{10,2},{16,24},{18,10},{24,28},{26,18},{28,20},... | collective-permute-start | bytes 786440 | tf_op jit(solution)/shard_map/ppermute | solution.py:54
  49.8 9.7 %collective-permute-start.5 = (bf16[32,4096]{1,0:T(8,128)(2,1)}, bf16[32,4096]{1,0:T(8,128)(2,1)S(1)}, u32[]{:S(2)}, u32[]{:S(2)}) collective-permute-start(bf16[32,4096]{1,0:T(8,128)(2,1)} %collective-permute-done.4), channel_id=1, source_target_pairs={{0,8},{2,6},{8,16},{10,2},{16,24},{18,10},{24,28},{26,18},{28,20},... | collective-permute-start | bytes 786440 | tf_op jit(solution)/shard_map/ppermute | solution.py:54
  55.0 7.0 %collective-permute-start.17 = (bf16[32,4096]{1,0:T(8,128)(2,1)}, bf16[32,4096]{1,0:T(8,128)(2,1)S(1)}, u32[]{:S(2)}, u32[]{:S(2)}) collective-permute-start(bf16[32,4096]{1,0:T(8,128)(2,1)} %collective-permute-done.16), channel_id=1, source_target_pairs={{0,8},{2,6},{8,16},{10,2},{16,24},{18,10},{24,28},{26,18},{28,20},... | collective-permute-start | bytes 786440 | tf_op jit(solution)/shard_map/ppermute | solution.py:54
  59.4 6.4 %collective-permute-start.6 = (bf16[32,4096]{1,0:T(8,128)(2,1)S(1)}, bf16[32,4096]{1,0:T(8,128)(2,1)S(1)}, u32[]{:S(2)}, u32[]{:S(2)}) collective-permute-start(bf16[32,4096]{1,0:T(8,128)(2,1)S(1)} %collective-permute-done.5), channel_id=1, source_target_pairs={{0,8},{2,6},{8,16},{10,2},{16,24},{18,10},{24,28},{26,18},{28,20},... | collective-permute-start | bytes 786440 | tf_op jit(solution)/shard_map/ppermute | solution.py:54
  62.0 6.7 %collective-permute-start.18 = (bf16[32,4096]{1,0:T(8,128)(2,1)S(1)}, bf16[32,4096]{1,0:T(8,128)(2,1)S(1)}, u32[]{:S(2)}, u32[]{:S(2)}) collective-permute-start(bf16[32,4096]{1,0:T(8,128)(2,1)S(1)} %collective-permute-done.17), channel_id=1, source_target_pairs={{0,8},{2,6},{8,16},{10,2},{16,24},{18,10},{24,28},{26,18},{28,20},... | collective-permute-start | bytes 786440 | tf_op jit(solution)/shard_map/ppermute | solution.py:54
  65.9 6.4 %collective-permute-start.7 = (bf16[32,4096]{1,0:T(8,128)(2,1)S(1)}, bf16[32,4096]{1,0:T(8,128)(2,1)S(1)}, u32[]{:S(2)}, u32[]{:S(2)}) collective-permute-start(bf16[32,4096]{1,0:T(8,128)(2,1)S(1)} %collective-permute-done.6), channel_id=1, source_target_pairs={{0,8},{2,6},{8,16},{10,2},{16,24},{18,10},{24,28},{26,18},{28,20},... | collective-permute-start | bytes 786440 | tf_op jit(solution)/shard_map/ppermute | solution.py:54
  68.7 6.4 %collective-permute-start.19 = (bf16[32,4096]{1,0:T(8,128)(2,1)S(1)}, bf16[32,4096]{1,0:T(8,128)(2,1)S(1)}, u32[]{:S(2)}, u32[]{:S(2)}) collective-permute-start(bf16[32,4096]{1,0:T(8,128)(2,1)S(1)} %collective-permute-done.18), channel_id=1, source_target_pairs={{0,8},{2,6},{8,16},{10,2},{16,24},{18,10},{24,28},{26,18},{28,20},... | collective-permute-start | bytes 786440 | tf_op jit(solution)/shard_map/ppermute | solution.py:54
  72.2 6.4 %collective-permute-start.8 = (bf16[32,4096]{1,0:T(8,128)(2,1)S(1)}, bf16[32,4096]{1,0:T(8,128)(2,1)S(1)}, u32[]{:S(2)}, u32[]{:S(2)}) collective-permute-start(bf16[32,4096]{1,0:T(8,128)(2,1)S(1)} %collective-permute-done.7), channel_id=1, source_target_pairs={{0,8},{2,6},{8,16},{10,2},{16,24},{18,10},{24,28},{26,18},{28,20},... | collective-permute-start | bytes 786440 | tf_op jit(solution)/shard_map/ppermute | solution.py:54
  75.0 6.4 %collective-permute-start.20 = (bf16[32,4096]{1,0:T(8,128)(2,1)S(1)}, bf16[32,4096]{1,0:T(8,128)(2,1)S(1)}, u32[]{:S(2)}, u32[]{:S(2)}) collective-permute-start(bf16[32,4096]{1,0:T(8,128)(2,1)S(1)} %collective-permute-done.19), channel_id=1, source_target_pairs={{0,8},{2,6},{8,16},{10,2},{16,24},{18,10},{24,28},{26,18},{28,20},... | collective-permute-start | bytes 786440 | tf_op jit(solution)/shard_map/ppermute | solution.py:54
  78.6 6.4 %collective-permute-start.9 = (bf16[32,4096]{1,0:T(8,128)(2,1)S(1)}, bf16[32,4096]{1,0:T(8,128)(2,1)S(1)}, u32[]{:S(2)}, u32[]{:S(2)}) collective-permute-start(bf16[32,4096]{1,0:T(8,128)(2,1)S(1)} %collective-permute-done.8), channel_id=1, source_target_pairs={{0,8},{2,6},{8,16},{10,2},{16,24},{18,10},{24,28},{26,18},{28,20},... | collective-permute-start | bytes 786440 | tf_op jit(solution)/shard_map/ppermute | solution.py:54
  81.4 6.4 %collective-permute-start.21 = (bf16[32,4096]{1,0:T(8,128)(2,1)S(1)}, bf16[32,4096]{1,0:T(8,128)(2,1)S(1)}, u32[]{:S(2)}, u32[]{:S(2)}) collective-permute-start(bf16[32,4096]{1,0:T(8,128)(2,1)S(1)} %collective-permute-done.20), channel_id=1, source_target_pairs={{0,8},{2,6},{8,16},{10,2},{16,24},{18,10},{24,28},{26,18},{28,20},... | collective-permute-start | bytes 786440 | tf_op jit(solution)/shard_map/ppermute | solution.py:54
  85.0 6.4 %collective-permute-start.10 = (bf16[32,4096]{1,0:T(8,128)(2,1)S(1)}, bf16[32,4096]{1,0:T(8,128)(2,1)S(1)}, u32[]{:S(2)}, u32[]{:S(2)}) collective-permute-start(bf16[32,4096]{1,0:T(8,128)(2,1)S(1)} %collective-permute-done.9), channel_id=1, source_target_pairs={{0,8},{2,6},{8,16},{10,2},{16,24},{18,10},{24,28},{26,18},{28,20},... | collective-permute-start | bytes 786440 | tf_op jit(solution)/shard_map/ppermute | solution.py:54
  87.8 6.4 %collective-permute-start.22 = (bf16[32,4096]{1,0:T(8,128)(2,1)S(1)}, bf16[32,4096]{1,0:T(8,128)(2,1)S(1)}, u32[]{:S(2)}, u32[]{:S(2)}) collective-permute-start(bf16[32,4096]{1,0:T(8,128)(2,1)S(1)} %collective-permute-done.21), channel_id=1, source_target_pairs={{0,8},{2,6},{8,16},{10,2},{16,24},{18,10},{24,28},{26,18},{28,20},... | collective-permute-start | bytes 786440 | tf_op jit(solution)/shard_map/ppermute | solution.py:54
  92.5 14.3 %collective-permute-start.11 = (bf16[128,4096]{1,0:T(8,128)(2,1)}, bf16[128,4096]{1,0:T(8,128)(2,1)}, u32[]{:S(2)}, u32[]{:S(2)}) collective-permute-start(bf16[128,4096]{1,0:T(8,128)(2,1)} %slice.79), channel_id=1, source_target_pairs={{0,2},{2,0},{4,6},{6,4},{8,10},{10,8},{12,14},{14,12},{16,18},{18,... | collective-permute-start | bytes 3145736 | tf_op jit(solution)/shard_map/ppermute | solution.py:101
  95.2 14.6 %collective-permute-start.23 = (bf16[128,4096]{1,0:T(8,128)(2,1)}, bf16[128,4096]{1,0:T(8,128)(2,1)}, u32[]{:S(2)}, u32[]{:S(2)}) collective-permute-start(bf16[128,4096]{1,0:T(8,128)(2,1)} %slice.86), channel_id=1, source_target_pairs={{0,2},{2,0},{4,6},{6,4},{8,10},{10,8},{12,14},{14,12},{16,18},{18,... | collective-permute-start | bytes 3145736 | tf_op jit(solution)/shard_map/ppermute | solution.py:102
  121.2 14.5 %collective-permute-start.25 = (bf16[64,4096]{1,0:T(8,128)(2,1)}, bf16[64,4096]{1,0:T(8,128)(2,1)}, u32[]{:S(2)}, u32[]{:S(2)}) collective-permute-start(bf16[64,4096]{1,0:T(8,128)(2,1)} %slice.119), channel_id=1, source_target_pairs={{0,1},{1,0},{2,3},{3,2},{4,5},{5,4},{6,7},{7,6},{8,9},{9,8},{10,11... | collective-permute-start | bytes 1572872 | tf_op jit(solution)/shard_map/ppermute | solution.py:127
  137.3 10.7 %collective-permute-start.26 = (bf16[8,4096]{1,0:T(8,128)(2,1)S(1)}, bf16[8,4096]{1,0:T(8,128)(2,1)S(1)}, u32[]{:S(2)}, u32[]{:S(2)}) collective-permute-start(bf16[8,4096]{1,0:T(8,128)(2,1)S(1)} %get-tuple-element.11), channel_id=1, source_target_pairs={{0,4},{2,6},{4,0},{6,2},{8,12},{10,14},{12,8},{14,10},{16,20},{18,... | collective-permute-start | bytes 196616 | tf_op jit(solution)/shard_map/ppermute | solution.py:135
  139.0 10.3 %collective-permute-start.32 = (bf16[8,4096]{1,0:T(8,128)(2,1)S(1)}, bf16[8,4096]{1,0:T(8,128)(2,1)S(1)}, u32[]{:S(2)}, u32[]{:S(2)}) collective-permute-start(bf16[8,4096]{1,0:T(8,128)(2,1)S(1)} %get-tuple-element.12), channel_id=1, source_target_pairs={{0,28},{2,30},{4,24},{6,26},{8,20},{10,22},{12,16},{14,18},{16,12}... | collective-permute-start | bytes 196616 | tf_op jit(solution)/shard_map/ppermute | solution.py:135
  144.0 8.5 %collective-permute-start.31 = (bf16[8,4096]{1,0:T(8,128)(2,1)S(1)}, bf16[8,4096]{1,0:T(8,128)(2,1)S(1)}, u32[]{:S(2)}, u32[]{:S(2)}) collective-permute-start(bf16[8,4096]{1,0:T(8,128)(2,1)S(1)} %get-tuple-element.13), channel_id=1, source_target_pairs={{0,24},{2,26},{4,28},{6,30},{8,16},{10,18},{12,20},{14,22},{16,8},... | collective-permute-start | bytes 196616 | tf_op jit(solution)/shard_map/ppermute | solution.py:135
  144.0 10.3 %collective-permute-start.30 = (bf16[8,4096]{1,0:T(8,128)(2,1)S(1)}, bf16[8,4096]{1,0:T(8,128)(2,1)S(1)}, u32[]{:S(2)}, u32[]{:S(2)}) collective-permute-start(bf16[8,4096]{1,0:T(8,128)(2,1)S(1)} %get-tuple-element.14), channel_id=1, source_target_pairs={{0,20},{2,22},{4,16},{6,18},{8,28},{10,30},{12,24},{14,26},{16,4},... | collective-permute-start | bytes 196616 | tf_op jit(solution)/shard_map/ppermute | solution.py:135
  145.9 8.5 %collective-permute-start.29 = (bf16[8,4096]{1,0:T(8,128)(2,1)S(1)}, bf16[8,4096]{1,0:T(8,128)(2,1)S(1)}, u32[]{:S(2)}, u32[]{:S(2)}) collective-permute-start(bf16[8,4096]{1,0:T(8,128)(2,1)S(1)} %get-tuple-element.15), channel_id=1, source_target_pairs={{0,16},{2,18},{4,20},{6,22},{8,24},{10,26},{12,28},{14,30},{16,0},... | collective-permute-start | bytes 196616 | tf_op jit(solution)/shard_map/ppermute | solution.py:135
  148.0 6.4 %collective-permute-start.28 = (bf16[8,4096]{1,0:T(8,128)(2,1)S(1)}, bf16[8,4096]{1,0:T(8,128)(2,1)S(1)}, u32[]{:S(2)}, u32[]{:S(2)}) collective-permute-start(bf16[8,4096]{1,0:T(8,128)(2,1)S(1)} %get-tuple-element.16), channel_id=1, source_target_pairs={{0,12},{2,14},{4,8},{6,10},{8,4},{10,6},{12,0},{14,2},{16,28},{18,... | collective-permute-start | bytes 196616 | tf_op jit(solution)/shard_map/ppermute | solution.py:135
  149.3 5.7 %collective-permute-start.27 = (bf16[8,4096]{1,0:T(8,128)(2,1)S(1)}, bf16[8,4096]{1,0:T(8,128)(2,1)S(1)}, u32[]{:S(2)}, u32[]{:S(2)}) collective-permute-start(bf16[8,4096]{1,0:T(8,128)(2,1)S(1)} %get-tuple-element.17), channel_id=1, source_target_pairs={{0,8},{2,10},{4,12},{6,14},{8,0},{10,2},{12,4},{14,6},{16,24},{18,... | collective-permute-start | bytes 196616 | tf_op jit(solution)/shard_map/ppermute | solution.py:135
  (22 other events, 113.6 us)
Sparse Core Ops, SparseCore 0:
  10.5 47.4 all-gather.1

commit v2 on v1

v2 whole, which is shorter than its diff:
```python
import math

import jax
import jax.numpy as jnp
from jax import lax
from jax.sharding import PartitionSpec as P

STEP = 24


def ring_order(n_chip):
    nz = n_chip // 2
    return [2 * z for z in range(nz)] + [2 * z + 1 for z in reversed(range(nz))]


def ring_pairs(n_chip):
    order = ring_order(n_chip)
    pairs = []
    for i, chip in enumerate(order):
        pairs.append((2 * chip, 2 * order[(i + 1) % n_chip]))
        pairs.append((2 * chip + 1, 2 * order[(i - 1) % n_chip] + 1))
    return pairs


def swap_pairs(n, bit):
    return [(i, i ^ bit) for i in range(n)]


def rows_at(x, tile, count):
    return lax.dynamic_slice_in_dim(x, tile * 8, count, 0)


def put_rows(x, rows, tile):
    return lax.dynamic_update_slice_in_dim(x, rows, tile * 8, 0)


def gather_rows(bank_s, bank_t, passages, owner, index, core):
    n_dev = lax.axis_size("wide")
    n_chip = n_dev // 2
    pool, width = bank_s.shape
    sub = passages.shape[0]
    far = n_chip // 2
    cut = 4 * STEP if pool >= 8 * STEP else pool // 2
    n_cut = cut // STEP
    n_shared = -(-(pool - 2 * cut) // STEP)
    chunks = n_cut + n_shared
    rounds = max(n_cut + n_chip - 2, chunks + far - 1)
    chip = index // 2

    def place(c):
        return jnp.where(c % 2 == 0, c // 2, n_chip - 1 - c // 2)

    def chip_at(p):
        return jnp.where(p < n_chip // 2, 2 * p, 2 * (n_chip - 1 - p) + 1)

    here = place(chip)
    turn = 1 - 2 * core
    distance = (turn * (here - place(owner // 2)) + n_chip) % n_chip
    own_chip = owner // 2 == chip
    own_core = owner == index
    near = distance <= far
    swap = swap_pairs(n_dev, 1)
    pairs = ring_pairs(n_chip)
    banks = (bank_s, bank_t)

    def start_of(j, side):
        shared = jnp.minimum((2 * cut + (j - n_cut) * STEP) // 8, (pool - STEP) // 8)
        return jnp.where(j < n_cut, side * (cut // 8) + j * (STEP // 8), shared)

    def handed(held, start, count):
        return [lax.ppermute(rows_at(b, start, count), "wide", swap) for b in held]

    early = 2 * STEP
    first = handed(banks, (1 - core) * (cut // 8), early)
    mine = [
        jnp.where(own_core, rows_at(b, core * (cut // 8), early), g) for b, g in zip(banks, first)
    ]

    def own_rows(i, j):
        if j < 2:
            return mine[i][j * STEP : (j + 1) * STEP]
        if j < n_cut:
            return later[i][(j - 2) * STEP : (j - 1) * STEP]
        at = min((j - n_cut) * STEP, pool - 2 * cut - STEP) + cut - early
        return later[i][at : at + STEP]

    pools = [jnp.zeros_like(bank_s), jnp.zeros_like(bank_t)]
    moving = [own_rows(i, 0) for i in range(2)]
    rows = put_rows(jnp.zeros((n_chip * sub, width), passages.dtype), passages, 0)
    riding = passages
    arrived = [[], []]
    for t in range(rounds):
        slot = jnp.where(own_chip, t, t - (distance - 1))
        take = (slot >= 0) & (slot < chunks)
        where_to = start_of(jnp.clip(slot, 0, chunks - 1), core)
        for i in range(2):
            ride = i == 0 and t < n_chip - 1
            sent = jnp.concatenate([moving[i], riding], 0) if ride else moving[i]
            if t >= 2:
                sent, arrived[1 - i][t - 2] = lax.optimization_barrier((sent, arrived[1 - i][t - 2]))
            got = lax.ppermute(sent, "wide", pairs)
            arrived[i].append(got)
            if ride:
                riding = got[STEP:]
                got = got[:STEP]
                origin = chip_at((here - turn * (t + 1) + n_chip) % n_chip)
                rows = put_rows(rows, riding, (origin ^ chip) * (sub // 8))
            kept = jnp.where(own_chip, own_rows(i, t), got) if t < chunks else got
            pools[i] = put_rows(
                pools[i], jnp.where(take, kept, rows_at(pools[i], where_to, STEP)), where_to
            )
            moving[i] = got
            if t + 1 < chunks:
                moving[i] = jnp.where(own_chip, own_rows(i, t + 1), got)
        if t == 0:
            held, arrived[0][0] = lax.optimization_barrier((banks, arrived[0][0]))
            second = handed(held, (1 - core) * (cut // 8) + early // 8, cut - early)
            third = handed(held, 2 * cut // 8, pool - 2 * cut)
            later = [
                jnp.concatenate(
                    [
                        jnp.where(own_core, rows_at(b, core * (cut // 8) + early // 8, cut - early), g),
                        jnp.where(own_core, b[2 * cut :], h),
                    ],
                    0,
                )
                for b, g, h in zip(held, second, third)
            ]
    full = []
    for p in pools:
        ring = rows_at(p, core * (cut // 8), cut)
        tail = p[2 * cut :]
        ring_other = lax.ppermute(ring, "wide", swap)
        tail_other = lax.ppermute(tail, "wide", swap)
        low = jnp.where(core == 0, ring, ring_other)
        high = jnp.where(core == 0, ring_other, ring)
        full.append(jnp.concatenate([low, high, jnp.where(near, tail, tail_other)], 0))
    return full[0], full[1], rows


def dot_t(a, b):
    return lax.dot_general(a, b, (((1,), (1,)), ((), ())), preferred_element_type=jnp.float32)


def body(
    queries, teacher_queries, passages, bank_student, bank_teacher, owner, positives, keep_mask
):
    n_dev = lax.axis_size("wide")
    n_chip = n_dev // 2
    n_dp = lax.axis_size("dp")
    index = lax.axis_index("wide")
    replica = lax.axis_index("dp")
    core = index % 2
    chip = index // 2
    block, width = passages.shape
    scale = 2.0 / math.sqrt(width)
    n_pass = block * n_dev
    parts = 2 if n_dp == 2 else 1
    sub = block // parts
    swap = swap_pairs(n_dev, 1)
    across = [(0, 1), (1, 0)]

    part = rows_at(passages, replica * (sub // 8), sub) if parts == 2 else passages
    pool_s, pool_t, rows = gather_rows(bank_student, bank_teacher, part, owner[0], index, core)
    if parts == 2:
        rows = jnp.concatenate([rows, lax.ppermute(rows, "dp", across)], 0)
    pieces = jnp.concatenate([rows, lax.ppermute(rows, "wide", swap)], 0)
    chip_of = (positives // (2 * block)) ^ chip
    core_of = ((positives // block) % 2) ^ core
    half_of = (positives // sub) % parts
    if parts == 2:
        half_of = half_of ^ replica
    column = ((core_of * parts + half_of) * n_chip + chip_of) * sub + positives % sub

    zp = dot_t(queries, pieces) * scale

    keep = keep_mask.astype(jnp.float32)
    zq = dot_t(queries, pool_s) * scale
    tt = dot_t(teacher_queries, pool_t) * scale
    weight = keep * jax.nn.sigmoid(-tt)
    top = jnp.maximum(jnp.max(zp, axis=1), jnp.max(zq, axis=1))
    total = jnp.sum(jnp.exp(zp - top[:, None]), axis=1) + jnp.sum(
        weight * jnp.exp(zq - top[:, None]), axis=1
    )
    lse = top + jnp.log(total)
    hit = (jnp.arange(n_pass, dtype=jnp.int32)[None, :] == column[:, None]).astype(jnp.float32)
    row_loss = lse - jnp.sum(zp * hit, axis=1)
    grad_p = (jnp.exp(zp - lse[:, None]) - hit).astype(jnp.bfloat16)
    grad_q = (weight * jnp.exp(zq - lse[:, None])).astype(jnp.bfloat16)

    mid = n_pass // 2
    bits = [("wide", 1 << (b + 1), swap_pairs(n_dev, 1 << (b + 1))) for b in range(n_chip.bit_length() - 1)]
    dims = [("x", bits[0][2])] + [("z%d" % i, b[2]) for i, b in enumerate(bits[1:])]
    names = (["y"] if parts == 2 else []) + [d[0] for d in reversed(dims)]
    pairs_of = dict(dims)

    def reduced(columns, orders):
        def terms(grads):
            return lax.dot_general(
                grads, columns, (((0,), (0,)), ((), ())), preferred_element_type=jnp.float32
            )

        got = lax.ppermute(terms(grad_p[:, mid:]), "wide", swap)
        sums = (terms(grad_p[:, :mid]) + got).reshape((2,) * len(names) + (sub, columns.shape[1]))
        left = list(names)
        for name in orders:
            at = left.index(name)
            sent = lax.index_in_dim(sums, 1, at, keepdims=False).astype(jnp.bfloat16)
            if name == "y":
                got = lax.ppermute(sent, "dp", across)
            else:
                got = lax.ppermute(sent, "wide", pairs_of[name])
            sums = lax.index_in_dim(sums, 0, at, keepdims=False) + got.astype(jnp.float32)
            left.pop(at)
        return sums

    zs = [d[0] for d in dims[1:]]
    if parts == 2:
        orders = (["y", "x"] + zs, ["x", "y"] + zs)
    else:
        orders = (["x"] + zs, zs + ["x"])
    cut = width // 2
    own = jnp.concatenate(
        [reduced(queries[:, :cut], orders[0]), reduced(queries[:, cut:], orders[1])], 1
    )
    if parts == 2:
        own = own * scale
        got = lax.ppermute(own, "dp", across)
        low, high = jnp.where(replica == 0, own, got), jnp.where(replica == 0, got, own)
        passage_grad = jnp.concatenate([low, high], 0)
    else:
        passage_grad = lax.psum(own, "dp") * scale

    qgrad = jnp.dot(grad_p, pieces, preferred_element_type=jnp.float32) + jnp.dot(
        grad_q, pool_s, preferred_element_type=jnp.float32
    )
    query_grad = (qgrad * scale).astype(jnp.bfloat16)
    return (row_loss, query_grad, passage_grad)


def solution(mesh):
    placed = (
        P(("wide", "dp"), None),
        P(("wide", "dp"), None),
        P("wide", None),
        P("wide", None),
        P("wide", None),
        P("dp"),
        P(("wide", "dp")),
        P(("wide", "dp"), None),
    )
    return jax.shard_map(
        body,
        mesh=mesh,
        in_specs=placed,
        out_specs=(P(("wide", "dp")), P(("wide", "dp"), None), P("wide", None)),
        check_vma=False,
    )
```

time: 168 us -> 139 us (0.83)
  between operations: 16.7 us -> 2.83 us
  local copies, waits for them, and re-layouts: 14.3 us -> 6.94 us
  other arithmetic: 12.1 us -> 7.16 us
  matrix products: 20.1 us -> 16.5 us
    dot_general x5 -> x3, matrix products: 11.5 us -> 5.35 us  [dot_t(): lax.dot_general(a, b, (((1,), (1,)), ((), ())), preferred_element_type=jn...]
    select_n x10 -> x11, other arithmetic: 7.94 us -> 3.45 us  [the longest x2 2.32 us: gather_rows(): jnp.where(own_core, rows_at(b, core * (cut // 8), early), g)]
    slice x6 -> x14, local copies, waits for them, and re-layouts: 3.89 us -> 0.3 us  [the longest x2 0.07 us: gather_rows(): tail = p[2 * cut:]]
    dynamic_update_slice x14 -> x2, local copies, waits for them, and re-layouts: 2.22 us -> 0.04 us  [put_rows(): return lax.dynamic_update_slice_in_dim(x, rows, tile * 8, 0)]
    unnamed x39 -> x31, local copies, waits for them, and re-layouts: 4.67 us -> 2.89 us
    dynamic_update_slice x0 -> x18, other arithmetic: none -> 1.72 us  [put_rows(): return lax.dynamic_update_slice_in_dim(x, rows, tile * 8, 0)]
    dot_general x4 -> x5, matrix products: 7.26 us -> 8.31 us  [the longest x4 5.64 us: terms(): lax.dot_general(grads, columns, (((0,), (0,)), ((), ())), preferred_eleme...]
    ppermute x33 -> x42, starting transfers between devices: 53.8 us -> 54.8 us  [the longest x20 38.9 us: gather_rows(): got = lax.ppermute(sent, 'wide', pairs)]
  transfers between devices with their start and end apart: 35 -> 43, of which waited for: 25 -> 26; matrix products, arithmetic and copies ran while one was open for 19% -> 13% of each run, Pallas kernels for 0% -> 0%
where the time goes in v2:
time: 139 us
  starting transfers between devices  55.4 us (40%)
  waiting for transfers between devices  50 us (36%)
  matrix products  16.5 us (12%)
  other arithmetic  7.16 us (5%)
  local copies, waits for them, and re-layouts  6.94 us (5%)
  between operations  2.83 us (2%)
    ppermute x20, starting transfers between devices, gather_rows(): got = lax.ppermute(sent, 'wide', pairs)  38.9 us
    ppermute x20, waiting for transfers between devices, gather_rows(): got = lax.ppermute(sent, 'wide', pairs)  33.1 us
    ppermute x6, waiting for transfers between devices, reduced(): got = lax.ppermute(sent, 'wide', pairs_of[name])  10 us
    ppermute x6, starting transfers between devices, reduced(): got = lax.ppermute(sent, 'wide', pairs_of[name])  9.91 us
    dot_general x4, matrix products, terms(): lax.dot_general(grads, columns, (((0,), (0,)), ((), ())), preferred_eleme...  5.64 us
    dot_general x3, matrix products, dot_t(): lax.dot_general(a, b, (((1,), (1,)), ((), ())), preferred_element_type=jn...  5.35 us
    ppermute x2, waiting for transfers between devices, reduced(): got = lax.ppermute(sent, 'dp', across)  4 us
    dynamic_slice x7, local copies, waits for them, and re-layouts, rows_at(): return lax.dynamic_slice_in_dim(x, tile * 8, count, 0)  3.14 us
  transfers between devices with their start and end apart: 43, of which 26 were waited for; matrix products, arithmetic and copies ran while one was open for 13% of the time, Pallas kernels for 0%

profile of v2, /device:TPU:0, one launch (start us, length us, event | category | flops | bytes accessed | tf_op | source)
XLA Modules:
  0.0 138.8 jit_solution(8660753776476966905)
XLA Ops:
  0.7 1.9 %constant_dynamic-slice_fusion.5 = bf16[48,4096]{1,0:T(8,128)(2,1)} fusion(bf16[256,4096]{1,0:T(8,128)(2,1)} %param.11, s32[]{:T(128)S(6)} %select_n.593), kind=kLoop, calls=%fused_computation.143 | loop fusion | bytes 786436 | tf_op jit(solution)/shard_map/dynamic_slice | solution.py:30
  9.1 3.1 %collective-permute-start.5 = (bf16[24,4096]{1,0:T(8,128)(2,1)S(1)}, bf16[24,4096]{1,0:T(8,128)(2,1)S(1)}, u32[]{:S(2)}, u32[]{:S(2)}) collective-permute-start(bf16[24,4096]{1,0:T(8,128)(2,1)S(1)} %slice.241), channel_id=1, source_target_pairs={{0,8},{2,6},{8,16},{10,2},{16,24},{18,10},{24,28},{26,18},{28,20},... | collective-permute-start | bytes 589832 | tf_op jit(solution)/shard_map/ppermute | solution.py:101
  13.9 1.9 %collective-permute-done.5 = bf16[24,4096]{1,0:T(8,128)(2,1)S(1)} collective-permute-done((bf16[24,4096]{1,0:T(8,128)(2,1)S(1)}, bf16[24,4096]{1,0:T(8,128)(2,1)S(1)}, u32[]{:S(2)}, u32[]{:S(2)}) %collective-permute-start.5) | collective-permute-done | bytes 196640 | tf_op jit(solution)/shard_map/ppermute | solution.py:101
  16.1 2.2 %collective-permute-start.7 = (bf16[24,4096]{1,0:T(8,128)(2,1)S(1)}, bf16[24,4096]{1,0:T(8,128)(2,1)S(1)}, u32[]{:S(2)}, u32[]{:S(2)}) collective-permute-start(bf16[24,4096]{1,0:T(8,128)(2,1)S(1)} %get-tuple-element.61), channel_id=1, source_target_pairs={{0,8},{2,6},{8,16},{10,2},{16,24},{18,10},{24,28},{26,18},{28,20},... | collective-permute-start | bytes 589832 | tf_op jit(solution)/shard_map/ppermute | solution.py:101
  19.1 2.1 %collective-permute-start.2 = (bf16[32,4096]{1,0:T(8,128)(2,1)S(1)}, bf16[32,4096]{1,0:T(8,128)(2,1)S(1)}, u32[]{:S(2)}, u32[]{:S(2)}) collective-permute-start(bf16[32,4096]{1,0:T(8,128)(2,1)S(1)} %pad_maximum_fusion.8), channel_id=1, source_target_pairs={{0,8},{2,6},{8,16},{10,2},{16,24},{18,10},{24,28},{26,18},{28,20},... | collective-permute-start | bytes 786440 | tf_op jit(solution)/shard_map/ppermute | solution.py:101
  22.0 3.5 %collective-permute-done.2 = bf16[32,4096]{1,0:T(8,128)(2,1)S(1)} collective-permute-done((bf16[32,4096]{1,0:T(8,128)(2,1)S(1)}, bf16[32,4096]{1,0:T(8,128)(2,1)S(1)}, u32[]{:S(2)}, u32[]{:S(2)}) %collective-permute-start.2) | collective-permute-done | bytes 262176 | tf_op jit(solution)/shard_map/ppermute | solution.py:101
  25.8 2.1 %collective-permute-start.6 = (bf16[32,4096]{1,0:T(8,128)(2,1)S(1)}, bf16[32,4096]{1,0:T(8,128)(2,1)S(1)}, u32[]{:S(2)}, u32[]{:S(2)}) collective-permute-start(bf16[32,4096]{1,0:T(8,128)(2,1)S(1)} %pad_maximum_fusion.9), channel_id=1, source_target_pairs={{0,8},{2,6},{8,16},{10,2},{16,24},{18,10},{24,28},{26,18},{28,20},... | collective-permute-start | bytes 786440 | tf_op jit(solution)/shard_map/ppermute | solution.py:101
  28.0 4.2 %collective-permute-done.6 = bf16[32,4096]{1,0:T(8,128)(2,1)S(1)} collective-permute-done((bf16[32,4096]{1,0:T(8,128)(2,1)S(1)}, bf16[32,4096]{1,0:T(8,128)(2,1)S(1)}, u32[]{:S(2)}, u32[]{:S(2)}) %collective-permute-start.6) | collective-permute-done | bytes 262176 | tf_op jit(solution)/shard_map/ppermute | solution.py:101
  32.4 2.1 %collective-permute-start.8 = (bf16[32,4096]{1,0:T(8,128)(2,1)S(1)}, bf16[32,4096]{1,0:T(8,128)(2,1)S(1)}, u32[]{:S(2)}, u32[]{:S(2)}) collective-permute-start(bf16[32,4096]{1,0:T(8,128)(2,1)S(1)} %pad_maximum_fusion.10), channel_id=1, source_target_pairs={{0,8},{2,6},{8,16},{10,2},{16,24},{18,10},{24,28},{26,18},{28,20},... | collective-permute-start | bytes 786440 | tf_op jit(solution)/shard_map/ppermute | solution.py:101
  34.5 4.3 %collective-permute-done.8 = bf16[32,4096]{1,0:T(8,128)(2,1)S(1)} collective-permute-done((bf16[32,4096]{1,0:T(8,128)(2,1)S(1)}, bf16[32,4096]{1,0:T(8,128)(2,1)S(1)}, u32[]{:S(2)}, u32[]{:S(2)}) %collective-permute-start.8) | collective-permute-done | bytes 262176 | tf_op jit(solution)/shard_map/ppermute | solution.py:101
  39.0 2.1 %collective-permute-start.11 = (bf16[24,4096]{1,0:T(8,128)(2,1)S(1)}, bf16[24,4096]{1,0:T(8,128)(2,1)S(1)}, u32[]{:S(2)}, u32[]{:S(2)}) collective-permute-start(bf16[24,4096]{1,0:T(8,128)(2,1)S(1)} %get-tuple-element.85), channel_id=1, source_target_pairs={{0,8},{2,6},{8,16},{10,2},{16,24},{18,10},{24,28},{26,18},{28,20},... | collective-permute-start | bytes 589832 | tf_op jit(solution)/shard_map/ppermute | solution.py:101
  41.1 3.6 %collective-permute-done.11 = bf16[24,4096]{1,0:T(8,128)(2,1)S(1)} collective-permute-done((bf16[24,4096]{1,0:T(8,128)(2,1)S(1)}, bf16[24,4096]{1,0:T(8,128)(2,1)S(1)}, u32[]{:S(2)}, u32[]{:S(2)}) %collective-permute-start.11) | collective-permute-done | bytes 196640 | tf_op jit(solution)/shard_map/ppermute | solution.py:101
  44.9 2.1 %collective-permute-start.13 = (bf16[24,4096]{1,0:T(8,128)(2,1)S(1)}, bf16[24,4096]{1,0:T(8,128)(2,1)S(1)}, u32[]{:S(2)}, u32[]{:S(2)}) collective-permute-start(bf16[24,4096]{1,0:T(8,128)(2,1)S(1)} %get-tuple-element.25), channel_id=1, source_target_pairs={{0,8},{2,6},{8,16},{10,2},{16,24},{18,10},{24,28},{26,18},{28,20},... | collective-permute-start | bytes 589832 | tf_op jit(solution)/shard_map/ppermute | solution.py:101
  48.6 2.0 %collective-permute-done.13 = bf16[24,4096]{1,0:T(8,128)(2,1)S(1)} collective-permute-done((bf16[24,4096]{1,0:T(8,128)(2,1)S(1)}, bf16[24,4096]{1,0:T(8,128)(2,1)S(1)}, u32[]{:S(2)}, u32[]{:S(2)}) %collective-permute-start.13) | collective-permute-done | bytes 196640 | tf_op jit(solution)/shard_map/ppermute | solution.py:101
  50.7 2.1 %collective-permute-start.16 = (bf16[24,4096]{1,0:T(8,128)(2,1)S(1)}, bf16[24,4096]{1,0:T(8,128)(2,1)S(1)}, u32[]{:S(2)}, u32[]{:S(2)}) collective-permute-start(bf16[24,4096]{1,0:T(8,128)(2,1)S(1)} %get-tuple-element.27), channel_id=1, source_target_pairs={{0,8},{2,6},{8,16},{10,2},{16,24},{18,10},{24,28},{26,18},{28,20},... | collective-permute-start | bytes 589832 | tf_op jit(solution)/shard_map/ppermute | solution.py:101
  53.6 2.1 %collective-permute-start.14 = (bf16[32,4096]{1,0:T(8,128)(2,1)S(1)}, bf16[32,4096]{1,0:T(8,128)(2,1)S(1)}, u32[]{:S(2)}, u32[]{:S(2)}) collective-permute-start(bf16[32,4096]{1,0:T(8,128)(2,1)S(1)} %pad_maximum_fusion.12), channel_id=1, source_target_pairs={{0,8},{2,6},{8,16},{10,2},{16,24},{18,10},{24,28},{26,18},{28,20},... | collective-permute-start | bytes 786440 | tf_op jit(solution)/shard_map/ppermute | solution.py:101
  56.5 2.1 %collective-permute-start.20 = (bf16[24,4096]{1,0:T(8,128)(2,1)S(1)}, bf16[24,4096]{1,0:T(8,128)(2,1)S(1)}, u32[]{:S(2)}, u32[]{:S(2)}) collective-permute-start(bf16[24,4096]{1,0:T(8,128)(2,1)S(1)} %get-tuple-element.29), channel_id=1, source_target_pairs={{0,8},{2,6},{8,16},{10,2},{16,24},{18,10},{24,28},{26,18},{28,20},... | collective-permute-start | bytes 589832 | tf_op jit(solution)/shard_map/ppermute | solution.py:101
  60.1 2.1 %collective-permute-start.17 = (bf16[32,4096]{1,0:T(8,128)(2,1)S(1)}, bf16[32,4096]{1,0:T(8,128)(2,1)S(1)}, u32[]{:S(2)}, u32[]{:S(2)}) collective-permute-start(bf16[32,4096]{1,0:T(8,128)(2,1)S(1)} %pad_maximum_fusion.13), channel_id=1, source_target_pairs={{0,8},{2,6},{8,16},{10,2},{16,24},{18,10},{24,28},{26,18},{28,20},... | collective-permute-start | bytes 786440 | tf_op jit(solution)/shard_map/ppermute | solution.py:101
  62.4 2.1 %collective-permute-start.22 = (bf16[24,4096]{1,0:T(8,128)(2,1)S(1)}, bf16[24,4096]{1,0:T(8,128)(2,1)S(1)}, u32[]{:S(2)}, u32[]{:S(2)}) collective-permute-start(bf16[24,4096]{1,0:T(8,128)(2,1)S(1)} %get-tuple-element.31), channel_id=1, source_target_pairs={{0,8},{2,6},{8,16},{10,2},{16,24},{18,10},{24,28},{26,18},{28,20},... | collective-permute-start | bytes 589832 | tf_op jit(solution)/shard_map/ppermute | solution.py:101
  64.5 2.1 %collective-permute-done.17 = bf16[32,4096]{1,0:T(8,128)(2,1)S(1)} collective-permute-done((bf16[32,4096]{1,0:T(8,128)(2,1)S(1)}, bf16[32,4096]{1,0:T(8,128)(2,1)S(1)}, u32[]{:S(2)}, u32[]{:S(2)}) %collective-permute-start.17) | collective-permute-done | bytes 262176 | tf_op jit(solution)/shard_map/ppermute | solution.py:101
  66.6 2.0 %collective-permute-start.18 = (bf16[64,4096]{1,0:T(8,128)(2,1)S(1)}, bf16[64,4096]{1,0:T(8,128)(2,1)S(1)}, u32[]{:S(2)}, u32[]{:S(2)}) collective-permute-start(bf16[64,4096]{1,0:T(8,128)(2,1)S(1)} %slice_dynamic-update-slice_fusion), channel_id=1, source_target_pairs={{0,1},{1,0},{2,3},{3,2},{4,5},{5,4},{6,7},{7,6},{8,9},{9,8},{10,11... | collective-permute-start | bytes 1572872 | tf_op jit(solution)/shard_map/ppermute | solution.py:166
  72.0 2.4 %collective-permute-done.21 = bf16[24,4096]{1,0:T(8,128)(2,1)S(1)} collective-permute-done((bf16[24,4096]{1,0:T(8,128)(2,1)S(1)}, bf16[24,4096]{1,0:T(8,128)(2,1)S(1)}, u32[]{:S(2)}, u32[]{:S(2)}) %collective-permute-start.21) | collective-permute-done | bytes 196640 | tf_op jit(solution)/shard_map/ppermute | solution.py:101
  78.2 1.9 %collective-permute-done.23 = bf16[24,4096]{1,0:T(8,128)(2,1)S(1)} collective-permute-done((bf16[24,4096]{1,0:T(8,128)(2,1)S(1)}, bf16[24,4096]{1,0:T(8,128)(2,1)S(1)}, u32[]{:S(2)}, u32[]{:S(2)}) %collective-permute-start.23) | collective-permute-done | bytes 196640 | tf_op jit(solution)/shard_map/ppermute | solution.py:101
  84.0 1.7 %collective-permute-done.25 = bf16[24,4096]{1,0:T(8,128)(2,1)S(1)} collective-permute-done((bf16[24,4096]{1,0:T(8,128)(2,1)S(1)}, bf16[24,4096]{1,0:T(8,128)(2,1)S(1)}, u32[]{:S(2)}, u32[]{:S(2)}) %collective-permute-start.25) | collective-permute-done | bytes 196640 | tf_op jit(solution)/shard_map/ppermute | solution.py:101
  95.6 2.3 %fusion.36 = (f32[512]{0:T(512)S(1)}, f32[512]{0:T(512)S(1)}, f32[512]{0:T(512)S(1)}, f32[512,256]{0,1:T(8,128)}) fusion(f32[256,512]{1,0:T(8,128)S(1)} %get-tuple-element.87, s32[512]{0:T(512)S(1)} %fusion.67, f32[512]{0:T(512)S(1)} %max.51, f32[256,512]{1,0:T(8,128)S(1)} %get-tuple-element.89, bf16[512,4096]{1,0:T(8,128)(2,1)S(1)} %copy-done.14, ...), kind=kOutput, calls=%fused_computation.44 | convolution fusion | flops 1081735680 | bytes 8398848 | tf_op jit(solution)/shard_map/dot_general | solution.py:142
  100.2 2.0 %fusion.9 = f32[128,2048]{1,0:T(8,128)S(1)} fusion(bf16[512,4096]{1,0:T(8,128)(2,1)} %param.8, bf16[512,256]{0,1:T(8,128)(2,1)S(1)} %fusion.39), kind=kOutput, calls=%fused_computation.14 | convolution fusion | flops 268435456 | bytes 3276800 | tf_op jit(solution)/shard_map/dot_general | solution.py:199
  102.8 2.7 %fusion.30 = f32[512,4096]{1,0:T(8,128)S(1)} fusion(bf16[64,4096]{1,0:T(8,128)(2,1)S(1)} %broadcast_select_fusion.5, bf16[96,4096]{1,0:T(8,128)(2,1)S(1)} %get-tuple-element.45, bf16[96,4096]{1,0:T(8,128)(2,1)S(1)} %get-tuple-element.44, f32[512,256]{0,1:T(8,128)} %get-tuple-element.90, f32[256,512]{1,0:T(8,128)} %copy-done.10, f32[512]{0:T(512)S(1)} %get-tuple-element.41), kind=kOutput, calls=%fused_computation.26 | convolution fusion | flops 1080426496 | bytes 11536384 | tf_op jit(solution)/shard_map/dot_general | solution.py:234
  109.9 5.6 %collective-permute-done.38 = bf16[2,2,2,8,2048]{4,3,1,2,0:T(8,128)(2,1)S(1)} collective-permute-done((bf16[2,2,2,8,2048]{4,3,1,2,0:T(8,128)(2,1)S(1)}, bf16[2,2,2,8,2048]{4,3,1,2,0:T(8,128)(2,1)S(1)}, u32[]{:S(2)}, u32[]{:S(2)}) %collective-permute-start.38) | collective-permute-done | bytes 262176 | tf_op jit(solution)/shard_map/ppermute | solution.py:212
  118.1 2.6 %collective-permute-done.39 = bf16[2,2,8,2048]{3,2,0,1:T(8,128)(2,1)S(1)} collective-permute-done((bf16[2,2,8,2048]{3,2,0,1:T(8,128)(2,1)S(1)}, bf16[2,2,8,2048]{3,2,0,1:T(8,128)(2,1)S(1)}, u32[]{:S(2)}, u32[]{:S(2)}) %collective-permute-start.39) | collective-permute-done | bytes 131104 | tf_op jit(solution)/shard_map/ppermute | solution.py:210
  125.1 3.0 %collective-permute-start.41 = (bf16[8,2048]{1,0:T(8,128)(2,1)S(1)}, bf16[8,2048]{1,0:T(8,128)(2,1)S(1)}, u32[]{:S(2)}, u32[]{:S(2)}) collective-permute-start(bf16[8,2048]{1,0:T(8,128)(2,1)S(1)} %fusion.58), channel_id=1, source_target_pairs={{0,16},{2,18},{4,20},{6,22},{8,24},{10,26},{12,28},{14,30},{16,0},... | collective-permute-start | bytes 98312 | tf_op jit(solution)/shard_map/ppermute | solution.py:212
  130.0 3.0 %collective-permute-done.36 = bf16[8,2048]{1,0:T(8,128)(2,1)S(1)} collective-permute-done((bf16[8,2048]{1,0:T(8,128)(2,1)S(1)}, bf16[8,2048]{1,0:T(8,128)(2,1)S(1)}, u32[]{:S(2)}, u32[]{:S(2)}) %collective-permute-start.36) | collective-permute-done | bytes 32800 | tf_op jit(solution)/shard_map/ppermute | solution.py:212
  133.6 2.9 %multiply_convert_fusion = bf16[512,4096]{1,0:T(8,128)(2,1)} fusion(f32[512,4096]{1,0:T(8,128)S(1)} %fusion.30, bf16[512,256]{0,1:T(8,128)(2,1)S(1)} %fusion.39, bf16[128,4096]{1,0:T(8,128)(2,1)S(1)} %copy-done.9, bf16[64,4096]{1,0:T(8,128)(2,1)S(1)} %copy-done.7, bf16[64,4096]{1,0:T(8,128)(2,1)S(1)} %slice_dynamic-update-slice_fusion), kind=kOutput, calls=%fused_computation | convolution fusion | flops 1086324736 | bytes 14942208 | tf_op jit(solution)/shard_map/dot_general | solution.py:234
  (179 shorter events, 54.2 us)
Async XLA Ops:
  9.1 6.6 %collective-permute-start.5 = (bf16[24,4096]{1,0:T(8,128)(2,1)S(1)}, bf16[24,4096]{1,0:T(8,128)(2,1)S(1)}, u32[]{:S(2)}, u32[]{:S(2)}) collective-permute-start(bf16[24,4096]{1,0:T(8,128)(2,1)S(1)} %slice.241), channel_id=1, source_target_pairs={{0,8},{2,6},{8,16},{10,2},{16,24},{18,10},{24,28},{26,18},{28,20},... | collective-permute-start | bytes 589832 | tf_op jit(solution)/shard_map/ppermute | solution.py:101
  12.2 6.4 %collective-permute-start.1 = (bf16[32,4096]{1,0:T(8,128)(2,1)S(1)}, bf16[32,4096]{1,0:T(8,128)(2,1)S(1)}, u32[]{:S(2)}, u32[]{:S(2)}) collective-permute-start(bf16[32,4096]{1,0:T(8,128)(2,1)S(1)} %pad_maximum_fusion.7), channel_id=1, source_target_pairs={{0,8},{2,6},{8,16},{10,2},{16,24},{18,10},{24,28},{26,18},{28,20},... | collective-permute-start | bytes 786440 | tf_op jit(solution)/shard_map/ppermute | solution.py:101
  16.1 16.2 %collective-permute-start.7 = (bf16[24,4096]{1,0:T(8,128)(2,1)S(1)}, bf16[24,4096]{1,0:T(8,128)(2,1)S(1)}, u32[]{:S(2)}, u32[]{:S(2)}) collective-permute-start(bf16[24,4096]{1,0:T(8,128)(2,1)S(1)} %get-tuple-element.61), channel_id=1, source_target_pairs={{0,8},{2,6},{8,16},{10,2},{16,24},{18,10},{24,28},{26,18},{28,20},... | collective-permute-start | bytes 589832 | tf_op jit(solution)/shard_map/ppermute | solution.py:101
  19.1 6.4 %collective-permute-start.2 = (bf16[32,4096]{1,0:T(8,128)(2,1)S(1)}, bf16[32,4096]{1,0:T(8,128)(2,1)S(1)}, u32[]{:S(2)}, u32[]{:S(2)}) collective-permute-start(bf16[32,4096]{1,0:T(8,128)(2,1)S(1)} %pad_maximum_fusion.8), channel_id=1, source_target_pairs={{0,8},{2,6},{8,16},{10,2},{16,24},{18,10},{24,28},{26,18},{28,20},... | collective-permute-start | bytes 786440 | tf_op jit(solution)/shard_map/ppermute | solution.py:101
  21.4 6.5 %collective-permute-start.10 = (bf16[48,4096]{1,0:T(8,128)(2,1)S(1)}, bf16[48,4096]{1,0:T(8,128)(2,1)S(1)}, u32[]{:S(2)}, u32[]{:S(2)}) collective-permute-start(bf16[48,4096]{1,0:T(8,128)(2,1)S(1)} %constant_dynamic-slice_fusion.2), channel_id=1, source_target_pairs={{0,2},{2,0},{4,6},{6,4},{8,10},{10,8},{12,14},{14,12},{16,18},{18,... | collective-permute-start | bytes 1179656 | tf_op jit(solution)/shard_map/ppermute | solution.py:71
  21.9 6.0 %collective-permute-start.9 = (bf16[64,4096]{1,0:T(8,128)(2,1)S(1)}, bf16[64,4096]{1,0:T(8,128)(2,1)S(1)}, u32[]{:S(2)}, u32[]{:S(2)}) collective-permute-start(bf16[64,4096]{1,0:T(8,128)(2,1)S(1)} %slice.195), channel_id=1, source_target_pairs={{0,2},{2,0},{4,6},{6,4},{8,10},{10,8},{12,14},{14,12},{16,18},{18,... | collective-permute-start | bytes 1572872 | tf_op jit(solution)/shard_map/ppermute | solution.py:71
  25.5 9.0 %collective-permute-start.15 = (bf16[64,4096]{1,0:T(8,128)(2,1)S(1)}, bf16[64,4096]{1,0:T(8,128)(2,1)S(1)}, u32[]{:S(2)}, u32[]{:S(2)}) collective-permute-start(bf16[64,4096]{1,0:T(8,128)(2,1)S(1)} %slice.206), channel_id=1, source_target_pairs={{0,2},{2,0},{4,6},{6,4},{8,10},{10,8},{12,14},{14,12},{16,18},{18,... | collective-permute-start | bytes 1572872 | tf_op jit(solution)/shard_map/ppermute | solution.py:71
  25.8 6.4 %collective-permute-start.6 = (bf16[32,4096]{1,0:T(8,128)(2,1)S(1)}, bf16[32,4096]{1,0:T(8,128)(2,1)S(1)}, u32[]{:S(2)}, u32[]{:S(2)}) collective-permute-start(bf16[32,4096]{1,0:T(8,128)(2,1)S(1)} %pad_maximum_fusion.9), channel_id=1, source_target_pairs={{0,8},{2,6},{8,16},{10,2},{16,24},{18,10},{24,28},{26,18},{28,20},... | collective-permute-start | bytes 786440 | tf_op jit(solution)/shard_map/ppermute | solution.py:101
  32.4 6.4 %collective-permute-start.8 = (bf16[32,4096]{1,0:T(8,128)(2,1)S(1)}, bf16[32,4096]{1,0:T(8,128)(2,1)S(1)}, u32[]{:S(2)}, u32[]{:S(2)}) collective-permute-start(bf16[32,4096]{1,0:T(8,128)(2,1)S(1)} %pad_maximum_fusion.10), channel_id=1, source_target_pairs={{0,8},{2,6},{8,16},{10,2},{16,24},{18,10},{24,28},{26,18},{28,20},... | collective-permute-start | bytes 786440 | tf_op jit(solution)/shard_map/ppermute | solution.py:101
  39.0 5.7 %collective-permute-start.11 = (bf16[24,4096]{1,0:T(8,128)(2,1)S(1)}, bf16[24,4096]{1,0:T(8,128)(2,1)S(1)}, u32[]{:S(2)}, u32[]{:S(2)}) collective-permute-start(bf16[24,4096]{1,0:T(8,128)(2,1)S(1)} %get-tuple-element.85), channel_id=1, source_target_pairs={{0,8},{2,6},{8,16},{10,2},{16,24},{18,10},{24,28},{26,18},{28,20},... | collective-permute-start | bytes 589832 | tf_op jit(solution)/shard_map/ppermute | solution.py:101
  44.9 5.7 %collective-permute-start.13 = (bf16[24,4096]{1,0:T(8,128)(2,1)S(1)}, bf16[24,4096]{1,0:T(8,128)(2,1)S(1)}, u32[]{:S(2)}, u32[]{:S(2)}) collective-permute-start(bf16[24,4096]{1,0:T(8,128)(2,1)S(1)} %get-tuple-element.25), channel_id=1, source_target_pairs={{0,8},{2,6},{8,16},{10,2},{16,24},{18,10},{24,28},{26,18},{28,20},... | collective-permute-start | bytes 589832 | tf_op jit(solution)/shard_map/ppermute | solution.py:101
  47.0 6.4 %collective-permute-start.12 = (bf16[32,4096]{1,0:T(8,128)(2,1)S(1)}, bf16[32,4096]{1,0:T(8,128)(2,1)S(1)}, u32[]{:S(2)}, u32[]{:S(2)}) collective-permute-start(bf16[32,4096]{1,0:T(8,128)(2,1)S(1)} %pad_maximum_fusion.11), channel_id=1, source_target_pairs={{0,8},{2,6},{8,16},{10,2},{16,24},{18,10},{24,28},{26,18},{28,20},... | collective-permute-start | bytes 786440 | tf_op jit(solution)/shard_map/ppermute | solution.py:101
  50.7 5.7 %collective-permute-start.16 = (bf16[24,4096]{1,0:T(8,128)(2,1)S(1)}, bf16[24,4096]{1,0:T(8,128)(2,1)S(1)}, u32[]{:S(2)}, u32[]{:S(2)}) collective-permute-start(bf16[24,4096]{1,0:T(8,128)(2,1)S(1)} %get-tuple-element.27), channel_id=1, source_target_pairs={{0,8},{2,6},{8,16},{10,2},{16,24},{18,10},{24,28},{26,18},{28,20},... | collective-permute-start | bytes 589832 | tf_op jit(solution)/shard_map/ppermute | solution.py:101
  53.6 6.4 %collective-permute-start.14 = (bf16[32,4096]{1,0:T(8,128)(2,1)S(1)}, bf16[32,4096]{1,0:T(8,128)(2,1)S(1)}, u32[]{:S(2)}, u32[]{:S(2)}) collective-permute-start(bf16[32,4096]{1,0:T(8,128)(2,1)S(1)} %pad_maximum_fusion.12), channel_id=1, source_target_pairs={{0,8},{2,6},{8,16},{10,2},{16,24},{18,10},{24,28},{26,18},{28,20},... | collective-permute-start | bytes 786440 | tf_op jit(solution)/shard_map/ppermute | solution.py:101
  56.5 5.7 %collective-permute-start.20 = (bf16[24,4096]{1,0:T(8,128)(2,1)S(1)}, bf16[24,4096]{1,0:T(8,128)(2,1)S(1)}, u32[]{:S(2)}, u32[]{:S(2)}) collective-permute-start(bf16[24,4096]{1,0:T(8,128)(2,1)S(1)} %get-tuple-element.29), channel_id=1, source_target_pairs={{0,8},{2,6},{8,16},{10,2},{16,24},{18,10},{24,28},{26,18},{28,20},... | collective-permute-start | bytes 589832 | tf_op jit(solution)/shard_map/ppermute | solution.py:101
  60.1 6.4 %collective-permute-start.17 = (bf16[32,4096]{1,0:T(8,128)(2,1)S(1)}, bf16[32,4096]{1,0:T(8,128)(2,1)S(1)}, u32[]{:S(2)}, u32[]{:S(2)}) collective-permute-start(bf16[32,4096]{1,0:T(8,128)(2,1)S(1)} %pad_maximum_fusion.13), channel_id=1, source_target_pairs={{0,8},{2,6},{8,16},{10,2},{16,24},{18,10},{24,28},{26,18},{28,20},... | collective-permute-start | bytes 786440 | tf_op jit(solution)/shard_map/ppermute | solution.py:101
  62.4 8.0 %collective-permute-start.22 = (bf16[24,4096]{1,0:T(8,128)(2,1)S(1)}, bf16[24,4096]{1,0:T(8,128)(2,1)S(1)}, u32[]{:S(2)}, u32[]{:S(2)}) collective-permute-start(bf16[24,4096]{1,0:T(8,128)(2,1)S(1)} %get-tuple-element.31), channel_id=1, source_target_pairs={{0,8},{2,6},{8,16},{10,2},{16,24},{18,10},{24,28},{26,18},{28,20},... | collective-permute-start | bytes 589832 | tf_op jit(solution)/shard_map/ppermute | solution.py:101
  66.6 17.3 %collective-permute-start.18 = (bf16[64,4096]{1,0:T(8,128)(2,1)S(1)}, bf16[64,4096]{1,0:T(8,128)(2,1)S(1)}, u32[]{:S(2)}, u32[]{:S(2)}) collective-permute-start(bf16[64,4096]{1,0:T(8,128)(2,1)S(1)} %slice_dynamic-update-slice_fusion), channel_id=1, source_target_pairs={{0,1},{1,0},{2,3},{3,2},{4,5},{5,4},{6,7},{7,6},{8,9},{9,8},{10,11... | collective-permute-start | bytes 1572872 | tf_op jit(solution)/shard_map/ppermute | solution.py:166
  68.7 5.7 %collective-permute-start.21 = (bf16[24,4096]{1,0:T(8,128)(2,1)S(1)}, bf16[24,4096]{1,0:T(8,128)(2,1)S(1)}, u32[]{:S(2)}, u32[]{:S(2)}) collective-permute-start(bf16[24,4096]{1,0:T(8,128)(2,1)S(1)} %get-tuple-element.30), channel_id=1, source_target_pairs={{0,8},{2,6},{8,16},{10,2},{16,24},{18,10},{24,28},{26,18},{28,20},... | collective-permute-start | bytes 589832 | tf_op jit(solution)/shard_map/ppermute | solution.py:101
  70.3 6.2 %collective-permute-start.24 = (bf16[24,4096]{1,0:T(8,128)(2,1)S(1)}, bf16[24,4096]{1,0:T(8,128)(2,1)S(1)}, u32[]{:S(2)}, u32[]{:S(2)}) collective-permute-start(bf16[24,4096]{1,0:T(8,128)(2,1)S(1)} %collective-permute-done.22), channel_id=1, source_target_pairs={{0,8},{2,6},{8,16},{10,2},{16,24},{18,10},{24,28},{26,18},{28,20},... | collective-permute-start | bytes 589832 | tf_op jit(solution)/shard_map/ppermute | solution.py:101
  74.4 5.7 %collective-permute-start.23 = (bf16[24,4096]{1,0:T(8,128)(2,1)S(1)}, bf16[24,4096]{1,0:T(8,128)(2,1)S(1)}, u32[]{:S(2)}, u32[]{:S(2)}) collective-permute-start(bf16[24,4096]{1,0:T(8,128)(2,1)S(1)} %collective-permute-done.21), channel_id=1, source_target_pairs={{0,8},{2,6},{8,16},{10,2},{16,24},{18,10},{24,28},{26,18},{28,20},... | collective-permute-start | bytes 589832 | tf_op jit(solution)/shard_map/ppermute | solution.py:101
  76.5 5.7 %collective-permute-start.28 = (bf16[24,4096]{1,0:T(8,128)(2,1)S(1)}, bf16[24,4096]{1,0:T(8,128)(2,1)S(1)}, u32[]{:S(2)}, u32[]{:S(2)}) collective-permute-start(bf16[24,4096]{1,0:T(8,128)(2,1)S(1)} %collective-permute-done.24), channel_id=1, source_target_pairs={{0,8},{2,6},{8,16},{10,2},{16,24},{18,10},{24,28},{26,18},{28,20},... | collective-permute-start | bytes 589832 | tf_op jit(solution)/shard_map/ppermute | solution.py:101
  80.1 5.7 %collective-permute-start.25 = (bf16[24,4096]{1,0:T(8,128)(2,1)S(1)}, bf16[24,4096]{1,0:T(8,128)(2,1)S(1)}, u32[]{:S(2)}, u32[]{:S(2)}) collective-permute-start(bf16[24,4096]{1,0:T(8,128)(2,1)S(1)} %collective-permute-done.23), channel_id=1, source_target_pairs={{0,8},{2,6},{8,16},{10,2},{16,24},{18,10},{24,28},{26,18},{28,20},... | collective-permute-start | bytes 589832 | tf_op jit(solution)/shard_map/ppermute | solution.py:101
  82.2 5.7 %collective-permute-start.29 = (bf16[24,4096]{1,0:T(8,128)(2,1)S(1)}, bf16[24,4096]{1,0:T(8,128)(2,1)S(1)}, u32[]{:S(2)}, u32[]{:S(2)}) collective-permute-start(bf16[24,4096]{1,0:T(8,128)(2,1)S(1)} %collective-permute-done.28), channel_id=1, source_target_pairs={{0,8},{2,6},{8,16},{10,2},{16,24},{18,10},{24,28},{26,18},{28,20},... | collective-permute-start | bytes 589832 | tf_op jit(solution)/shard_map/ppermute | solution.py:101
  84.0 9.0 %collective-permute-start.19 = (bf16[128,4096]{1,0:T(8,128)(2,1)S(1)}, bf16[128,4096]{1,0:T(8,128)(2,1)S(1)}, u32[]{:S(2)}, u32[]{:S(2)}) collective-permute-start(bf16[128,4096]{1,0:T(8,128)(2,1)S(1)} %pad_maximum_fusion.2), channel_id=1, source_target_pairs={{0,2},{2,0},{4,6},{6,4},{8,10},{10,8},{12,14},{14,12},{16,18},{18,... | collective-permute-start | bytes 3145736 | tf_op jit(solution)/shard_map/ppermute | solution.py:167
  100.2 5.3 %collective-permute-start.37 = (f32[128,2048]{1,0:T(8,128)}, f32[128,2048]{1,0:T(8,128)}, u32[]{:S(2)}, u32[]{:S(2)}) collective-permute-start(f32[128,2048]{1,0:T(8,128)} %fusion.6), channel_id=1, source_target_pairs={{0,2},{2,0},{4,6},{6,4},{8,10},{10,8},{12,14},{14,12},{16,18},{18,... | collective-permute-start | bytes 3145736 | tf_op jit(solution)/shard_map/ppermute | solution.py:203
  102.3 6.5 %collective-permute-start.32 = (f32[128,2048]{1,0:T(8,128)S(1)}, f32[128,2048]{1,0:T(8,128)S(1)}, u32[]{:S(2)}, u32[]{:S(2)}) collective-permute-start(f32[128,2048]{1,0:T(8,128)S(1)} %fusion.9), channel_id=1, source_target_pairs={{0,2},{2,0},{4,6},{6,4},{8,10},{10,8},{12,14},{14,12},{16,18},{18,... | collective-permute-start | bytes 3145736 | tf_op jit(solution)/shard_map/ppermute | solution.py:203
  107.2 8.3 %collective-permute-start.38 = (bf16[2,2,2,8,2048]{4,3,1,2,0:T(8,128)(2,1)S(1)}, bf16[2,2,2,8,2048]{4,3,1,2,0:T(8,128)(2,1)S(1)}, u32[]{:S(2)}, u32[]{:S(2)}) collective-permute-start(bf16[2,2,2,8,2048]{4,3,1,2,0:T(8,128)(2,1)S(1)} %fusion.41), channel_id=1, source_target_pairs={{0,4},{2,6},{4,0},{6,2},{8,12},{10,14},{12,8},{14,10},{16,20},{18,... | collective-permute-start | bytes 786440 | tf_op jit(solution)/shard_map/ppermute | solution.py:212
  109.4 8.0 %collective-permute-start.33 = (bf16[2,2,2,8,2048]{4,3,0,1,2:T(8,128)(2,1)S(1)}, bf16[2,2,2,8,2048]{4,3,0,1,2:T(8,128)(2,1)S(1)}, u32[]{:S(2)}, u32[]{:S(2)}) collective-permute-start(bf16[2,2,2,8,2048]{4,3,0,1,2:T(8,128)(2,1)S(1)} %copy.12), channel_id=1, source_target_pairs={{0,1},{1,0},{2,3},{3,2},{4,5},{5,4},{6,7},{7,6},{8,9},{9,8},{10,11... | collective-permute-start | bytes 786440 | tf_op jit(solution)/shard_map/ppermute | solution.py:210
  115.6 5.0 %collective-permute-start.39 = (bf16[2,2,8,2048]{3,2,0,1:T(8,128)(2,1)S(1)}, bf16[2,2,8,2048]{3,2,0,1:T(8,128)(2,1)S(1)}, u32[]{:S(2)}, u32[]{:S(2)}) collective-permute-start(bf16[2,2,8,2048]{3,2,0,1:T(8,128)(2,1)S(1)} %fusion.46), channel_id=1, source_target_pairs={{0,1},{1,0},{2,3},{3,2},{4,5},{5,4},{6,7},{7,6},{8,9},{9,8},{10,11... | collective-permute-start | bytes 393224 | tf_op jit(solution)/shard_map/ppermute | solution.py:210
  117.5 5.0 %collective-permute-start.34 = (bf16[2,2,8,2048]{3,2,0,1:T(8,128)(2,1)S(1)}, bf16[2,2,8,2048]{3,2,0,1:T(8,128)(2,1)S(1)}, u32[]{:S(2)}, u32[]{:S(2)}) collective-permute-start(bf16[2,2,8,2048]{3,2,0,1:T(8,128)(2,1)S(1)} %fusion.45), channel_id=1, source_target_pairs={{0,4},{2,6},{4,0},{6,2},{8,12},{10,14},{12,8},{14,10},{16,20},{18,... | collective-permute-start | bytes 393224 | tf_op jit(solution)/shard_map/ppermute | solution.py:212
  122.5 5.5 %collective-permute-start.35 = (bf16[2,8,2048]{2,1,0:T(8,128)(2,1)S(1)}, bf16[2,8,2048]{2,1,0:T(8,128)(2,1)S(1)}, u32[]{:S(2)}, u32[]{:S(2)}) collective-permute-start(bf16[2,8,2048]{2,1,0:T(8,128)(2,1)S(1)} %fusion.53), channel_id=1, source_target_pairs={{0,8},{2,10},{4,12},{6,14},{8,0},{10,2},{12,4},{14,6},{16,24},{18,... | collective-permute-start | bytes 196616 | tf_op jit(solution)/shard_map/ppermute | solution.py:212
  (26 other events, 126.4 us)

commit v3 on v0

v3 whole, which is shorter than its diff:
```python
import functools
import math

import jax
import jax.numpy as jnp
from jax import lax
from jax.experimental import pallas as pl
from jax.experimental.pallas import tpu as pltpu
from jax.sharding import PartitionSpec as P

STEP = 32
VMEM_LIMIT = 24 * 2**20


def ring_order(n_chip):
    nz = n_chip // 2
    return [2 * z for z in range(nz)] + [2 * z + 1 for z in reversed(range(nz))]


def ring_pairs(n_chip):
    order = ring_order(n_chip)
    pairs = []
    for i, chip in enumerate(order):
        pairs.append((2 * chip, 2 * order[(i + 1) % n_chip]))
        pairs.append((2 * chip + 1, 2 * order[(i - 1) % n_chip] + 1))
    return pairs


def swap_pairs(n, bit):
    return [(i, i ^ bit) for i in range(n)]


def rows_at(x, tile, count):
    return lax.dynamic_slice_in_dim(x, tile * 8, count, 0)


def put_rows(x, rows, tile):
    return lax.dynamic_update_slice_in_dim(x, rows, tile * 8, 0)


def gather_rows(bank_s, bank_t, passages, owner, index, core, waiting):
    n_dev = lax.axis_size("wide")
    n_chip = n_dev // 2
    pool, width = bank_s.shape
    n_chunk = pool // STEP
    n_cut = max(1, 3 * n_chunk // 8)
    n_own = n_chunk - n_cut
    rounds = max(n_cut + n_chip - 2, n_own + n_chip // 2 - 1)
    block = passages.shape[0]
    sub = block // 2
    chip = index // 2

    def place(c):
        return jnp.where(c % 2 == 0, c // 2, n_chip - 1 - c // 2)

    def chip_at(p):
        return jnp.where(p < n_chip // 2, 2 * p, 2 * (n_chip - 1 - p) + 1)

    here = place(chip)
    turn = 1 - 2 * core
    away = here - place(owner // 2)
    distance = (turn * away + n_chip) % n_chip
    distance_other = (n_chip - turn * away) % n_chip
    own_chip = owner // 2 == chip
    own_core = owner == index
    swap = swap_pairs(n_dev, 1)
    pairs = ring_pairs(n_chip)

    banks = [bank_s, bank_t]
    swapped = [None, lax.ppermute(bank_t, "wide", swap)]
    swapped[0] = lax.ppermute(bank_s, "wide", swap)

    def tile_of(side, slot):
        return jnp.where(side == 0, slot, n_chunk - 1 - slot) * (STEP // 8)

    def own_rows(i, j):
        at = tile_of(core, j)
        return jnp.where(own_core, rows_at(banks[i], at, STEP), rows_at(swapped[i], at, STEP))

    pools = [jnp.zeros_like(bank_s), jnp.zeros_like(bank_t)]
    rows = put_rows(jnp.zeros((n_chip * block, width), passages.dtype), passages, 0)
    moving = [own_rows(i, 0) for i in range(2)]
    riding = [passages[:sub], passages[sub:]]
    arrived = [[], []]

    def keep(i, t, sent):
        other = lax.ppermute(sent, "wide", swap)
        for side, away, piece in ((core, distance, sent), (1 - core, distance_other, other)):
            slot = t - away
            take = (slot >= 0) & (slot < n_own)
            at = tile_of(side, jnp.clip(slot, 0, n_own - 1))
            pools[i] = put_rows(pools[i], jnp.where(take, piece, rows_at(pools[i], at, STEP)), at)

    for t in range(rounds):
        for i in (1, 0):
            sent = jnp.concatenate([moving[i], riding[i]], 0) if t < n_chip - 1 else moving[i]
            before = t - 1 - i
            if before >= 0:
                sent, arrived[1 - i][before] = lax.optimization_barrier((sent, arrived[1 - i][before]))
            if t == 0:
                (banks[i], swapped[i]), sent = lax.optimization_barrier(((banks[i], swapped[i]), sent))
                full = jnp.where(own_core, banks[i], swapped[i])
                banks[i], swapped[i] = full, full
            got = lax.ppermute(sent, "wide", pairs)
            arrived[i].append(got)
            keep(i, t, sent[:STEP])
            if i == 0 and t == 3:
                waiting, got = lax.optimization_barrier((waiting, got))
            if t < n_chip - 1:
                riding[i] = got[STEP:]
                got = got[:STEP]
                origin = chip_at((here - turn * (t + 1) + n_chip) % n_chip)
                rows = put_rows(rows, riding[i], (origin ^ chip) * (block // 8) + i * (sub // 8))
            moving[i] = got
            if t + 1 < n_own:
                moving[i] = jnp.where(own_chip, own_rows(i, t + 1), got)
    for i in (1, 0):
        keep(i, rounds, moving[i])
    return pools[0], pools[1], rows, waiting


def dot_t(a, b):
    return lax.dot_general(a, b, (((1,), (1,)), ((), ())), preferred_element_type=jnp.float32)


def tail_kernel(scale, n_rows, *refs):
    pass_refs, refs = refs[:n_rows], refs[n_rows:]
    q, tq, pool_s, pool_t, mask, column = refs[:6]
    gp, gq, loss, pieces = refs[6:]
    n_query, width = q.shape
    first = 0
    for ref in pass_refs:
        pieces[first : first + ref.shape[0], :] = ref[...]
        first += ref.shape[0]
    block = min(256, n_query)

    @pl.loop(0, n_query // block)
    def _(b):
        at = pl.ds(pl.multiple_of(b * block, block), block)
        p = dot_t(q[at, :], pieces[...]) * scale
        z = dot_t(q[at, :], pool_s[...]) * scale
        tt = dot_t(tq[at, :], pool_t[...]) * scale
        weight = mask[at, :].astype(jnp.float32) * jax.nn.sigmoid(-tt)
        top = jnp.maximum(jnp.max(p, axis=1, keepdims=True), jnp.max(z, axis=1, keepdims=True))
        total = jnp.sum(jnp.exp(p - top), axis=1, keepdims=True) + jnp.sum(
            weight * jnp.exp(z - top), axis=1, keepdims=True
        )
        lse = top + jnp.log(total)
        hit = (lax.broadcasted_iota(jnp.int32, p.shape, 1) == column[at, :]).astype(jnp.float32)
        loss[at, :] = lse - jnp.sum(p * hit, axis=1, keepdims=True)
        gp[at, :] = (jnp.exp(p - lse) - hit).astype(jnp.bfloat16)
        gq[at, :] = (weight * jnp.exp(z - lse)).astype(jnp.bfloat16)


def tail(scale, pass_parts, queries, teacher, pool_s, pool_t, mask, column):
    n_query, width = queries.shape
    n_pass = sum(p.shape[0] for p in pass_parts)
    pool = pool_s.shape[0]
    bf16, f32 = jnp.bfloat16, jnp.float32
    arrays = [*pass_parts, queries, teacher, pool_s, pool_t, mask, column]
    vmem = pl.BlockSpec(memory_space=pltpu.VMEM)
    return pl.pallas_call(
        functools.partial(tail_kernel, scale, len(pass_parts)),
        out_shape=[
            jax.ShapeDtypeStruct((n_query, n_pass), bf16),
            jax.ShapeDtypeStruct((n_query, pool), bf16),
            jax.ShapeDtypeStruct((n_query, 1), f32),
            jax.ShapeDtypeStruct((n_pass, width), bf16),
        ],
        in_specs=[vmem] * len(arrays),
        out_specs=[vmem] * 4,
        compiler_params=pltpu.CompilerParams(vmem_limit_bytes=VMEM_LIMIT),
        cost_estimate=pl.CostEstimate(
            flops=2 * n_query * width * (n_pass + 2 * pool),
            bytes_accessed=4 * width * (n_query + 2 * n_pass + pool),
            transcendentals=0,
        ),
        name="scores",
    )(*arrays)


def body(
    queries, teacher_queries, passages, bank_student, bank_teacher, owner, positives, keep_mask
):
    n_dev = lax.axis_size("wide")
    n_chip = n_dev // 2
    n_dp = lax.axis_size("dp")
    index = lax.axis_index("wide")
    replica = lax.axis_index("dp")
    core = index % 2
    chip = index // 2
    block, width = passages.shape
    scale = 2.0 / math.sqrt(width)
    n_pass = block * n_dev
    swap = swap_pairs(n_dev, 1)
    across = [(0, 1), (1, 0)]
    pool_s, pool_t, rows, keep_mask = gather_rows(
        bank_student, bank_teacher, passages, owner[0], index, core, keep_mask
    )
    pass_parts = [rows, lax.ppermute(rows, "wide", swap)]
    chip_of = (positives // (2 * block)) ^ chip
    core_of = ((positives // block) % 2) ^ core
    column = (core_of * n_chip + chip_of) * block + positives % block
    grad_p, grad_q, row_loss, pieces = tail(
        scale, pass_parts, queries, teacher_queries, pool_s, pool_t, keep_mask, column[:, None]
    )

    chip_bits = ["x"] + ["z%d" % b for b in range(n_chip.bit_length() - 2)]
    pairs_of = {name: swap_pairs(n_dev, 2 << b) for b, name in enumerate(chip_bits)}
    first_sent = []

    def reduced(columns, order):
        def terms(grads):
            return lax.dot_general(
                grads, columns, (((0,), (0,)), ((), ())), preferred_element_type=jnp.float32
            )

        got = lax.ppermute(terms(grad_p[:, mid:]), "wide", swap)
        sums = (terms(grad_p[:, :mid]) + got).reshape(
            (2,) * len(chip_bits) + (block, columns.shape[1])
        )
        left = chip_bits[::-1]
        for name in order:
            at = left.index(name)
            sent = lax.index_in_dim(sums, 1, at, keepdims=False).astype(jnp.bfloat16)
            first_sent.append(sent)
            got = lax.ppermute(sent, "wide", pairs_of[name])
            sums = lax.index_in_dim(sums, 0, at, keepdims=False) + got.astype(jnp.float32)
            left.pop(at)
        if n_dp != 2:
            return lax.psum(sums, "dp") * scale
        return (sums + lax.ppermute(sums, "dp", across)) * scale

    mid, half = n_pass // 2, width // 2
    zs = chip_bits[1:]
    passage_grad = jnp.concatenate(
        [
            reduced(queries[:, :half], ["x"] + zs),
            reduced(queries[:, half:], zs[:1] + ["x"] + zs[1:]),
        ],
        1,
    )

    (late_p, grad_q), _ = lax.optimization_barrier(((grad_p, grad_q), first_sent[0]))
    qgrad = jnp.dot(late_p, pieces, preferred_element_type=jnp.float32) + jnp.dot(
        grad_q, pool_s, preferred_element_type=jnp.float32
    )
    query_grad = (qgrad * scale).astype(jnp.bfloat16)
    return (row_loss[:, 0], query_grad, passage_grad)


def solution(mesh):
    placed = (
        P(("wide", "dp"), None),
        P(("wide", "dp"), None),
        P("wide", None),
        P("wide", None),
        P("wide", None),
        P("dp"),
        P(("wide", "dp")),
        P(("wide", "dp"), None),
    )
    return jax.shard_map(
        body,
        mesh=mesh,
        in_specs=placed,
        out_specs=(P(("wide", "dp")), P(("wide", "dp"), None), P("wide", None)),
        check_vma=False,
    )
```

time: 282 us -> 126 us (0.45)
  waiting for transfers between devices: 234 us -> 48.3 us
  starting transfers between devices: 0.16 us -> 44.1 us
  matrix products: 27.3 us -> 12.2 us
  between operations: 14.5 us -> 2.85 us
  other arithmetic: 4.71 us -> 10.8 us
  Pallas kernels: 0 us -> 4.32 us
    psum x2 -> x0, waiting for transfers between devices: 133 us -> none  [the longest x1 115 us: broadcast(): return lax.psum(block, axis)]
    reduce_scatter x1 -> x0, waiting for transfers between devices: 64.9 us -> none  [body(): lax.psum_scatter(lax.dot_general(grad_p, queries, (((0,), (0,)), ((), ())...]
    ppermute x0 -> x51, waiting for transfers between devices: none -> 48.3 us  [the longest x18 23.9 us: gather_rows(): got = lax.ppermute(sent, 'wide', pairs)]
    ppermute x0 -> x51, starting transfers between devices: none -> 44.1 us  [the longest x18 30.1 us: gather_rows(): got = lax.ppermute(sent, 'wide', pairs)]
    all_gather x1 -> x0, waiting for transfers between devices: 36 us -> none  [body(): piece = lax.all_gather(passages, 'wide', axis=0, tiled=True)]
    dot_general x5, matrix products: 20.4 us -> 8.79 us  [the longest x4 7.52 us: terms(): lax.dot_general(grads, columns, (((0,), (0,)), ((), ())), preferred_eleme...]
    pallas_call x0 -> x1, Pallas kernels: none -> 4.32 us  [tail(): pl.pallas_call(functools.partial(tail_kernel, scale, len(pass_parts)), ou...]
    dot_general x1, matrix products: 6.93 us -> 3.41 us  [body(): jnp.dot(grad_q, pool_s, preferred_element_type=jnp.float32)]
  transfers between devices with their start and end apart: 4 -> 51, of which waited for: 4 -> 31; matrix products, arithmetic and copies ran while one was open for 7% -> 17% of each run, Pallas kernels for 0% -> 0%
where the time goes in v3:
time: 126 us
  waiting for transfers between devices  48.3 us (38%)
  starting transfers between devices  44.1 us (35%)
  matrix products  12.2 us (10%)
  other arithmetic  10.8 us (9%)
  Pallas kernels  4.32 us (3%)
  local copies, waits for them, and re-layouts  3.32 us (3%)
  between operations  2.85 us (2%)
    ppermute x18, starting transfers between devices, gather_rows(): got = lax.ppermute(sent, 'wide', pairs)  30.1 us
    ppermute x18, waiting for transfers between devices, gather_rows(): got = lax.ppermute(sent, 'wide', pairs)  23.9 us
    ppermute x20, waiting for transfers between devices, keep(): other = lax.ppermute(sent, 'wide', swap)  9.65 us
    ppermute x6, starting transfers between devices, reduced(): got = lax.ppermute(sent, 'wide', pairs_of[name])  8.41 us
    dot_general x4, matrix products, terms(): lax.dot_general(grads, columns, (((0,), (0,)), ((), ())), preferred_eleme...  7.52 us
    ppermute x6, waiting for transfers between devices, reduced(): got = lax.ppermute(sent, 'wide', pairs_of[name])  6.07 us
    ppermute x2, waiting for transfers between devices, reduced(): return (sums + lax.ppermute(sums, 'dp', across)) * scale  4.33 us
    pallas_call x1, Pallas kernels, tail(): pl.pallas_call(functools.partial(tail_kernel, scale, len(pass_parts)), ou...  4.32 us
  transfers between devices with their start and end apart: 51, of which 31 were waited for; matrix products, arithmetic and copies ran while one was open for 17% of the time, Pallas kernels for 0%

profile of v3, /device:TPU:0, one launch (start us, length us, event | category | flops | bytes accessed | tf_op | source)
XLA Modules:
  0.0 125.8 jit_solution(8348469668930961567)
XLA Ops:
  4.4 2.9 %collective-permute-done.2 = bf16[256,4096]{1,0:T(8,128)(2,1)S(1)} collective-permute-done((bf16[256,4096]{1,0:T(8,128)(2,1)}, bf16[256,4096]{1,0:T(8,128)(2,1)S(1)}, u32[]{:S(2)}, u32[]{:S(2)}) %collective-permute-start.2) | collective-permute-done | bytes 2097184 | tf_op jit(solution)/shard_map/ppermute | solution.py:71
  9.6 3.0 %collective-permute-start.1 = (bf16[40,4096]{1,0:T(8,128)(2,1)S(1)}, bf16[40,4096]{1,0:T(8,128)(2,1)S(1)}, u32[]{:S(2)}, u32[]{:S(2)}) collective-permute-start(bf16[40,4096]{1,0:T(8,128)(2,1)S(1)} %pad_maximum_fusion), channel_id=1, source_target_pairs={{0,8},{2,6},{8,16},{10,2},{16,24},{18,10},{24,28},{26,18},{28,20},... | collective-permute-start | bytes 983048 | tf_op jit(solution)/shard_map/ppermute | solution.py:104
  16.0 1.8 %broadcast_select_fusion = bf16[256,4096]{1,0:T(8,128)(2,1)S(1)} fusion(bf16[256,4096]{1,0:T(8,128)(2,1)S(1)} %copy-done.6, bf16[256,4096]{1,0:T(8,128)(2,1)} %copy-done.8, pred[]{:T(512)S(6)} %eq.34), kind=kLoop, calls=%fused_computation.3 | loop fusion | flops 1048576 | bytes 6291457 | tf_op jit(solution)/shard_map/jit(_where)/select_n | solution.py:102
  17.8 1.8 %broadcast_select_fusion.1 = bf16[256,4096]{1,0:T(8,128)(2,1)S(1)} fusion(bf16[256,4096]{1,0:T(8,128)(2,1)S(1)} %copy-done.7, bf16[256,4096]{1,0:T(8,128)(2,1)} %collective-permute-done, pred[]{:T(512)S(6)} %eq.34), kind=kLoop, calls=%fused_computation.4 | loop fusion | flops 1048576 | bytes 6291457 | tf_op jit(solution)/shard_map/jit(_where)/select_n | solution.py:102
  20.1 1.6 %collective-permute-start.4 = (bf16[40,4096]{1,0:T(8,128)(2,1)S(1)}, bf16[40,4096]{1,0:T(8,128)(2,1)S(1)}, u32[]{:S(2)}, u32[]{:S(2)}) collective-permute-start(bf16[40,4096]{1,0:T(8,128)(2,1)S(1)} %pad_maximum_fusion.2), channel_id=1, source_target_pairs={{0,8},{2,6},{8,16},{10,2},{16,24},{18,10},{24,28},{26,18},{28,20},... | collective-permute-start | bytes 983048 | tf_op jit(solution)/shard_map/ppermute | solution.py:104
  25.1 2.1 %collective-permute-done.4 = bf16[40,4096]{1,0:T(8,128)(2,1)S(1)} collective-permute-done((bf16[40,4096]{1,0:T(8,128)(2,1)S(1)}, bf16[40,4096]{1,0:T(8,128)(2,1)S(1)}, u32[]{:S(2)}, u32[]{:S(2)}) %collective-permute-start.4) | collective-permute-done | bytes 327712 | tf_op jit(solution)/shard_map/ppermute | solution.py:104
  27.3 1.6 %collective-permute-start.6 = (bf16[40,4096]{1,0:T(8,128)(2,1)S(1)}, bf16[40,4096]{1,0:T(8,128)(2,1)S(1)}, u32[]{:S(2)}, u32[]{:S(2)}) collective-permute-start(bf16[40,4096]{1,0:T(8,128)(2,1)S(1)} %pad_maximum_fusion.4), channel_id=1, source_target_pairs={{0,8},{2,6},{8,16},{10,2},{16,24},{18,10},{24,28},{26,18},{28,20},... | collective-permute-start | bytes 983048 | tf_op jit(solution)/shard_map/ppermute | solution.py:104
  29.1 1.6 %collective-permute-done.5 = bf16[40,4096]{1,0:T(8,128)(2,1)S(1)} collective-permute-done((bf16[40,4096]{1,0:T(8,128)(2,1)S(1)}, bf16[40,4096]{1,0:T(8,128)(2,1)S(1)}, u32[]{:S(2)}, u32[]{:S(2)}) %collective-permute-start.5) | collective-permute-done | bytes 327712 | tf_op jit(solution)/shard_map/ppermute | solution.py:104
  30.9 1.6 %collective-permute-start.7 = (bf16[40,4096]{1,0:T(8,128)(2,1)S(1)}, bf16[40,4096]{1,0:T(8,128)(2,1)S(1)}, u32[]{:S(2)}, u32[]{:S(2)}) collective-permute-start(bf16[40,4096]{1,0:T(8,128)(2,1)S(1)} %pad_maximum_fusion.5), channel_id=1, source_target_pairs={{0,8},{2,6},{8,16},{10,2},{16,24},{18,10},{24,28},{26,18},{28,20},... | collective-permute-start | bytes 983048 | tf_op jit(solution)/shard_map/ppermute | solution.py:104
  34.6 1.6 %collective-permute-start.8 = (bf16[40,4096]{1,0:T(8,128)(2,1)S(1)}, bf16[40,4096]{1,0:T(8,128)(2,1)S(1)}, u32[]{:S(2)}, u32[]{:S(2)}) collective-permute-start(bf16[40,4096]{1,0:T(8,128)(2,1)S(1)} %pad_maximum_fusion.6), channel_id=1, source_target_pairs={{0,8},{2,6},{8,16},{10,2},{16,24},{18,10},{24,28},{26,18},{28,20},... | collective-permute-start | bytes 983048 | tf_op jit(solution)/shard_map/ppermute | solution.py:104
  38.1 1.6 %collective-permute-start.9 = (bf16[40,4096]{1,0:T(8,128)(2,1)S(1)}, bf16[40,4096]{1,0:T(8,128)(2,1)S(1)}, u32[]{:S(2)}, u32[]{:S(2)}) collective-permute-start(bf16[40,4096]{1,0:T(8,128)(2,1)S(1)} %pad_maximum_fusion.7), channel_id=1, source_target_pairs={{0,8},{2,6},{8,16},{10,2},{16,24},{18,10},{24,28},{26,18},{28,20},... | collective-permute-start | bytes 983048 | tf_op jit(solution)/shard_map/ppermute | solution.py:104
  41.5 3.7 %collective-permute-done.9 = bf16[40,4096]{1,0:T(8,128)(2,1)S(1)} collective-permute-done((bf16[40,4096]{1,0:T(8,128)(2,1)S(1)}, bf16[40,4096]{1,0:T(8,128)(2,1)S(1)}, u32[]{:S(2)}, u32[]{:S(2)}) %collective-permute-start.9) | collective-permute-done | bytes 327712 | tf_op jit(solution)/shard_map/ppermute | solution.py:104
  45.4 1.6 %collective-permute-start.10 = (bf16[40,4096]{1,0:T(8,128)(2,1)S(1)}, bf16[40,4096]{1,0:T(8,128)(2,1)S(1)}, u32[]{:S(2)}, u32[]{:S(2)}) collective-permute-start(bf16[40,4096]{1,0:T(8,128)(2,1)S(1)} %pad_maximum_fusion.8), channel_id=1, source_target_pairs={{0,8},{2,6},{8,16},{10,2},{16,24},{18,10},{24,28},{26,18},{28,20},... | collective-permute-start | bytes 983048 | tf_op jit(solution)/shard_map/ppermute | solution.py:104
  50.6 2.0 %collective-permute-done.10 = bf16[40,4096]{1,0:T(8,128)(2,1)S(1)} collective-permute-done((bf16[40,4096]{1,0:T(8,128)(2,1)S(1)}, bf16[40,4096]{1,0:T(8,128)(2,1)S(1)}, u32[]{:S(2)}, u32[]{:S(2)}) %collective-permute-start.10) | collective-permute-done | bytes 327712 | tf_op jit(solution)/shard_map/ppermute | solution.py:104
  54.3 1.8 %collective-permute-done.11 = bf16[40,4096]{1,0:T(8,128)(2,1)S(1)} collective-permute-done((bf16[40,4096]{1,0:T(8,128)(2,1)S(1)}, bf16[40,4096]{1,0:T(8,128)(2,1)S(1)}, u32[]{:S(2)}, u32[]{:S(2)}) %collective-permute-start.11) | collective-permute-done | bytes 327712 | tf_op jit(solution)/shard_map/ppermute | solution.py:104
  61.4 1.8 %collective-permute-done.13 = bf16[40,4096]{1,0:T(8,128)(2,1)S(1)} collective-permute-done((bf16[40,4096]{1,0:T(8,128)(2,1)S(1)}, bf16[40,4096]{1,0:T(8,128)(2,1)S(1)}, u32[]{:S(2)}, u32[]{:S(2)}) %collective-permute-start.13) | collective-permute-done | bytes 327712 | tf_op jit(solution)/shard_map/ppermute | solution.py:104
  66.8 1.6 %collective-permute-start.26 = (bf16[32,4096]{1,0:T(8,128)(2,1)S(1)}, bf16[32,4096]{1,0:T(8,128)(2,1)S(1)}, u32[]{:S(2)}, u32[]{:S(2)}) collective-permute-start(bf16[32,4096]{1,0:T(8,128)(2,1)S(1)} %slice.257), channel_id=1, source_target_pairs={{0,8},{2,6},{8,16},{10,2},{16,24},{18,10},{24,28},{26,18},{28,20},... | collective-permute-start | bytes 786440 | tf_op jit(solution)/shard_map/ppermute | solution.py:104
  68.4 1.8 %collective-permute-done.15 = bf16[40,4096]{1,0:T(8,128)(2,1)S(1)} collective-permute-done((bf16[40,4096]{1,0:T(8,128)(2,1)S(1)}, bf16[40,4096]{1,0:T(8,128)(2,1)S(1)}, u32[]{:S(2)}, u32[]{:S(2)}) %collective-permute-start.15) | collective-permute-done | bytes 327712 | tf_op jit(solution)/shard_map/ppermute | solution.py:104
  70.3 1.6 %collective-permute-start.25 = (bf16[32,4096]{1,0:T(8,128)(2,1)S(1)}, bf16[32,4096]{1,0:T(8,128)(2,1)S(1)}, u32[]{:S(2)}, u32[]{:S(2)}) collective-permute-start(bf16[32,4096]{1,0:T(8,128)(2,1)S(1)} %slice.256), channel_id=1, source_target_pairs={{0,8},{2,6},{8,16},{10,2},{16,24},{18,10},{24,28},{26,18},{28,20},... | collective-permute-start | bytes 786440 | tf_op jit(solution)/shard_map/ppermute | solution.py:104
  74.8 1.9 %collective-permute-done.25 = bf16[32,4096]{1,0:T(8,128)(2,1)S(1)} collective-permute-done((bf16[32,4096]{1,0:T(8,128)(2,1)S(1)}, bf16[32,4096]{1,0:T(8,128)(2,1)S(1)}, u32[]{:S(2)}, u32[]{:S(2)}) %collective-permute-start.25) | collective-permute-done | bytes 262176 | tf_op jit(solution)/shard_map/ppermute | solution.py:104
  79.6 3.4 %collective-permute-done.28 = bf16[32,4096]{1,0:T(8,128)(2,1)S(1)} collective-permute-done((bf16[32,4096]{1,0:T(8,128)(2,1)S(1)}, bf16[32,4096]{1,0:T(8,128)(2,1)S(1)}, u32[]{:S(2)}, u32[]{:S(2)}) %collective-permute-start.28) | collective-permute-done | bytes 262176 | tf_op jit(solution)/shard_map/ppermute | solution.py:104
  85.4 4.3 %scores.1 = (bf16[512,256]{1,0:T(8,128)(2,1)S(1)}, bf16[512,256]{1,0:T(8,128)(2,1)S(1)}, f32[512,1]{1,0:T(8,128)S(1)}, bf16[256,4096]{1,0:T(8,128)(2,1)S(1)}) custom-call(bf16[128,4096]{1,0:T(8,128)(2,1)S(1)} %slice_dynamic-update-slice_fusion.refs_0_, bf16[128,4096]{1,0:T(8,128)(2,1)S(1)} %collective-permute-done.16.refs_1_, bf16[512,4096]{1,0:T(8,128)(2,1)S(1)} %copy-done, ...), custom_call_target="tpu_custom_call" | custom-call | flops 3221225472 | bytes 20971520 | tf_op jit(solution)/shard_map/scores/pallas_call | solution.py:162
  89.7 1.7 %fusion.3 = f32[128,2048]{1,0:T(8,128)} fusion(bf16[512,4096]{1,0:T(8,128)(2,1)S(1)} %copy-done, bf16[512,256]{1,0:T(8,128)(2,1)S(1)} %get-tuple-element.58), kind=kOutput, calls=%fused_computation.8 | convolution fusion | flops 268435456 | bytes 3276800 | tf_op jit(solution)/shard_map/dot_general | solution.py:214
  94.5 2.5 %convolution_add_fusion.1 = f32[128,2048]{1,0:T(8,128)S(1)} fusion(f32[128,2048]{1,0:T(8,128)} %collective-permute-done.41, bf16[512,4096]{1,0:T(8,128)(2,1)} %refs_2_.1, bf16[512,256]{1,0:T(8,128)(2,1)S(1)} %get-tuple-element.58), kind=kOutput, calls=%fused_computation.2 | convolution fusion | flops 268697600 | bytes 4325376 | tf_op jit(solution)/shard_map/dot_general | solution.py:214
  98.2 1.8 %convolution_add_fusion = f32[128,2048]{1,0:T(8,128)S(1)} fusion(f32[128,2048]{1,0:T(8,128)} %collective-permute-done.46, bf16[512,4096]{1,0:T(8,128)(2,1)S(1)} %copy-done.1, bf16[512,256]{1,0:T(8,128)(2,1)S(1)} %get-tuple-element.58), kind=kOutput, calls=%fused_computation.1 | convolution fusion | flops 268697600 | bytes 4325376 | tf_op jit(solution)/shard_map/dot_general | solution.py:214
  100.1 1.6 %collective-permute-start.47 = (bf16[2,2,16,2048]{3,2,0,1:T(8,128)(2,1)S(1)}, bf16[2,2,16,2048]{3,2,0,1:T(8,128)(2,1)S(1)}, u32[]{:S(2)}, u32[]{:S(2)}) collective-permute-start(bf16[2,2,16,2048]{3,2,0,1:T(8,128)(2,1)S(1)} %fusion.9), channel_id=1, source_target_pairs={{0,8},{2,10},{4,12},{6,14},{8,0},{10,2},{12,4},{14,6},{16,24},{18,... | collective-permute-start | bytes 786440 | tf_op jit(solution)/shard_map/ppermute | solution.py:227
  103.0 3.4 %multiply_convert_fusion = bf16[512,4096]{1,0:T(8,128)(2,1)} fusion(f32[512,4096]{1,0:T(8,128)S(1)} %fusion.53, bf16[512,256]{1,0:T(8,128)(2,1)S(1)} %get-tuple-element.60, bf16[256,4096]{1,0:T(8,128)(2,1)S(1)} %select_dynamic-update-slice_fusion.20.refs_4_), kind=kOutput, calls=%fused_computation | convolution fusion | flops 1080033280 | bytes 14942208 | tf_op jit(solution)/shard_map/dot_general | solution.py:245
  109.5 2.2 %collective-permute-done.43 = bf16[2,16,2048]{2,1,0:T(8,128)(2,1)S(1)} collective-permute-done((bf16[2,16,2048]{2,1,0:T(8,128)(2,1)S(1)}, bf16[2,16,2048]{2,1,0:T(8,128)(2,1)S(1)}, u32[]{:S(2)}, u32[]{:S(2)}) %collective-permute-start.43) | collective-permute-done | bytes 131104 | tf_op jit(solution)/shard_map/ppermute | solution.py:227
  111.8 1.6 %collective-permute-start.44 = (bf16[16,2048]{1,0:T(8,128)(2,1)S(1)}, bf16[16,2048]{1,0:T(8,128)(2,1)S(1)}, u32[]{:S(2)}, u32[]{:S(2)}) collective-permute-start(bf16[16,2048]{1,0:T(8,128)(2,1)S(1)} %fusion.20), channel_id=1, source_target_pairs={{0,16},{2,18},{4,20},{6,22},{8,24},{10,26},{12,28},{14,30},{16,0},... | collective-permute-start | bytes 196616 | tf_op jit(solution)/shard_map/ppermute | solution.py:227
  113.6 2.1 %collective-permute-start.49 = (bf16[16,2048]{1,0:T(8,128)(2,1)S(1)}, bf16[16,2048]{1,0:T(8,128)(2,1)S(1)}, u32[]{:S(2)}, u32[]{:S(2)}) collective-permute-start(bf16[16,2048]{1,0:T(8,128)(2,1)S(1)} %fusion.21), channel_id=1, source_target_pairs={{0,16},{2,18},{4,20},{6,22},{8,24},{10,26},{12,28},{14,30},{16,0},... | collective-permute-start | bytes 196616 | tf_op jit(solution)/shard_map/ppermute | solution.py:227
  115.7 2.8 %collective-permute-done.44 = bf16[16,2048]{1,0:T(8,128)(2,1)S(1)} collective-permute-done((bf16[16,2048]{1,0:T(8,128)(2,1)S(1)}, bf16[16,2048]{1,0:T(8,128)(2,1)S(1)}, u32[]{:S(2)}, u32[]{:S(2)}) %collective-permute-start.44) | collective-permute-done | bytes 65568 | tf_op jit(solution)/shard_map/ppermute | solution.py:227
  120.7 2.7 %collective-permute-done.45 = f32[16,2048]{1,0:T(8,128)S(1)} collective-permute-done((f32[16,2048]{1,0:T(8,128)S(1)}, f32[16,2048]{1,0:T(8,128)S(1)}, u32[]{:S(2)}, u32[]{:S(2)}) %collective-permute-start.45) | collective-permute-done | bytes 131104 | tf_op jit(solution)/shard_map/ppermute | solution.py:232
  (195 shorter events, 53.5 us)
Async XLA Ops:
  0.6 6.7 %collective-permute-start.2 = (bf16[256,4096]{1,0:T(8,128)(2,1)}, bf16[256,4096]{1,0:T(8,128)(2,1)S(1)}, u32[]{:S(2)}, u32[]{:S(2)}) collective-permute-start(bf16[256,4096]{1,0:T(8,128)(2,1)} %param.11), channel_id=1, source_target_pairs={{0,2},{2,0},{4,6},{6,4},{8,10},{10,8},{12,14},{14,12},{16,18},{18,... | collective-permute-start | bytes 6291464 | tf_op jit(solution)/shard_map/ppermute | solution.py:71
  1.2 7.1 %collective-permute-start = (bf16[256,4096]{1,0:T(8,128)(2,1)}, bf16[256,4096]{1,0:T(8,128)(2,1)}, u32[]{:S(2)}, u32[]{:S(2)}) collective-permute-start(bf16[256,4096]{1,0:T(8,128)(2,1)} %param.12), channel_id=1, source_target_pairs={{0,2},{2,0},{4,6},{6,4},{8,10},{10,8},{12,14},{14,12},{16,18},{18,... | collective-permute-start | bytes 6291464 | tf_op jit(solution)/shard_map/ppermute | solution.py:70
  9.6 10.2 %collective-permute-start.1 = (bf16[40,4096]{1,0:T(8,128)(2,1)S(1)}, bf16[40,4096]{1,0:T(8,128)(2,1)S(1)}, u32[]{:S(2)}, u32[]{:S(2)}) collective-permute-start(bf16[40,4096]{1,0:T(8,128)(2,1)S(1)} %pad_maximum_fusion), channel_id=1, source_target_pairs={{0,8},{2,6},{8,16},{10,2},{16,24},{18,10},{24,28},{26,18},{28,20},... | collective-permute-start | bytes 983048 | tf_op jit(solution)/shard_map/ppermute | solution.py:104
  12.6 9.1 %collective-permute-start.3 = (bf16[40,4096]{1,0:T(8,128)(2,1)S(1)}, bf16[40,4096]{1,0:T(8,128)(2,1)S(1)}, u32[]{:S(2)}, u32[]{:S(2)}) collective-permute-start(bf16[40,4096]{1,0:T(8,128)(2,1)S(1)} %pad_maximum_fusion.1), channel_id=1, source_target_pairs={{0,8},{2,6},{8,16},{10,2},{16,24},{18,10},{24,28},{26,18},{28,20},... | collective-permute-start | bytes 983048 | tf_op jit(solution)/shard_map/ppermute | solution.py:104
  20.1 7.1 %collective-permute-start.4 = (bf16[40,4096]{1,0:T(8,128)(2,1)S(1)}, bf16[40,4096]{1,0:T(8,128)(2,1)S(1)}, u32[]{:S(2)}, u32[]{:S(2)}) collective-permute-start(bf16[40,4096]{1,0:T(8,128)(2,1)S(1)} %pad_maximum_fusion.2), channel_id=1, source_target_pairs={{0,8},{2,6},{8,16},{10,2},{16,24},{18,10},{24,28},{26,18},{28,20},... | collective-permute-start | bytes 983048 | tf_op jit(solution)/shard_map/ppermute | solution.py:104
  21.8 8.9 %collective-permute-start.5 = (bf16[40,4096]{1,0:T(8,128)(2,1)S(1)}, bf16[40,4096]{1,0:T(8,128)(2,1)S(1)}, u32[]{:S(2)}, u32[]{:S(2)}) collective-permute-start(bf16[40,4096]{1,0:T(8,128)(2,1)S(1)} %pad_maximum_fusion.3), channel_id=1, source_target_pairs={{0,8},{2,6},{8,16},{10,2},{16,24},{18,10},{24,28},{26,18},{28,20},... | collective-permute-start | bytes 983048 | tf_op jit(solution)/shard_map/ppermute | solution.py:104
  27.3 7.1 %collective-permute-start.6 = (bf16[40,4096]{1,0:T(8,128)(2,1)S(1)}, bf16[40,4096]{1,0:T(8,128)(2,1)S(1)}, u32[]{:S(2)}, u32[]{:S(2)}) collective-permute-start(bf16[40,4096]{1,0:T(8,128)(2,1)S(1)} %pad_maximum_fusion.4), channel_id=1, source_target_pairs={{0,8},{2,6},{8,16},{10,2},{16,24},{18,10},{24,28},{26,18},{28,20},... | collective-permute-start | bytes 983048 | tf_op jit(solution)/shard_map/ppermute | solution.py:104
  30.9 7.1 %collective-permute-start.7 = (bf16[40,4096]{1,0:T(8,128)(2,1)S(1)}, bf16[40,4096]{1,0:T(8,128)(2,1)S(1)}, u32[]{:S(2)}, u32[]{:S(2)}) collective-permute-start(bf16[40,4096]{1,0:T(8,128)(2,1)S(1)} %pad_maximum_fusion.5), channel_id=1, source_target_pairs={{0,8},{2,6},{8,16},{10,2},{16,24},{18,10},{24,28},{26,18},{28,20},... | collective-permute-start | bytes 983048 | tf_op jit(solution)/shard_map/ppermute | solution.py:104
  34.6 10.7 %collective-permute-start.8 = (bf16[40,4096]{1,0:T(8,128)(2,1)S(1)}, bf16[40,4096]{1,0:T(8,128)(2,1)S(1)}, u32[]{:S(2)}, u32[]{:S(2)}) collective-permute-start(bf16[40,4096]{1,0:T(8,128)(2,1)S(1)} %pad_maximum_fusion.6), channel_id=1, source_target_pairs={{0,8},{2,6},{8,16},{10,2},{16,24},{18,10},{24,28},{26,18},{28,20},... | collective-permute-start | bytes 983048 | tf_op jit(solution)/shard_map/ppermute | solution.py:104
  38.1 7.1 %collective-permute-start.9 = (bf16[40,4096]{1,0:T(8,128)(2,1)S(1)}, bf16[40,4096]{1,0:T(8,128)(2,1)S(1)}, u32[]{:S(2)}, u32[]{:S(2)}) collective-permute-start(bf16[40,4096]{1,0:T(8,128)(2,1)S(1)} %pad_maximum_fusion.7), channel_id=1, source_target_pairs={{0,8},{2,6},{8,16},{10,2},{16,24},{18,10},{24,28},{26,18},{28,20},... | collective-permute-start | bytes 983048 | tf_op jit(solution)/shard_map/ppermute | solution.py:104
  45.4 7.1 %collective-permute-start.10 = (bf16[40,4096]{1,0:T(8,128)(2,1)S(1)}, bf16[40,4096]{1,0:T(8,128)(2,1)S(1)}, u32[]{:S(2)}, u32[]{:S(2)}) collective-permute-start(bf16[40,4096]{1,0:T(8,128)(2,1)S(1)} %pad_maximum_fusion.8), channel_id=1, source_target_pairs={{0,8},{2,6},{8,16},{10,2},{16,24},{18,10},{24,28},{26,18},{28,20},... | collective-permute-start | bytes 983048 | tf_op jit(solution)/shard_map/ppermute | solution.py:104
  47.3 8.8 %collective-permute-start.11 = (bf16[40,4096]{1,0:T(8,128)(2,1)S(1)}, bf16[40,4096]{1,0:T(8,128)(2,1)S(1)}, u32[]{:S(2)}, u32[]{:S(2)}) collective-permute-start(bf16[40,4096]{1,0:T(8,128)(2,1)S(1)} %pad_maximum_fusion.9), channel_id=1, source_target_pairs={{0,8},{2,6},{8,16},{10,2},{16,24},{18,10},{24,28},{26,18},{28,20},... | collective-permute-start | bytes 983048 | tf_op jit(solution)/shard_map/ppermute | solution.py:104
  52.6 7.1 %collective-permute-start.12 = (bf16[40,4096]{1,0:T(8,128)(2,1)S(1)}, bf16[40,4096]{1,0:T(8,128)(2,1)S(1)}, u32[]{:S(2)}, u32[]{:S(2)}) collective-permute-start(bf16[40,4096]{1,0:T(8,128)(2,1)S(1)} %collective-permute-done.10), channel_id=1, source_target_pairs={{0,8},{2,6},{8,16},{10,2},{16,24},{18,10},{24,28},{26,18},{28,20},... | collective-permute-start | bytes 983048 | tf_op jit(solution)/shard_map/ppermute | solution.py:104
  56.1 7.1 %collective-permute-start.13 = (bf16[40,4096]{1,0:T(8,128)(2,1)S(1)}, bf16[40,4096]{1,0:T(8,128)(2,1)S(1)}, u32[]{:S(2)}, u32[]{:S(2)}) collective-permute-start(bf16[40,4096]{1,0:T(8,128)(2,1)S(1)} %collective-permute-done.11), channel_id=1, source_target_pairs={{0,8},{2,6},{8,16},{10,2},{16,24},{18,10},{24,28},{26,18},{28,20},... | collective-permute-start | bytes 983048 | tf_op jit(solution)/shard_map/ppermute | solution.py:104
  59.6 7.1 %collective-permute-start.14 = (bf16[40,4096]{1,0:T(8,128)(2,1)S(1)}, bf16[40,4096]{1,0:T(8,128)(2,1)S(1)}, u32[]{:S(2)}, u32[]{:S(2)}) collective-permute-start(bf16[40,4096]{1,0:T(8,128)(2,1)S(1)} %collective-permute-done.12), channel_id=1, source_target_pairs={{0,8},{2,6},{8,16},{10,2},{16,24},{18,10},{24,28},{26,18},{28,20},... | collective-permute-start | bytes 983048 | tf_op jit(solution)/shard_map/ppermute | solution.py:104
  63.2 7.1 %collective-permute-start.15 = (bf16[40,4096]{1,0:T(8,128)(2,1)S(1)}, bf16[40,4096]{1,0:T(8,128)(2,1)S(1)}, u32[]{:S(2)}, u32[]{:S(2)}) collective-permute-start(bf16[40,4096]{1,0:T(8,128)(2,1)S(1)} %collective-permute-done.13), channel_id=1, source_target_pairs={{0,8},{2,6},{8,16},{10,2},{16,24},{18,10},{24,28},{26,18},{28,20},... | collective-permute-start | bytes 983048 | tf_op jit(solution)/shard_map/ppermute | solution.py:104
  66.7 9.9 %collective-permute-start.37 = (bf16[32,4096]{1,0:T(8,128)(2,1)S(1)}, bf16[32,4096]{1,0:T(8,128)(2,1)S(1)}, u32[]{:S(2)}, u32[]{:S(2)}) collective-permute-start(bf16[32,4096]{1,0:T(8,128)(2,1)S(1)} %slice.257), channel_id=1, source_target_pairs={{0,2},{2,0},{4,6},{6,4},{8,10},{10,8},{12,14},{14,12},{16,18},{18,... | collective-permute-start | bytes 786440 | tf_op jit(solution)/shard_map/ppermute | solution.py:87
  66.8 6.4 %collective-permute-start.26 = (bf16[32,4096]{1,0:T(8,128)(2,1)S(1)}, bf16[32,4096]{1,0:T(8,128)(2,1)S(1)}, u32[]{:S(2)}, u32[]{:S(2)}) collective-permute-start(bf16[32,4096]{1,0:T(8,128)(2,1)S(1)} %slice.257), channel_id=1, source_target_pairs={{0,8},{2,6},{8,16},{10,2},{16,24},{18,10},{24,28},{26,18},{28,20},... | collective-permute-start | bytes 786440 | tf_op jit(solution)/shard_map/ppermute | solution.py:104
  70.3 6.4 %collective-permute-start.25 = (bf16[32,4096]{1,0:T(8,128)(2,1)S(1)}, bf16[32,4096]{1,0:T(8,128)(2,1)S(1)}, u32[]{:S(2)}, u32[]{:S(2)}) collective-permute-start(bf16[32,4096]{1,0:T(8,128)(2,1)S(1)} %slice.256), channel_id=1, source_target_pairs={{0,8},{2,6},{8,16},{10,2},{16,24},{18,10},{24,28},{26,18},{28,20},... | collective-permute-start | bytes 786440 | tf_op jit(solution)/shard_map/ppermute | solution.py:104
  71.9 6.5 %collective-permute-start.24 = (bf16[32,4096]{1,0:T(8,128)(2,1)S(1)}, bf16[32,4096]{1,0:T(8,128)(2,1)S(1)}, u32[]{:S(2)}, u32[]{:S(2)}) collective-permute-start(bf16[32,4096]{1,0:T(8,128)(2,1)S(1)} %slice.256), channel_id=1, source_target_pairs={{0,2},{2,0},{4,6},{6,4},{8,10},{10,8},{12,14},{14,12},{16,18},{18,... | collective-permute-start | bytes 786440 | tf_op jit(solution)/shard_map/ppermute | solution.py:87
  72.1 12.6 %collective-permute-start.16 = (bf16[128,4096]{1,0:T(8,128)(2,1)S(1)}, bf16[128,4096]{1,0:T(8,128)(2,1)S(1)}, u32[]{:S(2)}, u32[]{:S(2)}) collective-permute-start(bf16[128,4096]{1,0:T(8,128)(2,1)S(1)} %slice_dynamic-update-slice_fusion.refs_0_), channel_id=1, source_target_pairs={{0,2},{2,0},{4,6},{6,4},{8,10},{10,8},{12,14},{14,12},{16,18},{18,... | collective-permute-start | bytes 3145736 | tf_op jit(solution)/shard_map/ppermute | solution.py:200
  73.2 6.4 %collective-permute-start.39 = (bf16[32,4096]{1,0:T(8,128)(2,1)S(1)}, bf16[32,4096]{1,0:T(8,128)(2,1)S(1)}, u32[]{:S(2)}, u32[]{:S(2)}) collective-permute-start(bf16[32,4096]{1,0:T(8,128)(2,1)S(1)} %collective-permute-done.26), channel_id=1, source_target_pairs={{0,8},{2,6},{8,16},{10,2},{16,24},{18,10},{24,28},{26,18},{28,20},... | collective-permute-start | bytes 786440 | tf_op jit(solution)/shard_map/ppermute | solution.py:104
  76.7 6.4 %collective-permute-start.38 = (bf16[32,4096]{1,0:T(8,128)(2,1)S(1)}, bf16[32,4096]{1,0:T(8,128)(2,1)S(1)}, u32[]{:S(2)}, u32[]{:S(2)}) collective-permute-start(bf16[32,4096]{1,0:T(8,128)(2,1)S(1)} %collective-permute-done.26), channel_id=1, source_target_pairs={{0,2},{2,0},{4,6},{6,4},{8,10},{10,8},{12,14},{14,12},{16,18},{18,... | collective-permute-start | bytes 786440 | tf_op jit(solution)/shard_map/ppermute | solution.py:87
  76.7 6.4 %collective-permute-start.28 = (bf16[32,4096]{1,0:T(8,128)(2,1)S(1)}, bf16[32,4096]{1,0:T(8,128)(2,1)S(1)}, u32[]{:S(2)}, u32[]{:S(2)}) collective-permute-start(bf16[32,4096]{1,0:T(8,128)(2,1)S(1)} %collective-permute-done.25), channel_id=1, source_target_pairs={{0,8},{2,6},{8,16},{10,2},{16,24},{18,10},{24,28},{26,18},{28,20},... | collective-permute-start | bytes 786440 | tf_op jit(solution)/shard_map/ppermute | solution.py:104
  97.1 9.3 %collective-permute-start.42 = (bf16[2,2,16,2048]{3,2,0,1:T(8,128)(2,1)S(1)}, bf16[2,2,16,2048]{3,2,0,1:T(8,128)(2,1)S(1)}, u32[]{:S(2)}, u32[]{:S(2)}) collective-permute-start(bf16[2,2,16,2048]{3,2,0,1:T(8,128)(2,1)S(1)} %fusion.8), channel_id=1, source_target_pairs={{0,4},{2,6},{4,0},{6,2},{8,12},{10,14},{12,8},{14,10},{16,20},{18,... | collective-permute-start | bytes 786440 | tf_op jit(solution)/shard_map/ppermute | solution.py:227
  100.1 8.3 %collective-permute-start.47 = (bf16[2,2,16,2048]{3,2,0,1:T(8,128)(2,1)S(1)}, bf16[2,2,16,2048]{3,2,0,1:T(8,128)(2,1)S(1)}, u32[]{:S(2)}, u32[]{:S(2)}) collective-permute-start(bf16[2,2,16,2048]{3,2,0,1:T(8,128)(2,1)S(1)} %fusion.9), channel_id=1, source_target_pairs={{0,8},{2,10},{4,12},{6,14},{8,0},{10,2},{12,4},{14,6},{16,24},{18,... | collective-permute-start | bytes 786440 | tf_op jit(solution)/shard_map/ppermute | solution.py:227
  106.5 5.2 %collective-permute-start.43 = (bf16[2,16,2048]{2,1,0:T(8,128)(2,1)S(1)}, bf16[2,16,2048]{2,1,0:T(8,128)(2,1)S(1)}, u32[]{:S(2)}, u32[]{:S(2)}) collective-permute-start(bf16[2,16,2048]{2,1,0:T(8,128)(2,1)S(1)} %fusion.12), channel_id=1, source_target_pairs={{0,8},{2,10},{4,12},{6,14},{8,0},{10,2},{12,4},{14,6},{16,24},{18,... | collective-permute-start | bytes 393224 | tf_op jit(solution)/shard_map/ppermute | solution.py:227
  108.5 5.0 %collective-permute-start.48 = (bf16[2,16,2048]{2,1,0:T(8,128)(2,1)S(1)}, bf16[2,16,2048]{2,1,0:T(8,128)(2,1)S(1)}, u32[]{:S(2)}, u32[]{:S(2)}) collective-permute-start(bf16[2,16,2048]{2,1,0:T(8,128)(2,1)S(1)} %fusion.13), channel_id=1, source_target_pairs={{0,4},{2,6},{4,0},{6,2},{8,12},{10,14},{12,8},{14,10},{16,20},{18,... | collective-permute-start | bytes 393224 | tf_op jit(solution)/shard_map/ppermute | solution.py:227
  111.8 6.6 %collective-permute-start.44 = (bf16[16,2048]{1,0:T(8,128)(2,1)S(1)}, bf16[16,2048]{1,0:T(8,128)(2,1)S(1)}, u32[]{:S(2)}, u32[]{:S(2)}) collective-permute-start(bf16[16,2048]{1,0:T(8,128)(2,1)S(1)} %fusion.20), channel_id=1, source_target_pairs={{0,16},{2,18},{4,20},{6,22},{8,24},{10,26},{12,28},{14,30},{16,0},... | collective-permute-start | bytes 196616 | tf_op jit(solution)/shard_map/ppermute | solution.py:227
  113.6 6.5 %collective-permute-start.49 = (bf16[16,2048]{1,0:T(8,128)(2,1)S(1)}, bf16[16,2048]{1,0:T(8,128)(2,1)S(1)}, u32[]{:S(2)}, u32[]{:S(2)}) collective-permute-start(bf16[16,2048]{1,0:T(8,128)(2,1)S(1)} %fusion.21), channel_id=1, source_target_pairs={{0,16},{2,18},{4,20},{6,22},{8,24},{10,26},{12,28},{14,30},{16,0},... | collective-permute-start | bytes 196616 | tf_op jit(solution)/shard_map/ppermute | solution.py:227
  118.5 5.0 %collective-permute-start.45 = (f32[16,2048]{1,0:T(8,128)S(1)}, f32[16,2048]{1,0:T(8,128)S(1)}, u32[]{:S(2)}, u32[]{:S(2)}) collective-permute-start(f32[16,2048]{1,0:T(8,128)S(1)} %fusion.15), channel_id=1, source_target_pairs={{0,1},{1,0},{2,3},{3,2},{4,5},{5,4},{6,7},{7,6},{8,9},{9,8},{10,11... | collective-permute-start | bytes 393224 | tf_op jit(solution)/shard_map/ppermute | solution.py:232
  120.1 5.0 %collective-permute-start.50 = (f32[16,2048]{1,0:T(8,128)S(1)}, f32[16,2048]{1,0:T(8,128)S(1)}, u32[]{:S(2)}, u32[]{:S(2)}) collective-permute-start(f32[16,2048]{1,0:T(8,128)S(1)} %fusion.14), channel_id=1, source_target_pairs={{0,1},{1,0},{2,3},{3,2},{4,5},{5,4},{6,7},{7,6},{8,9},{9,8},{10,11... | collective-permute-start | bytes 393224 | tf_op jit(solution)/shard_map/ppermute | solution.py:232
  (29 other events, 101.2 us)

commit v4 on v3

--- a/solution.py
+++ b/solution.py
@@ -38,7 +38,7 @@
     return lax.dynamic_update_slice_in_dim(x, rows, tile * 8, 0)
 
 
-def gather_rows(bank_s, bank_t, passages, owner, index, core, waiting):
+def gather_rows(bank_s, bank_t, passages, owner, index, core):
     n_dev = lax.axis_size("wide")
     n_chip = n_dev // 2
     pool, width = bank_s.shape
@@ -104,8 +104,6 @@
             got = lax.ppermute(sent, "wide", pairs)
             arrived[i].append(got)
             keep(i, t, sent[:STEP])
-            if i == 0 and t == 3:
-                waiting, got = lax.optimization_barrier((waiting, got))
             if t < n_chip - 1:
                 riding[i] = got[STEP:]
                 got = got[:STEP]
@@ -116,7 +114,7 @@
                 moving[i] = jnp.where(own_chip, own_rows(i, t + 1), got)
     for i in (1, 0):
         keep(i, rounds, moving[i])
-    return pools[0], pools[1], rows, waiting
+    return pools[0], pools[1], rows
 
 
 def dot_t(a, b):
@@ -194,9 +192,7 @@
     n_pass = block * n_dev
     swap = swap_pairs(n_dev, 1)
     across = [(0, 1), (1, 0)]
-    pool_s, pool_t, rows, keep_mask = gather_rows(
-        bank_student, bank_teacher, passages, owner[0], index, core, keep_mask
-    )
+    pool_s, pool_t, rows = gather_rows(bank_student, bank_teacher, passages, owner[0], index, core)
     pass_parts = [rows, lax.ppermute(rows, "wide", swap)]
     chip_of = (positives // (2 * block)) ^ chip
     core_of = ((positives // block) % 2) ^ core
@@ -207,41 +203,41 @@
 
     chip_bits = ["x"] + ["z%d" % b for b in range(n_chip.bit_length() - 2)]
     pairs_of = {name: swap_pairs(n_dev, 2 << b) for b, name in enumerate(chip_bits)}
-    first_sent = []
-
-    def reduced(columns, order):
+    zs = chip_bits[1:]
+    orders = (["x"] + zs, zs[:1] + ["x"] + zs[1:])
+    lefts = [chip_bits[::-1], chip_bits[::-1]]
+    sums = []
+    sent = [None, None]
+    mid, half = n_pass // 2, width // 2
+    for h in range(2):
+        columns = queries[:, h * half : (h + 1) * half]
+
         def terms(grads):
             return lax.dot_general(
                 grads, columns, (((0,), (0,)), ((), ())), preferred_element_type=jnp.float32
             )
 
         got = lax.ppermute(terms(grad_p[:, mid:]), "wide", swap)
-        sums = (terms(grad_p[:, :mid]) + got).reshape(
-            (2,) * len(chip_bits) + (block, columns.shape[1])
-        )
-        left = chip_bits[::-1]
-        for name in order:
-            at = left.index(name)
-            sent = lax.index_in_dim(sums, 1, at, keepdims=False).astype(jnp.bfloat16)
-            first_sent.append(sent)
-            got = lax.ppermute(sent, "wide", pairs_of[name])
-            sums = lax.index_in_dim(sums, 0, at, keepdims=False) + got.astype(jnp.float32)
-            left.pop(at)
-        if n_dp != 2:
-            return lax.psum(sums, "dp") * scale
-        return (sums + lax.ppermute(sums, "dp", across)) * scale
-
-    mid, half = n_pass // 2, width // 2
-    zs = chip_bits[1:]
-    passage_grad = jnp.concatenate(
-        [
-            reduced(queries[:, :half], ["x"] + zs),
-            reduced(queries[:, half:], zs[:1] + ["x"] + zs[1:]),
-        ],
-        1,
-    )
-
-    (late_p, grad_q), _ = lax.optimization_barrier(((grad_p, grad_q), first_sent[0]))
+        sums.append((terms(grad_p[:, :mid]) + got).reshape((2,) * len(chip_bits) + (block, half)))
+    for step in range(len(chip_bits)):
+        for h in range(2):
+            at = lefts[h].index(orders[h][step])
+            sent[h] = lax.index_in_dim(sums[h], 1, at, keepdims=False).astype(jnp.bfloat16)
+            sums[h] = lax.index_in_dim(sums[h], 0, at, keepdims=False)
+            lefts[h].pop(at)
+            if h == 1:
+                sent[1], _ = lax.optimization_barrier((sent[1], sent[0]))
+            got = lax.ppermute(sent[h], "wide", pairs_of[orders[h][step]])
+            sums[h] = sums[h] + got.astype(jnp.float32)
+        if step == 0:
+            (late_p, grad_q, row_loss), _ = lax.optimization_barrier(((grad_p, grad_q, row_loss), sent[1]))
+    if n_dp == 2:
+        sums[1], _ = lax.optimization_barrier((sums[1], sums[0]))
+        sums = [x + lax.ppermute(x, "dp", across) for x in sums]
+    else:
+        sums = [lax.psum(x, "dp") for x in sums]
+    passage_grad = jnp.concatenate(sums, 1) * scale
+
     qgrad = jnp.dot(late_p, pieces, preferred_element_type=jnp.float32) + jnp.dot(
         grad_q, pool_s, preferred_element_type=jnp.float32
     )

time: 126 us -> 120 us (0.952)
  matrix products: 12.2 us -> 6.48 us
    dot_general x4, matrix products: 7.52 us -> 1.85 us  [terms(): lax.dot_general(grads, columns, (((0,), (0,)), ((), ())), preferred_eleme...]
    ppermute x18, waiting for transfers between devices: 23.9 us -> 20.1 us  [gather_rows(): got = lax.ppermute(sent, 'wide', pairs)]
    ppermute x10, waiting for transfers between devices: 10.8 us -> 13.9 us  [the longest x6 11.2 us: body(): got = lax.ppermute(sent[h], 'wide', pairs_of[orders[h][step]])]
    ppermute x1, waiting for transfers between devices: 2.91 us -> 0.8 us  [gather_rows(): swapped[0] = lax.ppermute(bank_s, 'wide', swap)]
    ppermute x1, waiting for transfers between devices: 0.94 us -> 3 us  [gather_rows(): swapped = [None, lax.ppermute(bank_t, 'wide', swap)]]
  transfers between devices with their start and end apart: 51 -> 51, of which waited for: 31 -> 30; matrix products, arithmetic and copies ran while one was open for 17% -> 14% of each run, Pallas kernels for 0% -> 0%
where the time goes in v4:
time: 120 us
  waiting for transfers between devices  47.4 us (40%)
  starting transfers between devices  45.2 us (38%)
  other arithmetic  10.9 us (9%)
  matrix products  6.48 us (5%)
  Pallas kernels  4.33 us (4%)
  between operations  2.91 us (2%)
  local copies, waits for them, and re-layouts  2.65 us (2%)
    ppermute x18, starting transfers between devices, gather_rows(): got = lax.ppermute(sent, 'wide', pairs)  30.5 us
    ppermute x18, waiting for transfers between devices, gather_rows(): got = lax.ppermute(sent, 'wide', pairs)  20.1 us
    ppermute x6, waiting for transfers between devices, body(): got = lax.ppermute(sent[h], 'wide', pairs_of[orders[h][step]])  11.2 us
    ppermute x20, waiting for transfers between devices, keep(): other = lax.ppermute(sent, 'wide', swap)  9.66 us
    ppermute x6, starting transfers between devices, body(): got = lax.ppermute(sent[h], 'wide', pairs_of[orders[h][step]])  8.1 us
    pallas_call x1, Pallas kernels, tail(): pl.pallas_call(functools.partial(tail_kernel, scale, len(pass_parts)), ou...  4.33 us
    select_n x2, other arithmetic, gather_rows(): full = jnp.where(own_core, banks[i], swapped[i])  3.76 us
    dot_general x1, matrix products, body(): jnp.dot(grad_q, pool_s, preferred_element_type=jnp.float32)  3.35 us
  transfers between devices with their start and end apart: 51, of which 30 were waited for; matrix products, arithmetic and copies ran while one was open for 14% of the time, Pallas kernels for 0%

profile of v4, /device:TPU:0, one launch (start us, length us, event | category | flops | bytes accessed | tf_op | source)
XLA Modules:
  0.0 119.9 jit_solution(10089416882003087793)
XLA Ops:
  5.3 3.0 %collective-permute-done = bf16[256,4096]{1,0:T(8,128)(2,1)} collective-permute-done((bf16[256,4096]{1,0:T(8,128)(2,1)}, bf16[256,4096]{1,0:T(8,128)(2,1)}, u32[]{:S(2)}, u32[]{:S(2)}) %collective-permute-start) | collective-permute-done | bytes 2097184 | tf_op jit(solution)/shard_map/ppermute | solution.py:70
  9.6 3.0 %collective-permute-start.1 = (bf16[40,4096]{1,0:T(8,128)(2,1)S(1)}, bf16[40,4096]{1,0:T(8,128)(2,1)S(1)}, u32[]{:S(2)}, u32[]{:S(2)}) collective-permute-start(bf16[40,4096]{1,0:T(8,128)(2,1)S(1)} %pad_maximum_fusion), channel_id=1, source_target_pairs={{0,8},{2,6},{8,16},{10,2},{16,24},{18,10},{24,28},{26,18},{28,20},... | collective-permute-start | bytes 983048 | tf_op jit(solution)/shard_map/ppermute | solution.py:104
  15.3 1.9 %broadcast_select_fusion = bf16[256,4096]{1,0:T(8,128)(2,1)S(1)} fusion(bf16[256,4096]{1,0:T(8,128)(2,1)S(1)} %copy-done.3, bf16[256,4096]{1,0:T(8,128)(2,1)} %collective-permute-done.2, pred[]{:T(512)S(6)} %eq.34), kind=kLoop, calls=%fused_computation.3 | loop fusion | flops 1048576 | bytes 6291457 | tf_op jit(solution)/shard_map/jit(_where)/select_n | solution.py:102
  17.3 1.8 %broadcast_select_fusion.1 = bf16[256,4096]{1,0:T(8,128)(2,1)S(1)} fusion(bf16[256,4096]{1,0:T(8,128)(2,1)S(1)} %copy-done.4, bf16[256,4096]{1,0:T(8,128)(2,1)} %collective-permute-done, pred[]{:T(512)S(6)} %eq.34), kind=kLoop, calls=%fused_computation.4 | loop fusion | flops 1048576 | bytes 6291457 | tf_op jit(solution)/shard_map/jit(_where)/select_n | solution.py:102
  19.8 1.6 %collective-permute-start.4 = (bf16[40,4096]{1,0:T(8,128)(2,1)S(1)}, bf16[40,4096]{1,0:T(8,128)(2,1)S(1)}, u32[]{:S(2)}, u32[]{:S(2)}) collective-permute-start(bf16[40,4096]{1,0:T(8,128)(2,1)S(1)} %pad_maximum_fusion.2), channel_id=1, source_target_pairs={{0,8},{2,6},{8,16},{10,2},{16,24},{18,10},{24,28},{26,18},{28,20},... | collective-permute-start | bytes 983048 | tf_op jit(solution)/shard_map/ppermute | solution.py:104
  21.6 1.8 %collective-permute-start.5 = (bf16[40,4096]{1,0:T(8,128)(2,1)S(1)}, bf16[40,4096]{1,0:T(8,128)(2,1)S(1)}, u32[]{:S(2)}, u32[]{:S(2)}) collective-permute-start(bf16[40,4096]{1,0:T(8,128)(2,1)S(1)} %pad_maximum_fusion.3), channel_id=1, source_target_pairs={{0,8},{2,6},{8,16},{10,2},{16,24},{18,10},{24,28},{26,18},{28,20},... | collective-permute-start | bytes 983048 | tf_op jit(solution)/shard_map/ppermute | solution.py:104
  25.1 1.8 %collective-permute-done.4 = bf16[40,4096]{1,0:T(8,128)(2,1)S(1)} collective-permute-done((bf16[40,4096]{1,0:T(8,128)(2,1)S(1)}, bf16[40,4096]{1,0:T(8,128)(2,1)S(1)}, u32[]{:S(2)}, u32[]{:S(2)}) %collective-permute-start.4) | collective-permute-done | bytes 327712 | tf_op jit(solution)/shard_map/ppermute | solution.py:104
  27.1 1.6 %collective-permute-start.6 = (bf16[40,4096]{1,0:T(8,128)(2,1)S(1)}, bf16[40,4096]{1,0:T(8,128)(2,1)S(1)}, u32[]{:S(2)}, u32[]{:S(2)}) collective-permute-start(bf16[40,4096]{1,0:T(8,128)(2,1)S(1)} %pad_maximum_fusion.4), channel_id=1, source_target_pairs={{0,8},{2,6},{8,16},{10,2},{16,24},{18,10},{24,28},{26,18},{28,20},... | collective-permute-start | bytes 983048 | tf_op jit(solution)/shard_map/ppermute | solution.py:104
  28.8 1.6 %collective-permute-done.5 = bf16[40,4096]{1,0:T(8,128)(2,1)S(1)} collective-permute-done((bf16[40,4096]{1,0:T(8,128)(2,1)S(1)}, bf16[40,4096]{1,0:T(8,128)(2,1)S(1)}, u32[]{:S(2)}, u32[]{:S(2)}) %collective-permute-start.5) | collective-permute-done | bytes 327712 | tf_op jit(solution)/shard_map/ppermute | solution.py:104
  30.6 1.6 %collective-permute-start.7 = (bf16[40,4096]{1,0:T(8,128)(2,1)S(1)}, bf16[40,4096]{1,0:T(8,128)(2,1)S(1)}, u32[]{:S(2)}, u32[]{:S(2)}) collective-permute-start(bf16[40,4096]{1,0:T(8,128)(2,1)S(1)} %pad_maximum_fusion.5), channel_id=1, source_target_pairs={{0,8},{2,6},{8,16},{10,2},{16,24},{18,10},{24,28},{26,18},{28,20},... | collective-permute-start | bytes 983048 | tf_op jit(solution)/shard_map/ppermute | solution.py:104
  34.3 1.6 %collective-permute-start.8 = (bf16[40,4096]{1,0:T(8,128)(2,1)S(1)}, bf16[40,4096]{1,0:T(8,128)(2,1)S(1)}, u32[]{:S(2)}, u32[]{:S(2)}) collective-permute-start(bf16[40,4096]{1,0:T(8,128)(2,1)S(1)} %pad_maximum_fusion.6), channel_id=1, source_target_pairs={{0,8},{2,6},{8,16},{10,2},{16,24},{18,10},{24,28},{26,18},{28,20},... | collective-permute-start | bytes 983048 | tf_op jit(solution)/shard_map/ppermute | solution.py:104
  36.1 1.6 %collective-permute-done.7 = bf16[40,4096]{1,0:T(8,128)(2,1)S(1)} collective-permute-done((bf16[40,4096]{1,0:T(8,128)(2,1)S(1)}, bf16[40,4096]{1,0:T(8,128)(2,1)S(1)}, u32[]{:S(2)}, u32[]{:S(2)}) %collective-permute-start.7) | collective-permute-done | bytes 327712 | tf_op jit(solution)/shard_map/ppermute | solution.py:104
  37.8 1.6 %collective-permute-start.9 = (bf16[40,4096]{1,0:T(8,128)(2,1)S(1)}, bf16[40,4096]{1,0:T(8,128)(2,1)S(1)}, u32[]{:S(2)}, u32[]{:S(2)}) collective-permute-start(bf16[40,4096]{1,0:T(8,128)(2,1)S(1)} %pad_maximum_fusion.7), channel_id=1, source_target_pairs={{0,8},{2,6},{8,16},{10,2},{16,24},{18,10},{24,28},{26,18},{28,20},... | collective-permute-start | bytes 983048 | tf_op jit(solution)/shard_map/ppermute | solution.py:104
  41.5 1.6 %collective-permute-start.10 = (bf16[40,4096]{1,0:T(8,128)(2,1)S(1)}, bf16[40,4096]{1,0:T(8,128)(2,1)S(1)}, u32[]{:S(2)}, u32[]{:S(2)}) collective-permute-start(bf16[40,4096]{1,0:T(8,128)(2,1)S(1)} %pad_maximum_fusion.8), channel_id=1, source_target_pairs={{0,8},{2,6},{8,16},{10,2},{16,24},{18,10},{24,28},{26,18},{28,20},... | collective-permute-start | bytes 983048 | tf_op jit(solution)/shard_map/ppermute | solution.py:104
  43.3 1.6 %collective-permute-done.9 = bf16[40,4096]{1,0:T(8,128)(2,1)S(1)} collective-permute-done((bf16[40,4096]{1,0:T(8,128)(2,1)S(1)}, bf16[40,4096]{1,0:T(8,128)(2,1)S(1)}, u32[]{:S(2)}, u32[]{:S(2)}) %collective-permute-start.9) | collective-permute-done | bytes 327712 | tf_op jit(solution)/shard_map/ppermute | solution.py:104
  45.1 1.6 %collective-permute-start.11 = (bf16[40,4096]{1,0:T(8,128)(2,1)S(1)}, bf16[40,4096]{1,0:T(8,128)(2,1)S(1)}, u32[]{:S(2)}, u32[]{:S(2)}) collective-permute-start(bf16[40,4096]{1,0:T(8,128)(2,1)S(1)} %pad_maximum_fusion.9), channel_id=1, source_target_pairs={{0,8},{2,6},{8,16},{10,2},{16,24},{18,10},{24,28},{26,18},{28,20},... | collective-permute-start | bytes 983048 | tf_op jit(solution)/shard_map/ppermute | solution.py:104
  50.4 1.8 %collective-permute-done.11 = bf16[40,4096]{1,0:T(8,128)(2,1)S(1)} collective-permute-done((bf16[40,4096]{1,0:T(8,128)(2,1)S(1)}, bf16[40,4096]{1,0:T(8,128)(2,1)S(1)}, u32[]{:S(2)}, u32[]{:S(2)}) %collective-permute-start.11) | collective-permute-done | bytes 327712 | tf_op jit(solution)/shard_map/ppermute | solution.py:104
  57.5 1.8 %collective-permute-done.13 = bf16[40,4096]{1,0:T(8,128)(2,1)S(1)} collective-permute-done((bf16[40,4096]{1,0:T(8,128)(2,1)S(1)}, bf16[40,4096]{1,0:T(8,128)(2,1)S(1)}, u32[]{:S(2)}, u32[]{:S(2)}) %collective-permute-start.13) | collective-permute-done | bytes 327712 | tf_op jit(solution)/shard_map/ppermute | solution.py:104
  62.9 1.6 %collective-permute-start.26 = (bf16[32,4096]{1,0:T(8,128)(2,1)S(1)}, bf16[32,4096]{1,0:T(8,128)(2,1)S(1)}, u32[]{:S(2)}, u32[]{:S(2)}) collective-permute-start(bf16[32,4096]{1,0:T(8,128)(2,1)S(1)} %slice.259), channel_id=1, source_target_pairs={{0,8},{2,6},{8,16},{10,2},{16,24},{18,10},{24,28},{26,18},{28,20},... | collective-permute-start | bytes 786440 | tf_op jit(solution)/shard_map/ppermute | solution.py:104
  64.6 1.8 %collective-permute-done.15 = bf16[40,4096]{1,0:T(8,128)(2,1)S(1)} collective-permute-done((bf16[40,4096]{1,0:T(8,128)(2,1)S(1)}, bf16[40,4096]{1,0:T(8,128)(2,1)S(1)}, u32[]{:S(2)}, u32[]{:S(2)}) %collective-permute-start.15) | collective-permute-done | bytes 327712 | tf_op jit(solution)/shard_map/ppermute | solution.py:104
  66.4 1.6 %collective-permute-start.25 = (bf16[32,4096]{1,0:T(8,128)(2,1)S(1)}, bf16[32,4096]{1,0:T(8,128)(2,1)S(1)}, u32[]{:S(2)}, u32[]{:S(2)}) collective-permute-start(bf16[32,4096]{1,0:T(8,128)(2,1)S(1)} %slice.258), channel_id=1, source_target_pairs={{0,8},{2,6},{8,16},{10,2},{16,24},{18,10},{24,28},{26,18},{28,20},... | collective-permute-start | bytes 786440 | tf_op jit(solution)/shard_map/ppermute | solution.py:104
  70.9 1.9 %collective-permute-done.25 = bf16[32,4096]{1,0:T(8,128)(2,1)S(1)} collective-permute-done((bf16[32,4096]{1,0:T(8,128)(2,1)S(1)}, bf16[32,4096]{1,0:T(8,128)(2,1)S(1)}, u32[]{:S(2)}, u32[]{:S(2)}) %collective-permute-start.25) | collective-permute-done | bytes 262176 | tf_op jit(solution)/shard_map/ppermute | solution.py:104
  75.7 3.4 %collective-permute-done.28 = bf16[32,4096]{1,0:T(8,128)(2,1)S(1)} collective-permute-done((bf16[32,4096]{1,0:T(8,128)(2,1)S(1)}, bf16[32,4096]{1,0:T(8,128)(2,1)S(1)}, u32[]{:S(2)}, u32[]{:S(2)}) %collective-permute-start.28) | collective-permute-done | bytes 262176 | tf_op jit(solution)/shard_map/ppermute | solution.py:104
  81.5 4.3 %scores.1 = (bf16[512,256]{1,0:T(8,128)(2,1)S(1)}, bf16[512,256]{1,0:T(8,128)(2,1)S(1)}, f32[512,1]{1,0:T(8,128)S(1)}, bf16[256,4096]{1,0:T(8,128)(2,1)S(1)}) custom-call(bf16[128,4096]{1,0:T(8,128)(2,1)S(1)} %slice_dynamic-update-slice_fusion.refs_0_, bf16[128,4096]{1,0:T(8,128)(2,1)S(1)} %collective-permute-done.16.refs_1_, bf16[512,4096]{1,0:T(8,128)(2,1)S(1)} %copy-done, ...), custom_call_target="tpu_custom_call" | custom-call | flops 3221225472 | bytes 20971520 | tf_op jit(solution)/shard_map/scores/pallas_call | solution.py:160
  87.4 1.7 %collective-permute-done.41 = f32[128,2048]{1,0:T(8,128)S(1)} collective-permute-done((f32[128,2048]{1,0:T(8,128)S(1)}, f32[128,2048]{1,0:T(8,128)S(1)}, u32[]{:S(2)}, u32[]{:S(2)}) %collective-permute-start.41) | collective-permute-done | bytes 1048608 | tf_op jit(solution)/shard_map/ppermute | solution.py:220
  94.9 4.9 %collective-permute-done.43 = bf16[2,2,16,2048]{3,2,0,1:T(8,128)(2,1)S(1)} collective-permute-done((bf16[2,2,16,2048]{3,2,0,1:T(8,128)(2,1)S(1)}, bf16[2,2,16,2048]{3,2,0,1:T(8,128)(2,1)S(1)}, u32[]{:S(2)}, u32[]{:S(2)}) %collective-permute-start.43) | collective-permute-done | bytes 262176 | tf_op jit(solution)/shard_map/ppermute | solution.py:230
  99.9 1.6 %collective-permute-start.44 = (bf16[2,16,2048]{2,1,0:T(8,128)(2,1)S(1)}, bf16[2,16,2048]{2,1,0:T(8,128)(2,1)S(1)}, u32[]{:S(2)}, u32[]{:S(2)}) collective-permute-start(bf16[2,16,2048]{2,1,0:T(8,128)(2,1)S(1)} %fusion.12), channel_id=1, source_target_pairs={{0,8},{2,10},{4,12},{6,14},{8,0},{10,2},{12,4},{14,6},{16,24},{18,... | collective-permute-start | bytes 393224 | tf_op jit(solution)/shard_map/ppermute | solution.py:230
  102.5 2.4 %collective-permute-done.44 = bf16[2,16,2048]{2,1,0:T(8,128)(2,1)S(1)} collective-permute-done((bf16[2,16,2048]{2,1,0:T(8,128)(2,1)S(1)}, bf16[2,16,2048]{2,1,0:T(8,128)(2,1)S(1)}, u32[]{:S(2)}, u32[]{:S(2)}) %collective-permute-start.44) | collective-permute-done | bytes 131104 | tf_op jit(solution)/shard_map/ppermute | solution.py:230
  105.0 2.6 %collective-permute-start.45 = (bf16[16,2048]{1,0:T(8,128)(2,1)S(1)}, bf16[16,2048]{1,0:T(8,128)(2,1)S(1)}, u32[]{:S(2)}, u32[]{:S(2)}) collective-permute-start(bf16[16,2048]{1,0:T(8,128)(2,1)S(1)} %fusion.20), channel_id=1, source_target_pairs={{0,16},{2,18},{4,20},{6,22},{8,24},{10,26},{12,28},{14,30},{16,0},... | collective-permute-start | bytes 196616 | tf_op jit(solution)/shard_map/ppermute | solution.py:230
  108.2 3.8 %collective-permute-done.45 = bf16[16,2048]{1,0:T(8,128)(2,1)S(1)} collective-permute-done((bf16[16,2048]{1,0:T(8,128)(2,1)S(1)}, bf16[16,2048]{1,0:T(8,128)(2,1)S(1)}, u32[]{:S(2)}, u32[]{:S(2)}) %collective-permute-start.45) | collective-permute-done | bytes 65568 | tf_op jit(solution)/shard_map/ppermute | solution.py:230
  112.0 1.6 %collective-permute-start.46 = (f32[16,2048]{1,0:T(8,128)S(1)}, f32[16,2048]{1,0:T(8,128)S(1)}, u32[]{:S(2)}, u32[]{:S(2)}) collective-permute-start(f32[16,2048]{1,0:T(8,128)S(1)} %fusion.15), channel_id=1, source_target_pairs={{0,1},{1,0},{2,3},{3,2},{4,5},{5,4},{6,7},{7,6},{8,9},{9,8},{10,11... | collective-permute-start | bytes 393224 | tf_op jit(solution)/shard_map/ppermute | solution.py:236
  115.0 3.4 %multiply_convert_fusion = bf16[512,4096]{1,0:T(8,128)(2,1)} fusion(f32[512,4096]{1,0:T(8,128)S(1)} %fusion.53, bf16[512,256]{1,0:T(8,128)(2,1)S(1)} %get-tuple-element.63, bf16[256,4096]{1,0:T(8,128)(2,1)S(1)} %select_dynamic-update-slice_fusion.20.refs_4_), kind=kOutput, calls=%fused_computation | convolution fusion | flops 1080033280 | bytes 14942208 | tf_op jit(solution)/shard_map/dot_general | solution.py:241
  (187 shorter events, 47.1 us)
Async XLA Ops:
  1.2 7.1 %collective-permute-start = (bf16[256,4096]{1,0:T(8,128)(2,1)}, bf16[256,4096]{1,0:T(8,128)(2,1)}, u32[]{:S(2)}, u32[]{:S(2)}) collective-permute-start(bf16[256,4096]{1,0:T(8,128)(2,1)} %param.12), channel_id=1, source_target_pairs={{0,2},{2,0},{4,6},{6,4},{8,10},{10,8},{12,14},{14,12},{16,18},{18,... | collective-permute-start | bytes 6291464 | tf_op jit(solution)/shard_map/ppermute | solution.py:70
  9.6 9.7 %collective-permute-start.1 = (bf16[40,4096]{1,0:T(8,128)(2,1)S(1)}, bf16[40,4096]{1,0:T(8,128)(2,1)S(1)}, u32[]{:S(2)}, u32[]{:S(2)}) collective-permute-start(bf16[40,4096]{1,0:T(8,128)(2,1)S(1)} %pad_maximum_fusion), channel_id=1, source_target_pairs={{0,8},{2,6},{8,16},{10,2},{16,24},{18,10},{24,28},{26,18},{28,20},... | collective-permute-start | bytes 983048 | tf_op jit(solution)/shard_map/ppermute | solution.py:104
  12.6 8.8 %collective-permute-start.3 = (bf16[40,4096]{1,0:T(8,128)(2,1)S(1)}, bf16[40,4096]{1,0:T(8,128)(2,1)S(1)}, u32[]{:S(2)}, u32[]{:S(2)}) collective-permute-start(bf16[40,4096]{1,0:T(8,128)(2,1)S(1)} %pad_maximum_fusion.1), channel_id=1, source_target_pairs={{0,8},{2,6},{8,16},{10,2},{16,24},{18,10},{24,28},{26,18},{28,20},... | collective-permute-start | bytes 983048 | tf_op jit(solution)/shard_map/ppermute | solution.py:104
  19.8 7.1 %collective-permute-start.4 = (bf16[40,4096]{1,0:T(8,128)(2,1)S(1)}, bf16[40,4096]{1,0:T(8,128)(2,1)S(1)}, u32[]{:S(2)}, u32[]{:S(2)}) collective-permute-start(bf16[40,4096]{1,0:T(8,128)(2,1)S(1)} %pad_maximum_fusion.2), channel_id=1, source_target_pairs={{0,8},{2,6},{8,16},{10,2},{16,24},{18,10},{24,28},{26,18},{28,20},... | collective-permute-start | bytes 983048 | tf_op jit(solution)/shard_map/ppermute | solution.py:104
  21.6 8.9 %collective-permute-start.5 = (bf16[40,4096]{1,0:T(8,128)(2,1)S(1)}, bf16[40,4096]{1,0:T(8,128)(2,1)S(1)}, u32[]{:S(2)}, u32[]{:S(2)}) collective-permute-start(bf16[40,4096]{1,0:T(8,128)(2,1)S(1)} %pad_maximum_fusion.3), channel_id=1, source_target_pairs={{0,8},{2,6},{8,16},{10,2},{16,24},{18,10},{24,28},{26,18},{28,20},... | collective-permute-start | bytes 983048 | tf_op jit(solution)/shard_map/ppermute | solution.py:104
  27.1 7.1 %collective-permute-start.6 = (bf16[40,4096]{1,0:T(8,128)(2,1)S(1)}, bf16[40,4096]{1,0:T(8,128)(2,1)S(1)}, u32[]{:S(2)}, u32[]{:S(2)}) collective-permute-start(bf16[40,4096]{1,0:T(8,128)(2,1)S(1)} %pad_maximum_fusion.4), channel_id=1, source_target_pairs={{0,8},{2,6},{8,16},{10,2},{16,24},{18,10},{24,28},{26,18},{28,20},... | collective-permute-start | bytes 983048 | tf_op jit(solution)/shard_map/ppermute | solution.py:104
  30.6 7.1 %collective-permute-start.7 = (bf16[40,4096]{1,0:T(8,128)(2,1)S(1)}, bf16[40,4096]{1,0:T(8,128)(2,1)S(1)}, u32[]{:S(2)}, u32[]{:S(2)}) collective-permute-start(bf16[40,4096]{1,0:T(8,128)(2,1)S(1)} %pad_maximum_fusion.5), channel_id=1, source_target_pairs={{0,8},{2,6},{8,16},{10,2},{16,24},{18,10},{24,28},{26,18},{28,20},... | collective-permute-start | bytes 983048 | tf_op jit(solution)/shard_map/ppermute | solution.py:104
  34.3 7.1 %collective-permute-start.8 = (bf16[40,4096]{1,0:T(8,128)(2,1)S(1)}, bf16[40,4096]{1,0:T(8,128)(2,1)S(1)}, u32[]{:S(2)}, u32[]{:S(2)}) collective-permute-start(bf16[40,4096]{1,0:T(8,128)(2,1)S(1)} %pad_maximum_fusion.6), channel_id=1, source_target_pairs={{0,8},{2,6},{8,16},{10,2},{16,24},{18,10},{24,28},{26,18},{28,20},... | collective-permute-start | bytes 983048 | tf_op jit(solution)/shard_map/ppermute | solution.py:104
  37.8 7.1 %collective-permute-start.9 = (bf16[40,4096]{1,0:T(8,128)(2,1)S(1)}, bf16[40,4096]{1,0:T(8,128)(2,1)S(1)}, u32[]{:S(2)}, u32[]{:S(2)}) collective-permute-start(bf16[40,4096]{1,0:T(8,128)(2,1)S(1)} %pad_maximum_fusion.7), channel_id=1, source_target_pairs={{0,8},{2,6},{8,16},{10,2},{16,24},{18,10},{24,28},{26,18},{28,20},... | collective-permute-start | bytes 983048 | tf_op jit(solution)/shard_map/ppermute | solution.py:104
  41.5 7.1 %collective-permute-start.10 = (bf16[40,4096]{1,0:T(8,128)(2,1)S(1)}, bf16[40,4096]{1,0:T(8,128)(2,1)S(1)}, u32[]{:S(2)}, u32[]{:S(2)}) collective-permute-start(bf16[40,4096]{1,0:T(8,128)(2,1)S(1)} %pad_maximum_fusion.8), channel_id=1, source_target_pairs={{0,8},{2,6},{8,16},{10,2},{16,24},{18,10},{24,28},{26,18},{28,20},... | collective-permute-start | bytes 983048 | tf_op jit(solution)/shard_map/ppermute | solution.py:104
  45.1 7.1 %collective-permute-start.11 = (bf16[40,4096]{1,0:T(8,128)(2,1)S(1)}, bf16[40,4096]{1,0:T(8,128)(2,1)S(1)}, u32[]{:S(2)}, u32[]{:S(2)}) collective-permute-start(bf16[40,4096]{1,0:T(8,128)(2,1)S(1)} %pad_maximum_fusion.9), channel_id=1, source_target_pairs={{0,8},{2,6},{8,16},{10,2},{16,24},{18,10},{24,28},{26,18},{28,20},... | collective-permute-start | bytes 983048 | tf_op jit(solution)/shard_map/ppermute | solution.py:104
  48.7 7.1 %collective-permute-start.12 = (bf16[40,4096]{1,0:T(8,128)(2,1)S(1)}, bf16[40,4096]{1,0:T(8,128)(2,1)S(1)}, u32[]{:S(2)}, u32[]{:S(2)}) collective-permute-start(bf16[40,4096]{1,0:T(8,128)(2,1)S(1)} %collective-permute-done.10), channel_id=1, source_target_pairs={{0,8},{2,6},{8,16},{10,2},{16,24},{18,10},{24,28},{26,18},{28,20},... | collective-permute-start | bytes 983048 | tf_op jit(solution)/shard_map/ppermute | solution.py:104
  52.2 7.1 %collective-permute-start.13 = (bf16[40,4096]{1,0:T(8,128)(2,1)S(1)}, bf16[40,4096]{1,0:T(8,128)(2,1)S(1)}, u32[]{:S(2)}, u32[]{:S(2)}) collective-permute-start(bf16[40,4096]{1,0:T(8,128)(2,1)S(1)} %collective-permute-done.11), channel_id=1, source_target_pairs={{0,8},{2,6},{8,16},{10,2},{16,24},{18,10},{24,28},{26,18},{28,20},... | collective-permute-start | bytes 983048 | tf_op jit(solution)/shard_map/ppermute | solution.py:104
  55.8 7.1 %collective-permute-start.14 = (bf16[40,4096]{1,0:T(8,128)(2,1)S(1)}, bf16[40,4096]{1,0:T(8,128)(2,1)S(1)}, u32[]{:S(2)}, u32[]{:S(2)}) collective-permute-start(bf16[40,4096]{1,0:T(8,128)(2,1)S(1)} %collective-permute-done.12), channel_id=1, source_target_pairs={{0,8},{2,6},{8,16},{10,2},{16,24},{18,10},{24,28},{26,18},{28,20},... | collective-permute-start | bytes 983048 | tf_op jit(solution)/shard_map/ppermute | solution.py:104
  59.3 7.1 %collective-permute-start.15 = (bf16[40,4096]{1,0:T(8,128)(2,1)S(1)}, bf16[40,4096]{1,0:T(8,128)(2,1)S(1)}, u32[]{:S(2)}, u32[]{:S(2)}) collective-permute-start(bf16[40,4096]{1,0:T(8,128)(2,1)S(1)} %collective-permute-done.13), channel_id=1, source_target_pairs={{0,8},{2,6},{8,16},{10,2},{16,24},{18,10},{24,28},{26,18},{28,20},... | collective-permute-start | bytes 983048 | tf_op jit(solution)/shard_map/ppermute | solution.py:104
  62.8 9.9 %collective-permute-start.37 = (bf16[32,4096]{1,0:T(8,128)(2,1)S(1)}, bf16[32,4096]{1,0:T(8,128)(2,1)S(1)}, u32[]{:S(2)}, u32[]{:S(2)}) collective-permute-start(bf16[32,4096]{1,0:T(8,128)(2,1)S(1)} %slice.259), channel_id=1, source_target_pairs={{0,2},{2,0},{4,6},{6,4},{8,10},{10,8},{12,14},{14,12},{16,18},{18,... | collective-permute-start | bytes 786440 | tf_op jit(solution)/shard_map/ppermute | solution.py:87
  62.9 6.4 %collective-permute-start.26 = (bf16[32,4096]{1,0:T(8,128)(2,1)S(1)}, bf16[32,4096]{1,0:T(8,128)(2,1)S(1)}, u32[]{:S(2)}, u32[]{:S(2)}) collective-permute-start(bf16[32,4096]{1,0:T(8,128)(2,1)S(1)} %slice.259), channel_id=1, source_target_pairs={{0,8},{2,6},{8,16},{10,2},{16,24},{18,10},{24,28},{26,18},{28,20},... | collective-permute-start | bytes 786440 | tf_op jit(solution)/shard_map/ppermute | solution.py:104
  66.4 6.4 %collective-permute-start.25 = (bf16[32,4096]{1,0:T(8,128)(2,1)S(1)}, bf16[32,4096]{1,0:T(8,128)(2,1)S(1)}, u32[]{:S(2)}, u32[]{:S(2)}) collective-permute-start(bf16[32,4096]{1,0:T(8,128)(2,1)S(1)} %slice.258), channel_id=1, source_target_pairs={{0,8},{2,6},{8,16},{10,2},{16,24},{18,10},{24,28},{26,18},{28,20},... | collective-permute-start | bytes 786440 | tf_op jit(solution)/shard_map/ppermute | solution.py:104
  68.0 6.5 %collective-permute-start.24 = (bf16[32,4096]{1,0:T(8,128)(2,1)S(1)}, bf16[32,4096]{1,0:T(8,128)(2,1)S(1)}, u32[]{:S(2)}, u32[]{:S(2)}) collective-permute-start(bf16[32,4096]{1,0:T(8,128)(2,1)S(1)} %slice.258), channel_id=1, source_target_pairs={{0,2},{2,0},{4,6},{6,4},{8,10},{10,8},{12,14},{14,12},{16,18},{18,... | collective-permute-start | bytes 786440 | tf_op jit(solution)/shard_map/ppermute | solution.py:87
  68.2 12.6 %collective-permute-start.16 = (bf16[128,4096]{1,0:T(8,128)(2,1)S(1)}, bf16[128,4096]{1,0:T(8,128)(2,1)S(1)}, u32[]{:S(2)}, u32[]{:S(2)}) collective-permute-start(bf16[128,4096]{1,0:T(8,128)(2,1)S(1)} %slice_dynamic-update-slice_fusion.refs_0_), channel_id=1, source_target_pairs={{0,2},{2,0},{4,6},{6,4},{8,10},{10,8},{12,14},{14,12},{16,18},{18,... | collective-permute-start | bytes 3145736 | tf_op jit(solution)/shard_map/ppermute | solution.py:196
  69.4 6.4 %collective-permute-start.39 = (bf16[32,4096]{1,0:T(8,128)(2,1)S(1)}, bf16[32,4096]{1,0:T(8,128)(2,1)S(1)}, u32[]{:S(2)}, u32[]{:S(2)}) collective-permute-start(bf16[32,4096]{1,0:T(8,128)(2,1)S(1)} %collective-permute-done.26), channel_id=1, source_target_pairs={{0,8},{2,6},{8,16},{10,2},{16,24},{18,10},{24,28},{26,18},{28,20},... | collective-permute-start | bytes 786440 | tf_op jit(solution)/shard_map/ppermute | solution.py:104
  72.8 6.4 %collective-permute-start.38 = (bf16[32,4096]{1,0:T(8,128)(2,1)S(1)}, bf16[32,4096]{1,0:T(8,128)(2,1)S(1)}, u32[]{:S(2)}, u32[]{:S(2)}) collective-permute-start(bf16[32,4096]{1,0:T(8,128)(2,1)S(1)} %collective-permute-done.26), channel_id=1, source_target_pairs={{0,2},{2,0},{4,6},{6,4},{8,10},{10,8},{12,14},{14,12},{16,18},{18,... | collective-permute-start | bytes 786440 | tf_op jit(solution)/shard_map/ppermute | solution.py:87
  72.8 6.4 %collective-permute-start.28 = (bf16[32,4096]{1,0:T(8,128)(2,1)S(1)}, bf16[32,4096]{1,0:T(8,128)(2,1)S(1)}, u32[]{:S(2)}, u32[]{:S(2)}) collective-permute-start(bf16[32,4096]{1,0:T(8,128)(2,1)S(1)} %collective-permute-done.25), channel_id=1, source_target_pairs={{0,8},{2,6},{8,16},{10,2},{16,24},{18,10},{24,28},{26,18},{28,20},... | collective-permute-start | bytes 786440 | tf_op jit(solution)/shard_map/ppermute | solution.py:104
  74.5 4.7 %collective-permute-start.27 = (bf16[32,4096]{1,0:T(8,128)(2,1)S(1)}, bf16[32,4096]{1,0:T(8,128)(2,1)S(1)}, u32[]{:S(2)}, u32[]{:S(2)}) collective-permute-start(bf16[32,4096]{1,0:T(8,128)(2,1)S(1)} %collective-permute-done.25), channel_id=1, source_target_pairs={{0,2},{2,0},{4,6},{6,4},{8,10},{10,8},{12,14},{14,12},{16,18},{18,... | collective-permute-start | bytes 786440 | tf_op jit(solution)/shard_map/ppermute | solution.py:87
  91.2 8.6 %collective-permute-start.43 = (bf16[2,2,16,2048]{3,2,0,1:T(8,128)(2,1)S(1)}, bf16[2,2,16,2048]{3,2,0,1:T(8,128)(2,1)S(1)}, u32[]{:S(2)}, u32[]{:S(2)}) collective-permute-start(bf16[2,2,16,2048]{3,2,0,1:T(8,128)(2,1)S(1)} %fusion.9), channel_id=1, source_target_pairs={{0,4},{2,6},{4,0},{6,2},{8,12},{10,14},{12,8},{14,10},{16,20},{18,... | collective-permute-start | bytes 786440 | tf_op jit(solution)/shard_map/ppermute | solution.py:230
  92.0 9.5 %collective-permute-start.47 = (bf16[2,2,16,2048]{3,2,0,1:T(8,128)(2,1)S(1)}, bf16[2,2,16,2048]{3,2,0,1:T(8,128)(2,1)S(1)}, u32[]{:S(2)}, u32[]{:S(2)}) collective-permute-start(bf16[2,2,16,2048]{3,2,0,1:T(8,128)(2,1)S(1)} %fusion.8), channel_id=1, source_target_pairs={{0,8},{2,10},{4,12},{6,14},{8,0},{10,2},{12,4},{14,6},{16,24},{18,... | collective-permute-start | bytes 786440 | tf_op jit(solution)/shard_map/ppermute | solution.py:230
  99.9 5.0 %collective-permute-start.44 = (bf16[2,16,2048]{2,1,0:T(8,128)(2,1)S(1)}, bf16[2,16,2048]{2,1,0:T(8,128)(2,1)S(1)}, u32[]{:S(2)}, u32[]{:S(2)}) collective-permute-start(bf16[2,16,2048]{2,1,0:T(8,128)(2,1)S(1)} %fusion.12), channel_id=1, source_target_pairs={{0,8},{2,10},{4,12},{6,14},{8,0},{10,2},{12,4},{14,6},{16,24},{18,... | collective-permute-start | bytes 393224 | tf_op jit(solution)/shard_map/ppermute | solution.py:230
  101.6 5.9 %collective-permute-start.48 = (bf16[2,16,2048]{2,1,0:T(8,128)(2,1)S(1)}, bf16[2,16,2048]{2,1,0:T(8,128)(2,1)S(1)}, u32[]{:S(2)}, u32[]{:S(2)}) collective-permute-start(bf16[2,16,2048]{2,1,0:T(8,128)(2,1)S(1)} %fusion.13), channel_id=1, source_target_pairs={{0,4},{2,6},{4,0},{6,2},{8,12},{10,14},{12,8},{14,10},{16,20},{18,... | collective-permute-start | bytes 393224 | tf_op jit(solution)/shard_map/ppermute | solution.py:230
  105.0 7.0 %collective-permute-start.45 = (bf16[16,2048]{1,0:T(8,128)(2,1)S(1)}, bf16[16,2048]{1,0:T(8,128)(2,1)S(1)}, u32[]{:S(2)}, u32[]{:S(2)}) collective-permute-start(bf16[16,2048]{1,0:T(8,128)(2,1)S(1)} %fusion.20), channel_id=1, source_target_pairs={{0,16},{2,18},{4,20},{6,22},{8,24},{10,26},{12,28},{14,30},{16,0},... | collective-permute-start | bytes 196616 | tf_op jit(solution)/shard_map/ppermute | solution.py:230
  107.6 6.0 %collective-permute-start.49 = (bf16[16,2048]{1,0:T(8,128)(2,1)S(1)}, bf16[16,2048]{1,0:T(8,128)(2,1)S(1)}, u32[]{:S(2)}, u32[]{:S(2)}) collective-permute-start(bf16[16,2048]{1,0:T(8,128)(2,1)S(1)} %fusion.21), channel_id=1, source_target_pairs={{0,16},{2,18},{4,20},{6,22},{8,24},{10,26},{12,28},{14,30},{16,0},... | collective-permute-start | bytes 196616 | tf_op jit(solution)/shard_map/ppermute | solution.py:230
  112.0 7.1 %collective-permute-start.46 = (f32[16,2048]{1,0:T(8,128)S(1)}, f32[16,2048]{1,0:T(8,128)S(1)}, u32[]{:S(2)}, u32[]{:S(2)}) collective-permute-start(f32[16,2048]{1,0:T(8,128)S(1)} %fusion.15), channel_id=1, source_target_pairs={{0,1},{1,0},{2,3},{3,2},{4,5},{5,4},{6,7},{7,6},{8,9},{9,8},{10,11... | collective-permute-start | bytes 393224 | tf_op jit(solution)/shard_map/ppermute | solution.py:236
  113.6 5.5 %collective-permute-start.50 = (f32[16,2048]{1,0:T(8,128)S(1)}, f32[16,2048]{1,0:T(8,128)S(1)}, u32[]{:S(2)}, u32[]{:S(2)}) collective-permute-start(f32[16,2048]{1,0:T(8,128)S(1)} %fusion.14), channel_id=1, source_target_pairs={{0,1},{1,0},{2,3},{3,2},{4,5},{5,4},{6,7},{7,6},{8,9},{9,8},{10,11... | collective-permute-start | bytes 393224 | tf_op jit(solution)/shard_map/ppermute | solution.py:236
  (25 other events, 87.7 us)

commit v5 on v4

--- a/solution.py
+++ b/solution.py
@@ -43,9 +43,7 @@
     n_chip = n_dev // 2
     pool, width = bank_s.shape
     n_chunk = pool // STEP
-    n_cut = max(1, 3 * n_chunk // 8)
-    n_own = n_chunk - n_cut
-    rounds = max(n_cut + n_chip - 2, n_own + n_chip // 2 - 1)
+    rounds = max((n_chunk + n_chip - 1) // 2, n_chip - 1)
     block = passages.shape[0]
     sub = block // 2
     chip = index // 2
@@ -87,8 +85,8 @@
         other = lax.ppermute(sent, "wide", swap)
         for side, away, piece in ((core, distance, sent), (1 - core, distance_other, other)):
             slot = t - away
-            take = (slot >= 0) & (slot < n_own)
-            at = tile_of(side, jnp.clip(slot, 0, n_own - 1))
+            take = (slot >= 0) & (slot < n_chunk)
+            at = tile_of(side, jnp.clip(slot, 0, n_chunk - 1))
             pools[i] = put_rows(pools[i], jnp.where(take, piece, rows_at(pools[i], at, STEP)), at)
 
     for t in range(rounds):
@@ -110,7 +108,7 @@
                 origin = chip_at((here - turn * (t + 1) + n_chip) % n_chip)
                 rows = put_rows(rows, riding[i], (origin ^ chip) * (block // 8) + i * (sub // 8))
             moving[i] = got
-            if t + 1 < n_own:
+            if t + 1 < n_chunk:
                 moving[i] = jnp.where(own_chip, own_rows(i, t + 1), got)
     for i in (1, 0):
         keep(i, rounds, moving[i])
@@ -217,22 +215,30 @@
                 grads, columns, (((0,), (0,)), ((), ())), preferred_element_type=jnp.float32
             )
 
-        got = lax.ppermute(terms(grad_p[:, mid:]), "wide", swap)
-        sums.append((terms(grad_p[:, :mid]) + got).reshape((2,) * len(chip_bits) + (block, half)))
+        got = lax.ppermute(terms(grad_p[:, mid:]).astype(jnp.bfloat16), "wide", swap)
+        sums.append((terms(grad_p[:, :mid]) + got.astype(jnp.float32)).reshape((2,) * len(chip_bits) + (block, half)))
+    pending = None
     for step in range(len(chip_bits)):
         for h in range(2):
+            if h == 1 and step:
+                pending, _ = lax.optimization_barrier((pending, sent[0]))
+                sums[1] = sums[1] + pending.astype(jnp.float32)
             at = lefts[h].index(orders[h][step])
             sent[h] = lax.index_in_dim(sums[h], 1, at, keepdims=False).astype(jnp.bfloat16)
             sums[h] = lax.index_in_dim(sums[h], 0, at, keepdims=False)
             lefts[h].pop(at)
-            if h == 1:
+            if h == 1 and step == 0:
                 sent[1], _ = lax.optimization_barrier((sent[1], sent[0]))
             got = lax.ppermute(sent[h], "wide", pairs_of[orders[h][step]])
-            sums[h] = sums[h] + got.astype(jnp.float32)
+            if h == 0:
+                sums[0] = sums[0] + got.astype(jnp.float32)
+            else:
+                pending = got
         if step == 0:
             (late_p, grad_q, row_loss), _ = lax.optimization_barrier(((grad_p, grad_q, row_loss), sent[1]))
+    pending, _ = lax.optimization_barrier((pending, sums[0]))
+    sums[1] = sums[1] + pending.astype(jnp.float32)
     if n_dp == 2:
-        sums[1], _ = lax.optimization_barrier((sums[1], sums[0]))
         sums = [x + lax.ppermute(x, "dp", across) for x in sums]
     else:
         sums = [lax.psum(x, "dp") for x in sums]

time: 120 us -> 107 us (0.89)
  waiting for transfers between devices: 47.4 us -> 41.2 us
  starting transfers between devices: 45.2 us -> 39.4 us
    ppermute x18 -> x14, starting transfers between devices: 30.5 us -> 24.5 us  [gather_rows(): got = lax.ppermute(sent, 'wide', pairs)]
    ppermute x18 -> x14, waiting for transfers between devices: 20.1 us -> 14.3 us  [gather_rows(): got = lax.ppermute(sent, 'wide', pairs)]
    dot_general x1, matrix products: 3.35 us -> 1.26 us  [body(): jnp.dot(grad_q, pool_s, preferred_element_type=jnp.float32)]
    dot_general x1, matrix products: 1.27 us -> 3.35 us  [body(): jnp.dot(late_p, pieces, preferred_element_type=jnp.float32)]
    ppermute x2, waiting for transfers between devices: 2.73 us -> 1.12 us  [body(): lax.ppermute(terms(grad_p[:, mid:]).astype(jnp.bfloat16), 'wide', swap)]
    ppermute x1, waiting for transfers between devices: 0.01 us -> 1.43 us  [body(): pass_parts = [rows, lax.ppermute(rows, 'wide', swap)]]
    ppermute x20 -> x16, waiting for transfers between devices: 9.66 us -> 9.48 us  [keep(): other = lax.ppermute(sent, 'wide', swap)]
  transfers between devices with their start and end apart: 51 -> 43, of which waited for: 30 -> 27; matrix products, arithmetic and copies ran while one was open for 14% -> 15% of each run, Pallas kernels for 0% -> 0%
where the time goes in v5:
time: 107 us
  waiting for transfers between devices  41.2 us (39%)
  starting transfers between devices  39.4 us (37%)
  other arithmetic  10.7 us (10%)
  matrix products  6.47 us (6%)
  Pallas kernels  4.33 us (4%)
  between operations  2.74 us (3%)
  local copies, waits for them, and re-layouts  1.93 us (2%)
    ppermute x14, starting transfers between devices, gather_rows(): got = lax.ppermute(sent, 'wide', pairs)  24.5 us
    ppermute x14, waiting for transfers between devices, gather_rows(): got = lax.ppermute(sent, 'wide', pairs)  14.3 us
    ppermute x6, waiting for transfers between devices, body(): got = lax.ppermute(sent[h], 'wide', pairs_of[orders[h][step]])  11 us
    ppermute x16, waiting for transfers between devices, keep(): other = lax.ppermute(sent, 'wide', swap)  9.48 us
    ppermute x6, starting transfers between devices, body(): got = lax.ppermute(sent[h], 'wide', pairs_of[orders[h][step]])  8.1 us
    pallas_call x1, Pallas kernels, tail(): pl.pallas_call(functools.partial(tail_kernel, scale, len(pass_parts)), ou...  4.33 us
    select_n x2, other arithmetic, gather_rows(): full = jnp.where(own_core, banks[i], swapped[i])  3.76 us
    dot_general x1, matrix products, body(): jnp.dot(late_p, pieces, preferred_element_type=jnp.float32)  3.35 us
  transfers between devices with their start and end apart: 43, of which 27 were waited for; matrix products, arithmetic and copies ran while one was open for 15% of the time, Pallas kernels for 0%

profile of v5, /device:TPU:0, one launch (start us, length us, event | category | flops | bytes accessed | tf_op | source)
XLA Modules:
  0.0 106.8 jit_solution(9655629680115106958)
XLA Ops:
  5.3 3.0 %collective-permute-done = bf16[256,4096]{1,0:T(8,128)(2,1)} collective-permute-done((bf16[256,4096]{1,0:T(8,128)(2,1)}, bf16[256,4096]{1,0:T(8,128)(2,1)}, u32[]{:S(2)}, u32[]{:S(2)}) %collective-permute-start) | collective-permute-done | bytes 2097184 | tf_op jit(solution)/shard_map/ppermute | solution.py:68
  9.6 3.0 %collective-permute-start.1 = (bf16[40,4096]{1,0:T(8,128)(2,1)S(1)}, bf16[40,4096]{1,0:T(8,128)(2,1)S(1)}, u32[]{:S(2)}, u32[]{:S(2)}) collective-permute-start(bf16[40,4096]{1,0:T(8,128)(2,1)S(1)} %pad_maximum_fusion), channel_id=1, source_target_pairs={{0,8},{2,6},{8,16},{10,2},{16,24},{18,10},{24,28},{26,18},{28,20},... | collective-permute-start | bytes 983048 | tf_op jit(solution)/shard_map/ppermute | solution.py:102
  15.3 1.9 %broadcast_select_fusion = bf16[256,4096]{1,0:T(8,128)(2,1)S(1)} fusion(bf16[256,4096]{1,0:T(8,128)(2,1)S(1)} %copy-done.3, bf16[256,4096]{1,0:T(8,128)(2,1)} %collective-permute-done.2, pred[]{:T(512)S(6)} %eq.34), kind=kLoop, calls=%fused_computation.5 | loop fusion | flops 1048576 | bytes 6291457 | tf_op jit(solution)/shard_map/jit(_where)/select_n | solution.py:100
  17.3 1.8 %broadcast_select_fusion.1 = bf16[256,4096]{1,0:T(8,128)(2,1)S(1)} fusion(bf16[256,4096]{1,0:T(8,128)(2,1)S(1)} %copy-done.4, bf16[256,4096]{1,0:T(8,128)(2,1)} %collective-permute-done, pred[]{:T(512)S(6)} %eq.34), kind=kLoop, calls=%fused_computation.6 | loop fusion | flops 1048576 | bytes 6291457 | tf_op jit(solution)/shard_map/jit(_where)/select_n | solution.py:100
  19.8 1.6 %collective-permute-start.4 = (bf16[40,4096]{1,0:T(8,128)(2,1)S(1)}, bf16[40,4096]{1,0:T(8,128)(2,1)S(1)}, u32[]{:S(2)}, u32[]{:S(2)}) collective-permute-start(bf16[40,4096]{1,0:T(8,128)(2,1)S(1)} %pad_maximum_fusion.2), channel_id=1, source_target_pairs={{0,8},{2,6},{8,16},{10,2},{16,24},{18,10},{24,28},{26,18},{28,20},... | collective-permute-start | bytes 983048 | tf_op jit(solution)/shard_map/ppermute | solution.py:102
  21.6 1.8 %collective-permute-start.5 = (bf16[40,4096]{1,0:T(8,128)(2,1)S(1)}, bf16[40,4096]{1,0:T(8,128)(2,1)S(1)}, u32[]{:S(2)}, u32[]{:S(2)}) collective-permute-start(bf16[40,4096]{1,0:T(8,128)(2,1)S(1)} %pad_maximum_fusion.3), channel_id=1, source_target_pairs={{0,8},{2,6},{8,16},{10,2},{16,24},{18,10},{24,28},{26,18},{28,20},... | collective-permute-start | bytes 983048 | tf_op jit(solution)/shard_map/ppermute | solution.py:102
  25.1 1.8 %collective-permute-done.4 = bf16[40,4096]{1,0:T(8,128)(2,1)S(1)} collective-permute-done((bf16[40,4096]{1,0:T(8,128)(2,1)S(1)}, bf16[40,4096]{1,0:T(8,128)(2,1)S(1)}, u32[]{:S(2)}, u32[]{:S(2)}) %collective-permute-start.4) | collective-permute-done | bytes 327712 | tf_op jit(solution)/shard_map/ppermute | solution.py:102
  27.0 1.6 %collective-permute-start.6 = (bf16[40,4096]{1,0:T(8,128)(2,1)S(1)}, bf16[40,4096]{1,0:T(8,128)(2,1)S(1)}, u32[]{:S(2)}, u32[]{:S(2)}) collective-permute-start(bf16[40,4096]{1,0:T(8,128)(2,1)S(1)} %pad_maximum_fusion.4), channel_id=1, source_target_pairs={{0,8},{2,6},{8,16},{10,2},{16,24},{18,10},{24,28},{26,18},{28,20},... | collective-permute-start | bytes 983048 | tf_op jit(solution)/shard_map/ppermute | solution.py:102
  28.8 1.6 %collective-permute-done.5 = bf16[40,4096]{1,0:T(8,128)(2,1)S(1)} collective-permute-done((bf16[40,4096]{1,0:T(8,128)(2,1)S(1)}, bf16[40,4096]{1,0:T(8,128)(2,1)S(1)}, u32[]{:S(2)}, u32[]{:S(2)}) %collective-permute-start.5) | collective-permute-done | bytes 327712 | tf_op jit(solution)/shard_map/ppermute | solution.py:102
  30.6 1.6 %collective-permute-start.7 = (bf16[40,4096]{1,0:T(8,128)(2,1)S(1)}, bf16[40,4096]{1,0:T(8,128)(2,1)S(1)}, u32[]{:S(2)}, u32[]{:S(2)}) collective-permute-start(bf16[40,4096]{1,0:T(8,128)(2,1)S(1)} %pad_maximum_fusion.5), channel_id=1, source_target_pairs={{0,8},{2,6},{8,16},{10,2},{16,24},{18,10},{24,28},{26,18},{28,20},... | collective-permute-start | bytes 983048 | tf_op jit(solution)/shard_map/ppermute | solution.py:102
  34.3 1.6 %collective-permute-start.8 = (bf16[40,4096]{1,0:T(8,128)(2,1)S(1)}, bf16[40,4096]{1,0:T(8,128)(2,1)S(1)}, u32[]{:S(2)}, u32[]{:S(2)}) collective-permute-start(bf16[40,4096]{1,0:T(8,128)(2,1)S(1)} %pad_maximum_fusion.6), channel_id=1, source_target_pairs={{0,8},{2,6},{8,16},{10,2},{16,24},{18,10},{24,28},{26,18},{28,20},... | collective-permute-start | bytes 983048 | tf_op jit(solution)/shard_map/ppermute | solution.py:102
  36.1 1.6 %collective-permute-done.7 = bf16[40,4096]{1,0:T(8,128)(2,1)S(1)} collective-permute-done((bf16[40,4096]{1,0:T(8,128)(2,1)S(1)}, bf16[40,4096]{1,0:T(8,128)(2,1)S(1)}, u32[]{:S(2)}, u32[]{:S(2)}) %collective-permute-start.7) | collective-permute-done | bytes 327712 | tf_op jit(solution)/shard_map/ppermute | solution.py:102
  37.8 1.6 %collective-permute-start.9 = (bf16[40,4096]{1,0:T(8,128)(2,1)S(1)}, bf16[40,4096]{1,0:T(8,128)(2,1)S(1)}, u32[]{:S(2)}, u32[]{:S(2)}) collective-permute-start(bf16[40,4096]{1,0:T(8,128)(2,1)S(1)} %pad_maximum_fusion.7), channel_id=1, source_target_pairs={{0,8},{2,6},{8,16},{10,2},{16,24},{18,10},{24,28},{26,18},{28,20},... | collective-permute-start | bytes 983048 | tf_op jit(solution)/shard_map/ppermute | solution.py:102
  41.5 1.6 %collective-permute-start.10 = (bf16[40,4096]{1,0:T(8,128)(2,1)S(1)}, bf16[40,4096]{1,0:T(8,128)(2,1)S(1)}, u32[]{:S(2)}, u32[]{:S(2)}) collective-permute-start(bf16[40,4096]{1,0:T(8,128)(2,1)S(1)} %pad_maximum_fusion.8), channel_id=1, source_target_pairs={{0,8},{2,6},{8,16},{10,2},{16,24},{18,10},{24,28},{26,18},{28,20},... | collective-permute-start | bytes 983048 | tf_op jit(solution)/shard_map/ppermute | solution.py:102
  43.3 1.6 %collective-permute-done.9 = bf16[40,4096]{1,0:T(8,128)(2,1)S(1)} collective-permute-done((bf16[40,4096]{1,0:T(8,128)(2,1)S(1)}, bf16[40,4096]{1,0:T(8,128)(2,1)S(1)}, u32[]{:S(2)}, u32[]{:S(2)}) %collective-permute-start.9) | collective-permute-done | bytes 327712 | tf_op jit(solution)/shard_map/ppermute | solution.py:102
  45.1 1.6 %collective-permute-start.11 = (bf16[40,4096]{1,0:T(8,128)(2,1)S(1)}, bf16[40,4096]{1,0:T(8,128)(2,1)S(1)}, u32[]{:S(2)}, u32[]{:S(2)}) collective-permute-start(bf16[40,4096]{1,0:T(8,128)(2,1)S(1)} %pad_maximum_fusion.9), channel_id=1, source_target_pairs={{0,8},{2,6},{8,16},{10,2},{16,24},{18,10},{24,28},{26,18},{28,20},... | collective-permute-start | bytes 983048 | tf_op jit(solution)/shard_map/ppermute | solution.py:102
  48.8 1.6 %collective-permute-start.12 = (bf16[40,4096]{1,0:T(8,128)(2,1)S(1)}, bf16[40,4096]{1,0:T(8,128)(2,1)S(1)}, u32[]{:S(2)}, u32[]{:S(2)}) collective-permute-start(bf16[40,4096]{1,0:T(8,128)(2,1)S(1)} %pad_maximum_fusion.10), channel_id=1, source_target_pairs={{0,8},{2,6},{8,16},{10,2},{16,24},{18,10},{24,28},{26,18},{28,20},... | collective-permute-start | bytes 983048 | tf_op jit(solution)/shard_map/ppermute | solution.py:102
  50.6 1.6 %collective-permute-done.11 = bf16[40,4096]{1,0:T(8,128)(2,1)S(1)} collective-permute-done((bf16[40,4096]{1,0:T(8,128)(2,1)S(1)}, bf16[40,4096]{1,0:T(8,128)(2,1)S(1)}, u32[]{:S(2)}, u32[]{:S(2)}) %collective-permute-start.11) | collective-permute-done | bytes 327712 | tf_op jit(solution)/shard_map/ppermute | solution.py:102
  52.3 1.6 %collective-permute-start.13 = (bf16[40,4096]{1,0:T(8,128)(2,1)S(1)}, bf16[40,4096]{1,0:T(8,128)(2,1)S(1)}, u32[]{:S(2)}, u32[]{:S(2)}) collective-permute-start(bf16[40,4096]{1,0:T(8,128)(2,1)S(1)} %pad_maximum_fusion.11), channel_id=1, source_target_pairs={{0,8},{2,6},{8,16},{10,2},{16,24},{18,10},{24,28},{26,18},{28,20},... | collective-permute-start | bytes 983048 | tf_op jit(solution)/shard_map/ppermute | solution.py:102
  56.0 1.6 %collective-permute-start.14 = (bf16[40,4096]{1,0:T(8,128)(2,1)S(1)}, bf16[40,4096]{1,0:T(8,128)(2,1)S(1)}, u32[]{:S(2)}, u32[]{:S(2)}) collective-permute-start(bf16[40,4096]{1,0:T(8,128)(2,1)S(1)} %pad_maximum_fusion.12), channel_id=1, source_target_pairs={{0,8},{2,6},{8,16},{10,2},{16,24},{18,10},{24,28},{26,18},{28,20},... | collective-permute-start | bytes 983048 | tf_op jit(solution)/shard_map/ppermute | solution.py:102
  57.8 1.6 %collective-permute-done.13 = bf16[40,4096]{1,0:T(8,128)(2,1)S(1)} collective-permute-done((bf16[40,4096]{1,0:T(8,128)(2,1)S(1)}, bf16[40,4096]{1,0:T(8,128)(2,1)S(1)}, u32[]{:S(2)}, u32[]{:S(2)}) %collective-permute-start.13) | collective-permute-done | bytes 327712 | tf_op jit(solution)/shard_map/ppermute | solution.py:102
  59.6 1.8 %collective-permute-start.15 = (bf16[40,4096]{1,0:T(8,128)(2,1)S(1)}, bf16[40,4096]{1,0:T(8,128)(2,1)S(1)}, u32[]{:S(2)}, u32[]{:S(2)}) collective-permute-start(bf16[40,4096]{1,0:T(8,128)(2,1)S(1)} %pad_maximum_fusion.13), channel_id=1, source_target_pairs={{0,8},{2,6},{8,16},{10,2},{16,24},{18,10},{24,28},{26,18},{28,20},... | collective-permute-start | bytes 983048 | tf_op jit(solution)/shard_map/ppermute | solution.py:102
  63.5 3.4 %collective-permute-done.15 = bf16[40,4096]{1,0:T(8,128)(2,1)S(1)} collective-permute-done((bf16[40,4096]{1,0:T(8,128)(2,1)S(1)}, bf16[40,4096]{1,0:T(8,128)(2,1)S(1)}, u32[]{:S(2)}, u32[]{:S(2)}) %collective-permute-start.15) | collective-permute-done | bytes 327712 | tf_op jit(solution)/shard_map/ppermute | solution.py:102
  70.1 4.3 %scores.1 = (bf16[512,256]{1,0:T(8,128)(2,1)S(1)}, bf16[512,256]{1,0:T(8,128)(2,1)S(1)}, f32[512,1]{1,0:T(8,128)S(1)}, bf16[256,4096]{1,0:T(8,128)(2,1)S(1)}) custom-call(bf16[128,4096]{1,0:T(8,128)(2,1)S(1)} %slice_dynamic-update-slice_fusion.refs_0_, bf16[128,4096]{1,0:T(8,128)(2,1)S(1)} %collective-permute-done.16.refs_1_, bf16[512,4096]{1,0:T(8,128)(2,1)S(1)} %copy-done, ...), custom_call_target="tpu_custom_call" | custom-call | flops 3221225472 | bytes 20971520 | tf_op jit(solution)/shard_map/scores/pallas_call | solution.py:158
  79.1 1.6 %collective-permute-start.39 = (bf16[2,2,16,2048]{3,2,0,1:T(8,128)(2,1)S(1)}, bf16[2,2,16,2048]{3,2,0,1:T(8,128)(2,1)S(1)}, u32[]{:S(2)}, u32[]{:S(2)}) collective-permute-start(bf16[2,2,16,2048]{3,2,0,1:T(8,128)(2,1)S(1)} %fusion.6), channel_id=1, source_target_pairs={{0,8},{2,10},{4,12},{6,14},{8,0},{10,2},{12,4},{14,6},{16,24},{18,... | collective-permute-start | bytes 786440 | tf_op jit(solution)/shard_map/ppermute | solution.py:232
  81.9 4.8 %collective-permute-done.35 = bf16[2,2,16,2048]{3,2,0,1:T(8,128)(2,1)S(1)} collective-permute-done((bf16[2,2,16,2048]{3,2,0,1:T(8,128)(2,1)S(1)}, bf16[2,2,16,2048]{3,2,0,1:T(8,128)(2,1)S(1)}, u32[]{:S(2)}, u32[]{:S(2)}) %collective-permute-start.35) | collective-permute-done | bytes 262176 | tf_op jit(solution)/shard_map/ppermute | solution.py:232
  86.8 1.6 %collective-permute-start.36 = (bf16[2,16,2048]{2,1,0:T(8,128)(2,1)S(1)}, bf16[2,16,2048]{2,1,0:T(8,128)(2,1)S(1)}, u32[]{:S(2)}, u32[]{:S(2)}) collective-permute-start(bf16[2,16,2048]{2,1,0:T(8,128)(2,1)S(1)} %fusion.10), channel_id=1, source_target_pairs={{0,8},{2,10},{4,12},{6,14},{8,0},{10,2},{12,4},{14,6},{16,24},{18,... | collective-permute-start | bytes 393224 | tf_op jit(solution)/shard_map/ppermute | solution.py:232
  89.4 2.4 %collective-permute-done.36 = bf16[2,16,2048]{2,1,0:T(8,128)(2,1)S(1)} collective-permute-done((bf16[2,16,2048]{2,1,0:T(8,128)(2,1)S(1)}, bf16[2,16,2048]{2,1,0:T(8,128)(2,1)S(1)}, u32[]{:S(2)}, u32[]{:S(2)}) %collective-permute-start.36) | collective-permute-done | bytes 131104 | tf_op jit(solution)/shard_map/ppermute | solution.py:232
  91.9 2.6 %collective-permute-start.37 = (bf16[16,2048]{1,0:T(8,128)(2,1)S(1)}, bf16[16,2048]{1,0:T(8,128)(2,1)S(1)}, u32[]{:S(2)}, u32[]{:S(2)}) collective-permute-start(bf16[16,2048]{1,0:T(8,128)(2,1)S(1)} %fusion.18), channel_id=1, source_target_pairs={{0,16},{2,18},{4,20},{6,22},{8,24},{10,26},{12,28},{14,30},{16,0},... | collective-permute-start | bytes 196616 | tf_op jit(solution)/shard_map/ppermute | solution.py:232
  95.1 3.7 %collective-permute-done.37 = bf16[16,2048]{1,0:T(8,128)(2,1)S(1)} collective-permute-done((bf16[16,2048]{1,0:T(8,128)(2,1)S(1)}, bf16[16,2048]{1,0:T(8,128)(2,1)S(1)}, u32[]{:S(2)}, u32[]{:S(2)}) %collective-permute-start.37) | collective-permute-done | bytes 65568 | tf_op jit(solution)/shard_map/ppermute | solution.py:232
  98.8 1.6 %collective-permute-start.38 = (f32[16,2048]{1,0:T(8,128)S(1)}, f32[16,2048]{1,0:T(8,128)S(1)}, u32[]{:S(2)}, u32[]{:S(2)}) collective-permute-start(f32[16,2048]{1,0:T(8,128)S(1)} %fusion.13), channel_id=1, source_target_pairs={{0,1},{1,0},{2,3},{3,2},{4,5},{5,4},{6,7},{7,6},{8,9},{9,8},{10,11... | collective-permute-start | bytes 393224 | tf_op jit(solution)/shard_map/ppermute | solution.py:242
  101.9 3.4 %multiply_convert_fusion = bf16[512,4096]{1,0:T(8,128)(2,1)} fusion(f32[512,4096]{1,0:T(8,128)S(1)} %fusion.55, bf16[512,256]{1,0:T(8,128)(2,1)S(1)} %get-tuple-element.53, bf16[256,4096]{1,0:T(8,128)(2,1)S(1)} %get-tuple-element.54), kind=kOutput, calls=%fused_computation | convolution fusion | flops 1080033280 | bytes 14942208 | tf_op jit(solution)/shard_map/dot_general | solution.py:247
  (169 shorter events, 35.1 us)
Async XLA Ops:
  0.7 4.6 %collective-permute-start.2 = (bf16[256,4096]{1,0:T(8,128)(2,1)}, bf16[256,4096]{1,0:T(8,128)(2,1)}, u32[]{:S(2)}, u32[]{:S(2)}) collective-permute-start(bf16[256,4096]{1,0:T(8,128)(2,1)} %param.11), channel_id=1, source_target_pairs={{0,2},{2,0},{4,6},{6,4},{8,10},{10,8},{12,14},{14,12},{16,18},{18,... | collective-permute-start | bytes 6291464 | tf_op jit(solution)/shard_map/ppermute | solution.py:69
  1.2 7.1 %collective-permute-start = (bf16[256,4096]{1,0:T(8,128)(2,1)}, bf16[256,4096]{1,0:T(8,128)(2,1)}, u32[]{:S(2)}, u32[]{:S(2)}) collective-permute-start(bf16[256,4096]{1,0:T(8,128)(2,1)} %param.12), channel_id=1, source_target_pairs={{0,2},{2,0},{4,6},{6,4},{8,10},{10,8},{12,14},{14,12},{16,18},{18,... | collective-permute-start | bytes 6291464 | tf_op jit(solution)/shard_map/ppermute | solution.py:68
  9.6 9.7 %collective-permute-start.1 = (bf16[40,4096]{1,0:T(8,128)(2,1)S(1)}, bf16[40,4096]{1,0:T(8,128)(2,1)S(1)}, u32[]{:S(2)}, u32[]{:S(2)}) collective-permute-start(bf16[40,4096]{1,0:T(8,128)(2,1)S(1)} %pad_maximum_fusion), channel_id=1, source_target_pairs={{0,8},{2,6},{8,16},{10,2},{16,24},{18,10},{24,28},{26,18},{28,20},... | collective-permute-start | bytes 983048 | tf_op jit(solution)/shard_map/ppermute | solution.py:102
  12.6 8.8 %collective-permute-start.3 = (bf16[40,4096]{1,0:T(8,128)(2,1)S(1)}, bf16[40,4096]{1,0:T(8,128)(2,1)S(1)}, u32[]{:S(2)}, u32[]{:S(2)}) collective-permute-start(bf16[40,4096]{1,0:T(8,128)(2,1)S(1)} %pad_maximum_fusion.1), channel_id=1, source_target_pairs={{0,8},{2,6},{8,16},{10,2},{16,24},{18,10},{24,28},{26,18},{28,20},... | collective-permute-start | bytes 983048 | tf_op jit(solution)/shard_map/ppermute | solution.py:102
  14.8 4.4 %collective-permute-start.17 = (bf16[32,4096]{1,0:T(8,128)(2,1)S(1)}, bf16[32,4096]{1,0:T(8,128)(2,1)S(1)}, u32[]{:S(2)}, u32[]{:S(2)}) collective-permute-start(bf16[32,4096]{1,0:T(8,128)(2,1)S(1)} %get-tuple-element.87), channel_id=1, source_target_pairs={{0,2},{2,0},{4,6},{6,4},{8,10},{10,8},{12,14},{14,12},{16,18},{18,... | collective-permute-start | bytes 786440 | tf_op jit(solution)/shard_map/ppermute | solution.py:85
  14.9 4.4 %collective-permute-start.25 = (bf16[32,4096]{1,0:T(8,128)(2,1)S(1)}, bf16[32,4096]{1,0:T(8,128)(2,1)S(1)}, u32[]{:S(2)}, u32[]{:S(2)}) collective-permute-start(bf16[32,4096]{1,0:T(8,128)(2,1)S(1)} %get-tuple-element.111), channel_id=1, source_target_pairs={{0,2},{2,0},{4,6},{6,4},{8,10},{10,8},{12,14},{14,12},{16,18},{18,... | collective-permute-start | bytes 786440 | tf_op jit(solution)/shard_map/ppermute | solution.py:85
  19.4 4.1 %collective-permute-start.26 = (bf16[32,4096]{1,0:T(8,128)(2,1)S(1)}, bf16[32,4096]{1,0:T(8,128)(2,1)S(1)}, u32[]{:S(2)}, u32[]{:S(2)}) collective-permute-start(bf16[32,4096]{1,0:T(8,128)(2,1)S(1)} %get-tuple-element.62), channel_id=1, source_target_pairs={{0,2},{2,0},{4,6},{6,4},{8,10},{10,8},{12,14},{14,12},{16,18},{18,... | collective-permute-start | bytes 786440 | tf_op jit(solution)/shard_map/ppermute | solution.py:85
  19.8 7.1 %collective-permute-start.4 = (bf16[40,4096]{1,0:T(8,128)(2,1)S(1)}, bf16[40,4096]{1,0:T(8,128)(2,1)S(1)}, u32[]{:S(2)}, u32[]{:S(2)}) collective-permute-start(bf16[40,4096]{1,0:T(8,128)(2,1)S(1)} %pad_maximum_fusion.2), channel_id=1, source_target_pairs={{0,8},{2,6},{8,16},{10,2},{16,24},{18,10},{24,28},{26,18},{28,20},... | collective-permute-start | bytes 983048 | tf_op jit(solution)/shard_map/ppermute | solution.py:102
  21.6 8.9 %collective-permute-start.5 = (bf16[40,4096]{1,0:T(8,128)(2,1)S(1)}, bf16[40,4096]{1,0:T(8,128)(2,1)S(1)}, u32[]{:S(2)}, u32[]{:S(2)}) collective-permute-start(bf16[40,4096]{1,0:T(8,128)(2,1)S(1)} %pad_maximum_fusion.3), channel_id=1, source_target_pairs={{0,8},{2,6},{8,16},{10,2},{16,24},{18,10},{24,28},{26,18},{28,20},... | collective-permute-start | bytes 983048 | tf_op jit(solution)/shard_map/ppermute | solution.py:102
  27.0 7.1 %collective-permute-start.6 = (bf16[40,4096]{1,0:T(8,128)(2,1)S(1)}, bf16[40,4096]{1,0:T(8,128)(2,1)S(1)}, u32[]{:S(2)}, u32[]{:S(2)}) collective-permute-start(bf16[40,4096]{1,0:T(8,128)(2,1)S(1)} %pad_maximum_fusion.4), channel_id=1, source_target_pairs={{0,8},{2,6},{8,16},{10,2},{16,24},{18,10},{24,28},{26,18},{28,20},... | collective-permute-start | bytes 983048 | tf_op jit(solution)/shard_map/ppermute | solution.py:102
  28.8 3.6 %collective-permute-start.27 = (bf16[32,4096]{1,0:T(8,128)(2,1)S(1)}, bf16[32,4096]{1,0:T(8,128)(2,1)S(1)}, u32[]{:S(2)}, u32[]{:S(2)}) collective-permute-start(bf16[32,4096]{1,0:T(8,128)(2,1)S(1)} %get-tuple-element.73), channel_id=1, source_target_pairs={{0,2},{2,0},{4,6},{6,4},{8,10},{10,8},{12,14},{14,12},{16,18},{18,... | collective-permute-start | bytes 786440 | tf_op jit(solution)/shard_map/ppermute | solution.py:85
  30.6 7.1 %collective-permute-start.7 = (bf16[40,4096]{1,0:T(8,128)(2,1)S(1)}, bf16[40,4096]{1,0:T(8,128)(2,1)S(1)}, u32[]{:S(2)}, u32[]{:S(2)}) collective-permute-start(bf16[40,4096]{1,0:T(8,128)(2,1)S(1)} %pad_maximum_fusion.5), channel_id=1, source_target_pairs={{0,8},{2,6},{8,16},{10,2},{16,24},{18,10},{24,28},{26,18},{28,20},... | collective-permute-start | bytes 983048 | tf_op jit(solution)/shard_map/ppermute | solution.py:102
  34.3 7.1 %collective-permute-start.8 = (bf16[40,4096]{1,0:T(8,128)(2,1)S(1)}, bf16[40,4096]{1,0:T(8,128)(2,1)S(1)}, u32[]{:S(2)}, u32[]{:S(2)}) collective-permute-start(bf16[40,4096]{1,0:T(8,128)(2,1)S(1)} %pad_maximum_fusion.6), channel_id=1, source_target_pairs={{0,8},{2,6},{8,16},{10,2},{16,24},{18,10},{24,28},{26,18},{28,20},... | collective-permute-start | bytes 983048 | tf_op jit(solution)/shard_map/ppermute | solution.py:102
  37.8 7.1 %collective-permute-start.9 = (bf16[40,4096]{1,0:T(8,128)(2,1)S(1)}, bf16[40,4096]{1,0:T(8,128)(2,1)S(1)}, u32[]{:S(2)}, u32[]{:S(2)}) collective-permute-start(bf16[40,4096]{1,0:T(8,128)(2,1)S(1)} %pad_maximum_fusion.7), channel_id=1, source_target_pairs={{0,8},{2,6},{8,16},{10,2},{16,24},{18,10},{24,28},{26,18},{28,20},... | collective-permute-start | bytes 983048 | tf_op jit(solution)/shard_map/ppermute | solution.py:102
  41.5 7.1 %collective-permute-start.10 = (bf16[40,4096]{1,0:T(8,128)(2,1)S(1)}, bf16[40,4096]{1,0:T(8,128)(2,1)S(1)}, u32[]{:S(2)}, u32[]{:S(2)}) collective-permute-start(bf16[40,4096]{1,0:T(8,128)(2,1)S(1)} %pad_maximum_fusion.8), channel_id=1, source_target_pairs={{0,8},{2,6},{8,16},{10,2},{16,24},{18,10},{24,28},{26,18},{28,20},... | collective-permute-start | bytes 983048 | tf_op jit(solution)/shard_map/ppermute | solution.py:102
  43.3 3.6 %collective-permute-start.29 = (bf16[32,4096]{1,0:T(8,128)(2,1)S(1)}, bf16[32,4096]{1,0:T(8,128)(2,1)S(1)}, u32[]{:S(2)}, u32[]{:S(2)}) collective-permute-start(bf16[32,4096]{1,0:T(8,128)(2,1)S(1)} %get-tuple-element.69), channel_id=1, source_target_pairs={{0,2},{2,0},{4,6},{6,4},{8,10},{10,8},{12,14},{14,12},{16,18},{18,... | collective-permute-start | bytes 786440 | tf_op jit(solution)/shard_map/ppermute | solution.py:85
  45.1 7.1 %collective-permute-start.11 = (bf16[40,4096]{1,0:T(8,128)(2,1)S(1)}, bf16[40,4096]{1,0:T(8,128)(2,1)S(1)}, u32[]{:S(2)}, u32[]{:S(2)}) collective-permute-start(bf16[40,4096]{1,0:T(8,128)(2,1)S(1)} %pad_maximum_fusion.9), channel_id=1, source_target_pairs={{0,8},{2,6},{8,16},{10,2},{16,24},{18,10},{24,28},{26,18},{28,20},... | collective-permute-start | bytes 983048 | tf_op jit(solution)/shard_map/ppermute | solution.py:102
  48.8 7.1 %collective-permute-start.12 = (bf16[40,4096]{1,0:T(8,128)(2,1)S(1)}, bf16[40,4096]{1,0:T(8,128)(2,1)S(1)}, u32[]{:S(2)}, u32[]{:S(2)}) collective-permute-start(bf16[40,4096]{1,0:T(8,128)(2,1)S(1)} %pad_maximum_fusion.10), channel_id=1, source_target_pairs={{0,8},{2,6},{8,16},{10,2},{16,24},{18,10},{24,28},{26,18},{28,20},... | collective-permute-start | bytes 983048 | tf_op jit(solution)/shard_map/ppermute | solution.py:102
  50.5 3.6 %collective-permute-start.30 = (bf16[32,4096]{1,0:T(8,128)(2,1)S(1)}, bf16[32,4096]{1,0:T(8,128)(2,1)S(1)}, u32[]{:S(2)}, u32[]{:S(2)}) collective-permute-start(bf16[32,4096]{1,0:T(8,128)(2,1)S(1)} %get-tuple-element.67), channel_id=1, source_target_pairs={{0,2},{2,0},{4,6},{6,4},{8,10},{10,8},{12,14},{14,12},{16,18},{18,... | collective-permute-start | bytes 786440 | tf_op jit(solution)/shard_map/ppermute | solution.py:85
  52.3 7.1 %collective-permute-start.13 = (bf16[40,4096]{1,0:T(8,128)(2,1)S(1)}, bf16[40,4096]{1,0:T(8,128)(2,1)S(1)}, u32[]{:S(2)}, u32[]{:S(2)}) collective-permute-start(bf16[40,4096]{1,0:T(8,128)(2,1)S(1)} %pad_maximum_fusion.11), channel_id=1, source_target_pairs={{0,8},{2,6},{8,16},{10,2},{16,24},{18,10},{24,28},{26,18},{28,20},... | collective-permute-start | bytes 983048 | tf_op jit(solution)/shard_map/ppermute | solution.py:102
  56.0 7.1 %collective-permute-start.14 = (bf16[40,4096]{1,0:T(8,128)(2,1)S(1)}, bf16[40,4096]{1,0:T(8,128)(2,1)S(1)}, u32[]{:S(2)}, u32[]{:S(2)}) collective-permute-start(bf16[40,4096]{1,0:T(8,128)(2,1)S(1)} %pad_maximum_fusion.12), channel_id=1, source_target_pairs={{0,8},{2,6},{8,16},{10,2},{16,24},{18,10},{24,28},{26,18},{28,20},... | collective-permute-start | bytes 983048 | tf_op jit(solution)/shard_map/ppermute | solution.py:102
  57.7 3.8 %collective-permute-start.31 = (bf16[32,4096]{1,0:T(8,128)(2,1)S(1)}, bf16[32,4096]{1,0:T(8,128)(2,1)S(1)}, u32[]{:S(2)}, u32[]{:S(2)}) collective-permute-start(bf16[32,4096]{1,0:T(8,128)(2,1)S(1)} %get-tuple-element.65), channel_id=1, source_target_pairs={{0,2},{2,0},{4,6},{6,4},{8,10},{10,8},{12,14},{14,12},{16,18},{18,... | collective-permute-start | bytes 786440 | tf_op jit(solution)/shard_map/ppermute | solution.py:85
  59.6 7.3 %collective-permute-start.15 = (bf16[40,4096]{1,0:T(8,128)(2,1)S(1)}, bf16[40,4096]{1,0:T(8,128)(2,1)S(1)}, u32[]{:S(2)}, u32[]{:S(2)}) collective-permute-start(bf16[40,4096]{1,0:T(8,128)(2,1)S(1)} %pad_maximum_fusion.13), channel_id=1, source_target_pairs={{0,8},{2,6},{8,16},{10,2},{16,24},{18,10},{24,28},{26,18},{28,20},... | collective-permute-start | bytes 983048 | tf_op jit(solution)/shard_map/ppermute | solution.py:102
  63.3 4.4 %collective-permute-start.32 = (bf16[32,4096]{1,0:T(8,128)(2,1)S(1)}, bf16[32,4096]{1,0:T(8,128)(2,1)S(1)}, u32[]{:S(2)}, u32[]{:S(2)}) collective-permute-start(bf16[32,4096]{1,0:T(8,128)(2,1)S(1)} %get-tuple-element.60), channel_id=1, source_target_pairs={{0,2},{2,0},{4,6},{6,4},{8,10},{10,8},{12,14},{14,12},{16,18},{18,... | collective-permute-start | bytes 786440 | tf_op jit(solution)/shard_map/ppermute | solution.py:85
  78.2 8.6 %collective-permute-start.35 = (bf16[2,2,16,2048]{3,2,0,1:T(8,128)(2,1)S(1)}, bf16[2,2,16,2048]{3,2,0,1:T(8,128)(2,1)S(1)}, u32[]{:S(2)}, u32[]{:S(2)}) collective-permute-start(bf16[2,2,16,2048]{3,2,0,1:T(8,128)(2,1)S(1)} %fusion.7), channel_id=1, source_target_pairs={{0,4},{2,6},{4,0},{6,2},{8,12},{10,14},{12,8},{14,10},{16,20},{18,... | collective-permute-start | bytes 786440 | tf_op jit(solution)/shard_map/ppermute | solution.py:232
  79.1 9.4 %collective-permute-start.39 = (bf16[2,2,16,2048]{3,2,0,1:T(8,128)(2,1)S(1)}, bf16[2,2,16,2048]{3,2,0,1:T(8,128)(2,1)S(1)}, u32[]{:S(2)}, u32[]{:S(2)}) collective-permute-start(bf16[2,2,16,2048]{3,2,0,1:T(8,128)(2,1)S(1)} %fusion.6), channel_id=1, source_target_pairs={{0,8},{2,10},{4,12},{6,14},{8,0},{10,2},{12,4},{14,6},{16,24},{18,... | collective-permute-start | bytes 786440 | tf_op jit(solution)/shard_map/ppermute | solution.py:232
  86.8 5.0 %collective-permute-start.36 = (bf16[2,16,2048]{2,1,0:T(8,128)(2,1)S(1)}, bf16[2,16,2048]{2,1,0:T(8,128)(2,1)S(1)}, u32[]{:S(2)}, u32[]{:S(2)}) collective-permute-start(bf16[2,16,2048]{2,1,0:T(8,128)(2,1)S(1)} %fusion.10), channel_id=1, source_target_pairs={{0,8},{2,10},{4,12},{6,14},{8,0},{10,2},{12,4},{14,6},{16,24},{18,... | collective-permute-start | bytes 393224 | tf_op jit(solution)/shard_map/ppermute | solution.py:232
  88.5 5.9 %collective-permute-start.40 = (bf16[2,16,2048]{2,1,0:T(8,128)(2,1)S(1)}, bf16[2,16,2048]{2,1,0:T(8,128)(2,1)S(1)}, u32[]{:S(2)}, u32[]{:S(2)}) collective-permute-start(bf16[2,16,2048]{2,1,0:T(8,128)(2,1)S(1)} %fusion.11), channel_id=1, source_target_pairs={{0,4},{2,6},{4,0},{6,2},{8,12},{10,14},{12,8},{14,10},{16,20},{18,... | collective-permute-start | bytes 393224 | tf_op jit(solution)/shard_map/ppermute | solution.py:232
  91.9 6.9 %collective-permute-start.37 = (bf16[16,2048]{1,0:T(8,128)(2,1)S(1)}, bf16[16,2048]{1,0:T(8,128)(2,1)S(1)}, u32[]{:S(2)}, u32[]{:S(2)}) collective-permute-start(bf16[16,2048]{1,0:T(8,128)(2,1)S(1)} %fusion.18), channel_id=1, source_target_pairs={{0,16},{2,18},{4,20},{6,22},{8,24},{10,26},{12,28},{14,30},{16,0},... | collective-permute-start | bytes 196616 | tf_op jit(solution)/shard_map/ppermute | solution.py:232
  94.5 5.9 %collective-permute-start.41 = (bf16[16,2048]{1,0:T(8,128)(2,1)S(1)}, bf16[16,2048]{1,0:T(8,128)(2,1)S(1)}, u32[]{:S(2)}, u32[]{:S(2)}) collective-permute-start(bf16[16,2048]{1,0:T(8,128)(2,1)S(1)} %fusion.19), channel_id=1, source_target_pairs={{0,16},{2,18},{4,20},{6,22},{8,24},{10,26},{12,28},{14,30},{16,0},... | collective-permute-start | bytes 196616 | tf_op jit(solution)/shard_map/ppermute | solution.py:232
  98.8 7.2 %collective-permute-start.38 = (f32[16,2048]{1,0:T(8,128)S(1)}, f32[16,2048]{1,0:T(8,128)S(1)}, u32[]{:S(2)}, u32[]{:S(2)}) collective-permute-start(f32[16,2048]{1,0:T(8,128)S(1)} %fusion.13), channel_id=1, source_target_pairs={{0,1},{1,0},{2,3},{3,2},{4,5},{5,4},{6,7},{7,6},{8,9},{9,8},{10,11... | collective-permute-start | bytes 393224 | tf_op jit(solution)/shard_map/ppermute | solution.py:242
  100.4 5.6 %collective-permute-start.42 = (f32[16,2048]{1,0:T(8,128)S(1)}, f32[16,2048]{1,0:T(8,128)S(1)}, u32[]{:S(2)}, u32[]{:S(2)}) collective-permute-start(f32[16,2048]{1,0:T(8,128)S(1)} %fusion.12), channel_id=1, source_target_pairs={{0,1},{1,0},{2,3},{3,2},{4,5},{5,4},{6,7},{7,6},{8,9},{9,8},{10,11... | collective-permute-start | bytes 393224 | tf_op jit(solution)/shard_map/ppermute | solution.py:242
  (17 other events, 65.7 us)

commit v6 on v5

--- a/solution.py
+++ b/solution.py
@@ -36,6 +36,27 @@
 
 def put_rows(x, rows, tile):
     return lax.dynamic_update_slice_in_dim(x, rows, tile * 8, 0)
+
+
+def first_kernel(side_ref, bank_s, bank_t, *refs):
+    outs = refs
+    pool = bank_s.shape[0]
+    for n, out in enumerate(outs):
+        side = side_ref[0] if n < 2 else 1 - side_ref[0]
+        at = pl.multiple_of(side * (pool - 2 * STEP), STEP)
+        out[...] = (bank_s, bank_t)[n % 2][pl.ds(at, 2 * STEP), :]
+
+
+def first_chunks(bank_s, bank_t, core):
+    chunk = jax.ShapeDtypeStruct((2 * STEP, bank_s.shape[1]), bank_s.dtype)
+    return pl.pallas_call(
+        first_kernel,
+        out_shape=[chunk] * 4,
+        in_specs=[pl.BlockSpec(memory_space=pltpu.SMEM)] + [pl.BlockSpec(memory_space=pltpu.VMEM)] * 2,
+        out_specs=[pl.BlockSpec(memory_space=pltpu.VMEM)] * 4,
+        compiler_params=pltpu.CompilerParams(vmem_limit_bytes=VMEM_LIMIT),
+        name="first_chunks",
+    )(core.astype(jnp.int32)[None], bank_s, bank_t)
 
 
 def gather_rows(bank_s, bank_t, passages, owner, index, core):
@@ -65,21 +86,26 @@
     pairs = ring_pairs(n_chip)
 
     banks = [bank_s, bank_t]
-    swapped = [None, lax.ppermute(bank_t, "wide", swap)]
-    swapped[0] = lax.ppermute(bank_s, "wide", swap)
 
     def tile_of(side, slot):
         return jnp.where(side == 0, slot, n_chunk - 1 - slot) * (STEP // 8)
 
+    chunks = first_chunks(bank_s, bank_t, core)
+
+    first = [None, None]
+    for i in (1, 0):
+        first[i] = jnp.where(own_core, chunks[i], lax.ppermute(chunks[2 + i], "wide", swap))
+
     def own_rows(i, j):
-        at = tile_of(core, j)
-        return jnp.where(own_core, rows_at(banks[i], at, STEP), rows_at(swapped[i], at, STEP))
-
+        if j < 2:
+            return rows_at(first[i], jnp.where(core == 0, j, 1 - j) * (STEP // 8), STEP)
+        return rows_at(full[i], tile_of(core, j), STEP)
+
+    full = [None, None]
     pools = [jnp.zeros_like(bank_s), jnp.zeros_like(bank_t)]
     rows = put_rows(jnp.zeros((n_chip * block, width), passages.dtype), passages, 0)
     moving = [own_rows(i, 0) for i in range(2)]
     riding = [passages[:sub], passages[sub:]]
-    arrived = [[], []]
 
     def keep(i, t, sent):
         other = lax.ppermute(sent, "wide", swap)
@@ -89,27 +115,32 @@
             at = tile_of(side, jnp.clip(slot, 0, n_chunk - 1))
             pools[i] = put_rows(pools[i], jnp.where(take, piece, rows_at(pools[i], at, STEP)), at)
 
+    def arrive(i, t, got):
+        nonlocal rows
+        if t < n_chip - 1:
+            riding[i] = got[STEP:]
+            got = got[:STEP]
+            origin = chip_at((here - turn * (t + 1) + n_chip) % n_chip)
+            rows = put_rows(rows, riding[i], (origin ^ chip) * (block // 8) + i * (sub // 8))
+        moving[i] = jnp.where(own_chip, own_rows(i, t + 1), got) if t + 1 < n_chunk else got
+
+    lead, came = None, [None, None]
     for t in range(rounds):
         for i in (1, 0):
+            if t:
+                got, _ = lax.optimization_barrier((came[i], lead))
+                arrive(i, t - 1, got)
             sent = jnp.concatenate([moving[i], riding[i]], 0) if t < n_chip - 1 else moving[i]
-            before = t - 1 - i
-            if before >= 0:
-                sent, arrived[1 - i][before] = lax.optimization_barrier((sent, arrived[1 - i][before]))
             if t == 0:
-                (banks[i], swapped[i]), sent = lax.optimization_barrier(((banks[i], swapped[i]), sent))
-                full = jnp.where(own_core, banks[i], swapped[i])
-                banks[i], swapped[i] = full, full
-            got = lax.ppermute(sent, "wide", pairs)
-            arrived[i].append(got)
+                bank, sent = lax.optimization_barrier((banks[i], sent))
+                full[i] = jnp.where(own_core, bank, lax.ppermute(bank, "wide", swap))
+                if i == 0:
+                    sent, _ = lax.optimization_barrier((sent, lead))
+            lead = sent
+            came[i] = lax.ppermute(sent, "wide", pairs)
             keep(i, t, sent[:STEP])
-            if t < n_chip - 1:
-                riding[i] = got[STEP:]
-                got = got[:STEP]
-                origin = chip_at((here - turn * (t + 1) + n_chip) % n_chip)
-                rows = put_rows(rows, riding[i], (origin ^ chip) * (block // 8) + i * (sub // 8))
-            moving[i] = got
-            if t + 1 < n_chunk:
-                moving[i] = jnp.where(own_chip, own_rows(i, t + 1), got)
+    for i in (1, 0):
+        arrive(i, rounds - 1, came[i])
     for i in (1, 0):
         keep(i, rounds, moving[i])
     return pools[0], pools[1], rows

time: 107 us -> 105 us (0.981)
  other arithmetic: 10.7 us -> 5.39 us
  starting transfers between devices: 39.4 us -> 42.8 us
  local copies, waits for them, and re-layouts: 1.93 us -> 4.26 us
  waiting for transfers between devices: 41.2 us -> 39 us
    ppermute x16 -> x18, waiting for transfers between devices: 18.2 us -> 23.8 us  [the longest x14 23.2 us: gather_rows(): came[i] = lax.ppermute(sent, 'wide', pairs)]
    ppermute x16, waiting for transfers between devices: 9.48 us -> 3.83 us  [keep(): other = lax.ppermute(sent, 'wide', swap)]
    select_n x14 -> x4, other arithmetic: 5.71 us -> 0.55 us  [the longest x2 0.44 us: gather_rows(): full[i] = jnp.where(own_core, bank, lax.ppermute(bank, 'wide', swap))]
    unnamed x12 -> x18, local copies, waits for them, and re-layouts: 0.03 us -> 3.21 us
    ppermute x6, starting transfers between devices: 8.1 us -> 10.9 us  [body(): got = lax.ppermute(sent[h], 'wide', pairs_of[orders[h][step]])]
    ppermute x6, waiting for transfers between devices: 11 us -> 8.39 us  [body(): got = lax.ppermute(sent[h], 'wide', pairs_of[orders[h][step]])]
    ppermute x16 -> x18, starting transfers between devices: 25.1 us -> 27.2 us  [the longest x14 26 us: gather_rows(): came[i] = lax.ppermute(sent, 'wide', pairs)]
    dynamic_update_slice x19 -> x30, other arithmetic: 1.47 us -> 2.73 us  [put_rows(): return lax.dynamic_update_slice_in_dim(x, rows, tile * 8, 0)]
  transfers between devices with their start and end apart: 43 -> 45, of which waited for: 27 -> 24; matrix products, arithmetic and copies ran while one was open for 15% -> 10% of each run, Pallas kernels for 0% -> 0%
where the time goes in v6:
time: 105 us
  starting transfers between devices  42.8 us (41%)
  waiting for transfers between devices  39 us (37%)
  matrix products  6.43 us (6%)
  other arithmetic  5.39 us (5%)
  Pallas kernels  4.46 us (4%)
  local copies, waits for them, and re-layouts  4.26 us (4%)
  between operations  2.77 us (3%)
    ppermute x14, starting transfers between devices, gather_rows(): came[i] = lax.ppermute(sent, 'wide', pairs)  26 us
    ppermute x14, waiting for transfers between devices, gather_rows(): came[i] = lax.ppermute(sent, 'wide', pairs)  23.2 us
    ppermute x6, starting transfers between devices, body(): got = lax.ppermute(sent[h], 'wide', pairs_of[orders[h][step]])  10.9 us
    ppermute x6, waiting for transfers between devices, body(): got = lax.ppermute(sent[h], 'wide', pairs_of[orders[h][step]])  8.39 us
    pallas_call x1, Pallas kernels, tail(): pl.pallas_call(functools.partial(tail_kernel, scale, len(pass_parts)), ou...  4.33 us
    ppermute x16, waiting for transfers between devices, keep(): other = lax.ppermute(sent, 'wide', swap)  3.83 us
    dot_general x1, matrix products, body(): jnp.dot(late_p, pieces, preferred_element_type=jnp.float32)  3.29 us
    unnamed x18, local copies, waits for them, and re-layouts  3.21 us
  transfers between devices with their start and end apart: 45, of which 24 were waited for; matrix products, arithmetic and copies ran while one was open for 10% of the time, Pallas kernels for 0%

profile of v6, /device:TPU:0, one launch (start us, length us, event | category | flops | bytes accessed | tf_op | source)
XLA Modules:
  0.0 105.2 jit_solution(8713995673734595008)
XLA Ops:
  2.2 1.6 %copy-done.3 = bf16[256,4096]{1,0:T(8,128)(2,1)S(1)} copy-done((bf16[256,4096]{1,0:T(8,128)(2,1)S(1)}, bf16[256,4096]{1,0:T(8,128)(2,1)}, u32[]{:S(2)}) %copy-start.3) | copy-done | bytes 2097176
  6.9 3.0 %collective-permute-start.1 = (bf16[40,4096]{1,0:T(8,128)(2,1)S(1)}, bf16[40,4096]{1,0:T(8,128)(2,1)S(1)}, u32[]{:S(2)}, u32[]{:S(2)}) collective-permute-start(bf16[40,4096]{1,0:T(8,128)(2,1)S(1)} %get-tuple-element.37), channel_id=1, source_target_pairs={{0,8},{2,6},{8,16},{10,2},{16,24},{18,10},{24,28},{26,18},{28,20},... | collective-permute-start | bytes 983048 | tf_op jit(solution)/shard_map/ppermute | solution.py:140
  10.3 1.6 %collective-permute-start.3 = (bf16[40,4096]{1,0:T(8,128)(2,1)S(1)}, bf16[40,4096]{1,0:T(8,128)(2,1)S(1)}, u32[]{:S(2)}, u32[]{:S(2)}) collective-permute-start(bf16[40,4096]{1,0:T(8,128)(2,1)S(1)} %get-tuple-element.41), channel_id=1, source_target_pairs={{0,8},{2,6},{8,16},{10,2},{16,24},{18,10},{24,28},{26,18},{28,20},... | collective-permute-start | bytes 983048 | tf_op jit(solution)/shard_map/ppermute | solution.py:140
  15.2 2.2 %collective-permute-start.4 = (bf16[40,4096]{1,0:T(8,128)(2,1)S(1)}, bf16[40,4096]{1,0:T(8,128)(2,1)S(1)}, u32[]{:S(2)}, u32[]{:S(2)}) collective-permute-start(bf16[40,4096]{1,0:T(8,128)(2,1)S(1)} %pad_maximum_fusion.2), channel_id=1, source_target_pairs={{0,8},{2,6},{8,16},{10,2},{16,24},{18,10},{24,28},{26,18},{28,20},... | collective-permute-start | bytes 983048 | tf_op jit(solution)/shard_map/ppermute | solution.py:140
  18.7 1.9 %collective-permute-done.20 = bf16[32,4096]{1,0:T(8,128)(2,1)S(1)} collective-permute-done((bf16[32,4096]{1,0:T(8,128)(2,1)S(1)}, bf16[32,4096]{1,0:T(8,128)(2,1)S(1)}, u32[]{:S(2)}, u32[]{:S(2)}) %collective-permute-start.20) | collective-permute-done | bytes 262176 | tf_op jit(solution)/shard_map/ppermute | solution.py:111
  20.6 1.7 %collective-permute-start.5 = (bf16[40,4096]{1,0:T(8,128)(2,1)S(1)}, bf16[40,4096]{1,0:T(8,128)(2,1)S(1)}, u32[]{:S(2)}, u32[]{:S(2)}) collective-permute-start(bf16[40,4096]{1,0:T(8,128)(2,1)S(1)} %pad_maximum_fusion.3), channel_id=1, source_target_pairs={{0,8},{2,6},{8,16},{10,2},{16,24},{18,10},{24,28},{26,18},{28,20},... | collective-permute-start | bytes 983048 | tf_op jit(solution)/shard_map/ppermute | solution.py:140
  22.9 2.0 %collective-permute-start.7 = (bf16[40,4096]{1,0:T(8,128)(2,1)S(1)}, bf16[40,4096]{1,0:T(8,128)(2,1)S(1)}, u32[]{:S(2)}, u32[]{:S(2)}) collective-permute-start(bf16[40,4096]{1,0:T(8,128)(2,1)S(1)} %pad_maximum_fusion.4), channel_id=1, source_target_pairs={{0,8},{2,6},{8,16},{10,2},{16,24},{18,10},{24,28},{26,18},{28,20},... | collective-permute-start | bytes 983048 | tf_op jit(solution)/shard_map/ppermute | solution.py:140
  24.9 2.7 %collective-permute-done.5 = bf16[40,4096]{1,0:T(8,128)(2,1)S(1)} collective-permute-done((bf16[40,4096]{1,0:T(8,128)(2,1)S(1)}, bf16[40,4096]{1,0:T(8,128)(2,1)S(1)}, u32[]{:S(2)}, u32[]{:S(2)}) %collective-permute-start.5) | collective-permute-done | bytes 327712 | tf_op jit(solution)/shard_map/ppermute | solution.py:140
  28.1 1.7 %collective-permute-start.9 = (bf16[40,4096]{1,0:T(8,128)(2,1)S(1)}, bf16[40,4096]{1,0:T(8,128)(2,1)S(1)}, u32[]{:S(2)}, u32[]{:S(2)}) collective-permute-start(bf16[40,4096]{1,0:T(8,128)(2,1)S(1)} %pad_maximum_fusion.5), channel_id=1, source_target_pairs={{0,8},{2,6},{8,16},{10,2},{16,24},{18,10},{24,28},{26,18},{28,20},... | collective-permute-start | bytes 983048 | tf_op jit(solution)/shard_map/ppermute | solution.py:140
  31.4 1.7 %collective-permute-start.10 = (bf16[40,4096]{1,0:T(8,128)(2,1)S(1)}, bf16[40,4096]{1,0:T(8,128)(2,1)S(1)}, u32[]{:S(2)}, u32[]{:S(2)}) collective-permute-start(bf16[40,4096]{1,0:T(8,128)(2,1)S(1)} %pad_maximum_fusion.6), channel_id=1, source_target_pairs={{0,8},{2,6},{8,16},{10,2},{16,24},{18,10},{24,28},{26,18},{28,20},... | collective-permute-start | bytes 983048 | tf_op jit(solution)/shard_map/ppermute | solution.py:140
  33.1 2.1 %collective-permute-done.9 = bf16[40,4096]{1,0:T(8,128)(2,1)S(1)} collective-permute-done((bf16[40,4096]{1,0:T(8,128)(2,1)S(1)}, bf16[40,4096]{1,0:T(8,128)(2,1)S(1)}, u32[]{:S(2)}, u32[]{:S(2)}) %collective-permute-start.9) | collective-permute-done | bytes 327712 | tf_op jit(solution)/shard_map/ppermute | solution.py:140
  35.5 1.7 %collective-permute-start.11 = (bf16[40,4096]{1,0:T(8,128)(2,1)S(1)}, bf16[40,4096]{1,0:T(8,128)(2,1)S(1)}, u32[]{:S(2)}, u32[]{:S(2)}) collective-permute-start(bf16[40,4096]{1,0:T(8,128)(2,1)S(1)} %pad_maximum_fusion.7), channel_id=1, source_target_pairs={{0,8},{2,6},{8,16},{10,2},{16,24},{18,10},{24,28},{26,18},{28,20},... | collective-permute-start | bytes 983048 | tf_op jit(solution)/shard_map/ppermute | solution.py:140
  39.0 1.7 %collective-permute-start.12 = (bf16[40,4096]{1,0:T(8,128)(2,1)S(1)}, bf16[40,4096]{1,0:T(8,128)(2,1)S(1)}, u32[]{:S(2)}, u32[]{:S(2)}) collective-permute-start(bf16[40,4096]{1,0:T(8,128)(2,1)S(1)} %pad_maximum_fusion.8), channel_id=1, source_target_pairs={{0,8},{2,6},{8,16},{10,2},{16,24},{18,10},{24,28},{26,18},{28,20},... | collective-permute-start | bytes 983048 | tf_op jit(solution)/shard_map/ppermute | solution.py:140
  40.7 1.9 %collective-permute-done.11 = bf16[40,4096]{1,0:T(8,128)(2,1)S(1)} collective-permute-done((bf16[40,4096]{1,0:T(8,128)(2,1)S(1)}, bf16[40,4096]{1,0:T(8,128)(2,1)S(1)}, u32[]{:S(2)}, u32[]{:S(2)}) %collective-permute-start.11) | collective-permute-done | bytes 327712 | tf_op jit(solution)/shard_map/ppermute | solution.py:140
  42.9 1.7 %collective-permute-start.13 = (bf16[40,4096]{1,0:T(8,128)(2,1)S(1)}, bf16[40,4096]{1,0:T(8,128)(2,1)S(1)}, u32[]{:S(2)}, u32[]{:S(2)}) collective-permute-start(bf16[40,4096]{1,0:T(8,128)(2,1)S(1)} %pad_maximum_fusion.9), channel_id=1, source_target_pairs={{0,8},{2,6},{8,16},{10,2},{16,24},{18,10},{24,28},{26,18},{28,20},... | collective-permute-start | bytes 983048 | tf_op jit(solution)/shard_map/ppermute | solution.py:140
  46.4 1.7 %collective-permute-start.14 = (bf16[40,4096]{1,0:T(8,128)(2,1)S(1)}, bf16[40,4096]{1,0:T(8,128)(2,1)S(1)}, u32[]{:S(2)}, u32[]{:S(2)}) collective-permute-start(bf16[40,4096]{1,0:T(8,128)(2,1)S(1)} %pad_maximum_fusion.10), channel_id=1, source_target_pairs={{0,8},{2,6},{8,16},{10,2},{16,24},{18,10},{24,28},{26,18},{28,20},... | collective-permute-start | bytes 983048 | tf_op jit(solution)/shard_map/ppermute | solution.py:140
  48.1 1.9 %collective-permute-done.13 = bf16[40,4096]{1,0:T(8,128)(2,1)S(1)} collective-permute-done((bf16[40,4096]{1,0:T(8,128)(2,1)S(1)}, bf16[40,4096]{1,0:T(8,128)(2,1)S(1)}, u32[]{:S(2)}, u32[]{:S(2)}) %collective-permute-start.13) | collective-permute-done | bytes 327712 | tf_op jit(solution)/shard_map/ppermute | solution.py:140
  50.3 1.7 %collective-permute-start.15 = (bf16[40,4096]{1,0:T(8,128)(2,1)S(1)}, bf16[40,4096]{1,0:T(8,128)(2,1)S(1)}, u32[]{:S(2)}, u32[]{:S(2)}) collective-permute-start(bf16[40,4096]{1,0:T(8,128)(2,1)S(1)} %pad_maximum_fusion.11), channel_id=1, source_target_pairs={{0,8},{2,6},{8,16},{10,2},{16,24},{18,10},{24,28},{26,18},{28,20},... | collective-permute-start | bytes 983048 | tf_op jit(solution)/shard_map/ppermute | solution.py:140
  53.8 1.7 %collective-permute-start.16 = (bf16[40,4096]{1,0:T(8,128)(2,1)S(1)}, bf16[40,4096]{1,0:T(8,128)(2,1)S(1)}, u32[]{:S(2)}, u32[]{:S(2)}) collective-permute-start(bf16[40,4096]{1,0:T(8,128)(2,1)S(1)} %pad_maximum_fusion.12), channel_id=1, source_target_pairs={{0,8},{2,6},{8,16},{10,2},{16,24},{18,10},{24,28},{26,18},{28,20},... | collective-permute-start | bytes 983048 | tf_op jit(solution)/shard_map/ppermute | solution.py:140
  55.5 1.9 %collective-permute-done.15 = bf16[40,4096]{1,0:T(8,128)(2,1)S(1)} collective-permute-done((bf16[40,4096]{1,0:T(8,128)(2,1)S(1)}, bf16[40,4096]{1,0:T(8,128)(2,1)S(1)}, u32[]{:S(2)}, u32[]{:S(2)}) %collective-permute-start.15) | collective-permute-done | bytes 327712 | tf_op jit(solution)/shard_map/ppermute | solution.py:140
  57.7 1.9 %collective-permute-start.17 = (bf16[40,4096]{1,0:T(8,128)(2,1)S(1)}, bf16[40,4096]{1,0:T(8,128)(2,1)S(1)}, u32[]{:S(2)}, u32[]{:S(2)}) collective-permute-start(bf16[40,4096]{1,0:T(8,128)(2,1)S(1)} %pad_maximum_fusion.13), channel_id=1, source_target_pairs={{0,8},{2,6},{8,16},{10,2},{16,24},{18,10},{24,28},{26,18},{28,20},... | collective-permute-start | bytes 983048 | tf_op jit(solution)/shard_map/ppermute | solution.py:140
  59.7 5.3 %collective-permute-done.17 = bf16[40,4096]{1,0:T(8,128)(2,1)S(1)} collective-permute-done((bf16[40,4096]{1,0:T(8,128)(2,1)S(1)}, bf16[40,4096]{1,0:T(8,128)(2,1)S(1)}, u32[]{:S(2)}, u32[]{:S(2)}) %collective-permute-start.17) | collective-permute-done | bytes 327712 | tf_op jit(solution)/shard_map/ppermute | solution.py:140
  68.7 4.3 %scores.1 = (bf16[512,256]{1,0:T(8,128)(2,1)S(1)}, bf16[512,256]{1,0:T(8,128)(2,1)S(1)}, f32[512,1]{1,0:T(8,128)S(1)}, bf16[256,4096]{1,0:T(8,128)(2,1)S(1)}) custom-call(bf16[128,4096]{1,0:T(8,128)(2,1)S(1)} %slice_dynamic-update-slice_fusion.refs_0_, bf16[128,4096]{1,0:T(8,128)(2,1)S(1)} %collective-permute-done.18.refs_1_, bf16[512,4096]{1,0:T(8,128)(2,1)S(1)} %copy-done, ...), custom_call_target="tpu_custom_call" | custom-call | flops 3221225472 | bytes 20971520 | tf_op jit(solution)/shard_map/scores/pallas_call | solution.py:189
  76.8 1.6 %collective-permute-start.37 = (bf16[2,2,16,2048]{3,2,0,1:T(8,128)(2,1)S(1)}, bf16[2,2,16,2048]{3,2,0,1:T(8,128)(2,1)S(1)}, u32[]{:S(2)}, u32[]{:S(2)}) collective-permute-start(bf16[2,2,16,2048]{3,2,0,1:T(8,128)(2,1)S(1)} %fusion.7), channel_id=1, source_target_pairs={{0,4},{2,6},{4,0},{6,2},{8,12},{10,14},{12,8},{14,10},{16,20},{18,... | collective-permute-start | bytes 786440 | tf_op jit(solution)/shard_map/ppermute | solution.py:263
  81.3 4.0 %collective-permute-done.37 = bf16[2,2,16,2048]{3,2,0,1:T(8,128)(2,1)S(1)} collective-permute-done((bf16[2,2,16,2048]{3,2,0,1:T(8,128)(2,1)S(1)}, bf16[2,2,16,2048]{3,2,0,1:T(8,128)(2,1)S(1)}, u32[]{:S(2)}, u32[]{:S(2)}) %collective-permute-start.37) | collective-permute-done | bytes 262176 | tf_op jit(solution)/shard_map/ppermute | solution.py:263
  85.4 1.7 %collective-permute-start.38 = (bf16[2,16,2048]{2,1,0:T(8,128)(2,1)S(1)}, bf16[2,16,2048]{2,1,0:T(8,128)(2,1)S(1)}, u32[]{:S(2)}, u32[]{:S(2)}) collective-permute-start(bf16[2,16,2048]{2,1,0:T(8,128)(2,1)S(1)} %fusion.10), channel_id=1, source_target_pairs={{0,8},{2,10},{4,12},{6,14},{8,0},{10,2},{12,4},{14,6},{16,24},{18,... | collective-permute-start | bytes 393224 | tf_op jit(solution)/shard_map/ppermute | solution.py:263
  88.7 1.7 %collective-permute-done.38 = bf16[2,16,2048]{2,1,0:T(8,128)(2,1)S(1)} collective-permute-done((bf16[2,16,2048]{2,1,0:T(8,128)(2,1)S(1)}, bf16[2,16,2048]{2,1,0:T(8,128)(2,1)S(1)}, u32[]{:S(2)}, u32[]{:S(2)}) %collective-permute-start.38) | collective-permute-done | bytes 131104 | tf_op jit(solution)/shard_map/ppermute | solution.py:263
  90.4 2.7 %collective-permute-start.39 = (bf16[16,2048]{1,0:T(8,128)(2,1)S(1)}, bf16[16,2048]{1,0:T(8,128)(2,1)S(1)}, u32[]{:S(2)}, u32[]{:S(2)}) collective-permute-start(bf16[16,2048]{1,0:T(8,128)(2,1)S(1)} %fusion.18), channel_id=1, source_target_pairs={{0,16},{2,18},{4,20},{6,22},{8,24},{10,26},{12,28},{14,30},{16,0},... | collective-permute-start | bytes 196616 | tf_op jit(solution)/shard_map/ppermute | solution.py:263
  93.2 1.7 %collective-permute-start.43 = (bf16[16,2048]{1,0:T(8,128)(2,1)S(1)}, bf16[16,2048]{1,0:T(8,128)(2,1)S(1)}, u32[]{:S(2)}, u32[]{:S(2)}) collective-permute-start(bf16[16,2048]{1,0:T(8,128)(2,1)S(1)} %fusion.19), channel_id=1, source_target_pairs={{0,16},{2,18},{4,20},{6,22},{8,24},{10,26},{12,28},{14,30},{16,0},... | collective-permute-start | bytes 196616 | tf_op jit(solution)/shard_map/ppermute | solution.py:263
  94.9 2.7 %collective-permute-done.39 = bf16[16,2048]{1,0:T(8,128)(2,1)S(1)} collective-permute-done((bf16[16,2048]{1,0:T(8,128)(2,1)S(1)}, bf16[16,2048]{1,0:T(8,128)(2,1)S(1)}, u32[]{:S(2)}, u32[]{:S(2)}) %collective-permute-start.39) | collective-permute-done | bytes 65568 | tf_op jit(solution)/shard_map/ppermute | solution.py:263
  97.6 1.6 %collective-permute-start.40 = (f32[16,2048]{1,0:T(8,128)S(1)}, f32[16,2048]{1,0:T(8,128)S(1)}, u32[]{:S(2)}, u32[]{:S(2)}) collective-permute-start(f32[16,2048]{1,0:T(8,128)S(1)} %fusion.13), channel_id=1, source_target_pairs={{0,1},{1,0},{2,3},{3,2},{4,5},{5,4},{6,7},{7,6},{8,9},{9,8},{10,11... | collective-permute-start | bytes 393224 | tf_op jit(solution)/shard_map/ppermute | solution.py:273
  100.1 3.3 %multiply_convert_fusion = bf16[512,4096]{1,0:T(8,128)(2,1)} fusion(f32[512,4096]{1,0:T(8,128)S(1)} %fusion.44, bf16[512,256]{1,0:T(8,128)(2,1)S(1)} %get-tuple-element.61, bf16[256,4096]{1,0:T(8,128)(2,1)S(1)} %get-tuple-element.62), kind=kOutput, calls=%fused_computation | convolution fusion | flops 1080033280 | bytes 14942208 | tf_op jit(solution)/shard_map/dot_general | solution.py:278
  (171 shorter events, 31.7 us)
Async XLA Ops:
  6.9 8.0 %collective-permute-start.1 = (bf16[40,4096]{1,0:T(8,128)(2,1)S(1)}, bf16[40,4096]{1,0:T(8,128)(2,1)S(1)}, u32[]{:S(2)}, u32[]{:S(2)}) collective-permute-start(bf16[40,4096]{1,0:T(8,128)(2,1)S(1)} %get-tuple-element.37), channel_id=1, source_target_pairs={{0,8},{2,6},{8,16},{10,2},{16,24},{18,10},{24,28},{26,18},{28,20},... | collective-permute-start | bytes 983048 | tf_op jit(solution)/shard_map/ppermute | solution.py:140
  10.2 2.6 %collective-permute-start.27 = (bf16[32,4096]{1,0:T(8,128)(2,1)S(1)}, bf16[32,4096]{1,0:T(8,128)(2,1)S(1)}, u32[]{:S(2)}, u32[]{:S(2)}) collective-permute-start(bf16[32,4096]{1,0:T(8,128)(2,1)S(1)} %get-tuple-element.119), channel_id=1, source_target_pairs={{0,2},{2,0},{4,6},{6,4},{8,10},{10,8},{12,14},{14,12},{16,18},{18,... | collective-permute-start | bytes 786440 | tf_op jit(solution)/shard_map/ppermute | solution.py:111
  10.3 8.1 %collective-permute-start.3 = (bf16[40,4096]{1,0:T(8,128)(2,1)S(1)}, bf16[40,4096]{1,0:T(8,128)(2,1)S(1)}, u32[]{:S(2)}, u32[]{:S(2)}) collective-permute-start(bf16[40,4096]{1,0:T(8,128)(2,1)S(1)} %get-tuple-element.41), channel_id=1, source_target_pairs={{0,8},{2,6},{8,16},{10,2},{16,24},{18,10},{24,28},{26,18},{28,20},... | collective-permute-start | bytes 983048 | tf_op jit(solution)/shard_map/ppermute | solution.py:140
  12.3 15.3 %collective-permute-start.8 = (bf16[256,4096]{1,0:T(8,128)(2,1)S(1)}, bf16[256,4096]{1,0:T(8,128)(2,1)S(1)}, u32[]{:S(2)}, u32[]{:S(2)}) collective-permute-start(bf16[256,4096]{1,0:T(8,128)(2,1)S(1)} %copy-done.4), channel_id=1, source_target_pairs={{0,2},{2,0},{4,6},{6,4},{8,10},{10,8},{12,14},{14,12},{16,18},{18,... | collective-permute-start | bytes 6291464 | tf_op jit(solution)/shard_map/ppermute | solution.py:136
  12.8 9.6 %collective-permute-start.6 = (bf16[256,4096]{1,0:T(8,128)(2,1)S(1)}, bf16[256,4096]{1,0:T(8,128)(2,1)S(1)}, u32[]{:S(2)}, u32[]{:S(2)}) collective-permute-start(bf16[256,4096]{1,0:T(8,128)(2,1)S(1)} %copy-done.2), channel_id=1, source_target_pairs={{0,2},{2,0},{4,6},{6,4},{8,10},{10,8},{12,14},{14,12},{16,18},{18,... | collective-permute-start | bytes 6291464 | tf_op jit(solution)/shard_map/ppermute | solution.py:136
  15.0 7.3 %collective-permute-start.28 = (bf16[32,4096]{1,0:T(8,128)(2,1)S(1)}, bf16[32,4096]{1,0:T(8,128)(2,1)S(1)}, u32[]{:S(2)}, u32[]{:S(2)}) collective-permute-start(bf16[32,4096]{1,0:T(8,128)(2,1)S(1)} %get-tuple-element.80), channel_id=1, source_target_pairs={{0,2},{2,0},{4,6},{6,4},{8,10},{10,8},{12,14},{14,12},{16,18},{18,... | collective-permute-start | bytes 786440 | tf_op jit(solution)/shard_map/ppermute | solution.py:111
  15.2 7.2 %collective-permute-start.4 = (bf16[40,4096]{1,0:T(8,128)(2,1)S(1)}, bf16[40,4096]{1,0:T(8,128)(2,1)S(1)}, u32[]{:S(2)}, u32[]{:S(2)}) collective-permute-start(bf16[40,4096]{1,0:T(8,128)(2,1)S(1)} %pad_maximum_fusion.2), channel_id=1, source_target_pairs={{0,8},{2,6},{8,16},{10,2},{16,24},{18,10},{24,28},{26,18},{28,20},... | collective-permute-start | bytes 983048 | tf_op jit(solution)/shard_map/ppermute | solution.py:140
  20.6 7.1 %collective-permute-start.5 = (bf16[40,4096]{1,0:T(8,128)(2,1)S(1)}, bf16[40,4096]{1,0:T(8,128)(2,1)S(1)}, u32[]{:S(2)}, u32[]{:S(2)}) collective-permute-start(bf16[40,4096]{1,0:T(8,128)(2,1)S(1)} %pad_maximum_fusion.3), channel_id=1, source_target_pairs={{0,8},{2,6},{8,16},{10,2},{16,24},{18,10},{24,28},{26,18},{28,20},... | collective-permute-start | bytes 983048 | tf_op jit(solution)/shard_map/ppermute | solution.py:140
  22.8 7.1 %collective-permute-start.29 = (bf16[32,4096]{1,0:T(8,128)(2,1)S(1)}, bf16[32,4096]{1,0:T(8,128)(2,1)S(1)}, u32[]{:S(2)}, u32[]{:S(2)}) collective-permute-start(bf16[32,4096]{1,0:T(8,128)(2,1)S(1)} %get-tuple-element.78), channel_id=1, source_target_pairs={{0,2},{2,0},{4,6},{6,4},{8,10},{10,8},{12,14},{14,12},{16,18},{18,... | collective-permute-start | bytes 786440 | tf_op jit(solution)/shard_map/ppermute | solution.py:111
  22.9 8.3 %collective-permute-start.7 = (bf16[40,4096]{1,0:T(8,128)(2,1)S(1)}, bf16[40,4096]{1,0:T(8,128)(2,1)S(1)}, u32[]{:S(2)}, u32[]{:S(2)}) collective-permute-start(bf16[40,4096]{1,0:T(8,128)(2,1)S(1)} %pad_maximum_fusion.4), channel_id=1, source_target_pairs={{0,8},{2,6},{8,16},{10,2},{16,24},{18,10},{24,28},{26,18},{28,20},... | collective-permute-start | bytes 983048 | tf_op jit(solution)/shard_map/ppermute | solution.py:140
  28.1 7.1 %collective-permute-start.9 = (bf16[40,4096]{1,0:T(8,128)(2,1)S(1)}, bf16[40,4096]{1,0:T(8,128)(2,1)S(1)}, u32[]{:S(2)}, u32[]{:S(2)}) collective-permute-start(bf16[40,4096]{1,0:T(8,128)(2,1)S(1)} %pad_maximum_fusion.5), channel_id=1, source_target_pairs={{0,8},{2,6},{8,16},{10,2},{16,24},{18,10},{24,28},{26,18},{28,20},... | collective-permute-start | bytes 983048 | tf_op jit(solution)/shard_map/ppermute | solution.py:140
  31.3 6.0 %collective-permute-start.30 = (bf16[32,4096]{1,0:T(8,128)(2,1)S(1)}, bf16[32,4096]{1,0:T(8,128)(2,1)S(1)}, u32[]{:S(2)}, u32[]{:S(2)}) collective-permute-start(bf16[32,4096]{1,0:T(8,128)(2,1)S(1)} %get-tuple-element.76), channel_id=1, source_target_pairs={{0,2},{2,0},{4,6},{6,4},{8,10},{10,8},{12,14},{14,12},{16,18},{18,... | collective-permute-start | bytes 786440 | tf_op jit(solution)/shard_map/ppermute | solution.py:111
  31.4 7.4 %collective-permute-start.10 = (bf16[40,4096]{1,0:T(8,128)(2,1)S(1)}, bf16[40,4096]{1,0:T(8,128)(2,1)S(1)}, u32[]{:S(2)}, u32[]{:S(2)}) collective-permute-start(bf16[40,4096]{1,0:T(8,128)(2,1)S(1)} %pad_maximum_fusion.6), channel_id=1, source_target_pairs={{0,8},{2,6},{8,16},{10,2},{16,24},{18,10},{24,28},{26,18},{28,20},... | collective-permute-start | bytes 983048 | tf_op jit(solution)/shard_map/ppermute | solution.py:140
  35.5 7.1 %collective-permute-start.11 = (bf16[40,4096]{1,0:T(8,128)(2,1)S(1)}, bf16[40,4096]{1,0:T(8,128)(2,1)S(1)}, u32[]{:S(2)}, u32[]{:S(2)}) collective-permute-start(bf16[40,4096]{1,0:T(8,128)(2,1)S(1)} %pad_maximum_fusion.7), channel_id=1, source_target_pairs={{0,8},{2,6},{8,16},{10,2},{16,24},{18,10},{24,28},{26,18},{28,20},... | collective-permute-start | bytes 983048 | tf_op jit(solution)/shard_map/ppermute | solution.py:140
  38.9 5.8 %collective-permute-start.31 = (bf16[32,4096]{1,0:T(8,128)(2,1)S(1)}, bf16[32,4096]{1,0:T(8,128)(2,1)S(1)}, u32[]{:S(2)}, u32[]{:S(2)}) collective-permute-start(bf16[32,4096]{1,0:T(8,128)(2,1)S(1)} %get-tuple-element.74), channel_id=1, source_target_pairs={{0,2},{2,0},{4,6},{6,4},{8,10},{10,8},{12,14},{14,12},{16,18},{18,... | collective-permute-start | bytes 786440 | tf_op jit(solution)/shard_map/ppermute | solution.py:111
  39.0 7.1 %collective-permute-start.12 = (bf16[40,4096]{1,0:T(8,128)(2,1)S(1)}, bf16[40,4096]{1,0:T(8,128)(2,1)S(1)}, u32[]{:S(2)}, u32[]{:S(2)}) collective-permute-start(bf16[40,4096]{1,0:T(8,128)(2,1)S(1)} %pad_maximum_fusion.8), channel_id=1, source_target_pairs={{0,8},{2,6},{8,16},{10,2},{16,24},{18,10},{24,28},{26,18},{28,20},... | collective-permute-start | bytes 983048 | tf_op jit(solution)/shard_map/ppermute | solution.py:140
  42.9 7.1 %collective-permute-start.13 = (bf16[40,4096]{1,0:T(8,128)(2,1)S(1)}, bf16[40,4096]{1,0:T(8,128)(2,1)S(1)}, u32[]{:S(2)}, u32[]{:S(2)}) collective-permute-start(bf16[40,4096]{1,0:T(8,128)(2,1)S(1)} %pad_maximum_fusion.9), channel_id=1, source_target_pairs={{0,8},{2,6},{8,16},{10,2},{16,24},{18,10},{24,28},{26,18},{28,20},... | collective-permute-start | bytes 983048 | tf_op jit(solution)/shard_map/ppermute | solution.py:140
  46.3 5.8 %collective-permute-start.32 = (bf16[32,4096]{1,0:T(8,128)(2,1)S(1)}, bf16[32,4096]{1,0:T(8,128)(2,1)S(1)}, u32[]{:S(2)}, u32[]{:S(2)}) collective-permute-start(bf16[32,4096]{1,0:T(8,128)(2,1)S(1)} %get-tuple-element.72), channel_id=1, source_target_pairs={{0,2},{2,0},{4,6},{6,4},{8,10},{10,8},{12,14},{14,12},{16,18},{18,... | collective-permute-start | bytes 786440 | tf_op jit(solution)/shard_map/ppermute | solution.py:111
  46.4 7.1 %collective-permute-start.14 = (bf16[40,4096]{1,0:T(8,128)(2,1)S(1)}, bf16[40,4096]{1,0:T(8,128)(2,1)S(1)}, u32[]{:S(2)}, u32[]{:S(2)}) collective-permute-start(bf16[40,4096]{1,0:T(8,128)(2,1)S(1)} %pad_maximum_fusion.10), channel_id=1, source_target_pairs={{0,8},{2,6},{8,16},{10,2},{16,24},{18,10},{24,28},{26,18},{28,20},... | collective-permute-start | bytes 983048 | tf_op jit(solution)/shard_map/ppermute | solution.py:140
  50.3 7.1 %collective-permute-start.15 = (bf16[40,4096]{1,0:T(8,128)(2,1)S(1)}, bf16[40,4096]{1,0:T(8,128)(2,1)S(1)}, u32[]{:S(2)}, u32[]{:S(2)}) collective-permute-start(bf16[40,4096]{1,0:T(8,128)(2,1)S(1)} %pad_maximum_fusion.11), channel_id=1, source_target_pairs={{0,8},{2,6},{8,16},{10,2},{16,24},{18,10},{24,28},{26,18},{28,20},... | collective-permute-start | bytes 983048 | tf_op jit(solution)/shard_map/ppermute | solution.py:140
  53.7 6.0 %collective-permute-start.33 = (bf16[32,4096]{1,0:T(8,128)(2,1)S(1)}, bf16[32,4096]{1,0:T(8,128)(2,1)S(1)}, u32[]{:S(2)}, u32[]{:S(2)}) collective-permute-start(bf16[32,4096]{1,0:T(8,128)(2,1)S(1)} %get-tuple-element.70), channel_id=1, source_target_pairs={{0,2},{2,0},{4,6},{6,4},{8,10},{10,8},{12,14},{14,12},{16,18},{18,... | collective-permute-start | bytes 786440 | tf_op jit(solution)/shard_map/ppermute | solution.py:111
  53.8 11.4 %collective-permute-start.16 = (bf16[40,4096]{1,0:T(8,128)(2,1)S(1)}, bf16[40,4096]{1,0:T(8,128)(2,1)S(1)}, u32[]{:S(2)}, u32[]{:S(2)}) collective-permute-start(bf16[40,4096]{1,0:T(8,128)(2,1)S(1)} %pad_maximum_fusion.12), channel_id=1, source_target_pairs={{0,8},{2,6},{8,16},{10,2},{16,24},{18,10},{24,28},{26,18},{28,20},... | collective-permute-start | bytes 983048 | tf_op jit(solution)/shard_map/ppermute | solution.py:140
  57.7 7.3 %collective-permute-start.17 = (bf16[40,4096]{1,0:T(8,128)(2,1)S(1)}, bf16[40,4096]{1,0:T(8,128)(2,1)S(1)}, u32[]{:S(2)}, u32[]{:S(2)}) collective-permute-start(bf16[40,4096]{1,0:T(8,128)(2,1)S(1)} %pad_maximum_fusion.13), channel_id=1, source_target_pairs={{0,8},{2,6},{8,16},{10,2},{16,24},{18,10},{24,28},{26,18},{28,20},... | collective-permute-start | bytes 983048 | tf_op jit(solution)/shard_map/ppermute | solution.py:140
  65.9 2.7 %collective-permute-start.18 = (bf16[128,4096]{1,0:T(8,128)(2,1)S(1)}, bf16[128,4096]{1,0:T(8,128)(2,1)S(1)}, u32[]{:S(2)}, u32[]{:S(2)}) collective-permute-start(bf16[128,4096]{1,0:T(8,128)(2,1)S(1)} %slice_dynamic-update-slice_fusion.refs_0_), channel_id=1, source_target_pairs={{0,2},{2,0},{4,6},{6,4},{8,10},{10,8},{12,14},{14,12},{16,18},{18,... | collective-permute-start | bytes 3145736 | tf_op jit(solution)/shard_map/ppermute | solution.py:225
  76.8 8.5 %collective-permute-start.37 = (bf16[2,2,16,2048]{3,2,0,1:T(8,128)(2,1)S(1)}, bf16[2,2,16,2048]{3,2,0,1:T(8,128)(2,1)S(1)}, u32[]{:S(2)}, u32[]{:S(2)}) collective-permute-start(bf16[2,2,16,2048]{3,2,0,1:T(8,128)(2,1)S(1)} %fusion.7), channel_id=1, source_target_pairs={{0,4},{2,6},{4,0},{6,2},{8,12},{10,14},{12,8},{14,10},{16,20},{18,... | collective-permute-start | bytes 786440 | tf_op jit(solution)/shard_map/ppermute | solution.py:263
  78.4 8.7 %collective-permute-start.41 = (bf16[2,2,16,2048]{3,2,0,1:T(8,128)(2,1)S(1)}, bf16[2,2,16,2048]{3,2,0,1:T(8,128)(2,1)S(1)}, u32[]{:S(2)}, u32[]{:S(2)}) collective-permute-start(bf16[2,2,16,2048]{3,2,0,1:T(8,128)(2,1)S(1)} %fusion.6), channel_id=1, source_target_pairs={{0,8},{2,10},{4,12},{6,14},{8,0},{10,2},{12,4},{14,6},{16,24},{18,... | collective-permute-start | bytes 786440 | tf_op jit(solution)/shard_map/ppermute | solution.py:263
  85.4 5.0 %collective-permute-start.38 = (bf16[2,16,2048]{2,1,0:T(8,128)(2,1)S(1)}, bf16[2,16,2048]{2,1,0:T(8,128)(2,1)S(1)}, u32[]{:S(2)}, u32[]{:S(2)}) collective-permute-start(bf16[2,16,2048]{2,1,0:T(8,128)(2,1)S(1)} %fusion.10), channel_id=1, source_target_pairs={{0,8},{2,10},{4,12},{6,14},{8,0},{10,2},{12,4},{14,6},{16,24},{18,... | collective-permute-start | bytes 393224 | tf_op jit(solution)/shard_map/ppermute | solution.py:263
  87.2 6.0 %collective-permute-start.42 = (bf16[2,16,2048]{2,1,0:T(8,128)(2,1)S(1)}, bf16[2,16,2048]{2,1,0:T(8,128)(2,1)S(1)}, u32[]{:S(2)}, u32[]{:S(2)}) collective-permute-start(bf16[2,16,2048]{2,1,0:T(8,128)(2,1)S(1)} %fusion.11), channel_id=1, source_target_pairs={{0,4},{2,6},{4,0},{6,2},{8,12},{10,14},{12,8},{14,10},{16,20},{18,... | collective-permute-start | bytes 393224 | tf_op jit(solution)/shard_map/ppermute | solution.py:263
  90.4 7.2 %collective-permute-start.39 = (bf16[16,2048]{1,0:T(8,128)(2,1)S(1)}, bf16[16,2048]{1,0:T(8,128)(2,1)S(1)}, u32[]{:S(2)}, u32[]{:S(2)}) collective-permute-start(bf16[16,2048]{1,0:T(8,128)(2,1)S(1)} %fusion.18), channel_id=1, source_target_pairs={{0,16},{2,18},{4,20},{6,22},{8,24},{10,26},{12,28},{14,30},{16,0},... | collective-permute-start | bytes 196616 | tf_op jit(solution)/shard_map/ppermute | solution.py:263
  93.2 6.0 %collective-permute-start.43 = (bf16[16,2048]{1,0:T(8,128)(2,1)S(1)}, bf16[16,2048]{1,0:T(8,128)(2,1)S(1)}, u32[]{:S(2)}, u32[]{:S(2)}) collective-permute-start(bf16[16,2048]{1,0:T(8,128)(2,1)S(1)} %fusion.19), channel_id=1, source_target_pairs={{0,16},{2,18},{4,20},{6,22},{8,24},{10,26},{12,28},{14,30},{16,0},... | collective-permute-start | bytes 196616 | tf_op jit(solution)/shard_map/ppermute | solution.py:263
  97.6 6.8 %collective-permute-start.40 = (f32[16,2048]{1,0:T(8,128)S(1)}, f32[16,2048]{1,0:T(8,128)S(1)}, u32[]{:S(2)}, u32[]{:S(2)}) collective-permute-start(f32[16,2048]{1,0:T(8,128)S(1)} %fusion.13), channel_id=1, source_target_pairs={{0,1},{1,0},{2,3},{3,2},{4,5},{5,4},{6,7},{7,6},{8,9},{9,8},{10,11... | collective-permute-start | bytes 393224 | tf_op jit(solution)/shard_map/ppermute | solution.py:273
  99.2 5.2 %collective-permute-start.44 = (f32[16,2048]{1,0:T(8,128)S(1)}, f32[16,2048]{1,0:T(8,128)S(1)}, u32[]{:S(2)}, u32[]{:S(2)}) collective-permute-start(f32[16,2048]{1,0:T(8,128)S(1)} %fusion.12), channel_id=1, source_target_pairs={{0,1},{1,0},{2,3},{3,2},{4,5},{5,4},{6,7},{7,6},{8,9},{9,8},{10,11... | collective-permute-start | bytes 393224 | tf_op jit(solution)/shard_map/ppermute | solution.py:273
  (22 other events, 75.5 us)

commit v7 on v6

--- a/solution.py
+++ b/solution.py
@@ -96,12 +96,16 @@
     for i in (1, 0):
         first[i] = jnp.where(own_core, chunks[i], lax.ppermute(chunks[2 + i], "wide", swap))
 
+    full = [None, None]
+    for i in (1, 0):
+        bank, first[0] = lax.optimization_barrier((banks[i], first[0]))
+        full[i] = jnp.where(own_core, bank, lax.ppermute(bank, "wide", swap))
+
     def own_rows(i, j):
         if j < 2:
             return rows_at(first[i], jnp.where(core == 0, j, 1 - j) * (STEP // 8), STEP)
         return rows_at(full[i], tile_of(core, j), STEP)
 
-    full = [None, None]
     pools = [jnp.zeros_like(bank_s), jnp.zeros_like(bank_t)]
     rows = put_rows(jnp.zeros((n_chip * block, width), passages.dtype), passages, 0)
     moving = [own_rows(i, 0) for i in range(2)]
@@ -131,11 +135,8 @@
                 got, _ = lax.optimization_barrier((came[i], lead))
                 arrive(i, t - 1, got)
             sent = jnp.concatenate([moving[i], riding[i]], 0) if t < n_chip - 1 else moving[i]
-            if t == 0:
-                bank, sent = lax.optimization_barrier((banks[i], sent))
-                full[i] = jnp.where(own_core, bank, lax.ppermute(bank, "wide", swap))
-                if i == 0:
-                    sent, _ = lax.optimization_barrier((sent, lead))
+            if t == 0 and i == 0:
+                sent, _ = lax.optimization_barrier((sent, lead))
             lead = sent
             came[i] = lax.ppermute(sent, "wide", pairs)
             keep(i, t, sent[:STEP])

time: 105 us -> 105 us (level)
  starting transfers between devices: 42.8 us -> 41.1 us
  waiting for transfers between devices: 39 us -> 40.2 us
    ppermute x6, starting transfers between devices: 10.9 us -> 8.94 us  [body(): got = lax.ppermute(sent[h], 'wide', pairs_of[orders[h][step]])]
    ppermute x6, waiting for transfers between devices: 8.39 us -> 10.2 us  [body(): got = lax.ppermute(sent[h], 'wide', pairs_of[orders[h][step]])]
    dynamic_update_slice x30 -> x31, other arithmetic: 2.73 us -> 2.79 us  [put_rows(): return lax.dynamic_update_slice_in_dim(x, rows, tile * 8, 0)]
  transfers between devices with their start and end apart: 45 -> 45, of which waited for: 24 -> 23; matrix products, arithmetic and copies ran while one was open for 10% -> 11% of each run, Pallas kernels for 0% -> 0%
where the time goes in v7:
time: 105 us
  starting transfers between devices  41.1 us (39%)
  waiting for transfers between devices  40.2 us (38%)
  matrix products  6.43 us (6%)
  other arithmetic  5.39 us (5%)
  Pallas kernels  4.46 us (4%)
  local copies, waits for them, and re-layouts  4.23 us (4%)
  between operations  2.74 us (3%)
    ppermute x14, starting transfers between devices, gather_rows(): came[i] = lax.ppermute(sent, 'wide', pairs)  25.1 us
    ppermute x14, waiting for transfers between devices, gather_rows(): came[i] = lax.ppermute(sent, 'wide', pairs)  24.1 us
    ppermute x6, waiting for transfers between devices, body(): got = lax.ppermute(sent[h], 'wide', pairs_of[orders[h][step]])  10.2 us
    ppermute x6, starting transfers between devices, body(): got = lax.ppermute(sent[h], 'wide', pairs_of[orders[h][step]])  8.94 us
    pallas_call x1, Pallas kernels, tail(): pl.pallas_call(functools.partial(tail_kernel, scale, len(pass_parts)), ou...  4.33 us
    dot_general x1, matrix products, body(): jnp.dot(late_p, pieces, preferred_element_type=jnp.float32)  3.28 us
    unnamed x18, local copies, waits for them, and re-layouts  3.21 us
    ppermute x16, waiting for transfers between devices, keep(): other = lax.ppermute(sent, 'wide', swap)  3.21 us
  transfers between devices with their start and end apart: 45, of which 23 were waited for; matrix products, arithmetic and copies ran while one was open for 11% of the time, Pallas kernels for 0%

profile of v7, /device:TPU:0, one launch (start us, length us, event | category | flops | bytes accessed | tf_op | source)
XLA Modules:
  0.0 104.5 jit_solution(17727914764299563248)
XLA Ops:
  0.7 1.6 %copy-done.1 = bf16[256,4096]{1,0:T(8,128)(2,1)S(1)} copy-done((bf16[256,4096]{1,0:T(8,128)(2,1)S(1)}, bf16[256,4096]{1,0:T(8,128)(2,1)}, u32[]{:S(2)}) %copy-start.1) | copy-done | bytes 2097176
  2.2 1.6 %copy-done.3 = bf16[256,4096]{1,0:T(8,128)(2,1)S(1)} copy-done((bf16[256,4096]{1,0:T(8,128)(2,1)S(1)}, bf16[256,4096]{1,0:T(8,128)(2,1)}, u32[]{:S(2)}) %copy-start.3) | copy-done | bytes 2097176
  7.0 2.7 %collective-permute-start.1 = (bf16[40,4096]{1,0:T(8,128)(2,1)S(1)}, bf16[40,4096]{1,0:T(8,128)(2,1)S(1)}, u32[]{:S(2)}, u32[]{:S(2)}) collective-permute-start(bf16[40,4096]{1,0:T(8,128)(2,1)S(1)} %pad_maximum_fusion), channel_id=1, source_target_pairs={{0,8},{2,6},{8,16},{10,2},{16,24},{18,10},{24,28},{26,18},{28,20},... | collective-permute-start | bytes 983048 | tf_op jit(solution)/shard_map/ppermute | solution.py:141
  9.8 1.6 %collective-permute-start.3 = (bf16[40,4096]{1,0:T(8,128)(2,1)S(1)}, bf16[40,4096]{1,0:T(8,128)(2,1)S(1)}, u32[]{:S(2)}, u32[]{:S(2)}) collective-permute-start(bf16[40,4096]{1,0:T(8,128)(2,1)S(1)} %pad_maximum_fusion.1), channel_id=1, source_target_pairs={{0,8},{2,6},{8,16},{10,2},{16,24},{18,10},{24,28},{26,18},{28,20},... | collective-permute-start | bytes 983048 | tf_op jit(solution)/shard_map/ppermute | solution.py:141
  14.9 2.2 %collective-permute-start.4 = (bf16[40,4096]{1,0:T(8,128)(2,1)S(1)}, bf16[40,4096]{1,0:T(8,128)(2,1)S(1)}, u32[]{:S(2)}, u32[]{:S(2)}) collective-permute-start(bf16[40,4096]{1,0:T(8,128)(2,1)S(1)} %pad_maximum_fusion.2), channel_id=1, source_target_pairs={{0,8},{2,6},{8,16},{10,2},{16,24},{18,10},{24,28},{26,18},{28,20},... | collective-permute-start | bytes 983048 | tf_op jit(solution)/shard_map/ppermute | solution.py:141
  19.7 1.6 %collective-permute-start.5 = (bf16[40,4096]{1,0:T(8,128)(2,1)S(1)}, bf16[40,4096]{1,0:T(8,128)(2,1)S(1)}, u32[]{:S(2)}, u32[]{:S(2)}) collective-permute-start(bf16[40,4096]{1,0:T(8,128)(2,1)S(1)} %pad_maximum_fusion.3), channel_id=1, source_target_pairs={{0,8},{2,6},{8,16},{10,2},{16,24},{18,10},{24,28},{26,18},{28,20},... | collective-permute-start | bytes 983048 | tf_op jit(solution)/shard_map/ppermute | solution.py:141
  22.5 2.2 %collective-permute-start.7 = (bf16[40,4096]{1,0:T(8,128)(2,1)S(1)}, bf16[40,4096]{1,0:T(8,128)(2,1)S(1)}, u32[]{:S(2)}, u32[]{:S(2)}) collective-permute-start(bf16[40,4096]{1,0:T(8,128)(2,1)S(1)} %pad_maximum_fusion.4), channel_id=1, source_target_pairs={{0,8},{2,6},{8,16},{10,2},{16,24},{18,10},{24,28},{26,18},{28,20},... | collective-permute-start | bytes 983048 | tf_op jit(solution)/shard_map/ppermute | solution.py:141
  24.7 2.1 %collective-permute-done.5 = bf16[40,4096]{1,0:T(8,128)(2,1)S(1)} collective-permute-done((bf16[40,4096]{1,0:T(8,128)(2,1)S(1)}, bf16[40,4096]{1,0:T(8,128)(2,1)S(1)}, u32[]{:S(2)}, u32[]{:S(2)}) %collective-permute-start.5) | collective-permute-done | bytes 327712 | tf_op jit(solution)/shard_map/ppermute | solution.py:141
  27.3 1.6 %collective-permute-start.9 = (bf16[40,4096]{1,0:T(8,128)(2,1)S(1)}, bf16[40,4096]{1,0:T(8,128)(2,1)S(1)}, u32[]{:S(2)}, u32[]{:S(2)}) collective-permute-start(bf16[40,4096]{1,0:T(8,128)(2,1)S(1)} %pad_maximum_fusion.5), channel_id=1, source_target_pairs={{0,8},{2,6},{8,16},{10,2},{16,24},{18,10},{24,28},{26,18},{28,20},... | collective-permute-start | bytes 983048 | tf_op jit(solution)/shard_map/ppermute | solution.py:141
  30.6 1.6 %collective-permute-start.10 = (bf16[40,4096]{1,0:T(8,128)(2,1)S(1)}, bf16[40,4096]{1,0:T(8,128)(2,1)S(1)}, u32[]{:S(2)}, u32[]{:S(2)}) collective-permute-start(bf16[40,4096]{1,0:T(8,128)(2,1)S(1)} %pad_maximum_fusion.6), channel_id=1, source_target_pairs={{0,8},{2,6},{8,16},{10,2},{16,24},{18,10},{24,28},{26,18},{28,20},... | collective-permute-start | bytes 983048 | tf_op jit(solution)/shard_map/ppermute | solution.py:141
  32.2 2.2 %collective-permute-done.9 = bf16[40,4096]{1,0:T(8,128)(2,1)S(1)} collective-permute-done((bf16[40,4096]{1,0:T(8,128)(2,1)S(1)}, bf16[40,4096]{1,0:T(8,128)(2,1)S(1)}, u32[]{:S(2)}, u32[]{:S(2)}) %collective-permute-start.9) | collective-permute-done | bytes 327712 | tf_op jit(solution)/shard_map/ppermute | solution.py:141
  34.7 1.6 %collective-permute-start.11 = (bf16[40,4096]{1,0:T(8,128)(2,1)S(1)}, bf16[40,4096]{1,0:T(8,128)(2,1)S(1)}, u32[]{:S(2)}, u32[]{:S(2)}) collective-permute-start(bf16[40,4096]{1,0:T(8,128)(2,1)S(1)} %pad_maximum_fusion.7), channel_id=1, source_target_pairs={{0,8},{2,6},{8,16},{10,2},{16,24},{18,10},{24,28},{26,18},{28,20},... | collective-permute-start | bytes 983048 | tf_op jit(solution)/shard_map/ppermute | solution.py:141
  38.2 1.6 %collective-permute-start.12 = (bf16[40,4096]{1,0:T(8,128)(2,1)S(1)}, bf16[40,4096]{1,0:T(8,128)(2,1)S(1)}, u32[]{:S(2)}, u32[]{:S(2)}) collective-permute-start(bf16[40,4096]{1,0:T(8,128)(2,1)S(1)} %pad_maximum_fusion.8), channel_id=1, source_target_pairs={{0,8},{2,6},{8,16},{10,2},{16,24},{18,10},{24,28},{26,18},{28,20},... | collective-permute-start | bytes 983048 | tf_op jit(solution)/shard_map/ppermute | solution.py:141
  39.8 2.0 %collective-permute-done.11 = bf16[40,4096]{1,0:T(8,128)(2,1)S(1)} collective-permute-done((bf16[40,4096]{1,0:T(8,128)(2,1)S(1)}, bf16[40,4096]{1,0:T(8,128)(2,1)S(1)}, u32[]{:S(2)}, u32[]{:S(2)}) %collective-permute-start.11) | collective-permute-done | bytes 327712 | tf_op jit(solution)/shard_map/ppermute | solution.py:141
  42.1 1.6 %collective-permute-start.13 = (bf16[40,4096]{1,0:T(8,128)(2,1)S(1)}, bf16[40,4096]{1,0:T(8,128)(2,1)S(1)}, u32[]{:S(2)}, u32[]{:S(2)}) collective-permute-start(bf16[40,4096]{1,0:T(8,128)(2,1)S(1)} %pad_maximum_fusion.9), channel_id=1, source_target_pairs={{0,8},{2,6},{8,16},{10,2},{16,24},{18,10},{24,28},{26,18},{28,20},... | collective-permute-start | bytes 983048 | tf_op jit(solution)/shard_map/ppermute | solution.py:141
  45.6 1.6 %collective-permute-start.14 = (bf16[40,4096]{1,0:T(8,128)(2,1)S(1)}, bf16[40,4096]{1,0:T(8,128)(2,1)S(1)}, u32[]{:S(2)}, u32[]{:S(2)}) collective-permute-start(bf16[40,4096]{1,0:T(8,128)(2,1)S(1)} %pad_maximum_fusion.10), channel_id=1, source_target_pairs={{0,8},{2,6},{8,16},{10,2},{16,24},{18,10},{24,28},{26,18},{28,20},... | collective-permute-start | bytes 983048 | tf_op jit(solution)/shard_map/ppermute | solution.py:141
  47.2 2.0 %collective-permute-done.13 = bf16[40,4096]{1,0:T(8,128)(2,1)S(1)} collective-permute-done((bf16[40,4096]{1,0:T(8,128)(2,1)S(1)}, bf16[40,4096]{1,0:T(8,128)(2,1)S(1)}, u32[]{:S(2)}, u32[]{:S(2)}) %collective-permute-start.13) | collective-permute-done | bytes 327712 | tf_op jit(solution)/shard_map/ppermute | solution.py:141
  49.4 1.6 %collective-permute-start.15 = (bf16[40,4096]{1,0:T(8,128)(2,1)S(1)}, bf16[40,4096]{1,0:T(8,128)(2,1)S(1)}, u32[]{:S(2)}, u32[]{:S(2)}) collective-permute-start(bf16[40,4096]{1,0:T(8,128)(2,1)S(1)} %pad_maximum_fusion.11), channel_id=1, source_target_pairs={{0,8},{2,6},{8,16},{10,2},{16,24},{18,10},{24,28},{26,18},{28,20},... | collective-permute-start | bytes 983048 | tf_op jit(solution)/shard_map/ppermute | solution.py:141
  53.0 1.6 %collective-permute-start.16 = (bf16[40,4096]{1,0:T(8,128)(2,1)S(1)}, bf16[40,4096]{1,0:T(8,128)(2,1)S(1)}, u32[]{:S(2)}, u32[]{:S(2)}) collective-permute-start(bf16[40,4096]{1,0:T(8,128)(2,1)S(1)} %pad_maximum_fusion.12), channel_id=1, source_target_pairs={{0,8},{2,6},{8,16},{10,2},{16,24},{18,10},{24,28},{26,18},{28,20},... | collective-permute-start | bytes 983048 | tf_op jit(solution)/shard_map/ppermute | solution.py:141
  54.6 2.0 %collective-permute-done.15 = bf16[40,4096]{1,0:T(8,128)(2,1)S(1)} collective-permute-done((bf16[40,4096]{1,0:T(8,128)(2,1)S(1)}, bf16[40,4096]{1,0:T(8,128)(2,1)S(1)}, u32[]{:S(2)}, u32[]{:S(2)}) %collective-permute-start.15) | collective-permute-done | bytes 327712 | tf_op jit(solution)/shard_map/ppermute | solution.py:141
  56.8 1.8 %collective-permute-start.17 = (bf16[40,4096]{1,0:T(8,128)(2,1)S(1)}, bf16[40,4096]{1,0:T(8,128)(2,1)S(1)}, u32[]{:S(2)}, u32[]{:S(2)}) collective-permute-start(bf16[40,4096]{1,0:T(8,128)(2,1)S(1)} %pad_maximum_fusion.13), channel_id=1, source_target_pairs={{0,8},{2,6},{8,16},{10,2},{16,24},{18,10},{24,28},{26,18},{28,20},... | collective-permute-start | bytes 983048 | tf_op jit(solution)/shard_map/ppermute | solution.py:141
  58.8 5.3 %collective-permute-done.17 = bf16[40,4096]{1,0:T(8,128)(2,1)S(1)} collective-permute-done((bf16[40,4096]{1,0:T(8,128)(2,1)S(1)}, bf16[40,4096]{1,0:T(8,128)(2,1)S(1)}, u32[]{:S(2)}, u32[]{:S(2)}) %collective-permute-start.17) | collective-permute-done | bytes 327712 | tf_op jit(solution)/shard_map/ppermute | solution.py:141
  67.8 4.3 %scores.1 = (bf16[512,256]{1,0:T(8,128)(2,1)S(1)}, bf16[512,256]{1,0:T(8,128)(2,1)S(1)}, f32[512,1]{1,0:T(8,128)S(1)}, bf16[256,4096]{1,0:T(8,128)(2,1)S(1)}) custom-call(bf16[128,4096]{1,0:T(8,128)(2,1)S(1)} %slice_dynamic-update-slice_fusion.refs_0_, bf16[128,4096]{1,0:T(8,128)(2,1)S(1)} %collective-permute-done.18.refs_1_, bf16[512,4096]{1,0:T(8,128)(2,1)S(1)} %copy-done, ...), custom_call_target="tpu_custom_call" | custom-call | flops 3221225472 | bytes 20971520 | tf_op jit(solution)/shard_map/scores/pallas_call | solution.py:190
  77.0 1.6 %collective-permute-start.41 = (bf16[2,2,16,2048]{3,2,0,1:T(8,128)(2,1)S(1)}, bf16[2,2,16,2048]{3,2,0,1:T(8,128)(2,1)S(1)}, u32[]{:S(2)}, u32[]{:S(2)}) collective-permute-start(bf16[2,2,16,2048]{3,2,0,1:T(8,128)(2,1)S(1)} %fusion.6), channel_id=1, source_target_pairs={{0,8},{2,10},{4,12},{6,14},{8,0},{10,2},{12,4},{14,6},{16,24},{18,... | collective-permute-start | bytes 786440 | tf_op jit(solution)/shard_map/ppermute | solution.py:264
  79.8 4.6 %collective-permute-done.37 = bf16[2,2,16,2048]{3,2,0,1:T(8,128)(2,1)S(1)} collective-permute-done((bf16[2,2,16,2048]{3,2,0,1:T(8,128)(2,1)S(1)}, bf16[2,2,16,2048]{3,2,0,1:T(8,128)(2,1)S(1)}, u32[]{:S(2)}, u32[]{:S(2)}) %collective-permute-start.37) | collective-permute-done | bytes 262176 | tf_op jit(solution)/shard_map/ppermute | solution.py:264
  84.5 1.6 %collective-permute-start.38 = (bf16[2,16,2048]{2,1,0:T(8,128)(2,1)S(1)}, bf16[2,16,2048]{2,1,0:T(8,128)(2,1)S(1)}, u32[]{:S(2)}, u32[]{:S(2)}) collective-permute-start(bf16[2,16,2048]{2,1,0:T(8,128)(2,1)S(1)} %fusion.10), channel_id=1, source_target_pairs={{0,8},{2,10},{4,12},{6,14},{8,0},{10,2},{12,4},{14,6},{16,24},{18,... | collective-permute-start | bytes 393224 | tf_op jit(solution)/shard_map/ppermute | solution.py:264
  87.3 2.3 %collective-permute-done.38 = bf16[2,16,2048]{2,1,0:T(8,128)(2,1)S(1)} collective-permute-done((bf16[2,16,2048]{2,1,0:T(8,128)(2,1)S(1)}, bf16[2,16,2048]{2,1,0:T(8,128)(2,1)S(1)}, u32[]{:S(2)}, u32[]{:S(2)}) %collective-permute-start.38) | collective-permute-done | bytes 131104 | tf_op jit(solution)/shard_map/ppermute | solution.py:264
  89.6 2.6 %collective-permute-start.39 = (bf16[16,2048]{1,0:T(8,128)(2,1)S(1)}, bf16[16,2048]{1,0:T(8,128)(2,1)S(1)}, u32[]{:S(2)}, u32[]{:S(2)}) collective-permute-start(bf16[16,2048]{1,0:T(8,128)(2,1)S(1)} %fusion.18), channel_id=1, source_target_pairs={{0,16},{2,18},{4,20},{6,22},{8,24},{10,26},{12,28},{14,30},{16,0},... | collective-permute-start | bytes 196616 | tf_op jit(solution)/shard_map/ppermute | solution.py:264
  93.3 3.3 %collective-permute-done.39 = bf16[16,2048]{1,0:T(8,128)(2,1)S(1)} collective-permute-done((bf16[16,2048]{1,0:T(8,128)(2,1)S(1)}, bf16[16,2048]{1,0:T(8,128)(2,1)S(1)}, u32[]{:S(2)}, u32[]{:S(2)}) %collective-permute-start.39) | collective-permute-done | bytes 65568 | tf_op jit(solution)/shard_map/ppermute | solution.py:264
  96.6 1.6 %collective-permute-start.40 = (f32[16,2048]{1,0:T(8,128)S(1)}, f32[16,2048]{1,0:T(8,128)S(1)}, u32[]{:S(2)}, u32[]{:S(2)}) collective-permute-start(f32[16,2048]{1,0:T(8,128)S(1)} %fusion.13), channel_id=1, source_target_pairs={{0,1},{1,0},{2,3},{3,2},{4,5},{5,4},{6,7},{7,6},{8,9},{9,8},{10,11... | collective-permute-start | bytes 393224 | tf_op jit(solution)/shard_map/ppermute | solution.py:274
  98.2 1.6 %collective-permute-start.44 = (f32[16,2048]{1,0:T(8,128)S(1)}, f32[16,2048]{1,0:T(8,128)S(1)}, u32[]{:S(2)}, u32[]{:S(2)}) collective-permute-start(f32[16,2048]{1,0:T(8,128)S(1)} %fusion.12), channel_id=1, source_target_pairs={{0,1},{1,0},{2,3},{3,2},{4,5},{5,4},{6,7},{7,6},{8,9},{9,8},{10,11... | collective-permute-start | bytes 393224 | tf_op jit(solution)/shard_map/ppermute | solution.py:274
  99.7 3.3 %multiply_convert_fusion = bf16[512,4096]{1,0:T(8,128)(2,1)} fusion(f32[512,4096]{1,0:T(8,128)S(1)} %fusion.43, bf16[512,256]{1,0:T(8,128)(2,1)S(1)} %get-tuple-element.61, bf16[256,4096]{1,0:T(8,128)(2,1)S(1)} %get-tuple-element.62), kind=kOutput, calls=%fused_computation | convolution fusion | flops 1080033280 | bytes 14942208 | tf_op jit(solution)/shard_map/dot_general | solution.py:279
  (171 shorter events, 31.3 us)
Async XLA Ops:
  4.5 5.2 %collective-permute-start.2 = (bf16[64,4096]{1,0:T(8,128)(2,1)S(1)}, bf16[64,4096]{1,0:T(8,128)(2,1)S(1)}, u32[]{:S(2)}, u32[]{:S(2)}) collective-permute-start(bf16[64,4096]{1,0:T(8,128)(2,1)S(1)} %get-tuple-element.38), channel_id=1, source_target_pairs={{0,2},{2,0},{4,6},{6,4},{8,10},{10,8},{12,14},{14,12},{16,18},{18,... | collective-permute-start | bytes 1572872 | tf_op jit(solution)/shard_map/ppermute | solution.py:97
  6.5 5.9 %collective-permute-start.27 = (bf16[32,4096]{1,0:T(8,128)(2,1)S(1)}, bf16[32,4096]{1,0:T(8,128)(2,1)S(1)}, u32[]{:S(2)}, u32[]{:S(2)}) collective-permute-start(bf16[32,4096]{1,0:T(8,128)(2,1)S(1)} %get-tuple-element.82), channel_id=1, source_target_pairs={{0,2},{2,0},{4,6},{6,4},{8,10},{10,8},{12,14},{14,12},{16,18},{18,... | collective-permute-start | bytes 786440 | tf_op jit(solution)/shard_map/ppermute | solution.py:115
  7.0 7.7 %collective-permute-start.1 = (bf16[40,4096]{1,0:T(8,128)(2,1)S(1)}, bf16[40,4096]{1,0:T(8,128)(2,1)S(1)}, u32[]{:S(2)}, u32[]{:S(2)}) collective-permute-start(bf16[40,4096]{1,0:T(8,128)(2,1)S(1)} %pad_maximum_fusion), channel_id=1, source_target_pairs={{0,8},{2,6},{8,16},{10,2},{16,24},{18,10},{24,28},{26,18},{28,20},... | collective-permute-start | bytes 983048 | tf_op jit(solution)/shard_map/ppermute | solution.py:141
  9.8 8.3 %collective-permute-start.3 = (bf16[40,4096]{1,0:T(8,128)(2,1)S(1)}, bf16[40,4096]{1,0:T(8,128)(2,1)S(1)}, u32[]{:S(2)}, u32[]{:S(2)}) collective-permute-start(bf16[40,4096]{1,0:T(8,128)(2,1)S(1)} %pad_maximum_fusion.1), channel_id=1, source_target_pairs={{0,8},{2,6},{8,16},{10,2},{16,24},{18,10},{24,28},{26,18},{28,20},... | collective-permute-start | bytes 983048 | tf_op jit(solution)/shard_map/ppermute | solution.py:141
  11.8 15.0 %collective-permute-start.8 = (bf16[256,4096]{1,0:T(8,128)(2,1)S(1)}, bf16[256,4096]{1,0:T(8,128)(2,1)S(1)}, u32[]{:S(2)}, u32[]{:S(2)}) collective-permute-start(bf16[256,4096]{1,0:T(8,128)(2,1)S(1)} %copy-done.4), channel_id=1, source_target_pairs={{0,2},{2,0},{4,6},{6,4},{8,10},{10,8},{12,14},{14,12},{16,18},{18,... | collective-permute-start | bytes 6291464 | tf_op jit(solution)/shard_map/ppermute | solution.py:102
  12.3 9.7 %collective-permute-start.6 = (bf16[256,4096]{1,0:T(8,128)(2,1)S(1)}, bf16[256,4096]{1,0:T(8,128)(2,1)S(1)}, u32[]{:S(2)}, u32[]{:S(2)}) collective-permute-start(bf16[256,4096]{1,0:T(8,128)(2,1)S(1)} %copy-done.2), channel_id=1, source_target_pairs={{0,2},{2,0},{4,6},{6,4},{8,10},{10,8},{12,14},{14,12},{16,18},{18,... | collective-permute-start | bytes 6291464 | tf_op jit(solution)/shard_map/ppermute | solution.py:102
  14.8 4.9 %collective-permute-start.28 = (bf16[32,4096]{1,0:T(8,128)(2,1)S(1)}, bf16[32,4096]{1,0:T(8,128)(2,1)S(1)}, u32[]{:S(2)}, u32[]{:S(2)}) collective-permute-start(bf16[32,4096]{1,0:T(8,128)(2,1)S(1)} %get-tuple-element.80), channel_id=1, source_target_pairs={{0,2},{2,0},{4,6},{6,4},{8,10},{10,8},{12,14},{14,12},{16,18},{18,... | collective-permute-start | bytes 786440 | tf_op jit(solution)/shard_map/ppermute | solution.py:115
  14.9 7.1 %collective-permute-start.4 = (bf16[40,4096]{1,0:T(8,128)(2,1)S(1)}, bf16[40,4096]{1,0:T(8,128)(2,1)S(1)}, u32[]{:S(2)}, u32[]{:S(2)}) collective-permute-start(bf16[40,4096]{1,0:T(8,128)(2,1)S(1)} %pad_maximum_fusion.2), channel_id=1, source_target_pairs={{0,8},{2,6},{8,16},{10,2},{16,24},{18,10},{24,28},{26,18},{28,20},... | collective-permute-start | bytes 983048 | tf_op jit(solution)/shard_map/ppermute | solution.py:141
  19.7 7.1 %collective-permute-start.5 = (bf16[40,4096]{1,0:T(8,128)(2,1)S(1)}, bf16[40,4096]{1,0:T(8,128)(2,1)S(1)}, u32[]{:S(2)}, u32[]{:S(2)}) collective-permute-start(bf16[40,4096]{1,0:T(8,128)(2,1)S(1)} %pad_maximum_fusion.3), channel_id=1, source_target_pairs={{0,8},{2,6},{8,16},{10,2},{16,24},{18,10},{24,28},{26,18},{28,20},... | collective-permute-start | bytes 983048 | tf_op jit(solution)/shard_map/ppermute | solution.py:141
  22.4 6.6 %collective-permute-start.29 = (bf16[32,4096]{1,0:T(8,128)(2,1)S(1)}, bf16[32,4096]{1,0:T(8,128)(2,1)S(1)}, u32[]{:S(2)}, u32[]{:S(2)}) collective-permute-start(bf16[32,4096]{1,0:T(8,128)(2,1)S(1)} %get-tuple-element.78), channel_id=1, source_target_pairs={{0,2},{2,0},{4,6},{6,4},{8,10},{10,8},{12,14},{14,12},{16,18},{18,... | collective-permute-start | bytes 786440 | tf_op jit(solution)/shard_map/ppermute | solution.py:115
  22.5 7.8 %collective-permute-start.7 = (bf16[40,4096]{1,0:T(8,128)(2,1)S(1)}, bf16[40,4096]{1,0:T(8,128)(2,1)S(1)}, u32[]{:S(2)}, u32[]{:S(2)}) collective-permute-start(bf16[40,4096]{1,0:T(8,128)(2,1)S(1)} %pad_maximum_fusion.4), channel_id=1, source_target_pairs={{0,8},{2,6},{8,16},{10,2},{16,24},{18,10},{24,28},{26,18},{28,20},... | collective-permute-start | bytes 983048 | tf_op jit(solution)/shard_map/ppermute | solution.py:141
  27.3 7.1 %collective-permute-start.9 = (bf16[40,4096]{1,0:T(8,128)(2,1)S(1)}, bf16[40,4096]{1,0:T(8,128)(2,1)S(1)}, u32[]{:S(2)}, u32[]{:S(2)}) collective-permute-start(bf16[40,4096]{1,0:T(8,128)(2,1)S(1)} %pad_maximum_fusion.5), channel_id=1, source_target_pairs={{0,8},{2,6},{8,16},{10,2},{16,24},{18,10},{24,28},{26,18},{28,20},... | collective-permute-start | bytes 983048 | tf_op jit(solution)/shard_map/ppermute | solution.py:141
  30.4 5.9 %collective-permute-start.30 = (bf16[32,4096]{1,0:T(8,128)(2,1)S(1)}, bf16[32,4096]{1,0:T(8,128)(2,1)S(1)}, u32[]{:S(2)}, u32[]{:S(2)}) collective-permute-start(bf16[32,4096]{1,0:T(8,128)(2,1)S(1)} %get-tuple-element.76), channel_id=1, source_target_pairs={{0,2},{2,0},{4,6},{6,4},{8,10},{10,8},{12,14},{14,12},{16,18},{18,... | collective-permute-start | bytes 786440 | tf_op jit(solution)/shard_map/ppermute | solution.py:115
  30.6 7.4 %collective-permute-start.10 = (bf16[40,4096]{1,0:T(8,128)(2,1)S(1)}, bf16[40,4096]{1,0:T(8,128)(2,1)S(1)}, u32[]{:S(2)}, u32[]{:S(2)}) collective-permute-start(bf16[40,4096]{1,0:T(8,128)(2,1)S(1)} %pad_maximum_fusion.6), channel_id=1, source_target_pairs={{0,8},{2,6},{8,16},{10,2},{16,24},{18,10},{24,28},{26,18},{28,20},... | collective-permute-start | bytes 983048 | tf_op jit(solution)/shard_map/ppermute | solution.py:141
  34.7 7.1 %collective-permute-start.11 = (bf16[40,4096]{1,0:T(8,128)(2,1)S(1)}, bf16[40,4096]{1,0:T(8,128)(2,1)S(1)}, u32[]{:S(2)}, u32[]{:S(2)}) collective-permute-start(bf16[40,4096]{1,0:T(8,128)(2,1)S(1)} %pad_maximum_fusion.7), channel_id=1, source_target_pairs={{0,8},{2,6},{8,16},{10,2},{16,24},{18,10},{24,28},{26,18},{28,20},... | collective-permute-start | bytes 983048 | tf_op jit(solution)/shard_map/ppermute | solution.py:141
  38.1 5.7 %collective-permute-start.31 = (bf16[32,4096]{1,0:T(8,128)(2,1)S(1)}, bf16[32,4096]{1,0:T(8,128)(2,1)S(1)}, u32[]{:S(2)}, u32[]{:S(2)}) collective-permute-start(bf16[32,4096]{1,0:T(8,128)(2,1)S(1)} %get-tuple-element.74), channel_id=1, source_target_pairs={{0,2},{2,0},{4,6},{6,4},{8,10},{10,8},{12,14},{14,12},{16,18},{18,... | collective-permute-start | bytes 786440 | tf_op jit(solution)/shard_map/ppermute | solution.py:115
  38.2 7.1 %collective-permute-start.12 = (bf16[40,4096]{1,0:T(8,128)(2,1)S(1)}, bf16[40,4096]{1,0:T(8,128)(2,1)S(1)}, u32[]{:S(2)}, u32[]{:S(2)}) collective-permute-start(bf16[40,4096]{1,0:T(8,128)(2,1)S(1)} %pad_maximum_fusion.8), channel_id=1, source_target_pairs={{0,8},{2,6},{8,16},{10,2},{16,24},{18,10},{24,28},{26,18},{28,20},... | collective-permute-start | bytes 983048 | tf_op jit(solution)/shard_map/ppermute | solution.py:141
  42.1 7.1 %collective-permute-start.13 = (bf16[40,4096]{1,0:T(8,128)(2,1)S(1)}, bf16[40,4096]{1,0:T(8,128)(2,1)S(1)}, u32[]{:S(2)}, u32[]{:S(2)}) collective-permute-start(bf16[40,4096]{1,0:T(8,128)(2,1)S(1)} %pad_maximum_fusion.9), channel_id=1, source_target_pairs={{0,8},{2,6},{8,16},{10,2},{16,24},{18,10},{24,28},{26,18},{28,20},... | collective-permute-start | bytes 983048 | tf_op jit(solution)/shard_map/ppermute | solution.py:141
  45.4 5.7 %collective-permute-start.32 = (bf16[32,4096]{1,0:T(8,128)(2,1)S(1)}, bf16[32,4096]{1,0:T(8,128)(2,1)S(1)}, u32[]{:S(2)}, u32[]{:S(2)}) collective-permute-start(bf16[32,4096]{1,0:T(8,128)(2,1)S(1)} %get-tuple-element.72), channel_id=1, source_target_pairs={{0,2},{2,0},{4,6},{6,4},{8,10},{10,8},{12,14},{14,12},{16,18},{18,... | collective-permute-start | bytes 786440 | tf_op jit(solution)/shard_map/ppermute | solution.py:115
  45.6 7.1 %collective-permute-start.14 = (bf16[40,4096]{1,0:T(8,128)(2,1)S(1)}, bf16[40,4096]{1,0:T(8,128)(2,1)S(1)}, u32[]{:S(2)}, u32[]{:S(2)}) collective-permute-start(bf16[40,4096]{1,0:T(8,128)(2,1)S(1)} %pad_maximum_fusion.10), channel_id=1, source_target_pairs={{0,8},{2,6},{8,16},{10,2},{16,24},{18,10},{24,28},{26,18},{28,20},... | collective-permute-start | bytes 983048 | tf_op jit(solution)/shard_map/ppermute | solution.py:141
  49.4 7.1 %collective-permute-start.15 = (bf16[40,4096]{1,0:T(8,128)(2,1)S(1)}, bf16[40,4096]{1,0:T(8,128)(2,1)S(1)}, u32[]{:S(2)}, u32[]{:S(2)}) collective-permute-start(bf16[40,4096]{1,0:T(8,128)(2,1)S(1)} %pad_maximum_fusion.11), channel_id=1, source_target_pairs={{0,8},{2,6},{8,16},{10,2},{16,24},{18,10},{24,28},{26,18},{28,20},... | collective-permute-start | bytes 983048 | tf_op jit(solution)/shard_map/ppermute | solution.py:141
  52.8 5.9 %collective-permute-start.33 = (bf16[32,4096]{1,0:T(8,128)(2,1)S(1)}, bf16[32,4096]{1,0:T(8,128)(2,1)S(1)}, u32[]{:S(2)}, u32[]{:S(2)}) collective-permute-start(bf16[32,4096]{1,0:T(8,128)(2,1)S(1)} %get-tuple-element.70), channel_id=1, source_target_pairs={{0,2},{2,0},{4,6},{6,4},{8,10},{10,8},{12,14},{14,12},{16,18},{18,... | collective-permute-start | bytes 786440 | tf_op jit(solution)/shard_map/ppermute | solution.py:115
  53.0 11.4 %collective-permute-start.16 = (bf16[40,4096]{1,0:T(8,128)(2,1)S(1)}, bf16[40,4096]{1,0:T(8,128)(2,1)S(1)}, u32[]{:S(2)}, u32[]{:S(2)}) collective-permute-start(bf16[40,4096]{1,0:T(8,128)(2,1)S(1)} %pad_maximum_fusion.12), channel_id=1, source_target_pairs={{0,8},{2,6},{8,16},{10,2},{16,24},{18,10},{24,28},{26,18},{28,20},... | collective-permute-start | bytes 983048 | tf_op jit(solution)/shard_map/ppermute | solution.py:141
  56.8 7.3 %collective-permute-start.17 = (bf16[40,4096]{1,0:T(8,128)(2,1)S(1)}, bf16[40,4096]{1,0:T(8,128)(2,1)S(1)}, u32[]{:S(2)}, u32[]{:S(2)}) collective-permute-start(bf16[40,4096]{1,0:T(8,128)(2,1)S(1)} %pad_maximum_fusion.13), channel_id=1, source_target_pairs={{0,8},{2,6},{8,16},{10,2},{16,24},{18,10},{24,28},{26,18},{28,20},... | collective-permute-start | bytes 983048 | tf_op jit(solution)/shard_map/ppermute | solution.py:141
  75.9 8.5 %collective-permute-start.37 = (bf16[2,2,16,2048]{3,2,0,1:T(8,128)(2,1)S(1)}, bf16[2,2,16,2048]{3,2,0,1:T(8,128)(2,1)S(1)}, u32[]{:S(2)}, u32[]{:S(2)}) collective-permute-start(bf16[2,2,16,2048]{3,2,0,1:T(8,128)(2,1)S(1)} %fusion.7), channel_id=1, source_target_pairs={{0,4},{2,6},{4,0},{6,2},{8,12},{10,14},{12,8},{14,10},{16,20},{18,... | collective-permute-start | bytes 786440 | tf_op jit(solution)/shard_map/ppermute | solution.py:264
  77.0 9.2 %collective-permute-start.41 = (bf16[2,2,16,2048]{3,2,0,1:T(8,128)(2,1)S(1)}, bf16[2,2,16,2048]{3,2,0,1:T(8,128)(2,1)S(1)}, u32[]{:S(2)}, u32[]{:S(2)}) collective-permute-start(bf16[2,2,16,2048]{3,2,0,1:T(8,128)(2,1)S(1)} %fusion.6), channel_id=1, source_target_pairs={{0,8},{2,10},{4,12},{6,14},{8,0},{10,2},{12,4},{14,6},{16,24},{18,... | collective-permute-start | bytes 786440 | tf_op jit(solution)/shard_map/ppermute | solution.py:264
  84.5 5.0 %collective-permute-start.38 = (bf16[2,16,2048]{2,1,0:T(8,128)(2,1)S(1)}, bf16[2,16,2048]{2,1,0:T(8,128)(2,1)S(1)}, u32[]{:S(2)}, u32[]{:S(2)}) collective-permute-start(bf16[2,16,2048]{2,1,0:T(8,128)(2,1)S(1)} %fusion.10), channel_id=1, source_target_pairs={{0,8},{2,10},{4,12},{6,14},{8,0},{10,2},{12,4},{14,6},{16,24},{18,... | collective-permute-start | bytes 393224 | tf_op jit(solution)/shard_map/ppermute | solution.py:264
  86.2 5.9 %collective-permute-start.42 = (bf16[2,16,2048]{2,1,0:T(8,128)(2,1)S(1)}, bf16[2,16,2048]{2,1,0:T(8,128)(2,1)S(1)}, u32[]{:S(2)}, u32[]{:S(2)}) collective-permute-start(bf16[2,16,2048]{2,1,0:T(8,128)(2,1)S(1)} %fusion.11), channel_id=1, source_target_pairs={{0,4},{2,6},{4,0},{6,2},{8,12},{10,14},{12,8},{14,10},{16,20},{18,... | collective-permute-start | bytes 393224 | tf_op jit(solution)/shard_map/ppermute | solution.py:264
  89.6 7.0 %collective-permute-start.39 = (bf16[16,2048]{1,0:T(8,128)(2,1)S(1)}, bf16[16,2048]{1,0:T(8,128)(2,1)S(1)}, u32[]{:S(2)}, u32[]{:S(2)}) collective-permute-start(bf16[16,2048]{1,0:T(8,128)(2,1)S(1)} %fusion.18), channel_id=1, source_target_pairs={{0,16},{2,18},{4,20},{6,22},{8,24},{10,26},{12,28},{14,30},{16,0},... | collective-permute-start | bytes 196616 | tf_op jit(solution)/shard_map/ppermute | solution.py:264
  92.2 5.9 %collective-permute-start.43 = (bf16[16,2048]{1,0:T(8,128)(2,1)S(1)}, bf16[16,2048]{1,0:T(8,128)(2,1)S(1)}, u32[]{:S(2)}, u32[]{:S(2)}) collective-permute-start(bf16[16,2048]{1,0:T(8,128)(2,1)S(1)} %fusion.19), channel_id=1, source_target_pairs={{0,16},{2,18},{4,20},{6,22},{8,24},{10,26},{12,28},{14,30},{16,0},... | collective-permute-start | bytes 196616 | tf_op jit(solution)/shard_map/ppermute | solution.py:264
  96.6 7.2 %collective-permute-start.40 = (f32[16,2048]{1,0:T(8,128)S(1)}, f32[16,2048]{1,0:T(8,128)S(1)}, u32[]{:S(2)}, u32[]{:S(2)}) collective-permute-start(f32[16,2048]{1,0:T(8,128)S(1)} %fusion.13), channel_id=1, source_target_pairs={{0,1},{1,0},{2,3},{3,2},{4,5},{5,4},{6,7},{7,6},{8,9},{9,8},{10,11... | collective-permute-start | bytes 393224 | tf_op jit(solution)/shard_map/ppermute | solution.py:274
  98.2 5.6 %collective-permute-start.44 = (f32[16,2048]{1,0:T(8,128)S(1)}, f32[16,2048]{1,0:T(8,128)S(1)}, u32[]{:S(2)}, u32[]{:S(2)}) collective-permute-start(f32[16,2048]{1,0:T(8,128)S(1)} %fusion.12), channel_id=1, source_target_pairs={{0,1},{1,0},{2,3},{3,2},{4,5},{5,4},{6,7},{7,6},{8,9},{9,8},{10,11... | collective-permute-start | bytes 393224 | tf_op jit(solution)/shard_map/ppermute | solution.py:274
  (22 other events, 76.3 us)

commit v8 on v7

--- a/solution.py
+++ b/solution.py
@@ -111,8 +111,9 @@
     moving = [own_rows(i, 0) for i in range(2)]
     riding = [passages[:sub], passages[sub:]]
 
-    def keep(i, t, sent):
-        other = lax.ppermute(sent, "wide", swap)
+    def keep(i, t, sent, other=None):
+        if other is None:
+            other = lax.ppermute(sent, "wide", swap)
         for side, away, piece in ((core, distance, sent), (1 - core, distance_other, other)):
             slot = t - away
             take = (slot >= 0) & (slot < n_chunk)
@@ -140,11 +141,18 @@
             lead = sent
             came[i] = lax.ppermute(sent, "wide", pairs)
             keep(i, t, sent[:STEP])
+    rows_other = lax.ppermute(rows, "wide", swap)
     for i in (1, 0):
         arrive(i, rounds - 1, came[i])
     for i in (1, 0):
-        keep(i, rounds, moving[i])
-    return pools[0], pools[1], rows
+        if rounds > n_chip - 1:
+            keep(i, rounds, moving[i])
+            continue
+        other = lax.ppermute(jnp.concatenate([riding[i], moving[i]], 0), "wide", swap)
+        origin = chip_at((here + turn * rounds + n_chip) % n_chip)
+        rows_other = put_rows(rows_other, other[:sub], (origin ^ chip) * (block // 8) + i * (sub // 8))
+        keep(i, rounds, moving[i], other[sub:])
+    return pools[0], pools[1], [rows, rows_other]
 
 
 def dot_t(a, b):
@@ -222,8 +230,7 @@
     n_pass = block * n_dev
     swap = swap_pairs(n_dev, 1)
     across = [(0, 1), (1, 0)]
-    pool_s, pool_t, rows = gather_rows(bank_student, bank_teacher, passages, owner[0], index, core)
-    pass_parts = [rows, lax.ppermute(rows, "wide", swap)]
+    pool_s, pool_t, pass_parts = gather_rows(bank_student, bank_teacher, passages, owner[0], index, core)
     chip_of = (positives // (2 * block)) ^ chip
     core_of = ((positives // block) % 2) ^ core
     column = (core_of * n_chip + chip_of) * block + positives % block

time: 105 us -> 104 us (level)
    ppermute x16 -> x14, waiting for transfers between devices: 3.21 us -> 2.2 us  [keep(): other = lax.ppermute(sent, 'wide', swap)]
  transfers between devices with their start and end apart: 45 -> 45, of which waited for: 23 -> 22; matrix products, arithmetic and copies ran while one was open for 11% -> 11% of each run, Pallas kernels for 0% -> 0%
where the time goes in v8:
time: 104 us
  starting transfers between devices  40.9 us (39%)
  waiting for transfers between devices  39.2 us (38%)
  matrix products  6.42 us (6%)
  other arithmetic  5.44 us (5%)
  Pallas kernels  4.46 us (4%)
  local copies, waits for them, and re-layouts  4.26 us (4%)
  between operations  2.81 us (3%)
    ppermute x14, starting transfers between devices, gather_rows(): came[i] = lax.ppermute(sent, 'wide', pairs)  25.1 us
    ppermute x14, waiting for transfers between devices, gather_rows(): came[i] = lax.ppermute(sent, 'wide', pairs)  24.2 us
    ppermute x6, waiting for transfers between devices, body(): got = lax.ppermute(sent[h], 'wide', pairs_of[orders[h][step]])  10.3 us
    ppermute x6, starting transfers between devices, body(): got = lax.ppermute(sent[h], 'wide', pairs_of[orders[h][step]])  8.95 us
    pallas_call x1, Pallas kernels, tail(): pl.pallas_call(functools.partial(tail_kernel, scale, len(pass_parts)), ou...  4.33 us
    dot_general x1, matrix products, body(): jnp.dot(late_p, pieces, preferred_element_type=jnp.float32)  3.28 us
    unnamed x18, local copies, waits for them, and re-layouts  3.21 us
    ppermute x2, starting transfers between devices, body(): sums = [x + lax.ppermute(x, 'dp', across) for x in sums]  3.07 us
  transfers between devices with their start and end apart: 45, of which 22 were waited for; matrix products, arithmetic and copies ran while one was open for 11% of the time, Pallas kernels for 0%

profile of v8, /device:TPU:0, one launch (start us, length us, event | category | flops | bytes accessed | tf_op | source)
XLA Modules:
  0.0 103.5 jit_solution(14277394024916404232)
XLA Ops:
  0.7 1.6 %copy-done.1 = bf16[256,4096]{1,0:T(8,128)(2,1)S(1)} copy-done((bf16[256,4096]{1,0:T(8,128)(2,1)S(1)}, bf16[256,4096]{1,0:T(8,128)(2,1)}, u32[]{:S(2)}) %copy-start.1) | copy-done | bytes 2097176
  2.2 1.6 %copy-done.3 = bf16[256,4096]{1,0:T(8,128)(2,1)S(1)} copy-done((bf16[256,4096]{1,0:T(8,128)(2,1)S(1)}, bf16[256,4096]{1,0:T(8,128)(2,1)}, u32[]{:S(2)}) %copy-start.3) | copy-done | bytes 2097176
  7.0 2.7 %collective-permute-start.1 = (bf16[40,4096]{1,0:T(8,128)(2,1)S(1)}, bf16[40,4096]{1,0:T(8,128)(2,1)S(1)}, u32[]{:S(2)}, u32[]{:S(2)}) collective-permute-start(bf16[40,4096]{1,0:T(8,128)(2,1)S(1)} %pad_maximum_fusion), channel_id=1, source_target_pairs={{0,8},{2,6},{8,16},{10,2},{16,24},{18,10},{24,28},{26,18},{28,20},... | collective-permute-start | bytes 983048 | tf_op jit(solution)/shard_map/ppermute | solution.py:142
  9.8 1.6 %collective-permute-start.3 = (bf16[40,4096]{1,0:T(8,128)(2,1)S(1)}, bf16[40,4096]{1,0:T(8,128)(2,1)S(1)}, u32[]{:S(2)}, u32[]{:S(2)}) collective-permute-start(bf16[40,4096]{1,0:T(8,128)(2,1)S(1)} %pad_maximum_fusion.1), channel_id=1, source_target_pairs={{0,8},{2,6},{8,16},{10,2},{16,24},{18,10},{24,28},{26,18},{28,20},... | collective-permute-start | bytes 983048 | tf_op jit(solution)/shard_map/ppermute | solution.py:142
  14.9 2.2 %collective-permute-start.4 = (bf16[40,4096]{1,0:T(8,128)(2,1)S(1)}, bf16[40,4096]{1,0:T(8,128)(2,1)S(1)}, u32[]{:S(2)}, u32[]{:S(2)}) collective-permute-start(bf16[40,4096]{1,0:T(8,128)(2,1)S(1)} %pad_maximum_fusion.2), channel_id=1, source_target_pairs={{0,8},{2,6},{8,16},{10,2},{16,24},{18,10},{24,28},{26,18},{28,20},... | collective-permute-start | bytes 983048 | tf_op jit(solution)/shard_map/ppermute | solution.py:142
  19.7 1.6 %collective-permute-start.5 = (bf16[40,4096]{1,0:T(8,128)(2,1)S(1)}, bf16[40,4096]{1,0:T(8,128)(2,1)S(1)}, u32[]{:S(2)}, u32[]{:S(2)}) collective-permute-start(bf16[40,4096]{1,0:T(8,128)(2,1)S(1)} %pad_maximum_fusion.3), channel_id=1, source_target_pairs={{0,8},{2,6},{8,16},{10,2},{16,24},{18,10},{24,28},{26,18},{28,20},... | collective-permute-start | bytes 983048 | tf_op jit(solution)/shard_map/ppermute | solution.py:142
  22.5 2.2 %collective-permute-start.7 = (bf16[40,4096]{1,0:T(8,128)(2,1)S(1)}, bf16[40,4096]{1,0:T(8,128)(2,1)S(1)}, u32[]{:S(2)}, u32[]{:S(2)}) collective-permute-start(bf16[40,4096]{1,0:T(8,128)(2,1)S(1)} %pad_maximum_fusion.4), channel_id=1, source_target_pairs={{0,8},{2,6},{8,16},{10,2},{16,24},{18,10},{24,28},{26,18},{28,20},... | collective-permute-start | bytes 983048 | tf_op jit(solution)/shard_map/ppermute | solution.py:142
  24.7 2.1 %collective-permute-done.5 = bf16[40,4096]{1,0:T(8,128)(2,1)S(1)} collective-permute-done((bf16[40,4096]{1,0:T(8,128)(2,1)S(1)}, bf16[40,4096]{1,0:T(8,128)(2,1)S(1)}, u32[]{:S(2)}, u32[]{:S(2)}) %collective-permute-start.5) | collective-permute-done | bytes 327712 | tf_op jit(solution)/shard_map/ppermute | solution.py:142
  27.3 1.6 %collective-permute-start.9 = (bf16[40,4096]{1,0:T(8,128)(2,1)S(1)}, bf16[40,4096]{1,0:T(8,128)(2,1)S(1)}, u32[]{:S(2)}, u32[]{:S(2)}) collective-permute-start(bf16[40,4096]{1,0:T(8,128)(2,1)S(1)} %pad_maximum_fusion.5), channel_id=1, source_target_pairs={{0,8},{2,6},{8,16},{10,2},{16,24},{18,10},{24,28},{26,18},{28,20},... | collective-permute-start | bytes 983048 | tf_op jit(solution)/shard_map/ppermute | solution.py:142
  30.6 1.6 %collective-permute-start.10 = (bf16[40,4096]{1,0:T(8,128)(2,1)S(1)}, bf16[40,4096]{1,0:T(8,128)(2,1)S(1)}, u32[]{:S(2)}, u32[]{:S(2)}) collective-permute-start(bf16[40,4096]{1,0:T(8,128)(2,1)S(1)} %pad_maximum_fusion.6), channel_id=1, source_target_pairs={{0,8},{2,6},{8,16},{10,2},{16,24},{18,10},{24,28},{26,18},{28,20},... | collective-permute-start | bytes 983048 | tf_op jit(solution)/shard_map/ppermute | solution.py:142
  32.2 2.2 %collective-permute-done.9 = bf16[40,4096]{1,0:T(8,128)(2,1)S(1)} collective-permute-done((bf16[40,4096]{1,0:T(8,128)(2,1)S(1)}, bf16[40,4096]{1,0:T(8,128)(2,1)S(1)}, u32[]{:S(2)}, u32[]{:S(2)}) %collective-permute-start.9) | collective-permute-done | bytes 327712 | tf_op jit(solution)/shard_map/ppermute | solution.py:142
  34.7 1.6 %collective-permute-start.11 = (bf16[40,4096]{1,0:T(8,128)(2,1)S(1)}, bf16[40,4096]{1,0:T(8,128)(2,1)S(1)}, u32[]{:S(2)}, u32[]{:S(2)}) collective-permute-start(bf16[40,4096]{1,0:T(8,128)(2,1)S(1)} %pad_maximum_fusion.7), channel_id=1, source_target_pairs={{0,8},{2,6},{8,16},{10,2},{16,24},{18,10},{24,28},{26,18},{28,20},... | collective-permute-start | bytes 983048 | tf_op jit(solution)/shard_map/ppermute | solution.py:142
  38.2 1.6 %collective-permute-start.12 = (bf16[40,4096]{1,0:T(8,128)(2,1)S(1)}, bf16[40,4096]{1,0:T(8,128)(2,1)S(1)}, u32[]{:S(2)}, u32[]{:S(2)}) collective-permute-start(bf16[40,4096]{1,0:T(8,128)(2,1)S(1)} %pad_maximum_fusion.8), channel_id=1, source_target_pairs={{0,8},{2,6},{8,16},{10,2},{16,24},{18,10},{24,28},{26,18},{28,20},... | collective-permute-start | bytes 983048 | tf_op jit(solution)/shard_map/ppermute | solution.py:142
  39.8 2.0 %collective-permute-done.11 = bf16[40,4096]{1,0:T(8,128)(2,1)S(1)} collective-permute-done((bf16[40,4096]{1,0:T(8,128)(2,1)S(1)}, bf16[40,4096]{1,0:T(8,128)(2,1)S(1)}, u32[]{:S(2)}, u32[]{:S(2)}) %collective-permute-start.11) | collective-permute-done | bytes 327712 | tf_op jit(solution)/shard_map/ppermute | solution.py:142
  42.1 1.6 %collective-permute-start.13 = (bf16[40,4096]{1,0:T(8,128)(2,1)S(1)}, bf16[40,4096]{1,0:T(8,128)(2,1)S(1)}, u32[]{:S(2)}, u32[]{:S(2)}) collective-permute-start(bf16[40,4096]{1,0:T(8,128)(2,1)S(1)} %pad_maximum_fusion.9), channel_id=1, source_target_pairs={{0,8},{2,6},{8,16},{10,2},{16,24},{18,10},{24,28},{26,18},{28,20},... | collective-permute-start | bytes 983048 | tf_op jit(solution)/shard_map/ppermute | solution.py:142
  45.6 1.6 %collective-permute-start.14 = (bf16[40,4096]{1,0:T(8,128)(2,1)S(1)}, bf16[40,4096]{1,0:T(8,128)(2,1)S(1)}, u32[]{:S(2)}, u32[]{:S(2)}) collective-permute-start(bf16[40,4096]{1,0:T(8,128)(2,1)S(1)} %pad_maximum_fusion.10), channel_id=1, source_target_pairs={{0,8},{2,6},{8,16},{10,2},{16,24},{18,10},{24,28},{26,18},{28,20},... | collective-permute-start | bytes 983048 | tf_op jit(solution)/shard_map/ppermute | solution.py:142
  47.2 2.0 %collective-permute-done.13 = bf16[40,4096]{1,0:T(8,128)(2,1)S(1)} collective-permute-done((bf16[40,4096]{1,0:T(8,128)(2,1)S(1)}, bf16[40,4096]{1,0:T(8,128)(2,1)S(1)}, u32[]{:S(2)}, u32[]{:S(2)}) %collective-permute-start.13) | collective-permute-done | bytes 327712 | tf_op jit(solution)/shard_map/ppermute | solution.py:142
  49.5 1.6 %collective-permute-start.15 = (bf16[40,4096]{1,0:T(8,128)(2,1)S(1)}, bf16[40,4096]{1,0:T(8,128)(2,1)S(1)}, u32[]{:S(2)}, u32[]{:S(2)}) collective-permute-start(bf16[40,4096]{1,0:T(8,128)(2,1)S(1)} %pad_maximum_fusion.11), channel_id=1, source_target_pairs={{0,8},{2,6},{8,16},{10,2},{16,24},{18,10},{24,28},{26,18},{28,20},... | collective-permute-start | bytes 983048 | tf_op jit(solution)/shard_map/ppermute | solution.py:142
  53.0 1.6 %collective-permute-start.16 = (bf16[40,4096]{1,0:T(8,128)(2,1)S(1)}, bf16[40,4096]{1,0:T(8,128)(2,1)S(1)}, u32[]{:S(2)}, u32[]{:S(2)}) collective-permute-start(bf16[40,4096]{1,0:T(8,128)(2,1)S(1)} %pad_maximum_fusion.12), channel_id=1, source_target_pairs={{0,8},{2,6},{8,16},{10,2},{16,24},{18,10},{24,28},{26,18},{28,20},... | collective-permute-start | bytes 983048 | tf_op jit(solution)/shard_map/ppermute | solution.py:142
  54.6 2.0 %collective-permute-done.15 = bf16[40,4096]{1,0:T(8,128)(2,1)S(1)} collective-permute-done((bf16[40,4096]{1,0:T(8,128)(2,1)S(1)}, bf16[40,4096]{1,0:T(8,128)(2,1)S(1)}, u32[]{:S(2)}, u32[]{:S(2)}) %collective-permute-start.15) | collective-permute-done | bytes 327712 | tf_op jit(solution)/shard_map/ppermute | solution.py:142
  56.9 1.8 %collective-permute-start.17 = (bf16[40,4096]{1,0:T(8,128)(2,1)S(1)}, bf16[40,4096]{1,0:T(8,128)(2,1)S(1)}, u32[]{:S(2)}, u32[]{:S(2)}) collective-permute-start(bf16[40,4096]{1,0:T(8,128)(2,1)S(1)} %pad_maximum_fusion.13), channel_id=1, source_target_pairs={{0,8},{2,6},{8,16},{10,2},{16,24},{18,10},{24,28},{26,18},{28,20},... | collective-permute-start | bytes 983048 | tf_op jit(solution)/shard_map/ppermute | solution.py:142
  58.8 5.3 %collective-permute-done.17 = bf16[40,4096]{1,0:T(8,128)(2,1)S(1)} collective-permute-done((bf16[40,4096]{1,0:T(8,128)(2,1)S(1)}, bf16[40,4096]{1,0:T(8,128)(2,1)S(1)}, u32[]{:S(2)}, u32[]{:S(2)}) %collective-permute-start.17) | collective-permute-done | bytes 327712 | tf_op jit(solution)/shard_map/ppermute | solution.py:142
  66.8 4.3 %scores.1 = (bf16[512,256]{1,0:T(8,128)(2,1)S(1)}, bf16[512,256]{1,0:T(8,128)(2,1)S(1)}, f32[512,1]{1,0:T(8,128)S(1)}, bf16[256,4096]{1,0:T(8,128)(2,1)S(1)}) custom-call(bf16[128,4096]{1,0:T(8,128)(2,1)S(1)} %get-tuple-element.98.refs_0_, bf16[128,4096]{1,0:T(8,128)(2,1)S(1)} %slice_dynamic-update-slice_fusion.refs_1_, bf16[512,4096]{1,0:T(8,128)(2,1)S(1)} %copy-done, ...), custom_call_target="tpu_custom_call" | custom-call | flops 3221225472 | bytes 20971520 | tf_op jit(solution)/shard_map/scores/pallas_call | solution.py:198
  75.9 1.6 %collective-permute-start.41 = (bf16[2,2,16,2048]{3,2,0,1:T(8,128)(2,1)S(1)}, bf16[2,2,16,2048]{3,2,0,1:T(8,128)(2,1)S(1)}, u32[]{:S(2)}, u32[]{:S(2)}) collective-permute-start(bf16[2,2,16,2048]{3,2,0,1:T(8,128)(2,1)S(1)} %fusion.8), channel_id=1, source_target_pairs={{0,8},{2,10},{4,12},{6,14},{8,0},{10,2},{12,4},{14,6},{16,24},{18,... | collective-permute-start | bytes 786440 | tf_op jit(solution)/shard_map/ppermute | solution.py:271
  78.7 4.7 %collective-permute-done.37 = bf16[2,2,16,2048]{3,2,0,1:T(8,128)(2,1)S(1)} collective-permute-done((bf16[2,2,16,2048]{3,2,0,1:T(8,128)(2,1)S(1)}, bf16[2,2,16,2048]{3,2,0,1:T(8,128)(2,1)S(1)}, u32[]{:S(2)}, u32[]{:S(2)}) %collective-permute-start.37) | collective-permute-done | bytes 262176 | tf_op jit(solution)/shard_map/ppermute | solution.py:271
  83.5 1.6 %collective-permute-start.38 = (bf16[2,16,2048]{2,1,0:T(8,128)(2,1)S(1)}, bf16[2,16,2048]{2,1,0:T(8,128)(2,1)S(1)}, u32[]{:S(2)}, u32[]{:S(2)}) collective-permute-start(bf16[2,16,2048]{2,1,0:T(8,128)(2,1)S(1)} %fusion.14), channel_id=1, source_target_pairs={{0,8},{2,10},{4,12},{6,14},{8,0},{10,2},{12,4},{14,6},{16,24},{18,... | collective-permute-start | bytes 393224 | tf_op jit(solution)/shard_map/ppermute | solution.py:271
  86.3 2.3 %collective-permute-done.38 = bf16[2,16,2048]{2,1,0:T(8,128)(2,1)S(1)} collective-permute-done((bf16[2,16,2048]{2,1,0:T(8,128)(2,1)S(1)}, bf16[2,16,2048]{2,1,0:T(8,128)(2,1)S(1)}, u32[]{:S(2)}, u32[]{:S(2)}) %collective-permute-start.38) | collective-permute-done | bytes 131104 | tf_op jit(solution)/shard_map/ppermute | solution.py:271
  88.6 2.6 %collective-permute-start.39 = (bf16[16,2048]{1,0:T(8,128)(2,1)S(1)}, bf16[16,2048]{1,0:T(8,128)(2,1)S(1)}, u32[]{:S(2)}, u32[]{:S(2)}) collective-permute-start(bf16[16,2048]{1,0:T(8,128)(2,1)S(1)} %fusion.30), channel_id=1, source_target_pairs={{0,16},{2,18},{4,20},{6,22},{8,24},{10,26},{12,28},{14,30},{16,0},... | collective-permute-start | bytes 196616 | tf_op jit(solution)/shard_map/ppermute | solution.py:271
  92.2 3.4 %collective-permute-done.39 = bf16[16,2048]{1,0:T(8,128)(2,1)S(1)} collective-permute-done((bf16[16,2048]{1,0:T(8,128)(2,1)S(1)}, bf16[16,2048]{1,0:T(8,128)(2,1)S(1)}, u32[]{:S(2)}, u32[]{:S(2)}) %collective-permute-start.39) | collective-permute-done | bytes 65568 | tf_op jit(solution)/shard_map/ppermute | solution.py:271
  95.6 1.6 %collective-permute-start.40 = (f32[16,2048]{1,0:T(8,128)S(1)}, f32[16,2048]{1,0:T(8,128)S(1)}, u32[]{:S(2)}, u32[]{:S(2)}) collective-permute-start(f32[16,2048]{1,0:T(8,128)S(1)} %fusion.17), channel_id=1, source_target_pairs={{0,1},{1,0},{2,3},{3,2},{4,5},{5,4},{6,7},{7,6},{8,9},{9,8},{10,11... | collective-permute-start | bytes 393224 | tf_op jit(solution)/shard_map/ppermute | solution.py:281
  97.2 1.5 %collective-permute-start.44 = (f32[16,2048]{1,0:T(8,128)S(1)}, f32[16,2048]{1,0:T(8,128)S(1)}, u32[]{:S(2)}, u32[]{:S(2)}) collective-permute-start(f32[16,2048]{1,0:T(8,128)S(1)} %fusion.16), channel_id=1, source_target_pairs={{0,1},{1,0},{2,3},{3,2},{4,5},{5,4},{6,7},{7,6},{8,9},{9,8},{10,11... | collective-permute-start | bytes 393224 | tf_op jit(solution)/shard_map/ppermute | solution.py:281
  98.7 3.3 %multiply_convert_fusion = bf16[512,4096]{1,0:T(8,128)(2,1)} fusion(f32[512,4096]{1,0:T(8,128)S(1)} %fusion.57, bf16[512,256]{1,0:T(8,128)(2,1)S(1)} %get-tuple-element.61, bf16[256,4096]{1,0:T(8,128)(2,1)S(1)} %get-tuple-element.62), kind=kOutput, calls=%fused_computation | convolution fusion | flops 1080033280 | bytes 14942208 | tf_op jit(solution)/shard_map/dot_general | solution.py:286
  (175 shorter events, 30.1 us)
Async XLA Ops:
  4.5 5.2 %collective-permute-start.2 = (bf16[64,4096]{1,0:T(8,128)(2,1)S(1)}, bf16[64,4096]{1,0:T(8,128)(2,1)S(1)}, u32[]{:S(2)}, u32[]{:S(2)}) collective-permute-start(bf16[64,4096]{1,0:T(8,128)(2,1)S(1)} %get-tuple-element.38), channel_id=1, source_target_pairs={{0,2},{2,0},{4,6},{6,4},{8,10},{10,8},{12,14},{14,12},{16,18},{18,... | collective-permute-start | bytes 1572872 | tf_op jit(solution)/shard_map/ppermute | solution.py:97
  6.5 5.9 %collective-permute-start.28 = (bf16[32,4096]{1,0:T(8,128)(2,1)S(1)}, bf16[32,4096]{1,0:T(8,128)(2,1)S(1)}, u32[]{:S(2)}, u32[]{:S(2)}) collective-permute-start(bf16[32,4096]{1,0:T(8,128)(2,1)S(1)} %get-tuple-element.82), channel_id=1, source_target_pairs={{0,2},{2,0},{4,6},{6,4},{8,10},{10,8},{12,14},{14,12},{16,18},{18,... | collective-permute-start | bytes 786440 | tf_op jit(solution)/shard_map/ppermute | solution.py:116
  7.0 7.7 %collective-permute-start.1 = (bf16[40,4096]{1,0:T(8,128)(2,1)S(1)}, bf16[40,4096]{1,0:T(8,128)(2,1)S(1)}, u32[]{:S(2)}, u32[]{:S(2)}) collective-permute-start(bf16[40,4096]{1,0:T(8,128)(2,1)S(1)} %pad_maximum_fusion), channel_id=1, source_target_pairs={{0,8},{2,6},{8,16},{10,2},{16,24},{18,10},{24,28},{26,18},{28,20},... | collective-permute-start | bytes 983048 | tf_op jit(solution)/shard_map/ppermute | solution.py:142
  9.8 8.3 %collective-permute-start.3 = (bf16[40,4096]{1,0:T(8,128)(2,1)S(1)}, bf16[40,4096]{1,0:T(8,128)(2,1)S(1)}, u32[]{:S(2)}, u32[]{:S(2)}) collective-permute-start(bf16[40,4096]{1,0:T(8,128)(2,1)S(1)} %pad_maximum_fusion.1), channel_id=1, source_target_pairs={{0,8},{2,6},{8,16},{10,2},{16,24},{18,10},{24,28},{26,18},{28,20},... | collective-permute-start | bytes 983048 | tf_op jit(solution)/shard_map/ppermute | solution.py:142
  11.8 15.0 %collective-permute-start.8 = (bf16[256,4096]{1,0:T(8,128)(2,1)S(1)}, bf16[256,4096]{1,0:T(8,128)(2,1)S(1)}, u32[]{:S(2)}, u32[]{:S(2)}) collective-permute-start(bf16[256,4096]{1,0:T(8,128)(2,1)S(1)} %copy-done.4), channel_id=1, source_target_pairs={{0,2},{2,0},{4,6},{6,4},{8,10},{10,8},{12,14},{14,12},{16,18},{18,... | collective-permute-start | bytes 6291464 | tf_op jit(solution)/shard_map/ppermute | solution.py:102
  12.3 9.7 %collective-permute-start.6 = (bf16[256,4096]{1,0:T(8,128)(2,1)S(1)}, bf16[256,4096]{1,0:T(8,128)(2,1)S(1)}, u32[]{:S(2)}, u32[]{:S(2)}) collective-permute-start(bf16[256,4096]{1,0:T(8,128)(2,1)S(1)} %copy-done.2), channel_id=1, source_target_pairs={{0,2},{2,0},{4,6},{6,4},{8,10},{10,8},{12,14},{14,12},{16,18},{18,... | collective-permute-start | bytes 6291464 | tf_op jit(solution)/shard_map/ppermute | solution.py:102
  14.9 7.1 %collective-permute-start.4 = (bf16[40,4096]{1,0:T(8,128)(2,1)S(1)}, bf16[40,4096]{1,0:T(8,128)(2,1)S(1)}, u32[]{:S(2)}, u32[]{:S(2)}) collective-permute-start(bf16[40,4096]{1,0:T(8,128)(2,1)S(1)} %pad_maximum_fusion.2), channel_id=1, source_target_pairs={{0,8},{2,6},{8,16},{10,2},{16,24},{18,10},{24,28},{26,18},{28,20},... | collective-permute-start | bytes 983048 | tf_op jit(solution)/shard_map/ppermute | solution.py:142
  19.7 7.1 %collective-permute-start.5 = (bf16[40,4096]{1,0:T(8,128)(2,1)S(1)}, bf16[40,4096]{1,0:T(8,128)(2,1)S(1)}, u32[]{:S(2)}, u32[]{:S(2)}) collective-permute-start(bf16[40,4096]{1,0:T(8,128)(2,1)S(1)} %pad_maximum_fusion.3), channel_id=1, source_target_pairs={{0,8},{2,6},{8,16},{10,2},{16,24},{18,10},{24,28},{26,18},{28,20},... | collective-permute-start | bytes 983048 | tf_op jit(solution)/shard_map/ppermute | solution.py:142
  22.4 6.6 %collective-permute-start.30 = (bf16[32,4096]{1,0:T(8,128)(2,1)S(1)}, bf16[32,4096]{1,0:T(8,128)(2,1)S(1)}, u32[]{:S(2)}, u32[]{:S(2)}) collective-permute-start(bf16[32,4096]{1,0:T(8,128)(2,1)S(1)} %get-tuple-element.78), channel_id=1, source_target_pairs={{0,2},{2,0},{4,6},{6,4},{8,10},{10,8},{12,14},{14,12},{16,18},{18,... | collective-permute-start | bytes 786440 | tf_op jit(solution)/shard_map/ppermute | solution.py:116
  22.5 7.8 %collective-permute-start.7 = (bf16[40,4096]{1,0:T(8,128)(2,1)S(1)}, bf16[40,4096]{1,0:T(8,128)(2,1)S(1)}, u32[]{:S(2)}, u32[]{:S(2)}) collective-permute-start(bf16[40,4096]{1,0:T(8,128)(2,1)S(1)} %pad_maximum_fusion.4), channel_id=1, source_target_pairs={{0,8},{2,6},{8,16},{10,2},{16,24},{18,10},{24,28},{26,18},{28,20},... | collective-permute-start | bytes 983048 | tf_op jit(solution)/shard_map/ppermute | solution.py:142
  27.3 7.1 %collective-permute-start.9 = (bf16[40,4096]{1,0:T(8,128)(2,1)S(1)}, bf16[40,4096]{1,0:T(8,128)(2,1)S(1)}, u32[]{:S(2)}, u32[]{:S(2)}) collective-permute-start(bf16[40,4096]{1,0:T(8,128)(2,1)S(1)} %pad_maximum_fusion.5), channel_id=1, source_target_pairs={{0,8},{2,6},{8,16},{10,2},{16,24},{18,10},{24,28},{26,18},{28,20},... | collective-permute-start | bytes 983048 | tf_op jit(solution)/shard_map/ppermute | solution.py:142
  30.4 5.9 %collective-permute-start.31 = (bf16[32,4096]{1,0:T(8,128)(2,1)S(1)}, bf16[32,4096]{1,0:T(8,128)(2,1)S(1)}, u32[]{:S(2)}, u32[]{:S(2)}) collective-permute-start(bf16[32,4096]{1,0:T(8,128)(2,1)S(1)} %get-tuple-element.76), channel_id=1, source_target_pairs={{0,2},{2,0},{4,6},{6,4},{8,10},{10,8},{12,14},{14,12},{16,18},{18,... | collective-permute-start | bytes 786440 | tf_op jit(solution)/shard_map/ppermute | solution.py:116
  30.6 7.4 %collective-permute-start.10 = (bf16[40,4096]{1,0:T(8,128)(2,1)S(1)}, bf16[40,4096]{1,0:T(8,128)(2,1)S(1)}, u32[]{:S(2)}, u32[]{:S(2)}) collective-permute-start(bf16[40,4096]{1,0:T(8,128)(2,1)S(1)} %pad_maximum_fusion.6), channel_id=1, source_target_pairs={{0,8},{2,6},{8,16},{10,2},{16,24},{18,10},{24,28},{26,18},{28,20},... | collective-permute-start | bytes 983048 | tf_op jit(solution)/shard_map/ppermute | solution.py:142
  34.7 7.1 %collective-permute-start.11 = (bf16[40,4096]{1,0:T(8,128)(2,1)S(1)}, bf16[40,4096]{1,0:T(8,128)(2,1)S(1)}, u32[]{:S(2)}, u32[]{:S(2)}) collective-permute-start(bf16[40,4096]{1,0:T(8,128)(2,1)S(1)} %pad_maximum_fusion.7), channel_id=1, source_target_pairs={{0,8},{2,6},{8,16},{10,2},{16,24},{18,10},{24,28},{26,18},{28,20},... | collective-permute-start | bytes 983048 | tf_op jit(solution)/shard_map/ppermute | solution.py:142
  38.1 5.7 %collective-permute-start.32 = (bf16[32,4096]{1,0:T(8,128)(2,1)S(1)}, bf16[32,4096]{1,0:T(8,128)(2,1)S(1)}, u32[]{:S(2)}, u32[]{:S(2)}) collective-permute-start(bf16[32,4096]{1,0:T(8,128)(2,1)S(1)} %get-tuple-element.74), channel_id=1, source_target_pairs={{0,2},{2,0},{4,6},{6,4},{8,10},{10,8},{12,14},{14,12},{16,18},{18,... | collective-permute-start | bytes 786440 | tf_op jit(solution)/shard_map/ppermute | solution.py:116
  38.2 7.1 %collective-permute-start.12 = (bf16[40,4096]{1,0:T(8,128)(2,1)S(1)}, bf16[40,4096]{1,0:T(8,128)(2,1)S(1)}, u32[]{:S(2)}, u32[]{:S(2)}) collective-permute-start(bf16[40,4096]{1,0:T(8,128)(2,1)S(1)} %pad_maximum_fusion.8), channel_id=1, source_target_pairs={{0,8},{2,6},{8,16},{10,2},{16,24},{18,10},{24,28},{26,18},{28,20},... | collective-permute-start | bytes 983048 | tf_op jit(solution)/shard_map/ppermute | solution.py:142
  42.1 7.1 %collective-permute-start.13 = (bf16[40,4096]{1,0:T(8,128)(2,1)S(1)}, bf16[40,4096]{1,0:T(8,128)(2,1)S(1)}, u32[]{:S(2)}, u32[]{:S(2)}) collective-permute-start(bf16[40,4096]{1,0:T(8,128)(2,1)S(1)} %pad_maximum_fusion.9), channel_id=1, source_target_pairs={{0,8},{2,6},{8,16},{10,2},{16,24},{18,10},{24,28},{26,18},{28,20},... | collective-permute-start | bytes 983048 | tf_op jit(solution)/shard_map/ppermute | solution.py:142
  45.4 5.7 %collective-permute-start.33 = (bf16[32,4096]{1,0:T(8,128)(2,1)S(1)}, bf16[32,4096]{1,0:T(8,128)(2,1)S(1)}, u32[]{:S(2)}, u32[]{:S(2)}) collective-permute-start(bf16[32,4096]{1,0:T(8,128)(2,1)S(1)} %get-tuple-element.72), channel_id=1, source_target_pairs={{0,2},{2,0},{4,6},{6,4},{8,10},{10,8},{12,14},{14,12},{16,18},{18,... | collective-permute-start | bytes 786440 | tf_op jit(solution)/shard_map/ppermute | solution.py:116
  45.6 7.1 %collective-permute-start.14 = (bf16[40,4096]{1,0:T(8,128)(2,1)S(1)}, bf16[40,4096]{1,0:T(8,128)(2,1)S(1)}, u32[]{:S(2)}, u32[]{:S(2)}) collective-permute-start(bf16[40,4096]{1,0:T(8,128)(2,1)S(1)} %pad_maximum_fusion.10), channel_id=1, source_target_pairs={{0,8},{2,6},{8,16},{10,2},{16,24},{18,10},{24,28},{26,18},{28,20},... | collective-permute-start | bytes 983048 | tf_op jit(solution)/shard_map/ppermute | solution.py:142
  49.5 7.1 %collective-permute-start.15 = (bf16[40,4096]{1,0:T(8,128)(2,1)S(1)}, bf16[40,4096]{1,0:T(8,128)(2,1)S(1)}, u32[]{:S(2)}, u32[]{:S(2)}) collective-permute-start(bf16[40,4096]{1,0:T(8,128)(2,1)S(1)} %pad_maximum_fusion.11), channel_id=1, source_target_pairs={{0,8},{2,6},{8,16},{10,2},{16,24},{18,10},{24,28},{26,18},{28,20},... | collective-permute-start | bytes 983048 | tf_op jit(solution)/shard_map/ppermute | solution.py:142
  52.8 5.9 %collective-permute-start.34 = (bf16[32,4096]{1,0:T(8,128)(2,1)S(1)}, bf16[32,4096]{1,0:T(8,128)(2,1)S(1)}, u32[]{:S(2)}, u32[]{:S(2)}) collective-permute-start(bf16[32,4096]{1,0:T(8,128)(2,1)S(1)} %get-tuple-element.70), channel_id=1, source_target_pairs={{0,2},{2,0},{4,6},{6,4},{8,10},{10,8},{12,14},{14,12},{16,18},{18,... | collective-permute-start | bytes 786440 | tf_op jit(solution)/shard_map/ppermute | solution.py:116
  53.0 11.3 %collective-permute-start.16 = (bf16[40,4096]{1,0:T(8,128)(2,1)S(1)}, bf16[40,4096]{1,0:T(8,128)(2,1)S(1)}, u32[]{:S(2)}, u32[]{:S(2)}) collective-permute-start(bf16[40,4096]{1,0:T(8,128)(2,1)S(1)} %pad_maximum_fusion.12), channel_id=1, source_target_pairs={{0,8},{2,6},{8,16},{10,2},{16,24},{18,10},{24,28},{26,18},{28,20},... | collective-permute-start | bytes 983048 | tf_op jit(solution)/shard_map/ppermute | solution.py:142
  56.9 7.3 %collective-permute-start.17 = (bf16[40,4096]{1,0:T(8,128)(2,1)S(1)}, bf16[40,4096]{1,0:T(8,128)(2,1)S(1)}, u32[]{:S(2)}, u32[]{:S(2)}) collective-permute-start(bf16[40,4096]{1,0:T(8,128)(2,1)S(1)} %pad_maximum_fusion.13), channel_id=1, source_target_pairs={{0,8},{2,6},{8,16},{10,2},{16,24},{18,10},{24,28},{26,18},{28,20},... | collective-permute-start | bytes 983048 | tf_op jit(solution)/shard_map/ppermute | solution.py:142
  58.7 5.8 %collective-permute-start.18 = (bf16[128,4096]{1,0:T(8,128)(2,1)S(1)}, bf16[128,4096]{1,0:T(8,128)(2,1)S(1)}, u32[]{:S(2)}, u32[]{:S(2)}) collective-permute-start(bf16[128,4096]{1,0:T(8,128)(2,1)S(1)} %get-tuple-element.102), channel_id=1, source_target_pairs={{0,2},{2,0},{4,6},{6,4},{8,10},{10,8},{12,14},{14,12},{16,18},{18,... | collective-permute-start | bytes 3145736 | tf_op jit(solution)/shard_map/ppermute | solution.py:144
  74.8 8.6 %collective-permute-start.37 = (bf16[2,2,16,2048]{3,2,0,1:T(8,128)(2,1)S(1)}, bf16[2,2,16,2048]{3,2,0,1:T(8,128)(2,1)S(1)}, u32[]{:S(2)}, u32[]{:S(2)}) collective-permute-start(bf16[2,2,16,2048]{3,2,0,1:T(8,128)(2,1)S(1)} %fusion.9), channel_id=1, source_target_pairs={{0,4},{2,6},{4,0},{6,2},{8,12},{10,14},{12,8},{14,10},{16,20},{18,... | collective-permute-start | bytes 786440 | tf_op jit(solution)/shard_map/ppermute | solution.py:271
  75.9 9.2 %collective-permute-start.41 = (bf16[2,2,16,2048]{3,2,0,1:T(8,128)(2,1)S(1)}, bf16[2,2,16,2048]{3,2,0,1:T(8,128)(2,1)S(1)}, u32[]{:S(2)}, u32[]{:S(2)}) collective-permute-start(bf16[2,2,16,2048]{3,2,0,1:T(8,128)(2,1)S(1)} %fusion.8), channel_id=1, source_target_pairs={{0,8},{2,10},{4,12},{6,14},{8,0},{10,2},{12,4},{14,6},{16,24},{18,... | collective-permute-start | bytes 786440 | tf_op jit(solution)/shard_map/ppermute | solution.py:271
  83.5 5.0 %collective-permute-start.38 = (bf16[2,16,2048]{2,1,0:T(8,128)(2,1)S(1)}, bf16[2,16,2048]{2,1,0:T(8,128)(2,1)S(1)}, u32[]{:S(2)}, u32[]{:S(2)}) collective-permute-start(bf16[2,16,2048]{2,1,0:T(8,128)(2,1)S(1)} %fusion.14), channel_id=1, source_target_pairs={{0,8},{2,10},{4,12},{6,14},{8,0},{10,2},{12,4},{14,6},{16,24},{18,... | collective-permute-start | bytes 393224 | tf_op jit(solution)/shard_map/ppermute | solution.py:271
  85.2 5.9 %collective-permute-start.42 = (bf16[2,16,2048]{2,1,0:T(8,128)(2,1)S(1)}, bf16[2,16,2048]{2,1,0:T(8,128)(2,1)S(1)}, u32[]{:S(2)}, u32[]{:S(2)}) collective-permute-start(bf16[2,16,2048]{2,1,0:T(8,128)(2,1)S(1)} %fusion.15), channel_id=1, source_target_pairs={{0,4},{2,6},{4,0},{6,2},{8,12},{10,14},{12,8},{14,10},{16,20},{18,... | collective-permute-start | bytes 393224 | tf_op jit(solution)/shard_map/ppermute | solution.py:271
  88.6 7.0 %collective-permute-start.39 = (bf16[16,2048]{1,0:T(8,128)(2,1)S(1)}, bf16[16,2048]{1,0:T(8,128)(2,1)S(1)}, u32[]{:S(2)}, u32[]{:S(2)}) collective-permute-start(bf16[16,2048]{1,0:T(8,128)(2,1)S(1)} %fusion.30), channel_id=1, source_target_pairs={{0,16},{2,18},{4,20},{6,22},{8,24},{10,26},{12,28},{14,30},{16,0},... | collective-permute-start | bytes 196616 | tf_op jit(solution)/shard_map/ppermute | solution.py:271
  91.2 6.0 %collective-permute-start.43 = (bf16[16,2048]{1,0:T(8,128)(2,1)S(1)}, bf16[16,2048]{1,0:T(8,128)(2,1)S(1)}, u32[]{:S(2)}, u32[]{:S(2)}) collective-permute-start(bf16[16,2048]{1,0:T(8,128)(2,1)S(1)} %fusion.31), channel_id=1, source_target_pairs={{0,16},{2,18},{4,20},{6,22},{8,24},{10,26},{12,28},{14,30},{16,0},... | collective-permute-start | bytes 196616 | tf_op jit(solution)/shard_map/ppermute | solution.py:271
  95.6 7.1 %collective-permute-start.40 = (f32[16,2048]{1,0:T(8,128)S(1)}, f32[16,2048]{1,0:T(8,128)S(1)}, u32[]{:S(2)}, u32[]{:S(2)}) collective-permute-start(f32[16,2048]{1,0:T(8,128)S(1)} %fusion.17), channel_id=1, source_target_pairs={{0,1},{1,0},{2,3},{3,2},{4,5},{5,4},{6,7},{7,6},{8,9},{9,8},{10,11... | collective-permute-start | bytes 393224 | tf_op jit(solution)/shard_map/ppermute | solution.py:281
  97.2 5.5 %collective-permute-start.44 = (f32[16,2048]{1,0:T(8,128)S(1)}, f32[16,2048]{1,0:T(8,128)S(1)}, u32[]{:S(2)}, u32[]{:S(2)}) collective-permute-start(f32[16,2048]{1,0:T(8,128)S(1)} %fusion.16), channel_id=1, source_target_pairs={{0,1},{1,0},{2,3},{3,2},{4,5},{5,4},{6,7},{7,6},{8,9},{9,8},{10,11... | collective-permute-start | bytes 393224 | tf_op jit(solution)/shard_map/ppermute | solution.py:281
  (22 other events, 62.9 us)

commit v9 on v8

--- a/solution.py
+++ b/solution.py
@@ -268,6 +268,8 @@
             lefts[h].pop(at)
             if h == 1 and step == 0:
                 sent[1], _ = lax.optimization_barrier((sent[1], sent[0]))
+            if h == 0 and step == 1:
+                sent[0], query_grad = lax.optimization_barrier((sent[0], query_grad))
             got = lax.ppermute(sent[h], "wide", pairs_of[orders[h][step]])
             if h == 0:
                 sums[0] = sums[0] + got.astype(jnp.float32)
@@ -275,6 +277,10 @@
                 pending = got
         if step == 0:
             (late_p, grad_q, row_loss), _ = lax.optimization_barrier(((grad_p, grad_q, row_loss), sent[1]))
+            qgrad = jnp.dot(late_p, pieces, preferred_element_type=jnp.float32) + jnp.dot(
+                grad_q, pool_s, preferred_element_type=jnp.float32
+            )
+            query_grad = (qgrad * scale).astype(jnp.bfloat16)
     pending, _ = lax.optimization_barrier((pending, sums[0]))
     sums[1] = sums[1] + pending.astype(jnp.float32)
     if n_dp == 2:
@@ -282,11 +288,6 @@
     else:
         sums = [lax.psum(x, "dp") for x in sums]
     passage_grad = jnp.concatenate(sums, 1) * scale
-
-    qgrad = jnp.dot(late_p, pieces, preferred_element_type=jnp.float32) + jnp.dot(
-        grad_q, pool_s, preferred_element_type=jnp.float32
-    )
-    query_grad = (qgrad * scale).astype(jnp.bfloat16)
     return (row_loss[:, 0], query_grad, passage_grad)
 
 

time: 104 us -> 105 us (level)
  waiting for transfers between devices: 39.2 us -> 41.1 us
    ppermute x2, waiting for transfers between devices: 0.01 us -> 3.76 us  [body(): sums = [x + lax.ppermute(x, 'dp', across) for x in sums]]
    ppermute x6, waiting for transfers between devices: 10.3 us -> 8.52 us  [body(): got = lax.ppermute(sent[h], 'wide', pairs_of[orders[h][step]])]
  transfers between devices with their start and end apart: 45 -> 45, of which waited for: 22 -> 25; matrix products, arithmetic and copies ran while one was open for 11% -> 11% of each run, Pallas kernels for 0% -> 0%
where the time goes in v9:
time: 105 us; the launch traced here: 104 us
  waiting for transfers between devices  41.1 us (39%)
  starting transfers between devices  40 us (38%)
  matrix products  6.43 us (6%)
  other arithmetic  5.44 us (5%)
  Pallas kernels  4.46 us (4%)
  local copies, waits for them, and re-layouts  4.26 us (4%)
  between operations  2.8 us (3%)
    ppermute x14, starting transfers between devices, gather_rows(): came[i] = lax.ppermute(sent, 'wide', pairs)  25.1 us
    ppermute x14, waiting for transfers between devices, gather_rows(): came[i] = lax.ppermute(sent, 'wide', pairs)  24.2 us
    ppermute x6, starting transfers between devices, body(): got = lax.ppermute(sent[h], 'wide', pairs_of[orders[h][step]])  8.95 us
    ppermute x6, waiting for transfers between devices, body(): got = lax.ppermute(sent[h], 'wide', pairs_of[orders[h][step]])  8.52 us
    pallas_call x1, Pallas kernels, tail(): pl.pallas_call(functools.partial(tail_kernel, scale, len(pass_parts)), ou...  4.33 us
    ppermute x2, waiting for transfers between devices, body(): sums = [x + lax.ppermute(x, 'dp', across) for x in sums]  3.76 us
    dot_general x1, matrix products, body(): jnp.dot(late_p, pieces, preferred_element_type=jnp.float32)  3.29 us
    unnamed x18, local copies, waits for them, and re-layouts  3.21 us
  transfers between devices with their start and end apart: 45, of which 25 were waited for; matrix products, arithmetic and copies ran while one was open for 11% of the time, Pallas kernels for 0%

profile of v9, /device:TPU:0, one launch (start us, length us, event | category | flops | bytes accessed | tf_op | source)
XLA Modules:
  0.0 104.5 jit_solution(12260796913859897251)
XLA Ops:
  0.7 1.6 %copy-done.1 = bf16[256,4096]{1,0:T(8,128)(2,1)S(1)} copy-done((bf16[256,4096]{1,0:T(8,128)(2,1)S(1)}, bf16[256,4096]{1,0:T(8,128)(2,1)}, u32[]{:S(2)}) %copy-start.1) | copy-done | bytes 2097176
  2.2 1.6 %copy-done.3 = bf16[256,4096]{1,0:T(8,128)(2,1)S(1)} copy-done((bf16[256,4096]{1,0:T(8,128)(2,1)S(1)}, bf16[256,4096]{1,0:T(8,128)(2,1)}, u32[]{:S(2)}) %copy-start.3) | copy-done | bytes 2097176
  7.0 2.7 %collective-permute-start.1 = (bf16[40,4096]{1,0:T(8,128)(2,1)S(1)}, bf16[40,4096]{1,0:T(8,128)(2,1)S(1)}, u32[]{:S(2)}, u32[]{:S(2)}) collective-permute-start(bf16[40,4096]{1,0:T(8,128)(2,1)S(1)} %pad_maximum_fusion), channel_id=1, source_target_pairs={{0,8},{2,6},{8,16},{10,2},{16,24},{18,10},{24,28},{26,18},{28,20},... | collective-permute-start | bytes 983048 | tf_op jit(solution)/shard_map/ppermute | solution.py:142
  9.8 1.6 %collective-permute-start.3 = (bf16[40,4096]{1,0:T(8,128)(2,1)S(1)}, bf16[40,4096]{1,0:T(8,128)(2,1)S(1)}, u32[]{:S(2)}, u32[]{:S(2)}) collective-permute-start(bf16[40,4096]{1,0:T(8,128)(2,1)S(1)} %pad_maximum_fusion.1), channel_id=1, source_target_pairs={{0,8},{2,6},{8,16},{10,2},{16,24},{18,10},{24,28},{26,18},{28,20},... | collective-permute-start | bytes 983048 | tf_op jit(solution)/shard_map/ppermute | solution.py:142
  14.9 2.2 %collective-permute-start.4 = (bf16[40,4096]{1,0:T(8,128)(2,1)S(1)}, bf16[40,4096]{1,0:T(8,128)(2,1)S(1)}, u32[]{:S(2)}, u32[]{:S(2)}) collective-permute-start(bf16[40,4096]{1,0:T(8,128)(2,1)S(1)} %pad_maximum_fusion.2), channel_id=1, source_target_pairs={{0,8},{2,6},{8,16},{10,2},{16,24},{18,10},{24,28},{26,18},{28,20},... | collective-permute-start | bytes 983048 | tf_op jit(solution)/shard_map/ppermute | solution.py:142
  19.7 1.6 %collective-permute-start.5 = (bf16[40,4096]{1,0:T(8,128)(2,1)S(1)}, bf16[40,4096]{1,0:T(8,128)(2,1)S(1)}, u32[]{:S(2)}, u32[]{:S(2)}) collective-permute-start(bf16[40,4096]{1,0:T(8,128)(2,1)S(1)} %pad_maximum_fusion.3), channel_id=1, source_target_pairs={{0,8},{2,6},{8,16},{10,2},{16,24},{18,10},{24,28},{26,18},{28,20},... | collective-permute-start | bytes 983048 | tf_op jit(solution)/shard_map/ppermute | solution.py:142
  22.5 2.2 %collective-permute-start.7 = (bf16[40,4096]{1,0:T(8,128)(2,1)S(1)}, bf16[40,4096]{1,0:T(8,128)(2,1)S(1)}, u32[]{:S(2)}, u32[]{:S(2)}) collective-permute-start(bf16[40,4096]{1,0:T(8,128)(2,1)S(1)} %pad_maximum_fusion.4), channel_id=1, source_target_pairs={{0,8},{2,6},{8,16},{10,2},{16,24},{18,10},{24,28},{26,18},{28,20},... | collective-permute-start | bytes 983048 | tf_op jit(solution)/shard_map/ppermute | solution.py:142
  24.7 2.1 %collective-permute-done.5 = bf16[40,4096]{1,0:T(8,128)(2,1)S(1)} collective-permute-done((bf16[40,4096]{1,0:T(8,128)(2,1)S(1)}, bf16[40,4096]{1,0:T(8,128)(2,1)S(1)}, u32[]{:S(2)}, u32[]{:S(2)}) %collective-permute-start.5) | collective-permute-done | bytes 327712 | tf_op jit(solution)/shard_map/ppermute | solution.py:142
  27.3 1.6 %collective-permute-start.9 = (bf16[40,4096]{1,0:T(8,128)(2,1)S(1)}, bf16[40,4096]{1,0:T(8,128)(2,1)S(1)}, u32[]{:S(2)}, u32[]{:S(2)}) collective-permute-start(bf16[40,4096]{1,0:T(8,128)(2,1)S(1)} %pad_maximum_fusion.5), channel_id=1, source_target_pairs={{0,8},{2,6},{8,16},{10,2},{16,24},{18,10},{24,28},{26,18},{28,20},... | collective-permute-start | bytes 983048 | tf_op jit(solution)/shard_map/ppermute | solution.py:142
  30.6 1.6 %collective-permute-start.10 = (bf16[40,4096]{1,0:T(8,128)(2,1)S(1)}, bf16[40,4096]{1,0:T(8,128)(2,1)S(1)}, u32[]{:S(2)}, u32[]{:S(2)}) collective-permute-start(bf16[40,4096]{1,0:T(8,128)(2,1)S(1)} %pad_maximum_fusion.6), channel_id=1, source_target_pairs={{0,8},{2,6},{8,16},{10,2},{16,24},{18,10},{24,28},{26,18},{28,20},... | collective-permute-start | bytes 983048 | tf_op jit(solution)/shard_map/ppermute | solution.py:142
  32.2 2.2 %collective-permute-done.9 = bf16[40,4096]{1,0:T(8,128)(2,1)S(1)} collective-permute-done((bf16[40,4096]{1,0:T(8,128)(2,1)S(1)}, bf16[40,4096]{1,0:T(8,128)(2,1)S(1)}, u32[]{:S(2)}, u32[]{:S(2)}) %collective-permute-start.9) | collective-permute-done | bytes 327712 | tf_op jit(solution)/shard_map/ppermute | solution.py:142
  34.7 1.6 %collective-permute-start.11 = (bf16[40,4096]{1,0:T(8,128)(2,1)S(1)}, bf16[40,4096]{1,0:T(8,128)(2,1)S(1)}, u32[]{:S(2)}, u32[]{:S(2)}) collective-permute-start(bf16[40,4096]{1,0:T(8,128)(2,1)S(1)} %pad_maximum_fusion.7), channel_id=1, source_target_pairs={{0,8},{2,6},{8,16},{10,2},{16,24},{18,10},{24,28},{26,18},{28,20},... | collective-permute-start | bytes 983048 | tf_op jit(solution)/shard_map/ppermute | solution.py:142
  38.2 1.6 %collective-permute-start.12 = (bf16[40,4096]{1,0:T(8,128)(2,1)S(1)}, bf16[40,4096]{1,0:T(8,128)(2,1)S(1)}, u32[]{:S(2)}, u32[]{:S(2)}) collective-permute-start(bf16[40,4096]{1,0:T(8,128)(2,1)S(1)} %pad_maximum_fusion.8), channel_id=1, source_target_pairs={{0,8},{2,6},{8,16},{10,2},{16,24},{18,10},{24,28},{26,18},{28,20},... | collective-permute-start | bytes 983048 | tf_op jit(solution)/shard_map/ppermute | solution.py:142
  39.8 2.0 %collective-permute-done.11 = bf16[40,4096]{1,0:T(8,128)(2,1)S(1)} collective-permute-done((bf16[40,4096]{1,0:T(8,128)(2,1)S(1)}, bf16[40,4096]{1,0:T(8,128)(2,1)S(1)}, u32[]{:S(2)}, u32[]{:S(2)}) %collective-permute-start.11) | collective-permute-done | bytes 327712 | tf_op jit(solution)/shard_map/ppermute | solution.py:142
  42.1 1.6 %collective-permute-start.13 = (bf16[40,4096]{1,0:T(8,128)(2,1)S(1)}, bf16[40,4096]{1,0:T(8,128)(2,1)S(1)}, u32[]{:S(2)}, u32[]{:S(2)}) collective-permute-start(bf16[40,4096]{1,0:T(8,128)(2,1)S(1)} %pad_maximum_fusion.9), channel_id=1, source_target_pairs={{0,8},{2,6},{8,16},{10,2},{16,24},{18,10},{24,28},{26,18},{28,20},... | collective-permute-start | bytes 983048 | tf_op jit(solution)/shard_map/ppermute | solution.py:142
  45.6 1.6 %collective-permute-start.14 = (bf16[40,4096]{1,0:T(8,128)(2,1)S(1)}, bf16[40,4096]{1,0:T(8,128)(2,1)S(1)}, u32[]{:S(2)}, u32[]{:S(2)}) collective-permute-start(bf16[40,4096]{1,0:T(8,128)(2,1)S(1)} %pad_maximum_fusion.10), channel_id=1, source_target_pairs={{0,8},{2,6},{8,16},{10,2},{16,24},{18,10},{24,28},{26,18},{28,20},... | collective-permute-start | bytes 983048 | tf_op jit(solution)/shard_map/ppermute | solution.py:142
  47.2 2.0 %collective-permute-done.13 = bf16[40,4096]{1,0:T(8,128)(2,1)S(1)} collective-permute-done((bf16[40,4096]{1,0:T(8,128)(2,1)S(1)}, bf16[40,4096]{1,0:T(8,128)(2,1)S(1)}, u32[]{:S(2)}, u32[]{:S(2)}) %collective-permute-start.13) | collective-permute-done | bytes 327712 | tf_op jit(solution)/shard_map/ppermute | solution.py:142
  49.5 1.6 %collective-permute-start.15 = (bf16[40,4096]{1,0:T(8,128)(2,1)S(1)}, bf16[40,4096]{1,0:T(8,128)(2,1)S(1)}, u32[]{:S(2)}, u32[]{:S(2)}) collective-permute-start(bf16[40,4096]{1,0:T(8,128)(2,1)S(1)} %pad_maximum_fusion.11), channel_id=1, source_target_pairs={{0,8},{2,6},{8,16},{10,2},{16,24},{18,10},{24,28},{26,18},{28,20},... | collective-permute-start | bytes 983048 | tf_op jit(solution)/shard_map/ppermute | solution.py:142
  53.0 1.6 %collective-permute-start.16 = (bf16[40,4096]{1,0:T(8,128)(2,1)S(1)}, bf16[40,4096]{1,0:T(8,128)(2,1)S(1)}, u32[]{:S(2)}, u32[]{:S(2)}) collective-permute-start(bf16[40,4096]{1,0:T(8,128)(2,1)S(1)} %pad_maximum_fusion.12), channel_id=1, source_target_pairs={{0,8},{2,6},{8,16},{10,2},{16,24},{18,10},{24,28},{26,18},{28,20},... | collective-permute-start | bytes 983048 | tf_op jit(solution)/shard_map/ppermute | solution.py:142
  54.6 2.0 %collective-permute-done.15 = bf16[40,4096]{1,0:T(8,128)(2,1)S(1)} collective-permute-done((bf16[40,4096]{1,0:T(8,128)(2,1)S(1)}, bf16[40,4096]{1,0:T(8,128)(2,1)S(1)}, u32[]{:S(2)}, u32[]{:S(2)}) %collective-permute-start.15) | collective-permute-done | bytes 327712 | tf_op jit(solution)/shard_map/ppermute | solution.py:142
  56.9 1.8 %collective-permute-start.17 = (bf16[40,4096]{1,0:T(8,128)(2,1)S(1)}, bf16[40,4096]{1,0:T(8,128)(2,1)S(1)}, u32[]{:S(2)}, u32[]{:S(2)}) collective-permute-start(bf16[40,4096]{1,0:T(8,128)(2,1)S(1)} %pad_maximum_fusion.13), channel_id=1, source_target_pairs={{0,8},{2,6},{8,16},{10,2},{16,24},{18,10},{24,28},{26,18},{28,20},... | collective-permute-start | bytes 983048 | tf_op jit(solution)/shard_map/ppermute | solution.py:142
  58.8 5.3 %collective-permute-done.17 = bf16[40,4096]{1,0:T(8,128)(2,1)S(1)} collective-permute-done((bf16[40,4096]{1,0:T(8,128)(2,1)S(1)}, bf16[40,4096]{1,0:T(8,128)(2,1)S(1)}, u32[]{:S(2)}, u32[]{:S(2)}) %collective-permute-start.17) | collective-permute-done | bytes 327712 | tf_op jit(solution)/shard_map/ppermute | solution.py:142
  66.8 4.3 %scores.1 = (bf16[512,256]{1,0:T(8,128)(2,1)S(1)}, bf16[512,256]{1,0:T(8,128)(2,1)S(1)}, f32[512,1]{1,0:T(8,128)S(1)}, bf16[256,4096]{1,0:T(8,128)(2,1)S(1)}) custom-call(bf16[128,4096]{1,0:T(8,128)(2,1)S(1)} %get-tuple-element.102.refs_0_, bf16[128,4096]{1,0:T(8,128)(2,1)S(1)} %slice_dynamic-update-slice_fusion.refs_1_, bf16[512,4096]{1,0:T(8,128)(2,1)S(1)} %copy-done, ...), custom_call_target="tpu_custom_call" | custom-call | flops 3221225472 | bytes 20971520 | tf_op jit(solution)/shard_map/scores/pallas_call | solution.py:198
  75.9 1.6 %collective-permute-start.41 = (bf16[2,2,16,2048]{3,2,0,1:T(8,128)(2,1)S(1)}, bf16[2,2,16,2048]{3,2,0,1:T(8,128)(2,1)S(1)}, u32[]{:S(2)}, u32[]{:S(2)}) collective-permute-start(bf16[2,2,16,2048]{3,2,0,1:T(8,128)(2,1)S(1)} %fusion.8), channel_id=1, source_target_pairs={{0,8},{2,10},{4,12},{6,14},{8,0},{10,2},{12,4},{14,6},{16,24},{18,... | collective-permute-start | bytes 786440 | tf_op jit(solution)/shard_map/ppermute | solution.py:273
  78.7 3.3 %multiply_convert_fusion = bf16[512,4096]{1,0:T(8,128)(2,1)} fusion(f32[512,4096]{1,0:T(8,128)S(1)} %fusion.57, bf16[512,256]{1,0:T(8,128)(2,1)S(1)} %get-tuple-element.63, bf16[256,4096]{1,0:T(8,128)(2,1)S(1)} %get-tuple-element.64), kind=kOutput, calls=%fused_computation | convolution fusion | flops 1080033280 | bytes 14942208 | tf_op jit(solution)/shard_map/dot_general | solution.py:280
  83.5 1.6 %collective-permute-start.38 = (bf16[2,16,2048]{2,1,0:T(8,128)(2,1)S(1)}, bf16[2,16,2048]{2,1,0:T(8,128)(2,1)S(1)}, u32[]{:S(2)}, u32[]{:S(2)}) collective-permute-start(bf16[2,16,2048]{2,1,0:T(8,128)(2,1)S(1)} %fusion.14), channel_id=1, source_target_pairs={{0,8},{2,10},{4,12},{6,14},{8,0},{10,2},{12,4},{14,6},{16,24},{18,... | collective-permute-start | bytes 393224 | tf_op jit(solution)/shard_map/ppermute | solution.py:273
  86.3 2.3 %collective-permute-done.38 = bf16[2,16,2048]{2,1,0:T(8,128)(2,1)S(1)} collective-permute-done((bf16[2,16,2048]{2,1,0:T(8,128)(2,1)S(1)}, bf16[2,16,2048]{2,1,0:T(8,128)(2,1)S(1)}, u32[]{:S(2)}, u32[]{:S(2)}) %collective-permute-start.38) | collective-permute-done | bytes 131104 | tf_op jit(solution)/shard_map/ppermute | solution.py:273
  88.6 2.6 %collective-permute-start.39 = (bf16[16,2048]{1,0:T(8,128)(2,1)S(1)}, bf16[16,2048]{1,0:T(8,128)(2,1)S(1)}, u32[]{:S(2)}, u32[]{:S(2)}) collective-permute-start(bf16[16,2048]{1,0:T(8,128)(2,1)S(1)} %fusion.30), channel_id=1, source_target_pairs={{0,16},{2,18},{4,20},{6,22},{8,24},{10,26},{12,28},{14,30},{16,0},... | collective-permute-start | bytes 196616 | tf_op jit(solution)/shard_map/ppermute | solution.py:273
  92.2 3.4 %collective-permute-done.39 = bf16[16,2048]{1,0:T(8,128)(2,1)S(1)} collective-permute-done((bf16[16,2048]{1,0:T(8,128)(2,1)S(1)}, bf16[16,2048]{1,0:T(8,128)(2,1)S(1)}, u32[]{:S(2)}, u32[]{:S(2)}) %collective-permute-start.39) | collective-permute-done | bytes 65568 | tf_op jit(solution)/shard_map/ppermute | solution.py:273
  95.6 1.5 %collective-permute-done.43 = bf16[16,2048]{1,0:T(8,128)(2,1)S(1)} collective-permute-done((bf16[16,2048]{1,0:T(8,128)(2,1)S(1)}, bf16[16,2048]{1,0:T(8,128)(2,1)S(1)}, u32[]{:S(2)}, u32[]{:S(2)}) %collective-permute-start.43) | collective-permute-done | bytes 65568 | tf_op jit(solution)/shard_map/ppermute | solution.py:273
  97.1 1.6 %collective-permute-start.44 = (f32[16,2048]{1,0:T(8,128)S(1)}, f32[16,2048]{1,0:T(8,128)S(1)}, u32[]{:S(2)}, u32[]{:S(2)}) collective-permute-start(f32[16,2048]{1,0:T(8,128)S(1)} %fusion.16), channel_id=1, source_target_pairs={{0,1},{1,0},{2,3},{3,2},{4,5},{5,4},{6,7},{7,6},{8,9},{9,8},{10,11... | collective-permute-start | bytes 393224 | tf_op jit(solution)/shard_map/ppermute | solution.py:287
  100.0 2.4 %collective-permute-done.44 = f32[16,2048]{1,0:T(8,128)S(1)} collective-permute-done((f32[16,2048]{1,0:T(8,128)S(1)}, f32[16,2048]{1,0:T(8,128)S(1)}, u32[]{:S(2)}, u32[]{:S(2)}) %collective-permute-start.44) | collective-permute-done | bytes 131104 | tf_op jit(solution)/shard_map/ppermute | solution.py:287
  (175 shorter events, 33.3 us)
Async XLA Ops:
  4.5 5.2 %collective-permute-start.2 = (bf16[64,4096]{1,0:T(8,128)(2,1)S(1)}, bf16[64,4096]{1,0:T(8,128)(2,1)S(1)}, u32[]{:S(2)}, u32[]{:S(2)}) collective-permute-start(bf16[64,4096]{1,0:T(8,128)(2,1)S(1)} %get-tuple-element.40), channel_id=1, source_target_pairs={{0,2},{2,0},{4,6},{6,4},{8,10},{10,8},{12,14},{14,12},{16,18},{18,... | collective-permute-start | bytes 1572872 | tf_op jit(solution)/shard_map/ppermute | solution.py:97
  6.5 5.9 %collective-permute-start.28 = (bf16[32,4096]{1,0:T(8,128)(2,1)S(1)}, bf16[32,4096]{1,0:T(8,128)(2,1)S(1)}, u32[]{:S(2)}, u32[]{:S(2)}) collective-permute-start(bf16[32,4096]{1,0:T(8,128)(2,1)S(1)} %get-tuple-element.86), channel_id=1, source_target_pairs={{0,2},{2,0},{4,6},{6,4},{8,10},{10,8},{12,14},{14,12},{16,18},{18,... | collective-permute-start | bytes 786440 | tf_op jit(solution)/shard_map/ppermute | solution.py:116
  7.0 7.7 %collective-permute-start.1 = (bf16[40,4096]{1,0:T(8,128)(2,1)S(1)}, bf16[40,4096]{1,0:T(8,128)(2,1)S(1)}, u32[]{:S(2)}, u32[]{:S(2)}) collective-permute-start(bf16[40,4096]{1,0:T(8,128)(2,1)S(1)} %pad_maximum_fusion), channel_id=1, source_target_pairs={{0,8},{2,6},{8,16},{10,2},{16,24},{18,10},{24,28},{26,18},{28,20},... | collective-permute-start | bytes 983048 | tf_op jit(solution)/shard_map/ppermute | solution.py:142
  9.8 8.3 %collective-permute-start.3 = (bf16[40,4096]{1,0:T(8,128)(2,1)S(1)}, bf16[40,4096]{1,0:T(8,128)(2,1)S(1)}, u32[]{:S(2)}, u32[]{:S(2)}) collective-permute-start(bf16[40,4096]{1,0:T(8,128)(2,1)S(1)} %pad_maximum_fusion.1), channel_id=1, source_target_pairs={{0,8},{2,6},{8,16},{10,2},{16,24},{18,10},{24,28},{26,18},{28,20},... | collective-permute-start | bytes 983048 | tf_op jit(solution)/shard_map/ppermute | solution.py:142
  11.8 15.0 %collective-permute-start.8 = (bf16[256,4096]{1,0:T(8,128)(2,1)S(1)}, bf16[256,4096]{1,0:T(8,128)(2,1)S(1)}, u32[]{:S(2)}, u32[]{:S(2)}) collective-permute-start(bf16[256,4096]{1,0:T(8,128)(2,1)S(1)} %copy-done.4), channel_id=1, source_target_pairs={{0,2},{2,0},{4,6},{6,4},{8,10},{10,8},{12,14},{14,12},{16,18},{18,... | collective-permute-start | bytes 6291464 | tf_op jit(solution)/shard_map/ppermute | solution.py:102
  12.3 9.7 %collective-permute-start.6 = (bf16[256,4096]{1,0:T(8,128)(2,1)S(1)}, bf16[256,4096]{1,0:T(8,128)(2,1)S(1)}, u32[]{:S(2)}, u32[]{:S(2)}) collective-permute-start(bf16[256,4096]{1,0:T(8,128)(2,1)S(1)} %copy-done.2), channel_id=1, source_target_pairs={{0,2},{2,0},{4,6},{6,4},{8,10},{10,8},{12,14},{14,12},{16,18},{18,... | collective-permute-start | bytes 6291464 | tf_op jit(solution)/shard_map/ppermute | solution.py:102
  14.9 7.1 %collective-permute-start.4 = (bf16[40,4096]{1,0:T(8,128)(2,1)S(1)}, bf16[40,4096]{1,0:T(8,128)(2,1)S(1)}, u32[]{:S(2)}, u32[]{:S(2)}) collective-permute-start(bf16[40,4096]{1,0:T(8,128)(2,1)S(1)} %pad_maximum_fusion.2), channel_id=1, source_target_pairs={{0,8},{2,6},{8,16},{10,2},{16,24},{18,10},{24,28},{26,18},{28,20},... | collective-permute-start | bytes 983048 | tf_op jit(solution)/shard_map/ppermute | solution.py:142
  19.7 7.1 %collective-permute-start.5 = (bf16[40,4096]{1,0:T(8,128)(2,1)S(1)}, bf16[40,4096]{1,0:T(8,128)(2,1)S(1)}, u32[]{:S(2)}, u32[]{:S(2)}) collective-permute-start(bf16[40,4096]{1,0:T(8,128)(2,1)S(1)} %pad_maximum_fusion.3), channel_id=1, source_target_pairs={{0,8},{2,6},{8,16},{10,2},{16,24},{18,10},{24,28},{26,18},{28,20},... | collective-permute-start | bytes 983048 | tf_op jit(solution)/shard_map/ppermute | solution.py:142
  22.4 6.6 %collective-permute-start.30 = (bf16[32,4096]{1,0:T(8,128)(2,1)S(1)}, bf16[32,4096]{1,0:T(8,128)(2,1)S(1)}, u32[]{:S(2)}, u32[]{:S(2)}) collective-permute-start(bf16[32,4096]{1,0:T(8,128)(2,1)S(1)} %get-tuple-element.82), channel_id=1, source_target_pairs={{0,2},{2,0},{4,6},{6,4},{8,10},{10,8},{12,14},{14,12},{16,18},{18,... | collective-permute-start | bytes 786440 | tf_op jit(solution)/shard_map/ppermute | solution.py:116
  22.5 7.8 %collective-permute-start.7 = (bf16[40,4096]{1,0:T(8,128)(2,1)S(1)}, bf16[40,4096]{1,0:T(8,128)(2,1)S(1)}, u32[]{:S(2)}, u32[]{:S(2)}) collective-permute-start(bf16[40,4096]{1,0:T(8,128)(2,1)S(1)} %pad_maximum_fusion.4), channel_id=1, source_target_pairs={{0,8},{2,6},{8,16},{10,2},{16,24},{18,10},{24,28},{26,18},{28,20},... | collective-permute-start | bytes 983048 | tf_op jit(solution)/shard_map/ppermute | solution.py:142
  27.3 7.1 %collective-permute-start.9 = (bf16[40,4096]{1,0:T(8,128)(2,1)S(1)}, bf16[40,4096]{1,0:T(8,128)(2,1)S(1)}, u32[]{:S(2)}, u32[]{:S(2)}) collective-permute-start(bf16[40,4096]{1,0:T(8,128)(2,1)S(1)} %pad_maximum_fusion.5), channel_id=1, source_target_pairs={{0,8},{2,6},{8,16},{10,2},{16,24},{18,10},{24,28},{26,18},{28,20},... | collective-permute-start | bytes 983048 | tf_op jit(solution)/shard_map/ppermute | solution.py:142
  30.4 5.9 %collective-permute-start.31 = (bf16[32,4096]{1,0:T(8,128)(2,1)S(1)}, bf16[32,4096]{1,0:T(8,128)(2,1)S(1)}, u32[]{:S(2)}, u32[]{:S(2)}) collective-permute-start(bf16[32,4096]{1,0:T(8,128)(2,1)S(1)} %get-tuple-element.80), channel_id=1, source_target_pairs={{0,2},{2,0},{4,6},{6,4},{8,10},{10,8},{12,14},{14,12},{16,18},{18,... | collective-permute-start | bytes 786440 | tf_op jit(solution)/shard_map/ppermute | solution.py:116
  30.6 7.4 %collective-permute-start.10 = (bf16[40,4096]{1,0:T(8,128)(2,1)S(1)}, bf16[40,4096]{1,0:T(8,128)(2,1)S(1)}, u32[]{:S(2)}, u32[]{:S(2)}) collective-permute-start(bf16[40,4096]{1,0:T(8,128)(2,1)S(1)} %pad_maximum_fusion.6), channel_id=1, source_target_pairs={{0,8},{2,6},{8,16},{10,2},{16,24},{18,10},{24,28},{26,18},{28,20},... | collective-permute-start | bytes 983048 | tf_op jit(solution)/shard_map/ppermute | solution.py:142
  34.7 7.1 %collective-permute-start.11 = (bf16[40,4096]{1,0:T(8,128)(2,1)S(1)}, bf16[40,4096]{1,0:T(8,128)(2,1)S(1)}, u32[]{:S(2)}, u32[]{:S(2)}) collective-permute-start(bf16[40,4096]{1,0:T(8,128)(2,1)S(1)} %pad_maximum_fusion.7), channel_id=1, source_target_pairs={{0,8},{2,6},{8,16},{10,2},{16,24},{18,10},{24,28},{26,18},{28,20},... | collective-permute-start | bytes 983048 | tf_op jit(solution)/shard_map/ppermute | solution.py:142
  38.1 5.7 %collective-permute-start.32 = (bf16[32,4096]{1,0:T(8,128)(2,1)S(1)}, bf16[32,4096]{1,0:T(8,128)(2,1)S(1)}, u32[]{:S(2)}, u32[]{:S(2)}) collective-permute-start(bf16[32,4096]{1,0:T(8,128)(2,1)S(1)} %get-tuple-element.78), channel_id=1, source_target_pairs={{0,2},{2,0},{4,6},{6,4},{8,10},{10,8},{12,14},{14,12},{16,18},{18,... | collective-permute-start | bytes 786440 | tf_op jit(solution)/shard_map/ppermute | solution.py:116
  38.2 7.1 %collective-permute-start.12 = (bf16[40,4096]{1,0:T(8,128)(2,1)S(1)}, bf16[40,4096]{1,0:T(8,128)(2,1)S(1)}, u32[]{:S(2)}, u32[]{:S(2)}) collective-permute-start(bf16[40,4096]{1,0:T(8,128)(2,1)S(1)} %pad_maximum_fusion.8), channel_id=1, source_target_pairs={{0,8},{2,6},{8,16},{10,2},{16,24},{18,10},{24,28},{26,18},{28,20},... | collective-permute-start | bytes 983048 | tf_op jit(solution)/shard_map/ppermute | solution.py:142
  42.1 7.1 %collective-permute-start.13 = (bf16[40,4096]{1,0:T(8,128)(2,1)S(1)}, bf16[40,4096]{1,0:T(8,128)(2,1)S(1)}, u32[]{:S(2)}, u32[]{:S(2)}) collective-permute-start(bf16[40,4096]{1,0:T(8,128)(2,1)S(1)} %pad_maximum_fusion.9), channel_id=1, source_target_pairs={{0,8},{2,6},{8,16},{10,2},{16,24},{18,10},{24,28},{26,18},{28,20},... | collective-permute-start | bytes 983048 | tf_op jit(solution)/shard_map/ppermute | solution.py:142
  45.4 5.7 %collective-permute-start.33 = (bf16[32,4096]{1,0:T(8,128)(2,1)S(1)}, bf16[32,4096]{1,0:T(8,128)(2,1)S(1)}, u32[]{:S(2)}, u32[]{:S(2)}) collective-permute-start(bf16[32,4096]{1,0:T(8,128)(2,1)S(1)} %get-tuple-element.76), channel_id=1, source_target_pairs={{0,2},{2,0},{4,6},{6,4},{8,10},{10,8},{12,14},{14,12},{16,18},{18,... | collective-permute-start | bytes 786440 | tf_op jit(solution)/shard_map/ppermute | solution.py:116
  45.6 7.1 %collective-permute-start.14 = (bf16[40,4096]{1,0:T(8,128)(2,1)S(1)}, bf16[40,4096]{1,0:T(8,128)(2,1)S(1)}, u32[]{:S(2)}, u32[]{:S(2)}) collective-permute-start(bf16[40,4096]{1,0:T(8,128)(2,1)S(1)} %pad_maximum_fusion.10), channel_id=1, source_target_pairs={{0,8},{2,6},{8,16},{10,2},{16,24},{18,10},{24,28},{26,18},{28,20},... | collective-permute-start | bytes 983048 | tf_op jit(solution)/shard_map/ppermute | solution.py:142
  49.5 7.1 %collective-permute-start.15 = (bf16[40,4096]{1,0:T(8,128)(2,1)S(1)}, bf16[40,4096]{1,0:T(8,128)(2,1)S(1)}, u32[]{:S(2)}, u32[]{:S(2)}) collective-permute-start(bf16[40,4096]{1,0:T(8,128)(2,1)S(1)} %pad_maximum_fusion.11), channel_id=1, source_target_pairs={{0,8},{2,6},{8,16},{10,2},{16,24},{18,10},{24,28},{26,18},{28,20},... | collective-permute-start | bytes 983048 | tf_op jit(solution)/shard_map/ppermute | solution.py:142
  52.8 5.9 %collective-permute-start.34 = (bf16[32,4096]{1,0:T(8,128)(2,1)S(1)}, bf16[32,4096]{1,0:T(8,128)(2,1)S(1)}, u32[]{:S(2)}, u32[]{:S(2)}) collective-permute-start(bf16[32,4096]{1,0:T(8,128)(2,1)S(1)} %get-tuple-element.74), channel_id=1, source_target_pairs={{0,2},{2,0},{4,6},{6,4},{8,10},{10,8},{12,14},{14,12},{16,18},{18,... | collective-permute-start | bytes 786440 | tf_op jit(solution)/shard_map/ppermute | solution.py:116
  53.0 11.3 %collective-permute-start.16 = (bf16[40,4096]{1,0:T(8,128)(2,1)S(1)}, bf16[40,4096]{1,0:T(8,128)(2,1)S(1)}, u32[]{:S(2)}, u32[]{:S(2)}) collective-permute-start(bf16[40,4096]{1,0:T(8,128)(2,1)S(1)} %pad_maximum_fusion.12), channel_id=1, source_target_pairs={{0,8},{2,6},{8,16},{10,2},{16,24},{18,10},{24,28},{26,18},{28,20},... | collective-permute-start | bytes 983048 | tf_op jit(solution)/shard_map/ppermute | solution.py:142
  56.9 7.3 %collective-permute-start.17 = (bf16[40,4096]{1,0:T(8,128)(2,1)S(1)}, bf16[40,4096]{1,0:T(8,128)(2,1)S(1)}, u32[]{:S(2)}, u32[]{:S(2)}) collective-permute-start(bf16[40,4096]{1,0:T(8,128)(2,1)S(1)} %pad_maximum_fusion.13), channel_id=1, source_target_pairs={{0,8},{2,6},{8,16},{10,2},{16,24},{18,10},{24,28},{26,18},{28,20},... | collective-permute-start | bytes 983048 | tf_op jit(solution)/shard_map/ppermute | solution.py:142
  58.7 5.8 %collective-permute-start.18 = (bf16[128,4096]{1,0:T(8,128)(2,1)S(1)}, bf16[128,4096]{1,0:T(8,128)(2,1)S(1)}, u32[]{:S(2)}, u32[]{:S(2)}) collective-permute-start(bf16[128,4096]{1,0:T(8,128)(2,1)S(1)} %get-tuple-element.106), channel_id=1, source_target_pairs={{0,2},{2,0},{4,6},{6,4},{8,10},{10,8},{12,14},{14,12},{16,18},{18,... | collective-permute-start | bytes 3145736 | tf_op jit(solution)/shard_map/ppermute | solution.py:144
  74.8 8.6 %collective-permute-start.37 = (bf16[2,2,16,2048]{3,2,0,1:T(8,128)(2,1)S(1)}, bf16[2,2,16,2048]{3,2,0,1:T(8,128)(2,1)S(1)}, u32[]{:S(2)}, u32[]{:S(2)}) collective-permute-start(bf16[2,2,16,2048]{3,2,0,1:T(8,128)(2,1)S(1)} %fusion.9), channel_id=1, source_target_pairs={{0,4},{2,6},{4,0},{6,2},{8,12},{10,14},{12,8},{14,10},{16,20},{18,... | collective-permute-start | bytes 786440 | tf_op jit(solution)/shard_map/ppermute | solution.py:273
  75.9 9.2 %collective-permute-start.41 = (bf16[2,2,16,2048]{3,2,0,1:T(8,128)(2,1)S(1)}, bf16[2,2,16,2048]{3,2,0,1:T(8,128)(2,1)S(1)}, u32[]{:S(2)}, u32[]{:S(2)}) collective-permute-start(bf16[2,2,16,2048]{3,2,0,1:T(8,128)(2,1)S(1)} %fusion.8), channel_id=1, source_target_pairs={{0,8},{2,10},{4,12},{6,14},{8,0},{10,2},{12,4},{14,6},{16,24},{18,... | collective-permute-start | bytes 786440 | tf_op jit(solution)/shard_map/ppermute | solution.py:273
  83.5 5.0 %collective-permute-start.38 = (bf16[2,16,2048]{2,1,0:T(8,128)(2,1)S(1)}, bf16[2,16,2048]{2,1,0:T(8,128)(2,1)S(1)}, u32[]{:S(2)}, u32[]{:S(2)}) collective-permute-start(bf16[2,16,2048]{2,1,0:T(8,128)(2,1)S(1)} %fusion.14), channel_id=1, source_target_pairs={{0,8},{2,10},{4,12},{6,14},{8,0},{10,2},{12,4},{14,6},{16,24},{18,... | collective-permute-start | bytes 393224 | tf_op jit(solution)/shard_map/ppermute | solution.py:273
  85.2 5.9 %collective-permute-start.42 = (bf16[2,16,2048]{2,1,0:T(8,128)(2,1)S(1)}, bf16[2,16,2048]{2,1,0:T(8,128)(2,1)S(1)}, u32[]{:S(2)}, u32[]{:S(2)}) collective-permute-start(bf16[2,16,2048]{2,1,0:T(8,128)(2,1)S(1)} %fusion.15), channel_id=1, source_target_pairs={{0,4},{2,6},{4,0},{6,2},{8,12},{10,14},{12,8},{14,10},{16,20},{18,... | collective-permute-start | bytes 393224 | tf_op jit(solution)/shard_map/ppermute | solution.py:273
  88.6 7.0 %collective-permute-start.39 = (bf16[16,2048]{1,0:T(8,128)(2,1)S(1)}, bf16[16,2048]{1,0:T(8,128)(2,1)S(1)}, u32[]{:S(2)}, u32[]{:S(2)}) collective-permute-start(bf16[16,2048]{1,0:T(8,128)(2,1)S(1)} %fusion.30), channel_id=1, source_target_pairs={{0,16},{2,18},{4,20},{6,22},{8,24},{10,26},{12,28},{14,30},{16,0},... | collective-permute-start | bytes 196616 | tf_op jit(solution)/shard_map/ppermute | solution.py:273
  91.2 5.9 %collective-permute-start.43 = (bf16[16,2048]{1,0:T(8,128)(2,1)S(1)}, bf16[16,2048]{1,0:T(8,128)(2,1)S(1)}, u32[]{:S(2)}, u32[]{:S(2)}) collective-permute-start(bf16[16,2048]{1,0:T(8,128)(2,1)S(1)} %fusion.31), channel_id=1, source_target_pairs={{0,16},{2,18},{4,20},{6,22},{8,24},{10,26},{12,28},{14,30},{16,0},... | collective-permute-start | bytes 196616 | tf_op jit(solution)/shard_map/ppermute | solution.py:273
  97.1 5.2 %collective-permute-start.44 = (f32[16,2048]{1,0:T(8,128)S(1)}, f32[16,2048]{1,0:T(8,128)S(1)}, u32[]{:S(2)}, u32[]{:S(2)}) collective-permute-start(f32[16,2048]{1,0:T(8,128)S(1)} %fusion.16), channel_id=1, source_target_pairs={{0,1},{1,0},{2,3},{3,2},{4,5},{5,4},{6,7},{7,6},{8,9},{9,8},{10,11... | collective-permute-start | bytes 393224 | tf_op jit(solution)/shard_map/ppermute | solution.py:287
  98.7 5.0 %collective-permute-start.40 = (f32[16,2048]{1,0:T(8,128)S(1)}, f32[16,2048]{1,0:T(8,128)S(1)}, u32[]{:S(2)}, u32[]{:S(2)}) collective-permute-start(f32[16,2048]{1,0:T(8,128)S(1)} %fusion.17), channel_id=1, source_target_pairs={{0,1},{1,0},{2,3},{3,2},{4,5},{5,4},{6,7},{7,6},{8,9},{9,8},{10,11... | collective-permute-start | bytes 393224 | tf_op jit(solution)/shard_map/ppermute | solution.py:287
  (22 other events, 62.9 us)
